TPU v7x, 32 devices: a whole 2x2x4 slice. The times are simulated.
32 devices in a mesh: groups: 2 (over x), user: 2 (over core), hist: 8 (over z, y).
Axes of the slice: x: 2, y: 2, z: 4, core: 2. Of those that a mesh axis runs over, the one named last changes fastest.
Arguments:
- item_table: bfloat16 [512, 1024], P('hist')
- item_ids: int32 [4, 512], P(('groups', 'user'), 'hist'), parts along dimension 0, may hold values from 0 to 511
- candidate_counts: int32 [4], P(('groups', 'user')), parts along dimension 0, may hold values from 256 to 512, as said below
- domain_ids: int32 [4, 512], P(('groups', 'user'), 'hist'), parts along dimension 0, may hold values from 0 to 1, as said below
- history_lengths: int32 [4], P(('groups', 'user')), parts along dimension 0, may hold values from 2048 to 4096, as said below
- history_keys: bfloat16 [4, 4096, 1024], P(('groups', 'user'), 'hist'), parts along dimension 0, may hold values from -9 to 9
- history_values: bfloat16 [4, 4096, 1024], P(('groups', 'user'), 'hist'), parts along dimension 0
- w_query: bfloat16 [1024, 1024], replicated, may hold values from -0.1875 to 0.1875
- w_gate: bfloat16 [1024, 1024], replicated, may hold values from -0.1875 to 0.1875
- w_out: bfloat16 [1024, 1024], replicated, may hold values from -0.1875 to 0.1875
- attn_gain: float32 [1024], replicated, may hold values from 0.1 to 1.9
- expert_weights: bfloat16 [2, 2, 1024, 1024], P('user'), may hold values from -0.1875 to 0.1875
Outputs:
- candidate_states: bfloat16 [4, 512, 1024], P(('groups', 'user'), 'hist'), parts along dimension 0
There are 2 independent parts, one for each index of `groups`. A program takes and returns all parts, laid end to end along the dimension named above; an argument that names none is the same for every part. Nothing has to cross between parts.
Inputs may be any that keep to these rules, and one draw needn't show every extreme that they name: `candidate_counts`: slots at or past a user's count are padding; some user has 512. `history_lengths`: positions at or past a user's length are not attended; some user has 4096. `domain_ids`: in each aligned block of 64 slots of a user, at most 48 slots name one domain; in the first block of every user exactly 48 name the same domain.
All inputs are finite; a program needn't handle non-finite values.
Results may differ from a plain program's by a relative error of at most 0.0059.
Values may be sent and summed in bfloat16 or wider, within the bound.
No kernel may reach another device: no remote copies, remote signals or barrier semaphores. Data moves between devices by JAX's collectives and lax.ppermute only.
A program may use at most 64 MiB of HBM per device.

v0:
```python
import jax
import jax.numpy as jnp
from jax import lax
from jax.sharding import PartitionSpec as P

H = 8
LAYERS = 2
CAP = 48


norm_eps = 1e-05


def passed_along(value, axis, steps):
    count = lax.axis_size(axis)
    pairs = [(source, (source + steps) % count) for source in range(count)]
    return lax.ppermute(value, axis, pairs)


def rms_scale(matrix):
    return matrix * lax.rsqrt(jnp.mean(matrix * matrix, axis=-1, keepdims=True) + norm_eps)


def attend_local(query_rows, key_rows, value_rows, key_live):
    row_count = query_rows.shape[0]
    feat_width = query_rows.shape[1]
    head_size = feat_width // H
    query_heads = query_rows.reshape(row_count, H, head_size)
    key_heads = key_rows.reshape(key_rows.shape[0], H, head_size)
    value_heads = value_rows.reshape(value_rows.shape[0], H, head_size)
    scores = jnp.einsum("rhd,khd->hrk", query_heads, key_heads, preferred_element_type=jnp.float32)
    weights = jnp.where(
        key_live[None, None, :], jax.nn.silu(scores * head_size ** (-0.5)), 0.0
    ).astype(jnp.bfloat16)
    mixed_rows = jnp.einsum(
        "hrk,khd->rhd", weights, value_heads, preferred_element_type=jnp.float32
    )
    return mixed_rows.reshape(row_count, feat_width)


def on_device(
    item_table,
    item_ids,
    candidate_counts,
    domain_ids,
    history_lengths,
    history_keys,
    history_values,
    w_query,
    w_gate,
    w_out,
    attn_gain,
    expert_weights,
):
    slot_count = item_ids.shape[1]
    feat_width = item_table.shape[1]
    hist_index = lax.axis_index("hist")
    hist_devices = lax.axis_size("hist")
    slot_index = hist_index * slot_count + jnp.arange(slot_count, dtype=jnp.int32)
    cand_live = slot_index < candidate_counts[0]
    flat_ids = item_ids[0]
    shard_rows = lax.all_gather(item_table, "hist", axis=0, tiled=True)
    columns = jnp.arange(shard_rows.shape[0], dtype=jnp.int32)
    onehot = (flat_ids[:, None] == columns[None, :]).astype(jnp.bfloat16)
    embed_float = jnp.dot(onehot, shard_rows, preferred_element_type=jnp.float32)
    normed = rms_scale(embed_float).astype(jnp.bfloat16)
    queries = jnp.dot(normed, w_query, preferred_element_type=jnp.float32).astype(jnp.bfloat16)
    gating = jax.nn.silu(jnp.dot(normed, w_gate, preferred_element_type=jnp.float32))
    key_block = history_keys[0]
    value_block = history_values[0]
    key_count = key_block.shape[0]
    key_live = hist_index * key_count + jnp.arange(key_count, dtype=jnp.int32) < history_lengths[0]

    def attend_all(query_block):
        return attend_local(query_block, key_block, value_block, key_live)

    empty_sums = jnp.zeros((slot_count, feat_width), jnp.float32)

    def cycle_step(step_index, cycle_state):
        moving, summed = cycle_state
        summed = summed + attend_all(moving)
        moving = passed_along(moving, "hist", 1)
        summed = passed_along(summed, "hist", 1)
        return (moving, summed)

    moving, attended = lax.fori_loop(0, hist_devices, cycle_step, (queries, empty_sums))
    gated_rows = (rms_scale(attended) * attn_gain * gating).astype(jnp.bfloat16)
    item_state = (
        embed_float + jnp.dot(gated_rows, w_out, preferred_element_type=jnp.float32)
    ).astype(jnp.bfloat16)
    owner_count = lax.axis_size("user")
    domains = domain_ids[0]
    owner_match = (
        domains[:, None] == jnp.arange(owner_count, dtype=jnp.int32)[None, :]
    ) & cand_live[:, None]
    match_int = owner_match.astype(jnp.int32)
    rank_slot = jnp.cumsum(match_int, axis=0) - match_int
    target = jnp.where(cand_live, domains * CAP + jnp.sum(rank_slot * match_int, axis=1), -1)
    placing = (jnp.arange(owner_count * CAP, dtype=jnp.int32)[:, None] == target[None, :]).astype(
        jnp.bfloat16
    )
    outgoing = (
        jnp.dot(placing, item_state, preferred_element_type=jnp.float32)
        .astype(jnp.bfloat16)
        .reshape(owner_count, CAP, feat_width)
    )
    layer_weights = expert_weights[0]
    arrived = lax.all_to_all(outgoing, "user", split_axis=0, concat_axis=0, tiled=True)
    source_count = arrived.shape[0]
    item_count = arrived.shape[1]
    current = arrived.reshape(source_count * item_count, feat_width)
    for layer_index in range(LAYERS):
        lifted = jnp.dot(current, layer_weights[layer_index], preferred_element_type=jnp.float32)
        current = (current.astype(jnp.float32) + jax.nn.silu(lifted)).astype(jnp.bfloat16)
    shaped = current.reshape(source_count, item_count, feat_width)
    returned = lax.all_to_all(shaped, "user", split_axis=0, concat_axis=0, tiled=True)
    finished = lax.dot_general(
        placing,
        returned.reshape(owner_count * CAP, feat_width),
        (((0,), (0,)), ((), ())),
        preferred_element_type=jnp.float32,
    )
    return finished.astype(jnp.bfloat16).reshape(1, slot_count, feat_width)


def solution(mesh):
    in_specs = (
        P("hist", None),
        P(("groups", "user"), "hist"),
        P(("groups", "user")),
        P(("groups", "user"), "hist"),
        P(("groups", "user")),
        P(("groups", "user"), "hist", None),
        P(("groups", "user"), "hist", None),
        P(),
        P(),
        P(),
        P(),
        P("user", None, None, None),
    )
    out_specs = P(("groups", "user"), "hist", None)
    return jax.shard_map(
        on_device, mesh=mesh, in_specs=in_specs, out_specs=out_specs, check_vma=False
    )
```

profile of v0, /device:TPU:0, one launch (start us, length us, event | category | flops | bytes accessed | tf_op | source)
XLA Modules:
  0.0 246.9 jit_solution(9591378355522389523)
XLA Ops:
  10.4 42.0 %all-gather.2.cloned.1.call-done = bf16[512,1024]{1,0:T(8,128)(2,1)} async-done(((bf16[64,1024]{1,0:T(8,128)(2,1)}), bf16[512,1024]{1,0:T(8,128)(2,1)}) %all-gather.2.cloned.1.call-update) | async-done | bytes 1048592 | tf_op jit(solution)/shard_map/all_gather | solution.py:62
  52.4 1.7 multiply_reduce_fusion.1
  54.1 2.2 convolution_convert_fusion.2
  56.3 168.6 %while.13 = (s32[]{:T(128)}, bf16[64,1024]{1,0:T(8,128)(2,1)S(1)}, f32[64,1024]{1,0:T(8,128)S(1)}, bf16[1,512,1024]{2,1,0:T(8,128)(2,1)S(1)}, bf16[1,512,1024]{2...) while((s32[]{:T(128)}, bf16[64,1024]{1,0:T(8,128)(2,1)S(1)}, f32[64,1024]{1,0:T(8,128)S(1)}, ...), condition=%wide.region_4.5_spmd.clone, body=%wide.region_3.4_spmd.clone.sunk | while | flops 136119296 | bytes 9307309 | solution.py:86
  56.3 2.5 %copy.48 = bf16[64,8,8,128]{3,2,1,0:T(8,128)(2,1)} copy(bf16[64,8,8,128]{3,1,2,0:T(8,128)(2,1)} %bitcast.72) | data formatting | bytes 2097152 | tf_op jit(solution)/shard_map/while
  58.8 1.3 copy.49
  61.4 3.2 %convolution_bitcast_fusion.2 = f32[8,8,8,128]{3,2,1,0:T(8,128)} fusion(bf16[512,8,128]{2,1,0:T(8,128)(2,1)} %bitcast.73, bf16[512,8,128]{2,1,0:T(8,128)(2,1)} %bitcast.74, pred[512]{0:T(512)(128)(4,1)S(1)} %add_compare_fusion.3, bf16[64,1024]{1,0:T(8,128)(2,1)} %copy.54), kind=kOutput, calls=%fused_computation.2.clone.1 | convolution fusion | flops 136052736 | bytes 2490880 | tf_op jit(solution)/shard_map/while/body/eval_jaxpr/hrk,khd->rhd/dot_general | solution.py:35
  64.6 1.7 bitcast_add_fusion.3
  66.9 1.4 collective-permute-start
  68.3 10.8 %collective-permute-done = bf16[64,1024]{1,0:T(8,128)(2,1)S(1)} collective-permute-done((bf16[64,1024]{1,0:T(8,128)(2,1)}, bf16[64,1024]{1,0:T(8,128)(2,1)S(1)}, u32[]{:S(2)}, u32[]{:S(2)}) %collective-permute-start) | collective-permute-done | bytes 131104 | tf_op jit(solution)/shard_map/while/body/eval_jaxpr/ppermute | solution.py:17
  79.1 2.5 %copy.48 = bf16[64,8,8,128]{3,2,1,0:T(8,128)(2,1)} copy(bf16[64,8,8,128]{3,1,2,0:T(8,128)(2,1)} %bitcast.72) | data formatting | bytes 2097152 | tf_op jit(solution)/shard_map/while
  81.6 1.3 copy.49
  84.2 3.2 %convolution_bitcast_fusion.2 = f32[8,8,8,128]{3,2,1,0:T(8,128)} fusion(bf16[512,8,128]{2,1,0:T(8,128)(2,1)} %bitcast.73, bf16[512,8,128]{2,1,0:T(8,128)(2,1)} %bitcast.74, pred[512]{0:T(512)(128)(4,1)S(1)} %add_compare_fusion.3, bf16[64,1024]{1,0:T(8,128)(2,1)} %copy.54), kind=kOutput, calls=%fused_computation.2.clone.1 | convolution fusion | flops 136052736 | bytes 2490880 | tf_op jit(solution)/shard_map/while/body/eval_jaxpr/hrk,khd->rhd/dot_general | solution.py:35
  87.4 1.7 bitcast_add_fusion.3
  89.5 11.3 %collective-permute-done = bf16[64,1024]{1,0:T(8,128)(2,1)S(1)} collective-permute-done((bf16[64,1024]{1,0:T(8,128)(2,1)}, bf16[64,1024]{1,0:T(8,128)(2,1)S(1)}, u32[]{:S(2)}, u32[]{:S(2)}) %collective-permute-start) | collective-permute-done | bytes 131104 | tf_op jit(solution)/shard_map/while/body/eval_jaxpr/ppermute | solution.py:17
  100.9 2.5 %copy.48 = bf16[64,8,8,128]{3,2,1,0:T(8,128)(2,1)} copy(bf16[64,8,8,128]{3,1,2,0:T(8,128)(2,1)} %bitcast.72) | data formatting | bytes 2097152 | tf_op jit(solution)/shard_map/while
  103.4 1.3 copy.49
  106.0 3.2 %convolution_bitcast_fusion.2 = f32[8,8,8,128]{3,2,1,0:T(8,128)} fusion(bf16[512,8,128]{2,1,0:T(8,128)(2,1)} %bitcast.73, bf16[512,8,128]{2,1,0:T(8,128)(2,1)} %bitcast.74, pred[512]{0:T(512)(128)(4,1)S(1)} %add_compare_fusion.3, bf16[64,1024]{1,0:T(8,128)(2,1)} %copy.54), kind=kOutput, calls=%fused_computation.2.clone.1 | convolution fusion | flops 136052736 | bytes 2490880 | tf_op jit(solution)/shard_map/while/body/eval_jaxpr/hrk,khd->rhd/dot_general | solution.py:35
  109.2 1.7 bitcast_add_fusion.3
  110.8 10.9 %collective-permute-done = bf16[64,1024]{1,0:T(8,128)(2,1)S(1)} collective-permute-done((bf16[64,1024]{1,0:T(8,128)(2,1)}, bf16[64,1024]{1,0:T(8,128)(2,1)S(1)}, u32[]{:S(2)}, u32[]{:S(2)}) %collective-permute-start) | collective-permute-done | bytes 131104 | tf_op jit(solution)/shard_map/while/body/eval_jaxpr/ppermute | solution.py:17
  121.8 2.5 %copy.48 = bf16[64,8,8,128]{3,2,1,0:T(8,128)(2,1)} copy(bf16[64,8,8,128]{3,1,2,0:T(8,128)(2,1)} %bitcast.72) | data formatting | bytes 2097152 | tf_op jit(solution)/shard_map/while
  124.2 1.3 copy.49
  126.9 3.2 %convolution_bitcast_fusion.2 = f32[8,8,8,128]{3,2,1,0:T(8,128)} fusion(bf16[512,8,128]{2,1,0:T(8,128)(2,1)} %bitcast.73, bf16[512,8,128]{2,1,0:T(8,128)(2,1)} %bitcast.74, pred[512]{0:T(512)(128)(4,1)S(1)} %add_compare_fusion.3, bf16[64,1024]{1,0:T(8,128)(2,1)} %copy.54), kind=kOutput, calls=%fused_computation.2.clone.1 | convolution fusion | flops 136052736 | bytes 2490880 | tf_op jit(solution)/shard_map/while/body/eval_jaxpr/hrk,khd->rhd/dot_general | solution.py:35
  130.1 1.7 bitcast_add_fusion.3
  131.7 10.7 %collective-permute-done = bf16[64,1024]{1,0:T(8,128)(2,1)S(1)} collective-permute-done((bf16[64,1024]{1,0:T(8,128)(2,1)}, bf16[64,1024]{1,0:T(8,128)(2,1)S(1)}, u32[]{:S(2)}, u32[]{:S(2)}) %collective-permute-start) | collective-permute-done | bytes 131104 | tf_op jit(solution)/shard_map/while/body/eval_jaxpr/ppermute | solution.py:17
  142.4 2.5 %copy.48 = bf16[64,8,8,128]{3,2,1,0:T(8,128)(2,1)} copy(bf16[64,8,8,128]{3,1,2,0:T(8,128)(2,1)} %bitcast.72) | data formatting | bytes 2097152 | tf_op jit(solution)/shard_map/while
  144.9 1.3 copy.49
  147.5 3.2 %convolution_bitcast_fusion.2 = f32[8,8,8,128]{3,2,1,0:T(8,128)} fusion(bf16[512,8,128]{2,1,0:T(8,128)(2,1)} %bitcast.73, bf16[512,8,128]{2,1,0:T(8,128)(2,1)} %bitcast.74, pred[512]{0:T(512)(128)(4,1)S(1)} %add_compare_fusion.3, bf16[64,1024]{1,0:T(8,128)(2,1)} %copy.54), kind=kOutput, calls=%fused_computation.2.clone.1 | convolution fusion | flops 136052736 | bytes 2490880 | tf_op jit(solution)/shard_map/while/body/eval_jaxpr/hrk,khd->rhd/dot_general | solution.py:35
  150.7 1.7 bitcast_add_fusion.3
  152.4 10.7 %collective-permute-done = bf16[64,1024]{1,0:T(8,128)(2,1)S(1)} collective-permute-done((bf16[64,1024]{1,0:T(8,128)(2,1)}, bf16[64,1024]{1,0:T(8,128)(2,1)S(1)}, u32[]{:S(2)}, u32[]{:S(2)}) %collective-permute-start) | collective-permute-done | bytes 131104 | tf_op jit(solution)/shard_map/while/body/eval_jaxpr/ppermute | solution.py:17
  163.0 2.5 %copy.48 = bf16[64,8,8,128]{3,2,1,0:T(8,128)(2,1)} copy(bf16[64,8,8,128]{3,1,2,0:T(8,128)(2,1)} %bitcast.72) | data formatting | bytes 2097152 | tf_op jit(solution)/shard_map/while
  168.1 3.2 %convolution_bitcast_fusion.2 = f32[8,8,8,128]{3,2,1,0:T(8,128)} fusion(bf16[512,8,128]{2,1,0:T(8,128)(2,1)} %bitcast.73, bf16[512,8,128]{2,1,0:T(8,128)(2,1)} %bitcast.74, pred[512]{0:T(512)(128)(4,1)S(1)} %add_compare_fusion.3, bf16[64,1024]{1,0:T(8,128)(2,1)} %copy.54), kind=kOutput, calls=%fused_computation.2.clone.1 | convolution fusion | flops 136052736 | bytes 2490880 | tf_op jit(solution)/shard_map/while/body/eval_jaxpr/hrk,khd->rhd/dot_general | solution.py:35
  171.3 1.7 bitcast_add_fusion.3
  173.0 10.7 %collective-permute-done = bf16[64,1024]{1,0:T(8,128)(2,1)S(1)} collective-permute-done((bf16[64,1024]{1,0:T(8,128)(2,1)}, bf16[64,1024]{1,0:T(8,128)(2,1)S(1)}, u32[]{:S(2)}, u32[]{:S(2)}) %collective-permute-start) | collective-permute-done | bytes 131104 | tf_op jit(solution)/shard_map/while/body/eval_jaxpr/ppermute | solution.py:17
  183.7 2.5 %copy.48 = bf16[64,8,8,128]{3,2,1,0:T(8,128)(2,1)} copy(bf16[64,8,8,128]{3,1,2,0:T(8,128)(2,1)} %bitcast.72) | data formatting | bytes 2097152 | tf_op jit(solution)/shard_map/while
  186.2 1.3 copy.49
  188.8 3.2 %convolution_bitcast_fusion.2 = f32[8,8,8,128]{3,2,1,0:T(8,128)} fusion(bf16[512,8,128]{2,1,0:T(8,128)(2,1)} %bitcast.73, bf16[512,8,128]{2,1,0:T(8,128)(2,1)} %bitcast.74, pred[512]{0:T(512)(128)(4,1)S(1)} %add_compare_fusion.3, bf16[64,1024]{1,0:T(8,128)(2,1)} %copy.54), kind=kOutput, calls=%fused_computation.2.clone.1 | convolution fusion | flops 136052736 | bytes 2490880 | tf_op jit(solution)/shard_map/while/body/eval_jaxpr/hrk,khd->rhd/dot_general | solution.py:35
  192.0 1.7 bitcast_add_fusion.3
  193.7 10.7 %collective-permute-done = bf16[64,1024]{1,0:T(8,128)(2,1)S(1)} collective-permute-done((bf16[64,1024]{1,0:T(8,128)(2,1)}, bf16[64,1024]{1,0:T(8,128)(2,1)S(1)}, u32[]{:S(2)}, u32[]{:S(2)}) %collective-permute-start) | collective-permute-done | bytes 131104 | tf_op jit(solution)/shard_map/while/body/eval_jaxpr/ppermute | solution.py:17
  204.3 2.5 %copy.48 = bf16[64,8,8,128]{3,2,1,0:T(8,128)(2,1)} copy(bf16[64,8,8,128]{3,1,2,0:T(8,128)(2,1)} %bitcast.72) | data formatting | bytes 2097152 | tf_op jit(solution)/shard_map/while
  206.8 1.3 copy.49
  209.4 3.2 %convolution_bitcast_fusion.2 = f32[8,8,8,128]{3,2,1,0:T(8,128)} fusion(bf16[512,8,128]{2,1,0:T(8,128)(2,1)} %bitcast.73, bf16[512,8,128]{2,1,0:T(8,128)(2,1)} %bitcast.74, pred[512]{0:T(512)(128)(4,1)S(1)} %add_compare_fusion.3, bf16[64,1024]{1,0:T(8,128)(2,1)} %copy.54), kind=kOutput, calls=%fused_computation.2.clone.1 | convolution fusion | flops 136052736 | bytes 2490880 | tf_op jit(solution)/shard_map/while/body/eval_jaxpr/hrk,khd->rhd/dot_general | solution.py:35
  212.6 1.7 bitcast_add_fusion.3
  214.3 10.7 %collective-permute-done = bf16[64,1024]{1,0:T(8,128)(2,1)S(1)} collective-permute-done((bf16[64,1024]{1,0:T(8,128)(2,1)}, bf16[64,1024]{1,0:T(8,128)(2,1)S(1)}, u32[]{:S(2)}, u32[]{:S(2)}) %collective-permute-start) | collective-permute-done | bytes 131104 | tf_op jit(solution)/shard_map/while/body/eval_jaxpr/ppermute | solution.py:17
  225.1 2.2 fusion.46
  228.1 3.9 %all_to_all.10 = bf16[2,48,1024]{2,1,0:T(8,128)(2,1)S(1)} all-to-all(bf16[2,48,1024]{2,1,0:T(8,128)(2,1)S(1)} %bitcast.75), channel_id=1, replica_groups=mesh['groups'=2,'user'=2,'hist'=8] {'user'}, dimensions={0} | all-to-all | bytes 393216 | tf_op jit(solution)/shard_map/all_to_all | solution.py:108
  231.9 2.3 add_convert_fusion.1
  235.3 3.9 %all_to_all.11 = bf16[2,48,1024]{2,1,0:T(8,128)(2,1)S(1)} all-to-all(bf16[2,48,1024]{2,1,0:T(8,128)(2,1)S(1)} %bitcast.78), channel_id=1, replica_groups=mesh['groups'=2,'user'=2,'hist'=8] {'user'}, dimensions={0} | all-to-all | bytes 393216 | tf_op jit(solution)/shard_map/all_to_all | solution.py:116
  (66 shorter events, 18.8 us)
Async XLA Ops:
  6.5 220.8 %copy-start = (bf16[1024,1024]{1,0:T(8,128)(2,1)S(1)}, bf16[1024,1024]{1,0:T(8,128)(2,1)}, u32[]{:S(2)}) copy-start(bf16[1024,1024]{1,0:T(8,128)(2,1)} %param.23) | copy-start | bytes 6291460
  6.5 45.8 %all-gather.2.cloned.1.call-start = ((), (), s32[]{:S(2)}) async-start(), calls=%async_computation.2 | async-start | bytes 1179648 | tf_op jit(solution)/shard_map/all_gather | solution.py:62
  8.7 47.7 %copy-start.1 = (bf16[1,512,1024]{2,1,0:T(8,128)(2,1)S(1)}, bf16[1,512,1024]{2,1,0:T(8,128)(2,1)}, u32[]{:S(2)}) copy-start(bf16[1,512,1024]{2,1,0:T(8,128)(2,1)} %param.19) | copy-start | bytes 3145732
  54.1 2.2 copy-start.2
  66.3 12.8 %collective-permute-start.1 = (f32[64,1024]{1,0:T(8,128)}, f32[64,1024]{1,0:T(8,128)S(1)}, u32[]{:S(2)}, u32[]{:S(2)}) collective-permute-start(f32[64,1024]{1,0:T(8,128)} %bitcast_add_fusion.3), channel_id=1, source_target_pairs={{0,1},{1,2},{2,3},{3,4},{4,5},{5,6},{6,7},{7,0},{8,9},{9,10},{10,1... | collective-permute-start | bytes 786440 | tf_op jit(solution)/shard_map/while/body/eval_jaxpr/ppermute | solution.py:17
  66.9 12.2 %collective-permute-start = (bf16[64,1024]{1,0:T(8,128)(2,1)}, bf16[64,1024]{1,0:T(8,128)(2,1)S(1)}, u32[]{:S(2)}, u32[]{:S(2)}) collective-permute-start(bf16[64,1024]{1,0:T(8,128)(2,1)} %copy.54), channel_id=1, source_target_pairs={{0,1},{1,2},{2,3},{3,4},{4,5},{5,6},{6,7},{7,0},{8,9},{9,10},{10,1... | collective-permute-start | bytes 393224 | tf_op jit(solution)/shard_map/while/body/eval_jaxpr/ppermute | solution.py:17
  89.0 11.8 %collective-permute-start.1 = (f32[64,1024]{1,0:T(8,128)}, f32[64,1024]{1,0:T(8,128)S(1)}, u32[]{:S(2)}, u32[]{:S(2)}) collective-permute-start(f32[64,1024]{1,0:T(8,128)} %bitcast_add_fusion.3), channel_id=1, source_target_pairs={{0,1},{1,2},{2,3},{3,4},{4,5},{5,6},{6,7},{7,0},{8,9},{9,10},{10,1... | collective-permute-start | bytes 786440 | tf_op jit(solution)/shard_map/while/body/eval_jaxpr/ppermute | solution.py:17
  89.0 11.8 %collective-permute-start = (bf16[64,1024]{1,0:T(8,128)(2,1)}, bf16[64,1024]{1,0:T(8,128)(2,1)S(1)}, u32[]{:S(2)}, u32[]{:S(2)}) collective-permute-start(bf16[64,1024]{1,0:T(8,128)(2,1)} %copy.54), channel_id=1, source_target_pairs={{0,1},{1,2},{2,3},{3,4},{4,5},{5,6},{6,7},{7,0},{8,9},{9,10},{10,1... | collective-permute-start | bytes 393224 | tf_op jit(solution)/shard_map/while/body/eval_jaxpr/ppermute | solution.py:17
  110.8 10.9 %collective-permute-start.1 = (f32[64,1024]{1,0:T(8,128)}, f32[64,1024]{1,0:T(8,128)S(1)}, u32[]{:S(2)}, u32[]{:S(2)}) collective-permute-start(f32[64,1024]{1,0:T(8,128)} %bitcast_add_fusion.3), channel_id=1, source_target_pairs={{0,1},{1,2},{2,3},{3,4},{4,5},{5,6},{6,7},{7,0},{8,9},{9,10},{10,1... | collective-permute-start | bytes 786440 | tf_op jit(solution)/shard_map/while/body/eval_jaxpr/ppermute | solution.py:17
  110.8 10.9 %collective-permute-start = (bf16[64,1024]{1,0:T(8,128)(2,1)}, bf16[64,1024]{1,0:T(8,128)(2,1)S(1)}, u32[]{:S(2)}, u32[]{:S(2)}) collective-permute-start(bf16[64,1024]{1,0:T(8,128)(2,1)} %copy.54), channel_id=1, source_target_pairs={{0,1},{1,2},{2,3},{3,4},{4,5},{5,6},{6,7},{7,0},{8,9},{9,10},{10,1... | collective-permute-start | bytes 393224 | tf_op jit(solution)/shard_map/while/body/eval_jaxpr/ppermute | solution.py:17
  131.7 10.7 %collective-permute-start.1 = (f32[64,1024]{1,0:T(8,128)}, f32[64,1024]{1,0:T(8,128)S(1)}, u32[]{:S(2)}, u32[]{:S(2)}) collective-permute-start(f32[64,1024]{1,0:T(8,128)} %bitcast_add_fusion.3), channel_id=1, source_target_pairs={{0,1},{1,2},{2,3},{3,4},{4,5},{5,6},{6,7},{7,0},{8,9},{9,10},{10,1... | collective-permute-start | bytes 786440 | tf_op jit(solution)/shard_map/while/body/eval_jaxpr/ppermute | solution.py:17
  131.7 10.7 %collective-permute-start = (bf16[64,1024]{1,0:T(8,128)(2,1)}, bf16[64,1024]{1,0:T(8,128)(2,1)S(1)}, u32[]{:S(2)}, u32[]{:S(2)}) collective-permute-start(bf16[64,1024]{1,0:T(8,128)(2,1)} %copy.54), channel_id=1, source_target_pairs={{0,1},{1,2},{2,3},{3,4},{4,5},{5,6},{6,7},{7,0},{8,9},{9,10},{10,1... | collective-permute-start | bytes 393224 | tf_op jit(solution)/shard_map/while/body/eval_jaxpr/ppermute | solution.py:17
  152.4 10.7 %collective-permute-start.1 = (f32[64,1024]{1,0:T(8,128)}, f32[64,1024]{1,0:T(8,128)S(1)}, u32[]{:S(2)}, u32[]{:S(2)}) collective-permute-start(f32[64,1024]{1,0:T(8,128)} %bitcast_add_fusion.3), channel_id=1, source_target_pairs={{0,1},{1,2},{2,3},{3,4},{4,5},{5,6},{6,7},{7,0},{8,9},{9,10},{10,1... | collective-permute-start | bytes 786440 | tf_op jit(solution)/shard_map/while/body/eval_jaxpr/ppermute | solution.py:17
  152.4 10.7 %collective-permute-start = (bf16[64,1024]{1,0:T(8,128)(2,1)}, bf16[64,1024]{1,0:T(8,128)(2,1)S(1)}, u32[]{:S(2)}, u32[]{:S(2)}) collective-permute-start(bf16[64,1024]{1,0:T(8,128)(2,1)} %copy.54), channel_id=1, source_target_pairs={{0,1},{1,2},{2,3},{3,4},{4,5},{5,6},{6,7},{7,0},{8,9},{9,10},{10,1... | collective-permute-start | bytes 393224 | tf_op jit(solution)/shard_map/while/body/eval_jaxpr/ppermute | solution.py:17
  173.0 10.7 %collective-permute-start.1 = (f32[64,1024]{1,0:T(8,128)}, f32[64,1024]{1,0:T(8,128)S(1)}, u32[]{:S(2)}, u32[]{:S(2)}) collective-permute-start(f32[64,1024]{1,0:T(8,128)} %bitcast_add_fusion.3), channel_id=1, source_target_pairs={{0,1},{1,2},{2,3},{3,4},{4,5},{5,6},{6,7},{7,0},{8,9},{9,10},{10,1... | collective-permute-start | bytes 786440 | tf_op jit(solution)/shard_map/while/body/eval_jaxpr/ppermute | solution.py:17
  173.0 10.7 %collective-permute-start = (bf16[64,1024]{1,0:T(8,128)(2,1)}, bf16[64,1024]{1,0:T(8,128)(2,1)S(1)}, u32[]{:S(2)}, u32[]{:S(2)}) collective-permute-start(bf16[64,1024]{1,0:T(8,128)(2,1)} %copy.54), channel_id=1, source_target_pairs={{0,1},{1,2},{2,3},{3,4},{4,5},{5,6},{6,7},{7,0},{8,9},{9,10},{10,1... | collective-permute-start | bytes 393224 | tf_op jit(solution)/shard_map/while/body/eval_jaxpr/ppermute | solution.py:17
  193.6 10.7 %collective-permute-start.1 = (f32[64,1024]{1,0:T(8,128)}, f32[64,1024]{1,0:T(8,128)S(1)}, u32[]{:S(2)}, u32[]{:S(2)}) collective-permute-start(f32[64,1024]{1,0:T(8,128)} %bitcast_add_fusion.3), channel_id=1, source_target_pairs={{0,1},{1,2},{2,3},{3,4},{4,5},{5,6},{6,7},{7,0},{8,9},{9,10},{10,1... | collective-permute-start | bytes 786440 | tf_op jit(solution)/shard_map/while/body/eval_jaxpr/ppermute | solution.py:17
  193.7 10.7 %collective-permute-start = (bf16[64,1024]{1,0:T(8,128)(2,1)}, bf16[64,1024]{1,0:T(8,128)(2,1)S(1)}, u32[]{:S(2)}, u32[]{:S(2)}) collective-permute-start(bf16[64,1024]{1,0:T(8,128)(2,1)} %copy.54), channel_id=1, source_target_pairs={{0,1},{1,2},{2,3},{3,4},{4,5},{5,6},{6,7},{7,0},{8,9},{9,10},{10,1... | collective-permute-start | bytes 393224 | tf_op jit(solution)/shard_map/while/body/eval_jaxpr/ppermute | solution.py:17
  214.3 10.7 %collective-permute-start.1 = (f32[64,1024]{1,0:T(8,128)}, f32[64,1024]{1,0:T(8,128)S(1)}, u32[]{:S(2)}, u32[]{:S(2)}) collective-permute-start(f32[64,1024]{1,0:T(8,128)} %bitcast_add_fusion.3), channel_id=1, source_target_pairs={{0,1},{1,2},{2,3},{3,4},{4,5},{5,6},{6,7},{7,0},{8,9},{9,10},{10,1... | collective-permute-start | bytes 786440 | tf_op jit(solution)/shard_map/while/body/eval_jaxpr/ppermute | solution.py:17
  214.3 10.7 %collective-permute-start = (bf16[64,1024]{1,0:T(8,128)(2,1)}, bf16[64,1024]{1,0:T(8,128)(2,1)S(1)}, u32[]{:S(2)}, u32[]{:S(2)}) collective-permute-start(bf16[64,1024]{1,0:T(8,128)(2,1)} %copy.54), channel_id=1, source_target_pairs={{0,1},{1,2},{2,3},{3,4},{4,5},{5,6},{6,7},{7,0},{8,9},{9,10},{10,1... | collective-permute-start | bytes 393224 | tf_op jit(solution)/shard_map/while/body/eval_jaxpr/ppermute | solution.py:17
  225.0 2.4 copy-start.3
  225.0 2.4 copy-start.4
  231.9 2.8 %copy-start.5 = (bf16[1,2,1024,1024]{3,2,1,0:T(8,128)(2,1)S(1)}, bf16[1,2,1024,1024]{3,2,1,0:T(8,128)(2,1)}, u32[]{:S(2)}) copy-start(bf16[1,2,1024,1024]{3,2,1,0:T(8,128)(2,1)} %param.25) | copy-start | bytes 12582916
Sparse Core Ops, SparseCore 0:
  9.5 42.8 all-gather.1
where the time goes:
time: 248 us; the launch traced here: 247 us
  waiting for transfers between devices  129 us (52%)
  local copies, waits for them, and re-layouts  36.1 us (15%)
  matrix products  36 us (15%)
  other arithmetic  21.1 us (9%)
  between operations  14.2 us (6%)
  blocking collectives  7.78 us (3%)
  starting transfers between devices  2.53 us (1%)
    ppermute x16, waiting for transfers between devices, passed_along(): return lax.ppermute(value, axis, pairs)  86.4 us
    all_gather x1, waiting for transfers between devices, on_device(): shard_rows = lax.all_gather(item_table, 'hist', axis=0, tiled=True)  42 us
    while x24, local copies, waits for them, and re-layouts  35.5 us
    dot_general x8, matrix products, attend_local(): jnp.einsum('hrk,khd->rhd', weights, value_heads, preferred_element_type=j...  25.6 us
    add x8, other arithmetic, cycle_step(): summed = summed + attend_all(moving)  13.3 us
    lt x8, other arithmetic, on_device(): hist_index * key_count + jnp.arange(key_count, dtype=jnp.int32)  5.2 us
  transfers between devices with their start and end apart: 17, of which 9 were waited for; matrix products, arithmetic and copies ran while one was open for 1% of the time, Pallas kernels for 0%

commit v1 on v0

v1 whole, which is shorter than its diff:
```python
import functools

import jax
import jax.numpy as jnp
from jax import lax
from jax.experimental import pallas as pl
from jax.experimental.pallas import tpu as pltpu
from jax.sharding import PartitionSpec as P

H = 8
LAYERS = 2
ID_ROWS = 16
ID_BASE = 128

norm_eps = 1e-05
F32 = jnp.float32
BF16 = jnp.bfloat16


def rms_scale(matrix):
    return matrix * lax.rsqrt(jnp.mean(matrix * matrix, axis=-1, keepdims=True) + norm_eps)


def swapped(value, flip):
    count = lax.axis_size("hist")
    return lax.ppermute(value, "hist", [(i, i ^ flip) for i in range(count)])


def swapped_by_user(value, flips):
    count = lax.axis_size("hist")
    pairs = [
        (u * count + i, u * count + (i ^ flip)) for u, flip in enumerate(flips) for i in range(count)
    ]
    return lax.ppermute(value, ("user", "hist"), pairs)


def from_user(value, steps):
    count = lax.axis_size("user")
    return lax.ppermute(value, "user", [((i + steps) % count, i) for i in range(count)])


def silu_half(half_scores):
    return half_scores + half_scores * jnp.tanh(half_scores)


def attend_kernel(live_ref, rows_ref, w_query_ref, keys_ref, values_ref, sums_ref):
    feat_width = rows_ref.shape[1]
    head_size = feat_width // H
    normed = rms_scale(rows_ref[...].astype(F32)).astype(BF16)
    queries = jnp.dot(normed, w_query_ref[...], preferred_element_type=F32).astype(BF16)
    place = lax.broadcasted_iota(jnp.int32, (values_ref.shape[1], head_size), 0)
    live = place < live_ref[0]
    for head in range(H):
        cut = slice(head * head_size, (head + 1) * head_size)
        scores = lax.dot_general(
            queries[:, cut], keys_ref[0, :, cut], (((1,), (1,)), ((), ())), preferred_element_type=F32
        )
        weights = silu_half(scores * (0.5 * head_size ** (-0.5))).astype(BF16)
        values = jnp.where(live, values_ref[0, :, cut].astype(F32), 0.0).astype(BF16)
        sums_ref[:, cut] = jnp.dot(weights, values, preferred_element_type=F32).astype(BF16)


def attend(rows, live_count, w_query, keys, values):
    return pl.pallas_call(
        attend_kernel,
        out_shape=jax.ShapeDtypeStruct(rows.shape, BF16),
        in_specs=[pl.BlockSpec(memory_space=pltpu.SMEM)] + [pl.BlockSpec(memory_space=pltpu.VMEM)] * 4,
        out_specs=pl.BlockSpec(memory_space=pltpu.VMEM),
        compiler_params=pltpu.CompilerParams(vmem_limit_bytes=48 * 1024 * 1024),
        cost_estimate=pl.CostEstimate(
            flops=2 * rows.shape[0] * rows.shape[1] * (rows.shape[1] + 2 * keys.shape[1]),
            bytes_accessed=2 * (keys.size + values.size + w_query.size + 2 * rows.size),
            transcendentals=rows.shape[0] * keys.shape[1] * H,
        ),
        name="attend",
    )(live_count, rows, w_query, keys, values)


def chosen(ids, items, table):
    onehot = (ids[:, None] == items[None, :]).astype(BF16)
    return jnp.dot(onehot, table, preferred_element_type=F32)


def on_device(
    item_table,
    item_ids,
    candidate_counts,
    domain_ids,
    history_lengths,
    history_keys,
    history_values,
    w_query,
    w_gate,
    w_out,
    attn_gain,
    expert_weights,
):
    slot_count = item_ids.shape[1]
    shard_rows, feat_width = item_table.shape
    hist_devices = lax.axis_size("hist")
    users = lax.axis_size("user")
    hist_index = lax.axis_index("hist")
    user_index = lax.axis_index("user")
    bits = hist_devices.bit_length() - 1

    expert_sets = [expert_weights[0]] + [from_user(expert_weights[0], s) for s in range(1, users)]

    own_ids = item_ids[0]
    digits = jnp.concatenate([own_ids // ID_BASE, own_ids % ID_BASE]).astype(BF16)
    by_turn = [digits] + [from_user(digits, s) for s in range(1, users)]
    by_turn = jnp.stack(by_turn)
    by_user = by_turn[(jnp.arange(users) - user_index) % users].reshape(1, -1)
    id_block = jnp.pad(by_user, ((0, ID_ROWS - 1), (0, feat_width - by_user.shape[1])))
    payload = jnp.concatenate([item_table, id_block], axis=0)

    whole = (hist_devices - 1) // users
    groups = [tuple(1 + users * g + u for u in range(users)) for g in range(whole)]
    rest = list(range(1 + users * whole, hist_devices))
    pieces = []
    for group in groups:
        pieces.append(swapped_by_user(payload, group))
    part_rows = shard_rows // users
    if rest:
        part = lax.dynamic_slice_in_dim(item_table, user_index * part_rows, part_rows, 0)
        part = jnp.concatenate([part, id_block], axis=0)
        for flip in rest:
            pieces.append(swapped(part, flip))
    fetched = jnp.concatenate(pieces, axis=0)
    traded = [fetched] + [from_user(fetched, s) for s in range(1, users)]

    row_sets = [item_table]
    item_sets = [hist_index * shard_rows + jnp.arange(shard_rows, dtype=jnp.int32)]
    ids_of = [[None] * users for _ in range(hist_devices)]
    ids_of[0] = [by_user[0]] * users
    for s, block in enumerate(traded):
        owner = (user_index + s) % users
        at = 0
        for group in groups:
            flip = 1 + users * (group[0] // users) + owner
            row_sets.append(block[at : at + shard_rows])
            item_sets.append((hist_index ^ flip) * shard_rows + jnp.arange(shard_rows, dtype=jnp.int32))
            for u in range(users):
                ids_of[group[u]][s] = (owner == u, block[at + shard_rows])
            at += shard_rows + ID_ROWS
        for flip in rest:
            row_sets.append(block[at : at + part_rows])
            item_sets.append(
                (hist_index ^ flip) * shard_rows + owner * part_rows + jnp.arange(part_rows, dtype=jnp.int32)
            )
            ids_of[flip][s] = (owner == 0, block[at + part_rows])
            at += part_rows + ID_ROWS
    table = jnp.concatenate(row_sets, axis=0)
    items = jnp.concatenate(item_sets)

    def ids_at(flip):
        if flip == 0:
            return own_ids
        row = ids_of[flip][0][1]
        for mine, other in ids_of[flip][1:]:
            row = jnp.where(mine, other, row)
        pair = lax.dynamic_slice_in_dim(row, user_index * 2 * slot_count, 2 * slot_count)
        pair = pair.astype(jnp.int32)
        return pair[:slot_count] * ID_BASE + pair[slot_count:]

    all_ids = jnp.stack([ids_at(flip) for flip in range(hist_devices)])

    live_count = jnp.clip(history_lengths - hist_index * history_keys.shape[1], 0, history_keys.shape[1])
    sums = attend(table, live_count.astype(jnp.int32), w_query, history_keys, history_values)

    orders = [list(range(bits)), list(range(bits))]
    if bits > 1:
        orders[1][:2] = [1, 0]
    width = feat_width // 2
    held = []
    for side, order in enumerate(orders):
        flips = [sum(((r >> (bits - 1 - t)) & 1) << bit for t, bit in enumerate(order)) for r in range(hist_devices)]
        ids = all_ids[jnp.array(flips)].reshape(-1)
        picked = chosen(ids, items, sums[:, side * width : (side + 1) * width]).astype(BF16)
        held.append(picked)

    def halved(kept, sent, flip):
        return kept.astype(F32) + swapped(sent, flip).astype(F32)

    for turn in range(bits - 1):
        for side, order in enumerate(orders):
            half = held[side].shape[0] // 2
            held[side] = halved(held[side][:half], held[side][half:].astype(BF16), 1 << order[turn])
    final = jnp.concatenate(held, axis=1)
    if bits:
        half = final.shape[0] // 2
        final = halved(final[:half], final[half:].astype(BF16), 1 << (bits - 1))
    attended = final.astype(F32)

    embed_float = chosen(own_ids, items, table)
    normed = rms_scale(embed_float).astype(BF16)
    gating = jax.nn.silu(jnp.dot(normed, w_gate, preferred_element_type=F32))
    gated_rows = (rms_scale(attended) * attn_gain * gating).astype(BF16)
    item_state = (embed_float + jnp.dot(gated_rows, w_out, preferred_element_type=F32)).astype(BF16)

    domains = domain_ids[0]
    slot_index = hist_index * slot_count + jnp.arange(slot_count, dtype=jnp.int32)
    cand_live = slot_index < candidate_counts[0]
    result = jnp.zeros(item_state.shape, BF16)
    for s, layer_weights in enumerate(expert_sets):
        current = item_state
        for layer_index in range(LAYERS):
            lifted = jnp.dot(current, layer_weights[layer_index], preferred_element_type=F32)
            current = (current.astype(F32) + jax.nn.silu(lifted)).astype(BF16)
        wanted = (domains == (user_index + s) % users) & cand_live
        result = jnp.where(wanted[:, None], current, result)
    return result[None]


def solution(mesh):
    in_specs = (
        P("hist", None),
        P(("groups", "user"), "hist"),
        P(("groups", "user")),
        P(("groups", "user"), "hist"),
        P(("groups", "user")),
        P(("groups", "user"), "hist", None),
        P(("groups", "user"), "hist", None),
        P(),
        P(),
        P(),
        P(),
        P("user", None, None, None),
    )
    out_specs = P(("groups", "user"), "hist", None)
    return jax.shard_map(
        on_device, mesh=mesh, in_specs=in_specs, out_specs=out_specs, check_vma=False
    )
```

time: 248 us -> 78.9 us (0.32)
  waiting for transfers between devices: 129 us -> 26.6 us
  local copies, waits for them, and re-layouts: 36.1 us -> 10.3 us
  matrix products: 36 us -> 13.1 us
  other arithmetic: 21.1 us -> 4.9 us
  starting transfers between devices: 2.53 us -> 16.5 us
  between operations: 14.2 us -> 1.62 us
  blocking collectives: 7.78 us -> 0 us
  Pallas kernels: 0 us -> 5.35 us
    ppermute x16 -> x12, waiting for transfers between devices: 86.4 us -> 26.6 us  [the longest x6 25 us: swapped(): return lax.ppermute(value, 'hist', [(i, i ^ flip) for i in range(count)])]
    all_gather x1 -> x0, waiting for transfers between devices: 42 us -> none  [on_device(): shard_rows = lax.all_gather(item_table, 'hist', axis=0, tiled=True)]
    while x24 -> x0, local copies, waits for them, and re-layouts: 35.5 us -> none
    dot_general x15 -> x8, matrix products: 36 us -> 13.1 us  [the longest x4 9.14 us: on_device(): jnp.dot(current, layer_weights[layer_index], preferred_element_type=F32)]
    ppermute x16 -> x12, starting transfers between devices: 2.53 us -> 16.5 us  [the longest x3 8.08 us: swapped_by_user(): return lax.ppermute(value, ('user', 'hist'), pairs)]
    add x8 -> x16, other arithmetic: 13.3 us -> 0.72 us  [the longest x7 0.51 us: ids_at(): return pair[:slot_count] * ID_BASE + pair[slot_count:]]
    all_to_all x2 -> x0, blocking collectives: 7.78 us -> none  [the longest x1 3.89 us: on_device(): lax.all_to_all(outgoing, 'user', split_axis=0, concat_axis=0, tiled=True)]
    unnamed x12 -> x21, local copies, waits for them, and re-layouts: 0.58 us -> 6.51 us
  transfers between devices with their start and end apart: 17 -> 12, of which waited for: 9 -> 7; matrix products, arithmetic and copies ran while one was open for 1% -> 25% of each run, Pallas kernels for 0% -> 7%
where the time goes in v1:
time: 78.9 us; the launch traced here: 78.3 us
  waiting for transfers between devices  26.6 us (34%)
  starting transfers between devices  16.5 us (21%)
  matrix products  13.1 us (17%)
  local copies, waits for them, and re-layouts  10.3 us (13%)
  Pallas kernels  5.35 us (7%)
  other arithmetic  4.9 us (6%)
  between operations  1.62 us (2%)
    ppermute x6, waiting for transfers between devices, swapped(): return lax.ppermute(value, 'hist', [(i, i ^ flip) for i in range(count)])  25 us
    dot_general x4, matrix products, on_device(): jnp.dot(current, layer_weights[layer_index], preferred_element_type=F32)  9.14 us
    ppermute x3, starting transfers between devices, swapped_by_user(): return lax.ppermute(value, ('user', 'hist'), pairs)  8.08 us
    ppermute x6, starting transfers between devices, swapped(): return lax.ppermute(value, 'hist', [(i, i ^ flip) for i in range(count)])  6.59 us
    unnamed x21, local copies, waits for them, and re-layouts  6.51 us
    pallas_call x1, Pallas kernels, attend(): pl.pallas_call(attend_kernel, out_shape=jax.ShapeDtypeStruct(rows.shape,...  5.35 us
    dot_general x1, matrix products, on_device(): jnp.dot(gated_rows, w_out, preferred_element_type=F32)  2.54 us
    ppermute x3, starting transfers between devices, from_user(): lax.ppermute(value, 'user', [((i + steps) % count, i) for i in range(coun...  1.81 us
  transfers between devices with their start and end apart: 12, of which 7 were waited for; matrix products, arithmetic and copies ran while one was open for 25% of the time, Pallas kernels for 7%

profile of v1, /device:TPU:0, one launch (start us, length us, event | category | flops | bytes accessed | tf_op | source)
XLA Modules:
  0.0 78.3 jit_solution(6650407019511590628)
XLA Ops:
  0.0 0.8 %fusion.53 = (bf16[64]{0:T(256)(128)(2,1)S(1)}, bf16[64]{0:T(256)(128)(2,1)S(1)}) fusion(s32[1,64]{1,0:T(1,128)} %param.15), kind=kLoop, calls=%fused_computation.139 | loop fusion | flops 1344 | bytes 512 | tf_op jit(solution)/shard_map/convert.3
  0.8 0.1 pad_maximum_fusion.4
  0.9 0.5 collective-permute-start
  1.5 0.7 fusion.52
  3.5 0.9 %constant_dynamic-update-slice_fusion = bf16[512,1024]{1,0:T(8,128)(2,1)S(1)} fusion(bf16[64,1024]{1,0:T(8,128)(2,1)} %param.14), kind=kLoop, calls=%fused_computation.70 | loop fusion | bytes 262144
  4.4 0.9 %constant_dynamic-slice_fusion.8 = bf16[32,1024]{1,0:T(8,128)(2,1)S(1)} fusion(bf16[64,1024]{1,0:T(8,128)(2,1)} %param.14, s32[]{:T(128)S(6)} %select_n.129), kind=kLoop, calls=%fused_computation.83 | loop fusion | bytes 131076 | tf_op jit(solution)/shard_map/dynamic_slice | solution.py:124
  5.2 0.7 bitcast_and_fusion.1
  5.9 0.1 concatenate.32
  6.0 0.1 pad_maximum_fusion.5
  6.1 0.6 gather_fusion
  6.7 0.9 %pad_maximum_fusion.2 = bf16[80,1024]{1,0:T(8,128)(2,1)S(1)} fusion(bf16[16,1024]{1,0:T(8,128)(2,1)S(1)} %pad.4, bf16[64,1024]{1,0:T(8,128)(2,1)} %param.14), kind=kLoop, calls=%fused_computation.51 | loop fusion | flops 327680 | bytes 327680 | tf_op jit(solution)/shard_map/concatenate | solution.py:114
  7.6 5.0 %collective-permute-start.3 = (bf16[80,1024]{1,0:T(8,128)(2,1)S(1)}, bf16[80,1024]{1,0:T(8,128)(2,1)S(1)}, u32[]{:S(2)}, u32[]{:S(2)}) collective-permute-start(bf16[80,1024]{1,0:T(8,128)(2,1)S(1)} %pad_maximum_fusion.2), channel_id=1, source_target_pairs={{0,5},{1,4},{2,7},{3,6},{4,1},{5,0},{6,3},{7,2},{8,14},{9,15},{10,... | collective-permute-start | bytes 491528 | tf_op jit(solution)/shard_map/ppermute | solution.py:34
  12.6 1.5 %collective-permute-start.2 = (bf16[80,1024]{1,0:T(8,128)(2,1)S(1)}, bf16[80,1024]{1,0:T(8,128)(2,1)S(1)}, u32[]{:S(2)}, u32[]{:S(2)}) collective-permute-start(bf16[80,1024]{1,0:T(8,128)(2,1)S(1)} %pad_maximum_fusion.2), channel_id=1, source_target_pairs={{0,3},{1,2},{2,1},{3,0},{4,7},{5,6},{6,5},{7,4},{8,12},{9,13},{10,... | collective-permute-start | bytes 491528 | tf_op jit(solution)/shard_map/ppermute | solution.py:34
  14.1 1.5 %collective-permute-start.1 = (bf16[80,1024]{1,0:T(8,128)(2,1)S(1)}, bf16[80,1024]{1,0:T(8,128)(2,1)S(1)}, u32[]{:S(2)}, u32[]{:S(2)}) collective-permute-start(bf16[80,1024]{1,0:T(8,128)(2,1)S(1)} %pad_maximum_fusion.2), channel_id=1, source_target_pairs={{0,1},{1,0},{2,3},{3,2},{4,5},{5,4},{6,7},{7,6},{8,10},{9,11},{10,... | collective-permute-start | bytes 491528 | tf_op jit(solution)/shard_map/ppermute | solution.py:34
  15.8 0.7 pad_clamp_fusion
  16.4 8.3 %collective-permute-done.4 = bf16[48,1024]{1,0:T(8,128)(2,1)S(1)} collective-permute-done((bf16[48,1024]{1,0:T(8,128)(2,1)S(1)}, bf16[48,1024]{1,0:T(8,128)(2,1)S(1)}, u32[]{:S(2)}, u32[]{:S(2)}) %collective-permute-start.4) | collective-permute-done | bytes 98336 | tf_op jit(solution)/shard_map/ppermute | solution.py:26
  24.8 1.3 %collective-permute-start.5 = (bf16[288,1024]{1,0:T(8,128)(2,1)S(1)}, bf16[288,1024]{1,0:T(8,128)(2,1)S(1)}, u32[]{:S(2)}, u32[]{:S(2)}) collective-permute-start(bf16[288,1024]{1,0:T(8,128)(2,1)S(1)} %pad_maximum_fusion), channel_id=1, source_target_pairs={{8,0},{0,8},{9,1},{1,9},{10,2},{2,10},{11,3},{3,11},{12,4},{4,12},... | collective-permute-start | bytes 1769480 | tf_op jit(solution)/shard_map/ppermute | solution.py:39
  26.2 1.5 %collective-permute-done.5 = bf16[288,1024]{1,0:T(8,128)(2,1)S(1)} collective-permute-done((bf16[288,1024]{1,0:T(8,128)(2,1)S(1)}, bf16[288,1024]{1,0:T(8,128)(2,1)S(1)}, u32[]{:S(2)}, u32[]{:S(2)}) %collective-permute-start.5) | collective-permute-done | bytes 589856 | tf_op jit(solution)/shard_map/ppermute | solution.py:39
  28.2 0.3 copy-done.3
  28.6 0.6 gather_fusion.2
  29.2 0.6 gather_fusion.1
  29.8 0.1 eq.98
  29.9 0.9 %slice_dynamic-update-slice_fusion.2 = bf16[512,1024]{1,0:T(8,128)(2,1)S(1)} fusion(bf16[512,1024]{1,0:T(8,128)(2,1)S(1)} %slice_dynamic-update-slice_fusion.7, bf16[288,1024]{1,0:T(8,128)(2,1)} %copy-done.3), kind=kLoop, calls=%fused_computation.55 | loop fusion | bytes 262144
  30.8 0.9 %slice_dynamic-update-slice_fusion.1 = bf16[512,1024]{1,0:T(8,128)(2,1)S(1)} fusion(bf16[512,1024]{1,0:T(8,128)(2,1)S(1)} %slice_dynamic-update-slice_fusion.2, bf16[288,1024]{1,0:T(8,128)(2,1)} %copy-done.3), kind=kLoop, calls=%fused_computation.54 | loop fusion | bytes 262144
  31.7 0.9 %slice_dynamic-update-slice_fusion = bf16[512,1024]{1,0:T(8,128)(2,1)S(1)} fusion(bf16[512,1024]{1,0:T(8,128)(2,1)S(1)} %slice_dynamic-update-slice_fusion.1, bf16[288,1024]{1,0:T(8,128)(2,1)} %copy-done.3), kind=kLoop, calls=%fused_computation.53 | loop fusion | bytes 262144
  32.7 0.8 %slice_dynamic-update-slice_fusion.6.rows_ref = bf16[512,1024]{1,0:T(8,128)(2,1)S(1)} fusion(bf16[512,1024]{1,0:T(8,128)(2,1)S(1)} %slice_dynamic-update-slice_fusion, bf16[288,1024]{1,0:T(8,128)(2,1)} %copy-done.3), kind=kLoop, calls=%fused_computation.66 | loop fusion | bytes 131072 | tf_op jit(solution)/shard_map/concatenate | solution.py:152
  33.5 1.2 %copy-done.1 = bf16[1,512,1024]{2,1,0:T(8,128)(2,1)S(1)} copy-done((bf16[1,512,1024]{2,1,0:T(8,128)(2,1)S(1)}, bf16[1,512,1024]{2,1,0:T(8,128)(2,1)}, u32[]{:S(2)}) %copy-start.1) | copy-done | bytes 1048600
  34.7 1.2 %copy-done.2 = bf16[1,512,1024]{2,1,0:T(8,128)(2,1)S(1)} copy-done((bf16[1,512,1024]{2,1,0:T(8,128)(2,1)S(1)}, bf16[1,512,1024]{2,1,0:T(8,128)(2,1)}, u32[]{:S(2)}) %copy-start.2) | copy-done | bytes 1048600
  36.0 5.4 %attend.1 = bf16[512,1024]{1,0:T(8,128)(2,1)S(1)} custom-call(s32[1]{0:T(128)S(6)} %min.6.live_ref, bf16[512,1024]{1,0:T(8,128)(2,1)S(1)} %slice_dynamic-update-slice_fusion.6.rows_ref, bf16[1024,1024]{1,0:T(8,128)(2,1)} %w_query_ref.1, bf16[1,512,1024]{2,1,0:T(8,128)(2,1)S(1)} %copy-done.1, bf16[1,512,1024]{2,1,0:T(8,128)(2,1)S(1)} %copy-done.2), custom_call_target="tpu_custom_call" | custom-call | flops 2147483648 | bytes 6291456 | tf_op jit(solution)/shard_map/attend/pallas_call | solution.py:64
  41.3 0.5 convolution_convert_fusion
  41.8 3.0 %collective-permute-start.8 = (bf16[256,512]{1,0:T(8,128)(2,1)S(1)}, bf16[256,512]{1,0:T(8,128)(2,1)S(1)}, u32[]{:S(2)}, u32[]{:S(2)}) collective-permute-start(bf16[256,512]{1,0:T(8,128)(2,1)S(1)} %slice.238), channel_id=1, source_target_pairs={{0,2},{1,3},{2,0},{3,1},{4,6},{5,7},{6,4},{7,5},{8,10},{9,11},{10,... | collective-permute-start | bytes 786440 | tf_op jit(solution)/shard_map/ppermute | solution.py:26
  44.8 0.5 convolution_convert_fusion.1
  45.4 0.6 collective-permute-start.6
  45.9 0.4 multiply_reduce_fusion
  46.4 5.3 %collective-permute-done.8 = bf16[256,512]{1,0:T(8,128)(2,1)S(1)} collective-permute-done((bf16[256,512]{1,0:T(8,128)(2,1)S(1)}, bf16[256,512]{1,0:T(8,128)(2,1)S(1)}, u32[]{:S(2)}, u32[]{:S(2)}) %collective-permute-start.8) | collective-permute-done | bytes 262176 | tf_op jit(solution)/shard_map/ppermute | solution.py:26
  51.8 0.7 collective-permute-start.9
  52.5 1.2 %collective-permute-done.6 = bf16[256,512]{1,0:T(8,128)(2,1)S(1)} collective-permute-done((bf16[256,512]{1,0:T(8,128)(2,1)S(1)}, bf16[256,512]{1,0:T(8,128)(2,1)S(1)}, u32[]{:S(2)}, u32[]{:S(2)}) %collective-permute-start.6) | collective-permute-done | bytes 262176 | tf_op jit(solution)/shard_map/ppermute | solution.py:26
  53.8 0.5 collective-permute-start.7
  54.3 2.8 %collective-permute-done.9 = bf16[128,512]{1,0:T(8,128)(2,1)S(1)} collective-permute-done((bf16[128,512]{1,0:T(8,128)(2,1)S(1)}, bf16[128,512]{1,0:T(8,128)(2,1)S(1)}, u32[]{:S(2)}, u32[]{:S(2)}) %collective-permute-start.9) | collective-permute-done | bytes 131104 | tf_op jit(solution)/shard_map/ppermute | solution.py:26
  57.1 1.8 %collective-permute-done.7 = bf16[128,512]{1,0:T(8,128)(2,1)S(1)} collective-permute-done((bf16[128,512]{1,0:T(8,128)(2,1)S(1)}, bf16[128,512]{1,0:T(8,128)(2,1)S(1)}, u32[]{:S(2)}, u32[]{:S(2)}) %collective-permute-start.7) | collective-permute-done | bytes 131104 | tf_op jit(solution)/shard_map/ppermute | solution.py:26
  58.9 1.8 %collective-permute-start.10 = (bf16[64,1024]{1,0:T(8,128)(2,1)S(1)}, bf16[64,1024]{1,0:T(8,128)(2,1)S(1)}, u32[]{:S(2)}, u32[]{:S(2)}) collective-permute-start(bf16[64,1024]{1,0:T(8,128)(2,1)S(1)} %fusion.21), channel_id=1, source_target_pairs={{0,4},{1,5},{2,6},{3,7},{4,0},{5,1},{6,2},{7,3},{8,12},{9,13},{10,... | collective-permute-start | bytes 393224 | tf_op jit(solution)/shard_map/ppermute | solution.py:26
  60.7 5.7 %collective-permute-done.10 = bf16[64,1024]{1,0:T(8,128)(2,1)S(1)} collective-permute-done((bf16[64,1024]{1,0:T(8,128)(2,1)S(1)}, bf16[64,1024]{1,0:T(8,128)(2,1)S(1)}, u32[]{:S(2)}, u32[]{:S(2)}) %collective-permute-start.10) | collective-permute-done | bytes 131104 | tf_op jit(solution)/shard_map/ppermute | solution.py:26
  66.4 0.1 multiply_reduce_fusion.1
  66.6 2.5 %fusion.8 = bf16[64,1024]{1,0:T(8,128)(2,1)S(1)} fusion(f32[64,1024]{1,0:T(8,128)S(1)} %get-tuple-element.22, bf16[1024,1024]{1,0:T(8,128)(2,1)S(1)} %copy-done, bf16[1024,1024]{1,0:T(8,128)(2,1)} %param.22, f32[64]{0:T(128)S(1)} %add_rsqrt_fusion, f32[1024]{0:T(1024)S(1)} %copy-done.4, f32[64]{0:T(128)S(1)} %add_rsqrt_fusion.1, ...), kind=kOutput, calls=%fused_computation.16 | convolution fusion | flops 269418496 | bytes 5510144 | tf_op jit(solution)/shard_map/dot_general | solution.py:198
  69.1 2.1 %fusion.18 = bf16[64,1024]{1,0:T(8,128)(2,1)S(1)} fusion(bf16[64,1024]{1,0:T(8,128)(2,1)S(1)} %fusion.8, bf16[1,2,1024,1024]{3,2,1,0:T(8,128)(2,1)} %param.25), kind=kOutput, calls=%fused_computation.33 | convolution fusion | flops 134676480 | bytes 2490368 | tf_op jit(solution)/shard_map/dot_general | solution.py:207
  71.2 2.1 %fusion.24 = bf16[64,1024]{1,0:T(8,128)(2,1)S(1)} fusion(bf16[64,1024]{1,0:T(8,128)(2,1)S(1)} %fusion.18, bf16[1,2,1024,1024]{3,2,1,0:T(8,128)(2,1)} %param.25, pred[64]{0:T(512)(128)(4,1)S(1)} %get-tuple-element.16), kind=kOutput, calls=%fused_computation.43 | convolution fusion | flops 134742016 | bytes 2490880 | tf_op jit(solution)/shard_map/dot_general | solution.py:207
  73.4 2.1 %fusion.17 = bf16[64,1024]{1,0:T(8,128)(2,1)S(1)} fusion(bf16[64,1024]{1,0:T(8,128)(2,1)S(1)} %fusion.8, bf16[2,1024,1024]{2,1,0:T(8,128)(2,1)} %collective-permute-done.11), kind=kOutput, calls=%fused_computation.32 | convolution fusion | flops 134676480 | bytes 2490368 | tf_op jit(solution)/shard_map/dot_general | solution.py:207
  75.5 2.8 %fusion.30 = bf16[1,64,1024]{2,1,0:T(8,128)(2,1)} fusion(bf16[64,1024]{1,0:T(8,128)(2,1)S(1)} %fusion.24, bf16[64,1024]{1,0:T(8,128)(2,1)S(1)} %fusion.17, bf16[2,1024,1024]{2,1,0:T(8,128)(2,1)} %collective-permute-done.11, pred[64]{0:T(512)(128)(4,1)S(1)} %get-tuple-element.15), kind=kOutput, calls=%fused_computation.46 | convolution fusion | flops 134742016 | bytes 2621952 | tf_op jit(solution)/shard_map/dot_general | solution.py:207
  (58 shorter events, 1.3 us)
Async XLA Ops:
  0.0 66.5 %copy-start = (bf16[1024,1024]{1,0:T(8,128)(2,1)S(1)}, bf16[1024,1024]{1,0:T(8,128)(2,1)}, u32[]{:S(2)}) copy-start(bf16[1024,1024]{1,0:T(8,128)(2,1)} %param.23) | copy-start | bytes 6291460
  0.0 28.6 %copy-start.5 = (s32[1,64]{1,0:T(1,128)S(1)}, s32[1,64]{1,0:T(1,128)}, u32[]{:S(2)}) copy-start(s32[1,64]{1,0:T(1,128)} %param.15) | copy-start | bytes 772
  0.9 5.1 %collective-permute-start = (bf16[128]{0:T(256)(128)(2,1)S(1)}, bf16[128]{0:T(256)(128)(2,1)S(1)}, u32[]{:S(2)}, u32[]{:S(2)}) collective-permute-start(bf16[128]{0:T(256)(128)(2,1)S(1)} %pad_maximum_fusion.4), channel_id=1, source_target_pairs={{8,0},{0,8},{9,1},{1,9},{10,2},{2,10},{11,3},{3,11},{12,4},{4,12},... | collective-permute-start | bytes 776 | tf_op jit(solution)/shard_map/ppermute | solution.py:39
  1.4 72.0 %collective-permute-start.11 = (bf16[2,1024,1024]{2,1,0:T(8,128)(2,1)}, bf16[2,1024,1024]{2,1,0:T(8,128)(2,1)}, u32[]{:S(2)}, u32[]{:S(2)}) collective-permute-start(bf16[2,1024,1024]{2,1,0:T(8,128)(2,1)} %bitcast.62), channel_id=1, source_target_pairs={{8,0},{0,8},{9,1},{1,9},{10,2},{2,10},{11,3},{3,11},{12,4},{4,12},... | collective-permute-start | bytes 12582920 | tf_op jit(solution)/shard_map/ppermute | solution.py:39
  7.6 17.1 %collective-permute-start.3 = (bf16[80,1024]{1,0:T(8,128)(2,1)S(1)}, bf16[80,1024]{1,0:T(8,128)(2,1)S(1)}, u32[]{:S(2)}, u32[]{:S(2)}) collective-permute-start(bf16[80,1024]{1,0:T(8,128)(2,1)S(1)} %pad_maximum_fusion.2), channel_id=1, source_target_pairs={{0,5},{1,4},{2,7},{3,6},{4,1},{5,0},{6,3},{7,2},{8,14},{9,15},{10,... | collective-permute-start | bytes 491528 | tf_op jit(solution)/shard_map/ppermute | solution.py:34
  12.6 12.1 %collective-permute-start.2 = (bf16[80,1024]{1,0:T(8,128)(2,1)S(1)}, bf16[80,1024]{1,0:T(8,128)(2,1)S(1)}, u32[]{:S(2)}, u32[]{:S(2)}) collective-permute-start(bf16[80,1024]{1,0:T(8,128)(2,1)S(1)} %pad_maximum_fusion.2), channel_id=1, source_target_pairs={{0,3},{1,2},{2,1},{3,0},{4,7},{5,6},{6,5},{7,4},{8,12},{9,13},{10,... | collective-permute-start | bytes 491528 | tf_op jit(solution)/shard_map/ppermute | solution.py:34
  14.1 10.6 %collective-permute-start.1 = (bf16[80,1024]{1,0:T(8,128)(2,1)S(1)}, bf16[80,1024]{1,0:T(8,128)(2,1)S(1)}, u32[]{:S(2)}, u32[]{:S(2)}) collective-permute-start(bf16[80,1024]{1,0:T(8,128)(2,1)S(1)} %pad_maximum_fusion.2), channel_id=1, source_target_pairs={{0,1},{1,0},{2,3},{3,2},{4,5},{5,4},{6,7},{7,6},{8,10},{9,11},{10,... | collective-permute-start | bytes 491528 | tf_op jit(solution)/shard_map/ppermute | solution.py:34
  15.7 9.0 %collective-permute-start.4 = (bf16[48,1024]{1,0:T(8,128)(2,1)S(1)}, bf16[48,1024]{1,0:T(8,128)(2,1)S(1)}, u32[]{:S(2)}, u32[]{:S(2)}) collective-permute-start(bf16[48,1024]{1,0:T(8,128)(2,1)S(1)} %pad_maximum_fusion.3), channel_id=1, source_target_pairs={{0,7},{1,6},{2,5},{3,4},{4,3},{5,2},{6,1},{7,0},{8,15},{9,14},{10,... | collective-permute-start | bytes 294920 | tf_op jit(solution)/shard_map/ppermute | solution.py:26
  24.8 2.9 %collective-permute-start.5 = (bf16[288,1024]{1,0:T(8,128)(2,1)S(1)}, bf16[288,1024]{1,0:T(8,128)(2,1)S(1)}, u32[]{:S(2)}, u32[]{:S(2)}) collective-permute-start(bf16[288,1024]{1,0:T(8,128)(2,1)S(1)} %pad_maximum_fusion), channel_id=1, source_target_pairs={{8,0},{0,8},{9,1},{1,9},{10,2},{2,10},{11,3},{3,11},{12,4},{4,12},... | collective-permute-start | bytes 1769480 | tf_op jit(solution)/shard_map/ppermute | solution.py:39
  27.7 0.8 %copy-start.3 = (bf16[288,1024]{1,0:T(8,128)(2,1)}, bf16[288,1024]{1,0:T(8,128)(2,1)S(1)}, u32[]{:S(2)}) copy-start(bf16[288,1024]{1,0:T(8,128)(2,1)S(1)} %collective-permute-done.5) | copy-start | bytes 1769476
  33.5 1.2 %copy-start.1 = (bf16[1,512,1024]{2,1,0:T(8,128)(2,1)S(1)}, bf16[1,512,1024]{2,1,0:T(8,128)(2,1)}, u32[]{:S(2)}) copy-start(bf16[1,512,1024]{2,1,0:T(8,128)(2,1)} %keys_ref.1) | copy-start | bytes 3145732
  34.7 1.2 %copy-start.2 = (bf16[1,512,1024]{2,1,0:T(8,128)(2,1)S(1)}, bf16[1,512,1024]{2,1,0:T(8,128)(2,1)}, u32[]{:S(2)}) copy-start(bf16[1,512,1024]{2,1,0:T(8,128)(2,1)} %values_ref.1) | copy-start | bytes 3145732
  41.8 9.8 %collective-permute-start.8 = (bf16[256,512]{1,0:T(8,128)(2,1)S(1)}, bf16[256,512]{1,0:T(8,128)(2,1)S(1)}, u32[]{:S(2)}, u32[]{:S(2)}) collective-permute-start(bf16[256,512]{1,0:T(8,128)(2,1)S(1)} %slice.238), channel_id=1, source_target_pairs={{0,2},{1,3},{2,0},{3,1},{4,6},{5,7},{6,4},{7,5},{8,10},{9,11},{10,... | collective-permute-start | bytes 786440 | tf_op jit(solution)/shard_map/ppermute | solution.py:26
  45.4 8.4 %collective-permute-start.6 = (bf16[256,512]{1,0:T(8,128)(2,1)S(1)}, bf16[256,512]{1,0:T(8,128)(2,1)S(1)}, u32[]{:S(2)}, u32[]{:S(2)}) collective-permute-start(bf16[256,512]{1,0:T(8,128)(2,1)S(1)} %slice.233), channel_id=1, source_target_pairs={{0,1},{1,0},{2,3},{3,2},{4,5},{5,4},{6,7},{7,6},{8,9},{9,8},{10,11... | collective-permute-start | bytes 786440 | tf_op jit(solution)/shard_map/ppermute | solution.py:26
  51.7 14.8 %copy-start.4 = (f32[1024]{0:T(1024)S(1)}, f32[1024]{0:T(1024)}, u32[]{:S(2)}) copy-start(f32[1024]{0:T(1024)} %param.24) | copy-start | bytes 12292
  51.8 5.3 %collective-permute-start.9 = (bf16[128,512]{1,0:T(8,128)(2,1)S(1)}, bf16[128,512]{1,0:T(8,128)(2,1)S(1)}, u32[]{:S(2)}, u32[]{:S(2)}) collective-permute-start(bf16[128,512]{1,0:T(8,128)(2,1)S(1)} %slice.321), channel_id=1, source_target_pairs={{0,1},{1,0},{2,3},{3,2},{4,5},{5,4},{6,7},{7,6},{8,9},{9,8},{10,11... | collective-permute-start | bytes 393224 | tf_op jit(solution)/shard_map/ppermute | solution.py:26
  53.8 5.0 %collective-permute-start.7 = (bf16[128,512]{1,0:T(8,128)(2,1)S(1)}, bf16[128,512]{1,0:T(8,128)(2,1)S(1)}, u32[]{:S(2)}, u32[]{:S(2)}) collective-permute-start(bf16[128,512]{1,0:T(8,128)(2,1)S(1)} %slice.322), channel_id=1, source_target_pairs={{0,2},{1,3},{2,0},{3,1},{4,6},{5,7},{6,4},{7,5},{8,10},{9,11},{10,... | collective-permute-start | bytes 393224 | tf_op jit(solution)/shard_map/ppermute | solution.py:26
  58.9 7.5 %collective-permute-start.10 = (bf16[64,1024]{1,0:T(8,128)(2,1)S(1)}, bf16[64,1024]{1,0:T(8,128)(2,1)S(1)}, u32[]{:S(2)}, u32[]{:S(2)}) collective-permute-start(bf16[64,1024]{1,0:T(8,128)(2,1)S(1)} %fusion.21), channel_id=1, source_target_pairs={{0,4},{1,5},{2,6},{3,7},{4,0},{5,1},{6,2},{7,3},{8,12},{9,13},{10,... | collective-permute-start | bytes 393224 | tf_op jit(solution)/shard_map/ppermute | solution.py:26

commit v2 on v0

v2 whole, which is shorter than its diff:
```python
import functools

import jax
import jax.numpy as jnp
from jax import lax
from jax.experimental import pallas as pl
from jax.experimental.pallas import tpu as pltpu
from jax.sharding import PartitionSpec as P

H = 8
LAYERS = 2
VMEM_LIMIT = 24 * 1024 * 1024

norm_eps = 1e-05
F32 = jnp.float32
BF16 = jnp.bfloat16
ANY = pl.BlockSpec(memory_space=pl.ANY)
VMEM = pl.BlockSpec(memory_space=pltpu.VMEM)
SMEM = pl.BlockSpec(memory_space=pltpu.SMEM)


def rms_scale(matrix):
    return matrix * lax.rsqrt(jnp.mean(matrix * matrix, axis=-1, keepdims=True) + norm_eps)


def silu(value):
    half = 0.5 * value
    return half + half * jnp.tanh(half)


def swapped(value, flip):
    count = lax.axis_size("hist")
    return lax.ppermute(value, "hist", [(i, i ^ flip) for i in range(count)])


def swapped_by_user(value, flips):
    count = lax.axis_size("hist")
    pairs = [
        (u * count + i, u * count + (i ^ flip)) for u, flip in enumerate(flips) for i in range(count)
    ]
    return lax.ppermute(value, ("user", "hist"), pairs)


def from_user(value, steps):
    count = lax.axis_size("user")
    return lax.ppermute(value, "user", [((i + steps) % count, i) for i in range(count)])


def kernel_call(body, name, out_shapes, in_specs, scratch=(), flops=0, moved=0):
    return pl.pallas_call(
        body,
        out_shape=out_shapes,
        in_specs=in_specs,
        out_specs=[VMEM] * len(out_shapes),
        scratch_shapes=scratch,
        compiler_params=pltpu.CompilerParams(vmem_limit_bytes=VMEM_LIMIT),
        cost_estimate=pl.CostEstimate(flops=flops, bytes_accessed=moved, transcendentals=0),
        name=name,
    )


def attend_rows(row_refs, w_query_ref, keys_ref, values_ref, sums_ref):
    width = sums_ref.shape[1]
    head_size = width // H
    rows = jnp.concatenate([ref[...] for ref in row_refs], axis=0)
    normed = rms_scale(rows.astype(F32)).astype(BF16)
    queries = jnp.dot(normed, w_query_ref[...], preferred_element_type=F32).astype(BF16)
    for head in range(H):
        cut = slice(head * head_size, (head + 1) * head_size)
        scores = lax.dot_general(
            queries[:, cut], keys_ref[:, cut], (((1,), (1,)), ((), ())), preferred_element_type=F32
        )
        half = scores * (0.5 * head_size ** (-0.5))
        weights = (half + half * jnp.tanh(half)).astype(BF16)
        sums_ref[:, cut] = jnp.dot(weights, values_ref[:, cut], preferred_element_type=F32).astype(BF16)


def first_kernel(pieces, live_ref, w_query_hbm, keys_hbm, values_hbm, *refs):
    row_refs = refs[:pieces]
    sums_ref, w_query_ref, keys_ref, values_ref, sems = refs[pieces:]
    copies = [
        pltpu.make_async_copy(w_query_hbm, w_query_ref, sems.at[0]),
        pltpu.make_async_copy(keys_hbm.at[0], keys_ref, sems.at[1]),
        pltpu.make_async_copy(values_hbm.at[0], values_ref, sems.at[2]),
    ]
    for copy in copies:
        copy.start()
    for copy in copies:
        copy.wait()
    place = lax.broadcasted_iota(jnp.int32, values_ref.shape, 0)
    values_ref[...] = jnp.where(place < live_ref[0], values_ref[...].astype(F32), 0.0).astype(BF16)
    attend_rows(row_refs, w_query_ref, keys_ref, values_ref, sums_ref)


def next_kernel(pieces, w_query_ref, keys_ref, values_ref, *refs):
    attend_rows(refs[:pieces], w_query_ref, keys_ref, values_ref, refs[pieces])


def row_count(pieces):
    return sum(piece.shape[0] for piece in pieces)


def attend_cost(rows, width, history):
    return 2 * rows * width * (width + 2 * history)


def attend_first(pieces, live_count, w_query, keys, values):
    rows, width = row_count(pieces), w_query.shape[0]
    history = keys.shape[1]
    body = functools.partial(first_kernel, len(pieces))
    shapes = [(rows, width), w_query.shape, keys.shape[1:], values.shape[1:]]
    return kernel_call(
        body,
        "attend_first",
        [jax.ShapeDtypeStruct(shape, BF16) for shape in shapes],
        [SMEM, ANY, ANY, ANY] + [VMEM] * len(pieces),
        scratch=[pltpu.SemaphoreType.DMA((3,))],
        flops=attend_cost(rows, width, history),
        moved=4 * (w_query.size + keys.size + values.size),
    )(live_count, w_query, keys, values, *pieces)


def attend_next(pieces, w_query, keys, values):
    rows, width = row_count(pieces), w_query.shape[0]
    return kernel_call(
        functools.partial(next_kernel, len(pieces)),
        "attend_next",
        [jax.ShapeDtypeStruct((rows, width), BF16)],
        [VMEM] * (3 + len(pieces)),
        flops=attend_cost(rows, width, keys.shape[0]),
    )(w_query, keys, values, *pieces)[0]


def matches(layout, ids_row, hist_index, user_index, shard_rows):
    blocks = []
    for rows, steps, flips, split in layout:
        users = len(flips)
        owner = lax.rem(user_index + steps, users)
        flip = sum(jnp.where(owner == u, flip, 0) for u, flip in enumerate(flips))
        base = (hist_index ^ flip) * shard_rows + (owner * rows if split else 0)
        item = lax.broadcasted_iota(jnp.int32, (rows, ids_row.shape[1]), 0) + base
        blocks.append((item == ids_row).astype(F32).astype(BF16))
    return jnp.concatenate(blocks, axis=0)


TRANSPOSED = (((0,), (0,)), ((), ()))


def place_kernel(layout, orders, shard_rows, hist_axis, user_axis, ids_ref, first_ref, next_ref, *outs):
    slots = ids_ref.shape[1]
    ids_row = jnp.concatenate([ids_ref[flip : flip + 1, :] for flip in orders[0]], axis=1)
    onehot = matches(layout, ids_row, lax.axis_index(hist_axis), lax.axis_index(user_axis), shard_rows)
    width = first_ref.shape[1] // 2
    cut = first_ref.shape[0]
    for side, order in enumerate(orders):
        columns = slice(side * width, (side + 1) * width)
        sums = jnp.concatenate([first_ref[:, columns], next_ref[:, columns]], axis=0)
        placed = lax.dot_general(onehot, sums, TRANSPOSED, preferred_element_type=F32).astype(BF16)
        half = len(order) // 2
        for at, flip in enumerate(order):
            block = orders[0].index(flip)
            target = outs[2 * side + at // half]
            target[at % half * slots : (at % half + 1) * slots, :] = placed[block * slots : (block + 1) * slots, :]


def place(layout, orders, shard_rows, all_ids, first, following):
    devices, slots = all_ids.shape
    items = first.shape[0] + following.shape[0]
    width = first.shape[1]
    out = jax.ShapeDtypeStruct((devices * slots // 2, width // 2), BF16)
    body = functools.partial(place_kernel, layout, orders, shard_rows, "hist", "user")
    return kernel_call(
        body, "place", [out] * 4, [VMEM] * 3, flops=2 * items * devices * slots * width
    )(all_ids, first, following)


def prepare_kernel(pieces, layout, shard_rows, after_ref, ids_ref, w_gate_hbm, w_out_hbm, *refs):
    del after_ref
    users = len(layout[0][2])
    expert_hbm = refs[:users]
    row_refs = refs[users : users + pieces]
    refs = refs[users + pieces :]
    embed_ref, gating_ref, w_out_ref = refs[:3]
    expert_refs = refs[3 : 3 + users]
    w_gate_ref, sems = refs[3 + users :]
    copies = [
        pltpu.make_async_copy(source, target, sems.at[at])
        for at, (source, target) in enumerate(
            zip((w_gate_hbm, w_out_hbm) + expert_hbm, (w_gate_ref, w_out_ref) + expert_refs)
        )
    ]
    for copy in copies:
        copy.start()
    onehot = matches(layout, ids_ref[...], lax.axis_index("hist"), lax.axis_index("user"), shard_rows)
    table = jnp.concatenate([ref[...] for ref in row_refs], axis=0)
    embedded = lax.dot_general(onehot, table, TRANSPOSED, preferred_element_type=F32)
    embed_ref[...] = embedded
    normed = rms_scale(embedded).astype(BF16)
    copies[0].wait()
    gating_ref[...] = silu(jnp.dot(normed, w_gate_ref[...], preferred_element_type=F32))
    for copy in copies[1:]:
        copy.wait()


def prepare(layout, shard_rows, after, ids, w_gate, w_out, experts, pieces):
    slots, width = ids.shape[1], w_gate.shape[0]
    rows = jax.ShapeDtypeStruct((slots, width), F32)
    staged = [jax.ShapeDtypeStruct(part.shape, BF16) for part in (w_out, *experts)]
    moved = 2 * (w_gate.size + 2 * w_out.size + 2 * sum(part.size for part in experts))
    return kernel_call(
        functools.partial(prepare_kernel, len(pieces), layout, shard_rows),
        "prepare",
        [rows, rows, *staged],
        [ANY, VMEM, ANY, ANY] + [ANY] * len(experts) + [VMEM] * len(pieces),
        scratch=[pltpu.VMEM(w_gate.shape, BF16), pltpu.SemaphoreType.DMA((2 + len(experts),))],
        flops=2 * slots * width * (width + row_count(pieces)),
        moved=moved,
    )(after, ids, w_gate, w_out, *experts, *pieces)


def finish_kernel(users, kept_ref, come_ref, embed_ref, gating_ref, gain_ref, owner_ref, w_out_ref, *refs):
    expert_refs, out_ref = refs[:users], refs[users]
    attended = kept_ref[...] + come_ref[...].astype(F32)
    gated = (rms_scale(attended) * gain_ref[...] * gating_ref[...]).astype(BF16)
    mixed = jnp.dot(gated, w_out_ref[...], preferred_element_type=F32)
    state = (embed_ref[...] + mixed).astype(BF16)
    result = jnp.zeros(state.shape, F32)
    for steps, layers in enumerate(expert_refs):
        current = state
        for layer in range(LAYERS):
            lifted = jnp.dot(current, layers[layer], preferred_element_type=F32)
            current = (current.astype(F32) + silu(lifted)).astype(BF16)
        result = jnp.where(owner_ref[...] == steps, current.astype(F32), result)
    out_ref[0] = result.astype(BF16)


def finish(kept, come, embed, gating, gain, owner, w_out, experts):
    slots, width = kept.shape
    return kernel_call(
        functools.partial(finish_kernel, len(experts)),
        "finish",
        [jax.ShapeDtypeStruct((1, slots, width), BF16)],
        [VMEM] * (7 + len(experts)),
        flops=2 * slots * width * width * (1 + LAYERS * len(experts)),
    )(kept, come, embed, gating, gain, owner, w_out, *experts)[0]


def on_device(
    item_table,
    item_ids,
    candidate_counts,
    domain_ids,
    history_lengths,
    history_keys,
    history_values,
    w_query,
    w_gate,
    w_out,
    attn_gain,
    expert_weights,
):
    slot_count = item_ids.shape[1]
    shard_rows, feat_width = item_table.shape
    hist_devices = lax.axis_size("hist")
    users = lax.axis_size("user")
    hist_index = lax.axis_index("hist")
    user_index = lax.axis_index("user")
    bits = hist_devices.bit_length() - 1

    whole = (hist_devices - 1) // users
    flip_groups = [tuple(1 + users * g + u for u in range(users)) for g in range(whole)]
    flip_groups += [(flip,) * users for flip in range(1 + users * whole, hist_devices)]
    part_rows = shard_rows // users
    part = lax.dynamic_slice_in_dim(item_table, user_index * part_rows, part_rows, 0)
    pieces = [item_table]
    layout = [(shard_rows, 0, (0,) * users, False)]
    for flips in flip_groups:
        split = flips[0] == flips[-1]
        fetched = swapped_by_user(part if split else item_table, flips)
        for steps in range(users):
            pieces.append(from_user(fetched, steps) if steps else fetched)
            layout.append((fetched.shape[0], steps, flips, split))
    all_ids = item_ids
    for bit in range(bits):
        all_ids = jnp.concatenate([all_ids, swapped(all_ids, 1 << bit)], axis=0)

    own_layers = expert_weights[0]
    experts = [own_layers] + [from_user(own_layers, steps) for steps in range(1, users)]

    history = history_keys.shape[1]
    live_count = jnp.clip(history_lengths - hist_index * history, 0, history).astype(jnp.int32)
    early = 1 + users * (len(flip_groups) // 2)
    first, staged_query, staged_keys, staged_values = attend_first(
        pieces[:early], live_count, w_query, history_keys, history_values
    )
    following = attend_next(pieces[early:], staged_query, staged_keys, staged_values)

    turns = [list(range(bits)), list(range(bits))]
    if bits > 1:
        turns[1][:2] = [1, 0]
    orders = [
        [sum(((r >> (bits - 1 - t)) & 1) << bit for t, bit in enumerate(turn)) for r in range(hist_devices)]
        for turn in turns
    ]
    kept_a, sent_a, kept_b, sent_b = place(layout, orders, shard_rows, all_ids, first, following)
    held = [(kept_a, sent_a), (kept_b, sent_b)]
    embed, gating, staged_out, *staged_experts = prepare(
        layout, shard_rows, kept_a, item_ids, w_gate, w_out, experts, pieces
    )
    for at in range(bits - 1):
        for side, turn in enumerate(turns):
            kept, sent = held[side]
            total = kept.astype(F32) + swapped(sent, 1 << turn[at]).astype(F32)
            half = total.shape[0] // 2
            held[side] = (total[:half], total[half:].astype(BF16))
    kept = jnp.concatenate([pair[0] for pair in held], axis=1)
    sent = jnp.concatenate([pair[1] for pair in held], axis=1)
    come = swapped(sent, 1 << (bits - 1))

    slot_index = hist_index * slot_count + jnp.arange(slot_count, dtype=jnp.int32)
    steps_away = lax.rem(domain_ids[0] - user_index + users, users)
    owner = jnp.where(slot_index < candidate_counts[0], steps_away, -1)[:, None]
    return finish(kept, come, embed, gating, attn_gain[None], owner, staged_out, staged_experts)


def solution(mesh):
    in_specs = (
        P("hist", None),
        P(("groups", "user"), "hist"),
        P(("groups", "user")),
        P(("groups", "user"), "hist"),
        P(("groups", "user")),
        P(("groups", "user"), "hist", None),
        P(("groups", "user"), "hist", None),
        P(),
        P(),
        P(),
        P(),
        P("user", None, None, None),
    )
    out_specs = P(("groups", "user"), "hist", None)
    return jax.shard_map(
        on_device, mesh=mesh, in_specs=in_specs, out_specs=out_specs, check_vma=False
    )
```

time: 248 us -> 65.6 us (0.26)
  waiting for transfers between devices: 129 us -> 18.9 us
  matrix products: 36 us -> 0 us
  local copies, waits for them, and re-layouts: 36.1 us -> 8.9 us
  other arithmetic: 21.1 us -> 3.94 us
  starting transfers between devices: 2.53 us -> 19.2 us
  between operations: 14.2 us -> 1.56 us
  Pallas kernels: 0 us -> 12.6 us
  blocking collectives: 7.78 us -> 0 us
    ppermute x16 -> x17, waiting for transfers between devices: 86.4 us -> 18.9 us  [the longest x8 14.7 us: swapped(): return lax.ppermute(value, 'hist', [(i, i ^ flip) for i in range(count)])]
    all_gather x1 -> x0, waiting for transfers between devices: 42 us -> none  [on_device(): shard_rows = lax.all_gather(item_table, 'hist', axis=0, tiled=True)]
    dot_general x15 -> x0, matrix products: 36 us -> none  [the longest x8 25.6 us: attend_local(): jnp.einsum('hrk,khd->rhd', weights, value_heads, preferred_element_type=j...]
    while x24 -> x0, local copies, waits for them, and re-layouts: 35.5 us -> none
    ppermute x16 -> x17, starting transfers between devices: 2.53 us -> 19.2 us  [the longest x8 10.4 us: swapped(): return lax.ppermute(value, 'hist', [(i, i ^ flip) for i in range(count)])]
    pallas_call x0 -> x5, Pallas kernels: none -> 12.6 us  [the longest x1 2.92 us: attend_first(): kernel_call(body, 'attend_first', [jax.ShapeDtypeStruct(shape, BF16) for...]
    add x8 -> x5, other arithmetic: 13.3 us -> 1.14 us  [the longest x4 1.14 us: on_device(): total = kept.astype(F32) + swapped(sent, 1 << turn[at]).astype(F32)]
    all_to_all x2 -> x0, blocking collectives: 7.78 us -> none  [the longest x1 3.89 us: on_device(): lax.all_to_all(outgoing, 'user', split_axis=0, concat_axis=0, tiled=True)]
  transfers between devices with their start and end apart: 17 -> 17, of which waited for: 9 -> 6; matrix products, arithmetic and copies ran while one was open for 1% -> 9% of each run, Pallas kernels for 0% -> 15%
where the time goes in v2:
time: 65.6 us; the launch traced here: 65.1 us
  starting transfers between devices  19.2 us (29%)
  waiting for transfers between devices  18.9 us (29%)
  Pallas kernels  12.6 us (19%)
  local copies, waits for them, and re-layouts  8.9 us (14%)
  other arithmetic  3.94 us (6%)
  between operations  1.56 us (2%)
    ppermute x8, waiting for transfers between devices, swapped(): return lax.ppermute(value, 'hist', [(i, i ^ flip) for i in range(count)])  14.7 us
    ppermute x8, starting transfers between devices, swapped(): return lax.ppermute(value, 'hist', [(i, i ^ flip) for i in range(count)])  10.4 us
    ppermute x4, starting transfers between devices, swapped_by_user(): return lax.ppermute(value, ('user', 'hist'), pairs)  7.77 us
    unnamed x24, local copies, waits for them, and re-layouts  7.26 us
    ppermute x4, waiting for transfers between devices, swapped_by_user(): return lax.ppermute(value, ('user', 'hist'), pairs)  4.16 us
    pallas_call x1, Pallas kernels, attend_first(): kernel_call(body, 'attend_first', [jax.ShapeDtypeStruct(shape, BF16) for...  2.92 us
    pallas_call x1, Pallas kernels, finish(): kernel_call(functools.partial(finish_kernel, len(experts)), 'finish', [ja...  2.83 us
    pallas_call x1, Pallas kernels, prepare(): kernel_call(functools.partial(prepare_kernel, len(pieces), layout, shard_...  2.82 us
  transfers between devices with their start and end apart: 17, of which 6 were waited for; matrix products, arithmetic and copies ran while one was open for 9% of the time, Pallas kernels for 15%

profile of v2, /device:TPU:0, one launch (start us, length us, event | category | flops | bytes accessed | tf_op | source)
XLA Modules:
  0.0 65.1 jit_solution(6372205565661687037)
XLA Ops:
  0.0 0.5 collective-permute-start.16
  0.5 2.5 %collective-permute-start = (s32[1,64]{1,0:T(1,128)}, s32[1,64]{1,0:T(1,128)S(1)}, u32[]{:S(2)}, u32[]{:S(2)}) collective-permute-start(s32[1,64]{1,0:T(1,128)} %ids_ref.1), channel_id=1, source_target_pairs={{0,1},{1,0},{2,3},{3,2},{4,5},{5,4},{6,7},{7,6},{8,9},{9,8},{10,11... | collective-permute-start | bytes 776 | tf_op jit(solution)/shard_map/ppermute | solution.py:33
  3.0 0.1 collective-permute-start.3
  3.0 3.0 %collective-permute-start.5 = (bf16[64,1024]{1,0:T(8,128)(2,1)}, bf16[64,1024]{1,0:T(8,128)(2,1)S(1)}, u32[]{:S(2)}, u32[]{:S(2)}) collective-permute-start(bf16[64,1024]{1,0:T(8,128)(2,1)} %refs_2_.1), channel_id=1, source_target_pairs={{0,3},{1,2},{2,1},{3,0},{4,7},{5,6},{6,5},{7,4},{8,12},{9,13},{10,... | collective-permute-start | bytes 393224 | tf_op jit(solution)/shard_map/ppermute | solution.py:41
  6.0 2.5 %collective-permute-start.7 = (bf16[64,1024]{1,0:T(8,128)(2,1)}, bf16[64,1024]{1,0:T(8,128)(2,1)S(1)}, u32[]{:S(2)}, u32[]{:S(2)}) collective-permute-start(bf16[64,1024]{1,0:T(8,128)(2,1)} %refs_2_.1), channel_id=1, source_target_pairs={{0,5},{1,4},{2,7},{3,6},{4,1},{5,0},{6,3},{7,2},{8,14},{9,15},{10,... | collective-permute-start | bytes 393224 | tf_op jit(solution)/shard_map/ppermute | solution.py:41
  8.5 0.0 collective-permute-done
  8.5 0.7 %pad_add_fusion.2 = s32[2,64]{1,0:T(2,128)S(1)} fusion(s32[1,64]{1,0:T(1,128)S(1)} %collective-permute-done, s32[1,64]{1,0:T(1,128)} %ids_ref.1), kind=kLoop, calls=%fused_computation.17 | loop fusion | flops 128 | bytes 1024 | tf_op jit(solution)/shard_map/concatenate | solution.py:285
  9.2 0.4 collective-permute-start.1
  9.7 3.3 %collective-permute-done.1 = s32[2,64]{1,0:T(2,128)S(1)} collective-permute-done((s32[2,64]{1,0:T(2,128)S(1)}, s32[2,64]{1,0:T(2,128)S(1)}, u32[]{:S(2)}, u32[]{:S(2)}) %collective-permute-start.1) | collective-permute-done | bytes 544 | tf_op jit(solution)/shard_map/ppermute | solution.py:33
  13.0 0.7 %pad_add_fusion.1 = s32[4,64]{1,0:T(4,128)S(1)} fusion(s32[2,64]{1,0:T(2,128)S(1)} %collective-permute-done.1, s32[1,64]{1,0:T(1,128)S(1)} %collective-permute-done, s32[1,64]{1,0:T(1,128)} %ids_ref.1), kind=kLoop, calls=%fused_computation.16 | loop fusion | flops 512 | bytes 2048 | tf_op jit(solution)/shard_map/concatenate | solution.py:285
  13.6 2.7 %collective-permute-start.2 = (s32[4,64]{1,0:T(4,128)S(1)}, s32[4,64]{1,0:T(4,128)S(1)}, u32[]{:S(2)}, u32[]{:S(2)}) collective-permute-start(s32[4,64]{1,0:T(4,128)S(1)} %pad_add_fusion.1), channel_id=1, source_target_pairs={{0,4},{1,5},{2,6},{3,7},{4,0},{5,1},{6,2},{7,3},{8,12},{9,13},{10,... | collective-permute-start | bytes 3080 | tf_op jit(solution)/shard_map/ppermute | solution.py:33
  16.3 0.5 collective-permute-start.6
  16.8 0.8 %constant_dynamic-slice_fusion = bf16[32,1024]{1,0:T(8,128)(2,1)S(1)} fusion(bf16[64,1024]{1,0:T(8,128)(2,1)} %refs_2_.1, s32[]{:T(128)S(6)} %select_n.14), kind=kLoop, calls=%fused_computation.19 | loop fusion | bytes 131076 | tf_op jit(solution)/shard_map/dynamic_slice | solution.py:274
  18.3 0.0 collective-permute-done.2
  18.3 2.2 %collective-permute-start.9 = (bf16[32,1024]{1,0:T(8,128)(2,1)S(1)}, bf16[32,1024]{1,0:T(8,128)(2,1)S(1)}, u32[]{:S(2)}, u32[]{:S(2)}) collective-permute-start(bf16[32,1024]{1,0:T(8,128)(2,1)S(1)} %constant_dynamic-slice_fusion), channel_id=1, source_target_pairs={{0,7},{1,6},{2,5},{3,4},{4,3},{5,2},{6,1},{7,0},{8,15},{9,14},{10,... | collective-permute-start | bytes 196616 | tf_op jit(solution)/shard_map/ppermute | solution.py:41
  20.5 0.0 collective-permute-done.7.refs_0_.refs_7_
  20.5 0.0 collective-permute-start.8
  20.5 0.7 %pad_add_fusion.ids_ref = s32[8,64]{1,0:T(8,128)S(1)} fusion(s32[4,64]{1,0:T(4,128)S(1)} %collective-permute-done.2, s32[2,64]{1,0:T(2,128)S(1)} %collective-permute-done.1, s32[1,64]{1,0:T(1,128)S(1)} %collective-permute-done, s32[1,64]{1,0:T(1,128)} %ids_ref.1), kind=kLoop, calls=%fused_computation.15 | loop fusion | flops 1536 | bytes 4096 | tf_op jit(solution)/shard_map/concatenate | solution.py:285
  21.2 4.2 %collective-permute-done.9.refs_2_.refs_9_ = bf16[32,1024]{1,0:T(8,128)(2,1)S(1)} collective-permute-done((bf16[32,1024]{1,0:T(8,128)(2,1)S(1)}, bf16[32,1024]{1,0:T(8,128)(2,1)S(1)}, u32[]{:S(2)}, u32[]{:S(2)}) %collective-permute-start.9) | collective-permute-done | bytes 65568 | tf_op jit(solution)/shard_map/ppermute | solution.py:41
  25.4 0.0 copy-start.3
  25.4 0.9 %copy-done.3 = bf16[64,1024]{1,0:T(8,128)(2,1)S(1)} copy-done((bf16[64,1024]{1,0:T(8,128)(2,1)S(1)}, bf16[64,1024]{1,0:T(8,128)(2,1)}, u32[]{:S(2)}) %copy-start.3) | copy-done | bytes 131096
  26.3 1.6 %copy-done.7 = bf16[1024,1024]{1,0:T(8,128)(2,1)S(1)} copy-done((bf16[1024,1024]{1,0:T(8,128)(2,1)S(1)}, bf16[1024,1024]{1,0:T(8,128)(2,1)}, u32[]{:S(2)}) %copy-start.7) | copy-done | bytes 2097176
  27.9 1.2 %copy-done.8 = bf16[1,512,1024]{2,1,0:T(8,128)(2,1)S(1)} copy-done((bf16[1,512,1024]{2,1,0:T(8,128)(2,1)S(1)}, bf16[1,512,1024]{2,1,0:T(8,128)(2,1)}, u32[]{:S(2)}) %copy-start.8) | copy-done | bytes 1048600
  29.1 1.2 %copy-done.9 = bf16[1,512,1024]{2,1,0:T(8,128)(2,1)S(1)} copy-done((bf16[1,512,1024]{2,1,0:T(8,128)(2,1)S(1)}, bf16[1,512,1024]{2,1,0:T(8,128)(2,1)}, u32[]{:S(2)}) %copy-start.9) | copy-done | bytes 1048600
  30.3 2.9 %attend_first.1 = (bf16[320,1024]{1,0:T(8,128)(2,1)S(1)}, bf16[1024,1024]{1,0:T(8,128)(2,1)S(1)}, bf16[512,1024]{1,0:T(8,128)(2,1)S(1)}, bf16[512,1024]{1,0:T(8,128)(2,1)S(1)}) custom-call(s32[1]{0:T(128)S(6)} %min.6.live_ref, bf16[1024,1024]{1,0:T(8,128)(2,1)S(1)} %copy-done.7, bf16[1,512,1024]{2,1,0:T(8,128)(2,1)S(1)} %copy-done.8, ...), custom_call_target="tpu_custom_call" | custom-call | flops 1342177280 | bytes 8388608 | tf_op jit(solution)/shard_map/attend_first/pallas_call | solution.py:112
  33.3 0.0 copy-start.11
  33.3 2.4 %attend_next.1.next_ref = bf16[192,1024]{1,0:T(8,128)(2,1)S(1)} custom-call(bf16[1024,1024]{1,0:T(8,128)(2,1)S(1)} %get-tuple-element.19.w_query_ref, bf16[512,1024]{1,0:T(8,128)(2,1)S(1)} %get-tuple-element.20.keys_ref, bf16[512,1024]{1,0:T(8,128)(2,1)S(1)} %get-tuple-element.21.values_ref, bf16[64,1024]{1,0:T(8,128)(2,1)S(1)} %collective-permute-done.7.refs_0_.refs_7_, ...), custom_call_target="tpu_custom_call" | custom-call | flops 805306368 | tf_op jit(solution)/shard_map/attend_next/pallas_call | solution.py:125
  35.7 0.0 copy-start.1
  35.7 1.6 %place.1 = (bf16[256,512]{1,0:T(8,128)(2,1)S(1)}, bf16[256,512]{1,0:T(8,128)(2,1)S(1)}, bf16[256,512]{1,0:T(8,128)(2,1)S(1)}, bf16[256,512]{1,0:T(8,128)(2,1)}) custom-call(s32[8,64]{1,0:T(8,128)S(1)} %pad_add_fusion.ids_ref, bf16[320,1024]{1,0:T(8,128)(2,1)S(1)} %get-tuple-element.18.first_ref, bf16[192,1024]{1,0:T(8,128)(2,1)S(1)} %attend_next.1.next_ref), custom_call_target="tpu_custom_call" | custom-call | flops 536870912 | tf_op jit(solution)/shard_map/place/pallas_call | solution.py:172
  37.3 0.7 %copy-done.10 = bf16[256,512]{1,0:T(8,128)(2,1)} copy-done((bf16[256,512]{1,0:T(8,128)(2,1)}, bf16[256,512]{1,0:T(8,128)(2,1)S(1)}, u32[]{:S(2)}) %copy-start.10) | copy-done | bytes 262168
  38.0 1.0 %collective-permute-start.13 = (bf16[256,512]{1,0:T(8,128)(2,1)}, bf16[256,512]{1,0:T(8,128)(2,1)}, u32[]{:S(2)}, u32[]{:S(2)}) collective-permute-start(bf16[256,512]{1,0:T(8,128)(2,1)} %get-tuple-element.25), channel_id=1, source_target_pairs={{0,2},{1,3},{2,0},{3,1},{4,6},{5,7},{6,4},{7,5},{8,10},{9,11},{10,... | collective-permute-start | bytes 786440 | tf_op jit(solution)/shard_map/ppermute | solution.py:33
  39.1 0.7 %copy.13 = s32[64,1]{1,0:T(8,128)} copy(s32[64,1]{0,1:T(1,128)S(1)} %add_bitcast_fusion) | data formatting | bytes 512 | tf_op jit(solution)/shard_map/add | solution.py:321
  40.5 0.1 collective-permute-start.11
  40.5 0.8 %fusion.1.owner_ref = s32[64,1]{1,0:T(8,128)S(1)} fusion(s32[64,1]{1,0:T(8,128)} %copy.13, s32[]{:T(128)} %bitcast.6, s32[]{:T(128)S(6)} %mul.11), kind=kLoop, calls=%fused_computation.13 | loop fusion | flops 576 | bytes 520 | tf_op jit(solution)/shard_map/jit(_where)/select_n | solution.py:322
  41.3 5.8 %collective-permute-done.13 = bf16[256,512]{1,0:T(8,128)(2,1)} collective-permute-done((bf16[256,512]{1,0:T(8,128)(2,1)}, bf16[256,512]{1,0:T(8,128)(2,1)}, u32[]{:S(2)}, u32[]{:S(2)}) %collective-permute-start.13) | collective-permute-done | bytes 262176 | tf_op jit(solution)/shard_map/ppermute | solution.py:33
  47.1 1.0 %convert_add_fusion = f32[256,512]{1,0:T(8,128)S(1)} fusion(bf16[256,512]{1,0:T(8,128)(2,1)} %collective-permute-done.13, bf16[256,512]{1,0:T(8,128)(2,1)S(1)} %get-tuple-element.24), kind=kLoop, calls=%fused_computation | loop fusion | flops 393216 | bytes 1048576 | tf_op jit(solution)/shard_map/add | solution.py:313
  48.1 0.0 copy-start.4
  48.1 1.1 %collective-permute-start.14 = (bf16[128,512]{1,0:T(8,128)(2,1)S(1)}, bf16[128,512]{1,0:T(8,128)(2,1)S(1)}, u32[]{:S(2)}, u32[]{:S(2)}) collective-permute-start(bf16[128,512]{1,0:T(8,128)(2,1)S(1)} %slice.50), channel_id=1, source_target_pairs={{0,1},{1,0},{2,3},{3,2},{4,5},{5,4},{6,7},{7,6},{8,9},{9,8},{10,11... | collective-permute-start | bytes 393224 | tf_op jit(solution)/shard_map/ppermute | solution.py:33
  49.2 0.1 convert_add_fusion.1
  49.3 1.0 %collective-permute-start.12 = (bf16[128,512]{1,0:T(8,128)(2,1)S(1)}, bf16[128,512]{1,0:T(8,128)(2,1)S(1)}, u32[]{:S(2)}, u32[]{:S(2)}) collective-permute-start(bf16[128,512]{1,0:T(8,128)(2,1)S(1)} %slice.51), channel_id=1, source_target_pairs={{0,2},{1,3},{2,0},{3,1},{4,6},{5,7},{6,4},{7,5},{8,10},{9,11},{10,... | collective-permute-start | bytes 393224 | tf_op jit(solution)/shard_map/ppermute | solution.py:33
  50.3 3.0 %collective-permute-done.14 = bf16[128,512]{1,0:T(8,128)(2,1)S(1)} collective-permute-done((bf16[128,512]{1,0:T(8,128)(2,1)S(1)}, bf16[128,512]{1,0:T(8,128)(2,1)S(1)}, u32[]{:S(2)}, u32[]{:S(2)}) %collective-permute-start.14) | collective-permute-done | bytes 131104 | tf_op jit(solution)/shard_map/ppermute | solution.py:33
  53.4 1.0 %collective-permute-done.12 = bf16[128,512]{1,0:T(8,128)(2,1)S(1)} collective-permute-done((bf16[128,512]{1,0:T(8,128)(2,1)S(1)}, bf16[128,512]{1,0:T(8,128)(2,1)S(1)}, u32[]{:S(2)}, u32[]{:S(2)}) %collective-permute-start.12) | collective-permute-done | bytes 131104 | tf_op jit(solution)/shard_map/ppermute | solution.py:33
  54.5 1.6 %collective-permute-start.15 = (bf16[64,1024]{1,0:T(8,128)(2,1)S(1)}, bf16[64,1024]{1,0:T(8,128)(2,1)S(1)}, u32[]{:S(2)}, u32[]{:S(2)}) collective-permute-start(bf16[64,1024]{1,0:T(8,128)(2,1)S(1)} %pad_maximum_fusion.1), channel_id=1, source_target_pairs={{0,4},{1,5},{2,6},{3,7},{4,0},{5,1},{6,2},{7,3},{8,12},{9,13},{10,... | collective-permute-start | bytes 393224 | tf_op jit(solution)/shard_map/ppermute | solution.py:33
  56.1 0.0 copy-start.2
  56.1 1.6 %copy-done.2 = bf16[1024,1024]{1,0:T(8,128)(2,1)S(1)} copy-done((bf16[1024,1024]{1,0:T(8,128)(2,1)S(1)}, bf16[1024,1024]{1,0:T(8,128)(2,1)}, u32[]{:S(2)}) %copy-start.2) | copy-done | bytes 2097176
  57.7 2.8 %prepare.1 = (f32[64,1024]{1,0:T(8,128)S(1)}, f32[64,1024]{1,0:T(8,128)S(1)}, bf16[1024,1024]{1,0:T(8,128)(2,1)S(1)}, bf16[2,1024,1024]{2,1,0:T(8,128)(2,1)S(1)}, bf16[2,1024,1024]{2,1,0:T(8,128)(2,1)S(1)}) custom-call(bf16[256,512]{1,0:T(8,128)(2,1)S(1)} %get-tuple-element.22.after_ref, s32[1,64]{1,0:T(1,128)S(1)} %copy-done.5, ...), custom_call_target="tpu_custom_call" | custom-call | flops 201326592 | bytes 23068672 | tf_op jit(solution)/shard_map/prepare/pallas_call | solution.py:210
  60.6 1.7 %collective-permute-done.15.come_ref = bf16[64,1024]{1,0:T(8,128)(2,1)S(1)} collective-permute-done((bf16[64,1024]{1,0:T(8,128)(2,1)S(1)}, bf16[64,1024]{1,0:T(8,128)(2,1)S(1)}, u32[]{:S(2)}, u32[]{:S(2)}) %collective-permute-start.15) | collective-permute-done | bytes 131104 | tf_op jit(solution)/shard_map/ppermute | solution.py:33
  62.2 2.8 %finish.1 = bf16[1,64,1024]{2,1,0:T(8,128)(2,1)} custom-call(f32[64,1024]{1,0:T(8,128)S(1)} %pad_maximum_fusion.kept_ref, bf16[64,1024]{1,0:T(8,128)(2,1)S(1)} %collective-permute-done.15.come_ref, f32[64,1024]{1,0:T(8,128)S(1)} %get-tuple-element.26.embed_ref, f32[64,1024]{1,0:T(8,128)S(1)} %get-tuple-element.27.gating_ref, f32[1,1024]{1,0:T(1,128)S(1)} %bitcast.9, ...), custom_call_target="tpu_custom_call" | custom-call | flops 671088640 | tf_op jit(solution)/shard_map/finish/pallas_call | solution.py:239
  (34 shorter events, 0.2 us)
Async XLA Ops:
  0.0 56.1 %collective-permute-start.16 = (bf16[2,1024,1024]{2,1,0:T(8,128)(2,1)}, bf16[2,1024,1024]{2,1,0:T(8,128)(2,1)}, u32[]{:S(2)}, u32[]{:S(2)}) collective-permute-start(bf16[2,1024,1024]{2,1,0:T(8,128)(2,1)} %bitcast.7), channel_id=1, source_target_pairs={{8,0},{0,8},{9,1},{1,9},{10,2},{2,10},{11,3},{3,11},{12,4},{4,12},... | collective-permute-start | bytes 12582920 | tf_op jit(solution)/shard_map/ppermute | solution.py:46
  0.5 8.1 %collective-permute-start = (s32[1,64]{1,0:T(1,128)}, s32[1,64]{1,0:T(1,128)S(1)}, u32[]{:S(2)}, u32[]{:S(2)}) collective-permute-start(s32[1,64]{1,0:T(1,128)} %ids_ref.1), channel_id=1, source_target_pairs={{0,1},{1,0},{2,3},{3,2},{4,5},{5,4},{6,7},{7,6},{8,9},{9,8},{10,11... | collective-permute-start | bytes 776 | tf_op jit(solution)/shard_map/ppermute | solution.py:33
  3.0 13.3 %collective-permute-start.3 = (bf16[64,1024]{1,0:T(8,128)(2,1)}, bf16[64,1024]{1,0:T(8,128)(2,1)S(1)}, u32[]{:S(2)}, u32[]{:S(2)}) collective-permute-start(bf16[64,1024]{1,0:T(8,128)(2,1)} %refs_2_.1), channel_id=1, source_target_pairs={{0,1},{1,0},{2,3},{3,2},{4,5},{5,4},{6,7},{7,6},{8,10},{9,11},{10,... | collective-permute-start | bytes 393224 | tf_op jit(solution)/shard_map/ppermute | solution.py:41
  3.0 13.3 %collective-permute-start.5 = (bf16[64,1024]{1,0:T(8,128)(2,1)}, bf16[64,1024]{1,0:T(8,128)(2,1)S(1)}, u32[]{:S(2)}, u32[]{:S(2)}) collective-permute-start(bf16[64,1024]{1,0:T(8,128)(2,1)} %refs_2_.1), channel_id=1, source_target_pairs={{0,3},{1,2},{2,1},{3,0},{4,7},{5,6},{6,5},{7,4},{8,12},{9,13},{10,... | collective-permute-start | bytes 393224 | tf_op jit(solution)/shard_map/ppermute | solution.py:41
  6.0 14.5 %collective-permute-start.7 = (bf16[64,1024]{1,0:T(8,128)(2,1)}, bf16[64,1024]{1,0:T(8,128)(2,1)S(1)}, u32[]{:S(2)}, u32[]{:S(2)}) collective-permute-start(bf16[64,1024]{1,0:T(8,128)(2,1)} %refs_2_.1), channel_id=1, source_target_pairs={{0,5},{1,4},{2,7},{3,6},{4,1},{5,0},{6,3},{7,2},{8,14},{9,15},{10,... | collective-permute-start | bytes 393224 | tf_op jit(solution)/shard_map/ppermute | solution.py:41
  9.2 3.8 %collective-permute-start.1 = (s32[2,64]{1,0:T(2,128)S(1)}, s32[2,64]{1,0:T(2,128)S(1)}, u32[]{:S(2)}, u32[]{:S(2)}) collective-permute-start(s32[2,64]{1,0:T(2,128)S(1)} %pad_add_fusion.2), channel_id=1, source_target_pairs={{0,2},{1,3},{2,0},{3,1},{4,6},{5,7},{6,4},{7,5},{8,10},{9,11},{10,... | collective-permute-start | bytes 1544 | tf_op jit(solution)/shard_map/ppermute | solution.py:33
  13.6 4.7 %collective-permute-start.2 = (s32[4,64]{1,0:T(4,128)S(1)}, s32[4,64]{1,0:T(4,128)S(1)}, u32[]{:S(2)}, u32[]{:S(2)}) collective-permute-start(s32[4,64]{1,0:T(4,128)S(1)} %pad_add_fusion.1), channel_id=1, source_target_pairs={{0,4},{1,5},{2,6},{3,7},{4,0},{5,1},{6,2},{7,3},{8,12},{9,13},{10,... | collective-permute-start | bytes 3080 | tf_op jit(solution)/shard_map/ppermute | solution.py:33
  16.3 9.1 %collective-permute-start.4 = (bf16[64,1024]{1,0:T(8,128)(2,1)S(1)}, bf16[64,1024]{1,0:T(8,128)(2,1)S(1)}, u32[]{:S(2)}, u32[]{:S(2)}) collective-permute-start(bf16[64,1024]{1,0:T(8,128)(2,1)S(1)} %collective-permute-done.3.refs_1_.refs_3_), channel_id=1, source_target_pairs={{8,0},{0,8},{9,1},{1,9},{10,2},{2,10},{11,3},{3,11},{12,4},{4,12},... | collective-permute-start | bytes 393224 | tf_op jit(solution)/shard_map/ppermute | solution.py:46
  16.3 9.1 %collective-permute-start.6 = (bf16[64,1024]{1,0:T(8,128)(2,1)S(1)}, bf16[64,1024]{1,0:T(8,128)(2,1)S(1)}, u32[]{:S(2)}, u32[]{:S(2)}) collective-permute-start(bf16[64,1024]{1,0:T(8,128)(2,1)S(1)} %collective-permute-done.5.refs_3_.refs_5_), channel_id=1, source_target_pairs={{8,0},{0,8},{9,1},{1,9},{10,2},{2,10},{11,3},{3,11},{12,4},{4,12},... | collective-permute-start | bytes 393224 | tf_op jit(solution)/shard_map/ppermute | solution.py:46
  18.3 7.0 %collective-permute-start.9 = (bf16[32,1024]{1,0:T(8,128)(2,1)S(1)}, bf16[32,1024]{1,0:T(8,128)(2,1)S(1)}, u32[]{:S(2)}, u32[]{:S(2)}) collective-permute-start(bf16[32,1024]{1,0:T(8,128)(2,1)S(1)} %constant_dynamic-slice_fusion), channel_id=1, source_target_pairs={{0,7},{1,6},{2,5},{3,4},{4,3},{5,2},{6,1},{7,0},{8,15},{9,14},{10,... | collective-permute-start | bytes 196616 | tf_op jit(solution)/shard_map/ppermute | solution.py:41
  20.5 12.7 %collective-permute-start.8 = (bf16[64,1024]{1,0:T(8,128)(2,1)S(1)}, bf16[64,1024]{1,0:T(8,128)(2,1)S(1)}, u32[]{:S(2)}, u32[]{:S(2)}) collective-permute-start(bf16[64,1024]{1,0:T(8,128)(2,1)S(1)} %collective-permute-done.7.refs_0_.refs_7_), channel_id=1, source_target_pairs={{8,0},{0,8},{9,1},{1,9},{10,2},{2,10},{11,3},{3,11},{12,4},{4,12},... | collective-permute-start | bytes 393224 | tf_op jit(solution)/shard_map/ppermute | solution.py:46
  25.4 7.9 %collective-permute-start.10 = (bf16[32,1024]{1,0:T(8,128)(2,1)S(1)}, bf16[32,1024]{1,0:T(8,128)(2,1)S(1)}, u32[]{:S(2)}, u32[]{:S(2)}) collective-permute-start(bf16[32,1024]{1,0:T(8,128)(2,1)S(1)} %collective-permute-done.9.refs_2_.refs_9_), channel_id=1, source_target_pairs={{8,0},{0,8},{9,1},{1,9},{10,2},{2,10},{11,3},{3,11},{12,4},{4,12},... | collective-permute-start | bytes 196616 | tf_op jit(solution)/shard_map/ppermute | solution.py:46
  25.4 0.9 %copy-start.3 = (bf16[64,1024]{1,0:T(8,128)(2,1)S(1)}, bf16[64,1024]{1,0:T(8,128)(2,1)}, u32[]{:S(2)}) copy-start(bf16[64,1024]{1,0:T(8,128)(2,1)} %refs_2_.1) | copy-start | bytes 393220
  26.3 1.6 %copy-start.7 = (bf16[1024,1024]{1,0:T(8,128)(2,1)S(1)}, bf16[1024,1024]{1,0:T(8,128)(2,1)}, u32[]{:S(2)}) copy-start(bf16[1024,1024]{1,0:T(8,128)(2,1)} %w_query_hbm.1) | copy-start | bytes 6291460
  27.9 1.2 %copy-start.8 = (bf16[1,512,1024]{2,1,0:T(8,128)(2,1)S(1)}, bf16[1,512,1024]{2,1,0:T(8,128)(2,1)}, u32[]{:S(2)}) copy-start(bf16[1,512,1024]{2,1,0:T(8,128)(2,1)} %keys_hbm.1) | copy-start | bytes 3145732
  29.1 1.2 %copy-start.9 = (bf16[1,512,1024]{2,1,0:T(8,128)(2,1)S(1)}, bf16[1,512,1024]{2,1,0:T(8,128)(2,1)}, u32[]{:S(2)}) copy-start(bf16[1,512,1024]{2,1,0:T(8,128)(2,1)} %values_hbm.1) | copy-start | bytes 3145732
  33.3 5.8 %copy-start.11 = (s32[1,64]{1,0:T(1,128)S(1)}, s32[1,64]{1,0:T(1,128)}, u32[]{:S(2)}) copy-start(s32[1,64]{1,0:T(1,128)} %param.15) | copy-start | bytes 772
  35.7 20.4 %copy-start.1 = (bf16[1024,1024]{1,0:T(8,128)(2,1)S(1)}, bf16[1024,1024]{1,0:T(8,128)(2,1)}, u32[]{:S(2)}) copy-start(bf16[1024,1024]{1,0:T(8,128)(2,1)} %w_gate_hbm.1) | copy-start | bytes 6291460
  37.3 0.7 %copy-start.10 = (bf16[256,512]{1,0:T(8,128)(2,1)}, bf16[256,512]{1,0:T(8,128)(2,1)S(1)}, u32[]{:S(2)}) copy-start(bf16[256,512]{1,0:T(8,128)(2,1)S(1)} %get-tuple-element.23) | copy-start | bytes 786436
  38.0 9.0 %collective-permute-start.13 = (bf16[256,512]{1,0:T(8,128)(2,1)}, bf16[256,512]{1,0:T(8,128)(2,1)}, u32[]{:S(2)}, u32[]{:S(2)}) collective-permute-start(bf16[256,512]{1,0:T(8,128)(2,1)} %get-tuple-element.25), channel_id=1, source_target_pairs={{0,2},{1,3},{2,0},{3,1},{4,6},{5,7},{6,4},{7,5},{8,10},{9,11},{10,... | collective-permute-start | bytes 786440 | tf_op jit(solution)/shard_map/ppermute | solution.py:33
  40.5 8.8 %collective-permute-start.11 = (bf16[256,512]{1,0:T(8,128)(2,1)}, bf16[256,512]{1,0:T(8,128)(2,1)S(1)}, u32[]{:S(2)}, u32[]{:S(2)}) collective-permute-start(bf16[256,512]{1,0:T(8,128)(2,1)} %copy-done.10), channel_id=1, source_target_pairs={{0,1},{1,0},{2,3},{3,2},{4,5},{5,4},{6,7},{7,6},{8,9},{9,8},{10,11... | collective-permute-start | bytes 786440 | tf_op jit(solution)/shard_map/ppermute | solution.py:33
  48.1 8.0 %copy-start.4 = (bf16[64,1024]{1,0:T(8,128)(2,1)S(1)}, bf16[64,1024]{1,0:T(8,128)(2,1)}, u32[]{:S(2)}) copy-start(bf16[64,1024]{1,0:T(8,128)(2,1)} %refs_2_.1) | copy-start | bytes 393220
  48.1 5.2 %collective-permute-start.14 = (bf16[128,512]{1,0:T(8,128)(2,1)S(1)}, bf16[128,512]{1,0:T(8,128)(2,1)S(1)}, u32[]{:S(2)}, u32[]{:S(2)}) collective-permute-start(bf16[128,512]{1,0:T(8,128)(2,1)S(1)} %slice.50), channel_id=1, source_target_pairs={{0,1},{1,0},{2,3},{3,2},{4,5},{5,4},{6,7},{7,6},{8,9},{9,8},{10,11... | collective-permute-start | bytes 393224 | tf_op jit(solution)/shard_map/ppermute | solution.py:33
  49.2 6.9 %copy-start = (bf16[1,2,1024,1024]{3,2,1,0:T(8,128)(2,1)S(1)}, bf16[1,2,1024,1024]{3,2,1,0:T(8,128)(2,1)}, u32[]{:S(2)}) copy-start(bf16[1,2,1024,1024]{3,2,1,0:T(8,128)(2,1)} %param.23) | copy-start | bytes 12582916
  49.2 6.9 %copy-start.5 = (s32[1,64]{1,0:T(1,128)S(1)}, s32[1,64]{1,0:T(1,128)}, u32[]{:S(2)}) copy-start(s32[1,64]{1,0:T(1,128)} %ids_ref.1) | copy-start | bytes 772
  49.3 5.0 %collective-permute-start.12 = (bf16[128,512]{1,0:T(8,128)(2,1)S(1)}, bf16[128,512]{1,0:T(8,128)(2,1)S(1)}, u32[]{:S(2)}, u32[]{:S(2)}) collective-permute-start(bf16[128,512]{1,0:T(8,128)(2,1)S(1)} %slice.51), channel_id=1, source_target_pairs={{0,2},{1,3},{2,0},{3,1},{4,6},{5,7},{6,4},{7,5},{8,10},{9,11},{10,... | collective-permute-start | bytes 393224 | tf_op jit(solution)/shard_map/ppermute | solution.py:33
  54.5 7.8 %collective-permute-start.15 = (bf16[64,1024]{1,0:T(8,128)(2,1)S(1)}, bf16[64,1024]{1,0:T(8,128)(2,1)S(1)}, u32[]{:S(2)}, u32[]{:S(2)}) collective-permute-start(bf16[64,1024]{1,0:T(8,128)(2,1)S(1)} %pad_maximum_fusion.1), channel_id=1, source_target_pairs={{0,4},{1,5},{2,6},{3,7},{4,0},{5,1},{6,2},{7,3},{8,12},{9,13},{10,... | collective-permute-start | bytes 393224 | tf_op jit(solution)/shard_map/ppermute | solution.py:33
  56.1 1.6 %copy-start.2 = (bf16[1024,1024]{1,0:T(8,128)(2,1)S(1)}, bf16[1024,1024]{1,0:T(8,128)(2,1)}, u32[]{:S(2)}) copy-start(bf16[1024,1024]{1,0:T(8,128)(2,1)} %w_out_hbm.1) | copy-start | bytes 6291460
  57.7 4.5 %copy-start.6 = (f32[1024]{0:T(1024)S(1)}, f32[1024]{0:T(1024)}, u32[]{:S(2)}) copy-start(f32[1024]{0:T(1024)} %param.22) | copy-start | bytes 12292

commit v3 on v2

v3 whole, which is shorter than its diff:
```python
import functools

import jax
import jax.numpy as jnp
from jax import lax
from jax.experimental import pallas as pl
from jax.experimental.pallas import tpu as pltpu
from jax.sharding import PartitionSpec as P

H = 8
LAYERS = 2
VMEM_LIMIT = 24 * 1024 * 1024

norm_eps = 1e-05
F32 = jnp.float32
BF16 = jnp.bfloat16
ANY = pl.BlockSpec(memory_space=pl.ANY)
VMEM = pl.BlockSpec(memory_space=pltpu.VMEM)
SMEM = pl.BlockSpec(memory_space=pltpu.SMEM)
HBM = pl.BlockSpec(memory_space=pltpu.HBM)


def rms_scale(matrix):
    return matrix * lax.rsqrt(jnp.mean(matrix * matrix, axis=-1, keepdims=True) + norm_eps)


def silu(value):
    half = 0.5 * value
    return half + half * jnp.tanh(half)


def swapped(value, flip):
    count = lax.axis_size("hist")
    return lax.ppermute(value, "hist", [(i, i ^ flip) for i in range(count)])


def swapped_by_user(value, flips):
    count = lax.axis_size("hist")
    pairs = [
        (u * count + i, u * count + (i ^ flip)) for u, flip in enumerate(flips) for i in range(count)
    ]
    return lax.ppermute(value, ("user", "hist"), pairs)


def from_user(value, steps):
    count = lax.axis_size("user")
    return lax.ppermute(value, "user", [((i + steps) % count, i) for i in range(count)])


def kernel_call(body, name, out_shapes, in_specs, scratch=(), flops=0, moved=0):
    return pl.pallas_call(
        body,
        out_shape=out_shapes,
        in_specs=in_specs,
        out_specs=[VMEM] * len(out_shapes),
        scratch_shapes=scratch,
        compiler_params=pltpu.CompilerParams(vmem_limit_bytes=VMEM_LIMIT),
        cost_estimate=pl.CostEstimate(flops=flops, bytes_accessed=moved, transcendentals=0),
        name=name,
    )


def attend_rows(row_refs, w_query_ref, keys_ref, values_ref, sums_ref):
    width = sums_ref.shape[1]
    head_size = width // H
    rows = jnp.concatenate([ref[...] for ref in row_refs], axis=0)
    normed = rms_scale(rows.astype(F32)).astype(BF16)
    queries = jnp.dot(normed, w_query_ref[...], preferred_element_type=F32).astype(BF16)
    for head in range(H):
        cut = slice(head * head_size, (head + 1) * head_size)
        scores = lax.dot_general(
            queries[:, cut], keys_ref[0, :, cut], (((1,), (1,)), ((), ())), preferred_element_type=F32
        )
        half = scores * (0.5 * head_size ** (-0.5))
        weights = (half + half * jnp.tanh(half)).astype(BF16)
        sums_ref[:, cut] = jnp.dot(weights, values_ref[:, cut], preferred_element_type=F32).astype(BF16)


def own_kernel(live_ref, w_query_ref, keys_ref, values_ref, rows_ref, sums_ref, masked_ref):
    place = lax.broadcasted_iota(jnp.int32, masked_ref.shape, 0)
    masked_ref[...] = jnp.where(place < live_ref[0], values_ref[0].astype(F32), 0.0).astype(BF16)
    attend_rows([rows_ref], w_query_ref, keys_ref, masked_ref, sums_ref)


def next_kernel(pieces, w_query_ref, keys_ref, values_ref, *refs):
    attend_rows(refs[:pieces], w_query_ref, keys_ref, values_ref, refs[pieces])


def row_count(pieces):
    return sum(piece.shape[0] for piece in pieces)


def attend_cost(rows, width, history):
    return 2 * rows * width * (width + 2 * history)


def attend_own(rows, live_count, w_query, keys, values):
    shapes = [rows.shape, values.shape[1:]]
    return kernel_call(
        own_kernel,
        "attend_own",
        [jax.ShapeDtypeStruct(shape, BF16) for shape in shapes],
        [SMEM] + [VMEM] * 4,
        flops=attend_cost(rows.shape[0], rows.shape[1], keys.shape[1]),
    )(live_count, w_query, keys, values, rows)


def attend_next(pieces, w_query, keys, values):
    rows, width = row_count(pieces), w_query.shape[0]
    return kernel_call(
        functools.partial(next_kernel, len(pieces)),
        "attend_next",
        [jax.ShapeDtypeStruct((rows, width), BF16)],
        [VMEM] * (3 + len(pieces)),
        flops=attend_cost(rows, width, keys.shape[1]),
    )(w_query, keys, values, *pieces)[0]


def matches(layout, ids_row, hist_index, user_index, shard_rows):
    blocks = []
    for rows, steps, flips in layout:
        users = len(flips)
        owner = lax.rem(user_index + steps, users)
        flip = sum(jnp.where(owner == u, flip, 0) for u, flip in enumerate(flips))
        base = (hist_index ^ flip) * shard_rows
        item = lax.broadcasted_iota(jnp.int32, (rows, ids_row.shape[1]), 0) + base
        blocks.append((item == ids_row).astype(F32).astype(BF16))
    return jnp.concatenate(blocks, axis=0)


TRANSPOSED = (((0,), (0,)), ((), ()))


def place_kernel(layout, orders, shard_rows, parts, ids_ref, *refs):
    sums_refs, outs = refs[:parts], refs[parts:]
    slots = ids_ref.shape[1]
    ids_row = jnp.concatenate([ids_ref[flip : flip + 1, :] for flip in orders[0]], axis=1)
    onehot = matches(layout, ids_row, lax.axis_index("hist"), lax.axis_index("user"), shard_rows)
    width = sums_refs[0].shape[1] // 2
    for side, order in enumerate(orders):
        columns = slice(side * width, (side + 1) * width)
        sums = jnp.concatenate([ref[:, columns] for ref in sums_refs], axis=0)
        placed = lax.dot_general(onehot, sums, TRANSPOSED, preferred_element_type=F32).astype(BF16)
        half = len(order) // 2
        for at, flip in enumerate(order):
            block = orders[0].index(flip)
            target = outs[2 * side + at // half]
            target[at % half * slots : (at % half + 1) * slots, :] = placed[block * slots : (block + 1) * slots, :]


def place(layout, orders, shard_rows, all_ids, sums):
    devices, slots = all_ids.shape
    items, width = row_count(sums), sums[0].shape[1]
    out = jax.ShapeDtypeStruct((devices * slots // 2, width // 2), BF16)
    body = functools.partial(place_kernel, layout, orders, shard_rows, len(sums))
    return kernel_call(
        body, "place", [out] * 4, [VMEM] * (1 + len(sums)), flops=2 * items * devices * slots * width
    )(all_ids, *sums)


def prepare_kernel(layout, shard_rows, after_ref, ids_ref, w_gate_hbm, w_out_hbm, layers_hbm, *refs):
    del after_ref
    row_refs, refs = refs[: len(layout)], refs[len(layout) :]
    embed_ref, gating_ref, w_out_ref, layers_ref, w_gate_ref, sems = refs
    copies = [
        pltpu.make_async_copy(w_gate_hbm, w_gate_ref, sems.at[0]),
        pltpu.make_async_copy(w_out_hbm, w_out_ref, sems.at[1]),
        pltpu.make_async_copy(layers_hbm.at[0], layers_ref, sems.at[2]),
    ]
    for copy in copies:
        copy.start()
    onehot = matches(layout, ids_ref[...], lax.axis_index("hist"), lax.axis_index("user"), shard_rows)
    table = jnp.concatenate([ref[...] for ref in row_refs], axis=0)
    embedded = lax.dot_general(onehot, table, TRANSPOSED, preferred_element_type=F32)
    embed_ref[...] = embedded
    normed = rms_scale(embedded).astype(BF16)
    copies[0].wait()
    gating_ref[...] = silu(jnp.dot(normed, w_gate_ref[...], preferred_element_type=F32))
    for copy in copies[1:]:
        copy.wait()


def prepare(layout, shard_rows, after, ids, w_gate, w_out, expert_weights, pieces):
    slots, width = ids.shape[1], w_gate.shape[0]
    rows = jax.ShapeDtypeStruct((slots, width), F32)
    staged = [jax.ShapeDtypeStruct(shape, BF16) for shape in (w_out.shape, expert_weights.shape[1:])]
    return kernel_call(
        functools.partial(prepare_kernel, layout, shard_rows),
        "prepare",
        [rows, rows, *staged],
        [ANY, VMEM, HBM, HBM, HBM] + [VMEM] * len(pieces),
        scratch=[pltpu.VMEM(w_gate.shape, BF16), pltpu.SemaphoreType.DMA((3,))],
        flops=2 * slots * width * (width + row_count(pieces)),
        moved=2 * (w_gate.size + w_out.size + expert_weights.size),
    )(after, ids, w_gate, w_out, expert_weights, *pieces)


def finish_kernel(users, kept_ref, come_ref, embed_ref, gating_ref, gain_ref, live_ref, domain_ref, w_out_ref, *refs):
    expert_refs, out_ref = refs[:users], refs[users]
    attended = kept_ref[...] + come_ref[...].astype(F32)
    gated = (rms_scale(attended) * gain_ref[...] * gating_ref[...]).astype(BF16)
    mixed = jnp.dot(gated, w_out_ref[...], preferred_element_type=F32)
    state = (embed_ref[...] + mixed).astype(BF16)

    slots = state.shape[0]
    row_at = lax.broadcasted_iota(jnp.int32, (slots, slots), 0)
    lane_at = lax.broadcasted_iota(jnp.int32, (slots, slots), 1)
    steps_away = lax.rem(domain_ref[...] - lax.axis_index("user") + users, users)
    wanted = jnp.where(lane_at < live_ref[0], steps_away, -1)
    owner = jnp.sum(jnp.where(row_at == lane_at, wanted, 0).astype(F32), axis=1, keepdims=True)

    result = jnp.zeros(state.shape, F32)
    for steps, layers in enumerate(expert_refs):
        current = state
        for layer in range(LAYERS):
            lifted = jnp.dot(current, layers[layer], preferred_element_type=F32)
            current = (current.astype(F32) + silu(lifted)).astype(BF16)
        result = jnp.where(owner == steps, current.astype(F32), result)
    out_ref[0] = result.astype(BF16)


def finish(kept, come, embed, gating, gain, live_slots, domains, w_out, experts):
    slots, width = kept.shape
    return kernel_call(
        functools.partial(finish_kernel, len(experts)),
        "finish",
        [jax.ShapeDtypeStruct((1, slots, width), BF16)],
        [VMEM] * 5 + [SMEM] + [VMEM] * (2 + len(experts)),
        flops=2 * slots * width * width * (1 + LAYERS * len(experts)),
    )(kept, come, embed, gating, gain, live_slots, domains, w_out, *experts)[0]


def on_device(
    item_table,
    item_ids,
    candidate_counts,
    domain_ids,
    history_lengths,
    history_keys,
    history_values,
    w_query,
    w_gate,
    w_out,
    attn_gain,
    expert_weights,
):
    slot_count = item_ids.shape[1]
    shard_rows, feat_width = item_table.shape
    hist_devices = lax.axis_size("hist")
    users = lax.axis_size("user")
    hist_index = lax.axis_index("hist")
    user_index = lax.axis_index("user")
    bits = hist_devices.bit_length() - 1

    flip_groups = [tuple(range(at, min(at + users, hist_devices))) for at in range(1, hist_devices, users)]
    fetched = [swapped_by_user(item_table, flips) for flips in flip_groups]
    all_ids = item_ids
    for bit in range(bits):
        all_ids = jnp.concatenate([all_ids, swapped(all_ids, 1 << bit)], axis=0)

    def traded(block, flips):
        if len(flips) == users:
            return [from_user(block, steps) if steps else block for steps in range(users)]
        everyone = [from_user(block, steps) if steps else block for steps in range(users)]
        return [
            functools.reduce(
                lambda other, steps: jnp.where((user_index + steps) % users == u, everyone[steps], other),
                range(1, users),
                everyone[0],
            )
            for u in range(len(flips))
        ]

    def described(flips):
        if len(flips) == users:
            return [(shard_rows, steps, flips) for steps in range(users)]
        return [(shard_rows, 0, (flip,) * users) for flip in flips]

    history = history_keys.shape[1]
    live_count = jnp.clip(history_lengths - hist_index * history, 0, history).astype(jnp.int32)
    own, masked_values = attend_own(item_table, live_count, w_query, history_keys, history_values)
    sums, pieces, layout = [own], [item_table], [(shard_rows, 0, (0,) * users)]
    early = len(flip_groups) // 2
    for part in (slice(0, early), slice(early, None)):
        blocks = fetched[part]
        if part.start and early:
            *blocks, _ = lax.optimization_barrier((*blocks, sums[-1]))
        arrived = []
        for block, flips in zip(blocks, flip_groups[part]):
            arrived += traded(block, flips)
            layout += described(flips)
        if arrived:
            pieces += arrived
            sums.append(attend_next(arrived, w_query, history_keys, masked_values))

    turns = [list(range(bits)), list(range(bits))]
    if bits > 1:
        turns[1][:2] = [1, 0]
    orders = [
        [sum(((r >> (bits - 1 - t)) & 1) << bit for t, bit in enumerate(turn)) for r in range(hist_devices)]
        for turn in turns
    ]
    kept_a, sent_a, kept_b, sent_b = place(layout, orders, shard_rows, all_ids, sums)
    held = [(kept_a, sent_a), (kept_b, sent_b)]

    leaving, kept_a = lax.optimization_barrier((expert_weights[0], kept_a))
    other_layers = [from_user(leaving, steps) for steps in range(1, users)]
    embed, gating, staged_out, own_layers = prepare(
        layout, shard_rows, kept_a, item_ids, w_gate, w_out, expert_weights, pieces
    )
    for at in range(bits - 1):
        arriving = [swapped(held[side][1], 1 << turn[at]) for side, turn in enumerate(turns)]
        if at == 0:
            *arriving, embed = lax.optimization_barrier((*arriving, embed))
        for side in range(len(turns)):
            total = held[side][0].astype(F32) + arriving[side].astype(F32)
            half = total.shape[0] // 2
            held[side] = (total[:half], total[half:].astype(BF16))
    kept = jnp.concatenate([pair[0] for pair in held], axis=1)
    sent = jnp.concatenate([pair[1] for pair in held], axis=1)
    come = swapped(sent, 1 << (bits - 1))

    live_slots = candidate_counts - hist_index * slot_count
    return finish(kept, come, embed, gating, attn_gain[None], live_slots, domain_ids, staged_out, [own_layers] + other_layers)


def solution(mesh):
    in_specs = (
        P("hist", None),
        P(("groups", "user"), "hist"),
        P(("groups", "user")),
        P(("groups", "user"), "hist"),
        P(("groups", "user")),
        P(("groups", "user"), "hist", None),
        P(("groups", "user"), "hist", None),
        P(),
        P(),
        P(),
        P(),
        P("user", None, None, None),
    )
    out_specs = P(("groups", "user"), "hist", None)
    return jax.shard_map(
        on_device, mesh=mesh, in_specs=in_specs, out_specs=out_specs, check_vma=False
    )
```

time: 65.6 us -> 67.4 us (1.027)
  waiting for transfers between devices: 18.9 us -> 14.6 us
  starting transfers between devices: 19.2 us -> 23 us
  Pallas kernels: 12.6 us -> 15.5 us
  other arithmetic: 3.94 us -> 1.86 us
  local copies, waits for them, and re-layouts: 8.9 us -> 10.3 us
    ppermute x4, waiting for transfers between devices: 4.16 us -> 0.01 us  [swapped_by_user(): return lax.ppermute(value, ('user', 'hist'), pairs)]
    unnamed x24 -> x48, local copies, waits for them, and re-layouts: 7.26 us -> 10.2 us
    pallas_call x1 -> x2, Pallas kernels: 2.43 us -> 5.11 us  [attend_next(): kernel_call(functools.partial(next_kernel, len(pieces)), 'attend_next', [...]
    ppermute x4, starting transfers between devices: 7.77 us -> 9.94 us  [swapped_by_user(): return lax.ppermute(value, ('user', 'hist'), pairs)]
    pallas_call x1, Pallas kernels: 2.83 us -> 4.98 us  [finish(): kernel_call(functools.partial(finish_kernel, len(experts)), 'finish', [ja...]
    pallas_call x3, Pallas kernels: 7.33 us -> 5.39 us  [the longest x1 2.53 us: prepare(): kernel_call(functools.partial(prepare_kernel, layout, shard_rows), 'prepa...]
    ppermute x8, starting transfers between devices: 10.4 us -> 12.3 us  [swapped(): return lax.ppermute(value, 'hist', [(i, i ^ flip) for i in range(count)])]
    concatenate x3, other arithmetic: 1.99 us -> 0.7 us  [on_device(): all_ids = jnp.concatenate([all_ids, swapped(all_ids, 1 << bit)], axis=0)]
  transfers between devices with their start and end apart: 17 -> 17, of which waited for: 6 -> 7; matrix products, arithmetic and copies ran while one was open for 9% -> 3% of each run, Pallas kernels for 15% -> 11%
where the time goes in v3:
time: 67.4 us; the launch traced here: 66.9 us
  starting transfers between devices  23 us (34%)
  Pallas kernels  15.5 us (23%)
  waiting for transfers between devices  14.6 us (22%)
  local copies, waits for them, and re-layouts  10.3 us (15%)
  other arithmetic  1.86 us (3%)
  between operations  1.7 us (3%)
    ppermute x8, waiting for transfers between devices, swapped(): return lax.ppermute(value, 'hist', [(i, i ^ flip) for i in range(count)])  14.1 us
    ppermute x8, starting transfers between devices, swapped(): return lax.ppermute(value, 'hist', [(i, i ^ flip) for i in range(count)])  12.3 us
    unnamed x48, local copies, waits for them, and re-layouts  10.2 us
    ppermute x4, starting transfers between devices, swapped_by_user(): return lax.ppermute(value, ('user', 'hist'), pairs)  9.94 us
    pallas_call x2, Pallas kernels, attend_next(): kernel_call(functools.partial(next_kernel, len(pieces)), 'attend_next', [...  5.11 us
    pallas_call x1, Pallas kernels, finish(): kernel_call(functools.partial(finish_kernel, len(experts)), 'finish', [ja...  4.98 us
    pallas_call x1, Pallas kernels, prepare(): kernel_call(functools.partial(prepare_kernel, layout, shard_rows), 'prepa...  2.53 us
    pallas_call x1, Pallas kernels, attend_own(): kernel_call(own_kernel, 'attend_own', [jax.ShapeDtypeStruct(shape, BF16)...  2 us
  transfers between devices with their start and end apart: 17, of which 7 were waited for; matrix products, arithmetic and copies ran while one was open for 3% of the time, Pallas kernels for 11%

profile of v3, /device:TPU:0, one launch (start us, length us, event | category | flops | bytes accessed | tf_op | source)
XLA Modules:
  0.0 66.9 jit_solution(2808938197084816660)
XLA Ops:
  0.0 3.0 %collective-permute-start.3 = (bf16[64,1024]{1,0:T(8,128)(2,1)}, bf16[64,1024]{1,0:T(8,128)(2,1)S(1)}, u32[]{:S(2)}, u32[]{:S(2)}) collective-permute-start(bf16[64,1024]{1,0:T(8,128)(2,1)} %refs_0_.1), channel_id=1, source_target_pairs={{0,1},{1,0},{2,3},{3,2},{4,5},{5,4},{6,7},{7,6},{8,10},{9,11},{10,... | collective-permute-start | bytes 393224 | tf_op jit(solution)/shard_map/ppermute | solution.py:42
  3.0 1.5 %collective-permute-start.5 = (bf16[64,1024]{1,0:T(8,128)(2,1)}, bf16[64,1024]{1,0:T(8,128)(2,1)S(1)}, u32[]{:S(2)}, u32[]{:S(2)}) collective-permute-start(bf16[64,1024]{1,0:T(8,128)(2,1)} %refs_0_.1), channel_id=1, source_target_pairs={{0,3},{1,2},{2,1},{3,0},{4,7},{5,6},{6,5},{7,4},{8,12},{9,13},{10,... | collective-permute-start | bytes 393224 | tf_op jit(solution)/shard_map/ppermute | solution.py:42
  4.5 3.5 %collective-permute-start.7 = (bf16[64,1024]{1,0:T(8,128)(2,1)}, bf16[64,1024]{1,0:T(8,128)(2,1)S(1)}, u32[]{:S(2)}, u32[]{:S(2)}) collective-permute-start(bf16[64,1024]{1,0:T(8,128)(2,1)} %refs_0_.1), channel_id=1, source_target_pairs={{0,5},{1,4},{2,7},{3,6},{4,1},{5,0},{6,3},{7,2},{8,14},{9,15},{10,... | collective-permute-start | bytes 393224 | tf_op jit(solution)/shard_map/ppermute | solution.py:42
  8.0 1.9 %collective-permute-start.8 = (bf16[64,1024]{1,0:T(8,128)(2,1)}, bf16[64,1024]{1,0:T(8,128)(2,1)}, u32[]{:S(2)}, u32[]{:S(2)}) collective-permute-start(bf16[64,1024]{1,0:T(8,128)(2,1)} %refs_0_.1), channel_id=1, source_target_pairs={{0,7},{1,6},{2,5},{3,4},{4,3},{5,2},{6,1},{7,0},{16,23},{17,22},{1... | collective-permute-start | bytes 393224 | tf_op jit(solution)/shard_map/ppermute | solution.py:42
  10.0 1.7 %collective-permute-start = (s32[1,64]{1,0:T(1,128)}, s32[1,64]{1,0:T(1,128)S(1)}, u32[]{:S(2)}, u32[]{:S(2)}) collective-permute-start(s32[1,64]{1,0:T(1,128)} %ids_ref.1), channel_id=1, source_target_pairs={{0,1},{1,0},{2,3},{3,2},{4,5},{5,4},{6,7},{7,6},{8,9},{9,8},{10,11... | collective-permute-start | bytes 776 | tf_op jit(solution)/shard_map/ppermute | solution.py:34
  12.4 0.0 collective-permute-done.3.refs_0_.refs_1_
  12.4 0.1 collective-permute-start.4
  12.5 0.5 collective-permute-start.6
  12.9 1.6 %copy-done = bf16[1024,1024]{1,0:T(8,128)(2,1)S(1)} copy-done((bf16[1024,1024]{1,0:T(8,128)(2,1)S(1)}, bf16[1024,1024]{1,0:T(8,128)(2,1)}, u32[]{:S(2)}) %copy-start) | copy-done | bytes 2097176
  14.5 1.2 %copy-done.2 = bf16[1,512,1024]{2,1,0:T(8,128)(2,1)S(1)} copy-done((bf16[1,512,1024]{2,1,0:T(8,128)(2,1)S(1)}, bf16[1,512,1024]{2,1,0:T(8,128)(2,1)}, u32[]{:S(2)}) %copy-start.2) | copy-done | bytes 1048600
  15.8 1.2 %copy-done.10 = bf16[1,512,1024]{2,1,0:T(8,128)(2,1)S(1)} copy-done((bf16[1,512,1024]{2,1,0:T(8,128)(2,1)S(1)}, bf16[1,512,1024]{2,1,0:T(8,128)(2,1)}, u32[]{:S(2)}) %copy-start.10) | copy-done | bytes 1048600
  17.0 0.9 %copy-done.11 = bf16[64,1024]{1,0:T(8,128)(2,1)S(1)} copy-done((bf16[64,1024]{1,0:T(8,128)(2,1)S(1)}, bf16[64,1024]{1,0:T(8,128)(2,1)}, u32[]{:S(2)}) %copy-start.11) | copy-done | bytes 131096
  17.9 2.0 %attend_own.1 = (bf16[64,1024]{1,0:T(8,128)(2,1)S(1)}, bf16[512,1024]{1,0:T(8,128)(2,1)S(1)}) custom-call(s32[1]{0:T(128)S(6)} %min.6.live_ref, bf16[1024,1024]{1,0:T(8,128)(2,1)S(1)} %copy-done, bf16[1,512,1024]{2,1,0:T(8,128)(2,1)S(1)} %copy-done.2, bf16[1,512,1024]{2,1,0:T(8,128)(2,1)S(1)} %copy-done.10, bf16[64,1024]{1,0:T(8,128)(2,1)S(1)} %copy-done.11), custom_call_target="tpu_custom_call" | custom-call | flops 268435456 | tf_op jit(solution)/shard_map/attend_own/pallas_call | solution.py:99
  19.9 0.0 copy-start.22
  19.9 0.0 collective-permute-done
  20.0 0.7 %collective-permute-start.1 = (s32[2,64]{1,0:T(2,128)S(1)}, s32[2,64]{1,0:T(2,128)S(1)}, u32[]{:S(2)}, u32[]{:S(2)}) collective-permute-start(s32[2,64]{1,0:T(2,128)S(1)} %pad_add_fusion.2), channel_id=1, source_target_pairs={{0,2},{1,3},{2,0},{3,1},{4,6},{5,7},{6,4},{7,5},{8,10},{9,11},{10,... | collective-permute-start | bytes 1544 | tf_op jit(solution)/shard_map/ppermute | solution.py:34
  20.7 0.0 collective-permute-done.4.refs_1_.refs_2_
  20.7 2.7 %attend_next.2.refs_1_ = bf16[256,1024]{1,0:T(8,128)(2,1)S(1)} custom-call(bf16[1024,1024]{1,0:T(8,128)(2,1)S(1)} %copy-done.1, bf16[1,512,1024]{2,1,0:T(8,128)(2,1)S(1)} %copy-done.3, bf16[512,1024]{1,0:T(8,128)(2,1)S(1)} %get-tuple-element.23.values_ref, bf16[64,1024]{1,0:T(8,128)(2,1)S(1)} %collective-permute-done.3.refs_0_.refs_1_, ...), custom_call_target="tpu_custom_call" | custom-call | flops 1073741824 | tf_op jit(solution)/shard_map/attend_next/pallas_call | solution.py:110
  23.5 0.8 %copy-done.17 = bf16[256,1024]{1,0:T(8,128)(2,1)} copy-done((bf16[256,1024]{1,0:T(8,128)(2,1)}, bf16[256,1024]{1,0:T(8,128)(2,1)S(1)}, u32[]{:S(2)}) %copy-start.17) | copy-done | bytes 524312
  24.3 0.0 collective-permute-done.7.refs_0_.refs_5_
  24.3 0.0 collective-permute-done.8
  24.3 0.0 collective-permute-start.10
  24.3 0.0 collective-permute-done.1
  24.3 3.6 %collective-permute-start.2 = (s32[4,64]{1,0:T(4,128)S(1)}, s32[4,64]{1,0:T(4,128)}, u32[]{:S(2)}, u32[]{:S(2)}) collective-permute-start(s32[4,64]{1,0:T(4,128)S(1)} %pad_add_fusion.1), channel_id=1, source_target_pairs={{0,4},{1,5},{2,6},{3,7},{4,0},{5,1},{6,2},{7,3},{8,12},{9,13},{10,... | collective-permute-start | bytes 3080 | tf_op jit(solution)/shard_map/ppermute | solution.py:34
  27.9 1.7 %collective-permute-done.2 = s32[4,64]{1,0:T(4,128)} collective-permute-done((s32[4,64]{1,0:T(4,128)S(1)}, s32[4,64]{1,0:T(4,128)}, u32[]{:S(2)}, u32[]{:S(2)}) %collective-permute-start.2) | collective-permute-done | bytes 1056 | tf_op jit(solution)/shard_map/ppermute | solution.py:34
  29.5 0.7 %pad_add_fusion.ids_ref = s32[8,64]{1,0:T(8,128)S(1)} fusion(s32[4,64]{1,0:T(4,128)} %collective-permute-done.2, s32[2,64]{1,0:T(2,128)S(1)} %collective-permute-done.1, s32[1,64]{1,0:T(1,128)S(1)} %collective-permute-done, s32[1,64]{1,0:T(1,128)S(1)} %copy-done.19), kind=kLoop, calls=%fused_computation.11 | loop fusion | flops 1536 | bytes 4096 | tf_op jit(solution)/shard_map/concatenate | solution.py:259
  30.3 0.9 %broadcast_select_fusion.refs_2_.refs_7_ = bf16[64,1024]{1,0:T(8,128)(2,1)S(1)} fusion(bf16[64,1024]{1,0:T(8,128)(2,1)} %collective-permute-done.10, bf16[64,1024]{1,0:T(8,128)(2,1)} %collective-permute-done.8, pred[]{:T(512)S(6)} %eq.5), kind=kLoop, calls=%fused_computation.10 | loop fusion | flops 65536 | bytes 393217 | tf_op jit(solution)/shard_map/jit(_where)/select_n | solution.py:267
  31.2 0.4 collective-permute-done.9.refs_1_.refs_6_
  31.6 1.2 %copy-done.5 = bf16[512,1024]{1,0:T(8,128)(2,1)S(1)} copy-done((bf16[512,1024]{1,0:T(8,128)(2,1)S(1)}, bf16[512,1024]{1,0:T(8,128)(2,1)}, u32[]{:S(2)}) %copy-start.5) | copy-done | bytes 1048600
  32.8 2.4 %attend_next.3.refs_2_ = bf16[192,1024]{1,0:T(8,128)(2,1)S(1)} custom-call(bf16[1024,1024]{1,0:T(8,128)(2,1)S(1)} %copy-done.1, bf16[1,512,1024]{2,1,0:T(8,128)(2,1)S(1)} %copy-done.3, bf16[512,1024]{1,0:T(8,128)(2,1)S(1)} %copy-done.5, bf16[64,1024]{1,0:T(8,128)(2,1)S(1)} %collective-permute-done.7.refs_0_.refs_5_, ...), custom_call_target="tpu_custom_call" | custom-call | flops 805306368 | tf_op jit(solution)/shard_map/attend_next/pallas_call | solution.py:110
  35.3 1.0 %copy-done.18 = bf16[256,1024]{1,0:T(8,128)(2,1)S(1)} copy-done((bf16[256,1024]{1,0:T(8,128)(2,1)S(1)}, bf16[256,1024]{1,0:T(8,128)(2,1)}, u32[]{:S(2)}) %copy-start.18) | copy-done | bytes 524312
  36.3 0.9 %place.1 = (bf16[256,512]{1,0:T(8,128)(2,1)S(1)}, bf16[256,512]{1,0:T(8,128)(2,1)S(1)}, bf16[256,512]{1,0:T(8,128)(2,1)S(1)}, bf16[256,512]{1,0:T(8,128)(2,1)S(1)}) custom-call(s32[8,64]{1,0:T(8,128)S(1)} %pad_add_fusion.ids_ref, bf16[64,1024]{1,0:T(8,128)(2,1)S(1)} %copy-done.23, bf16[256,1024]{1,0:T(8,128)(2,1)S(1)} %copy-done.18, ...), custom_call_target="tpu_custom_call" | custom-call | flops 536870912 | tf_op jit(solution)/shard_map/place/pallas_call | solution.py:156
  37.2 0.2 collective-permute-start.16
  37.4 0.5 collective-permute-start.11
  37.9 0.6 collective-permute-start.12
  38.6 2.5 %prepare.1 = (f32[64,1024]{1,0:T(8,128)S(1)}, f32[64,1024]{1,0:T(8,128)S(1)}, bf16[1024,1024]{1,0:T(8,128)(2,1)S(1)}, bf16[2,1024,1024]{2,1,0:T(8,128)(2,1)S(1)}) custom-call(bf16[256,512]{1,0:T(8,128)(2,1)S(1)} %get-tuple-element.29.after_ref, s32[1,64]{1,0:T(1,128)S(1)} %copy-done.19, bf16[1024,1024]{1,0:T(8,128)(2,1)S(1)} %copy-done.8, ...), custom_call_target="tpu_custom_call" | custom-call | flops 201326592 | bytes 8388608 | tf_op jit(solution)/shard_map/prepare/pallas_call | solution.py:187
  41.1 4.8 %collective-permute-done.11 = bf16[256,512]{1,0:T(8,128)(2,1)S(1)} collective-permute-done((bf16[256,512]{1,0:T(8,128)(2,1)S(1)}, bf16[256,512]{1,0:T(8,128)(2,1)S(1)}, u32[]{:S(2)}, u32[]{:S(2)}) %collective-permute-start.11) | collective-permute-done | bytes 262176 | tf_op jit(solution)/shard_map/ppermute | solution.py:34
  46.0 0.2 collective-permute-done.12
  46.2 0.1 convert_add_fusion.1
  46.3 0.7 %collective-permute-start.13 = (bf16[128,512]{1,0:T(8,128)(2,1)S(1)}, bf16[128,512]{1,0:T(8,128)(2,1)S(1)}, u32[]{:S(2)}, u32[]{:S(2)}) collective-permute-start(bf16[128,512]{1,0:T(8,128)(2,1)S(1)} %slice.51), channel_id=1, source_target_pairs={{0,2},{1,3},{2,0},{3,1},{4,6},{5,7},{6,4},{7,5},{8,10},{9,11},{10,... | collective-permute-start | bytes 393224 | tf_op jit(solution)/shard_map/ppermute | solution.py:34
  47.0 0.1 convert_add_fusion
  47.1 1.7 %collective-permute-start.14 = (bf16[128,512]{1,0:T(8,128)(2,1)S(1)}, bf16[128,512]{1,0:T(8,128)(2,1)S(1)}, u32[]{:S(2)}, u32[]{:S(2)}) collective-permute-start(bf16[128,512]{1,0:T(8,128)(2,1)S(1)} %slice.50), channel_id=1, source_target_pairs={{0,1},{1,0},{2,3},{3,2},{4,5},{5,4},{6,7},{7,6},{8,9},{9,8},{10,11... | collective-permute-start | bytes 393224 | tf_op jit(solution)/shard_map/ppermute | solution.py:34
  48.8 2.5 %collective-permute-done.13 = bf16[128,512]{1,0:T(8,128)(2,1)S(1)} collective-permute-done((bf16[128,512]{1,0:T(8,128)(2,1)S(1)}, bf16[128,512]{1,0:T(8,128)(2,1)S(1)}, u32[]{:S(2)}, u32[]{:S(2)}) %collective-permute-start.13) | collective-permute-done | bytes 131104 | tf_op jit(solution)/shard_map/ppermute | solution.py:34
  51.4 0.7 %collective-permute-done.14 = bf16[128,512]{1,0:T(8,128)(2,1)S(1)} collective-permute-done((bf16[128,512]{1,0:T(8,128)(2,1)S(1)}, bf16[128,512]{1,0:T(8,128)(2,1)S(1)}, u32[]{:S(2)}, u32[]{:S(2)}) %collective-permute-start.14) | collective-permute-done | bytes 131104 | tf_op jit(solution)/shard_map/ppermute | solution.py:34
  52.2 2.6 %collective-permute-start.15 = (bf16[64,1024]{1,0:T(8,128)(2,1)S(1)}, bf16[64,1024]{1,0:T(8,128)(2,1)S(1)}, u32[]{:S(2)}, u32[]{:S(2)}) collective-permute-start(bf16[64,1024]{1,0:T(8,128)(2,1)S(1)} %pad_maximum_fusion.1), channel_id=1, source_target_pairs={{0,4},{1,5},{2,6},{3,7},{4,0},{5,1},{6,2},{7,3},{8,12},{9,13},{10,... | collective-permute-start | bytes 393224 | tf_op jit(solution)/shard_map/ppermute | solution.py:34
  55.5 4.2 %collective-permute-done.15.come_ref = bf16[64,1024]{1,0:T(8,128)(2,1)S(1)} collective-permute-done((bf16[64,1024]{1,0:T(8,128)(2,1)S(1)}, bf16[64,1024]{1,0:T(8,128)(2,1)S(1)}, u32[]{:S(2)}, u32[]{:S(2)}) %collective-permute-start.15) | collective-permute-done | bytes 131104 | tf_op jit(solution)/shard_map/ppermute | solution.py:34
  59.7 2.2 %copy-done.7 = bf16[2,1024,1024]{2,1,0:T(8,128)(2,1)S(1)} copy-done((bf16[2,1024,1024]{2,1,0:T(8,128)(2,1)S(1)}, bf16[2,1024,1024]{2,1,0:T(8,128)(2,1)}, u32[]{:S(2)}) %copy-start.7) | copy-done | bytes 4194328
  61.9 5.0 %finish.1 = bf16[1,64,1024]{2,1,0:T(8,128)(2,1)} custom-call(f32[64,1024]{1,0:T(8,128)S(1)} %pad_maximum_fusion.kept_ref, bf16[64,1024]{1,0:T(8,128)(2,1)S(1)} %collective-permute-done.15.come_ref, f32[64,1024]{1,0:T(8,128)S(1)} %get-tuple-element.34.embed_ref, f32[64,1024]{1,0:T(8,128)S(1)} %get-tuple-element.35.gating_ref, f32[1,1024]{1,0:T(1,128)S(1)} %bitcast.4, ...), custom_call_target="tpu_custom_call" | custom-call | flops 671088640 | tf_op jit(solution)/shard_map/finish/pallas_call | solution.py:224
  (56 shorter events, 0.3 us)
Async XLA Ops:
  0.0 12.4 %collective-permute-start.3 = (bf16[64,1024]{1,0:T(8,128)(2,1)}, bf16[64,1024]{1,0:T(8,128)(2,1)S(1)}, u32[]{:S(2)}, u32[]{:S(2)}) collective-permute-start(bf16[64,1024]{1,0:T(8,128)(2,1)} %refs_0_.1), channel_id=1, source_target_pairs={{0,1},{1,0},{2,3},{3,2},{4,5},{5,4},{6,7},{7,6},{8,10},{9,11},{10,... | collective-permute-start | bytes 393224 | tf_op jit(solution)/shard_map/ppermute | solution.py:42
  3.0 9.5 %collective-permute-start.5 = (bf16[64,1024]{1,0:T(8,128)(2,1)}, bf16[64,1024]{1,0:T(8,128)(2,1)S(1)}, u32[]{:S(2)}, u32[]{:S(2)}) collective-permute-start(bf16[64,1024]{1,0:T(8,128)(2,1)} %refs_0_.1), channel_id=1, source_target_pairs={{0,3},{1,2},{2,1},{3,0},{4,7},{5,6},{6,5},{7,4},{8,12},{9,13},{10,... | collective-permute-start | bytes 393224 | tf_op jit(solution)/shard_map/ppermute | solution.py:42
  4.5 19.8 %collective-permute-start.7 = (bf16[64,1024]{1,0:T(8,128)(2,1)}, bf16[64,1024]{1,0:T(8,128)(2,1)S(1)}, u32[]{:S(2)}, u32[]{:S(2)}) collective-permute-start(bf16[64,1024]{1,0:T(8,128)(2,1)} %refs_0_.1), channel_id=1, source_target_pairs={{0,5},{1,4},{2,7},{3,6},{4,1},{5,0},{6,3},{7,2},{8,14},{9,15},{10,... | collective-permute-start | bytes 393224 | tf_op jit(solution)/shard_map/ppermute | solution.py:42
  8.0 16.2 %collective-permute-start.8 = (bf16[64,1024]{1,0:T(8,128)(2,1)}, bf16[64,1024]{1,0:T(8,128)(2,1)}, u32[]{:S(2)}, u32[]{:S(2)}) collective-permute-start(bf16[64,1024]{1,0:T(8,128)(2,1)} %refs_0_.1), channel_id=1, source_target_pairs={{0,7},{1,6},{2,5},{3,4},{4,3},{5,2},{6,1},{7,0},{16,23},{17,22},{1... | collective-permute-start | bytes 393224 | tf_op jit(solution)/shard_map/ppermute | solution.py:42
  10.0 10.0 %collective-permute-start = (s32[1,64]{1,0:T(1,128)}, s32[1,64]{1,0:T(1,128)S(1)}, u32[]{:S(2)}, u32[]{:S(2)}) collective-permute-start(s32[1,64]{1,0:T(1,128)} %ids_ref.1), channel_id=1, source_target_pairs={{0,1},{1,0},{2,3},{3,2},{4,5},{5,4},{6,7},{7,6},{8,9},{9,8},{10,11... | collective-permute-start | bytes 776 | tf_op jit(solution)/shard_map/ppermute | solution.py:34
  12.3 7.6 %copy-start.19 = (s32[1,64]{1,0:T(1,128)S(1)}, s32[1,64]{1,0:T(1,128)}, u32[]{:S(2)}) copy-start(s32[1,64]{1,0:T(1,128)} %ids_ref.1) | copy-start | bytes 772
  12.4 8.3 %collective-permute-start.4 = (bf16[64,1024]{1,0:T(8,128)(2,1)S(1)}, bf16[64,1024]{1,0:T(8,128)(2,1)S(1)}, u32[]{:S(2)}, u32[]{:S(2)}) collective-permute-start(bf16[64,1024]{1,0:T(8,128)(2,1)S(1)} %collective-permute-done.3.refs_0_.refs_1_), channel_id=1, source_target_pairs={{8,0},{0,8},{9,1},{1,9},{10,2},{2,10},{11,3},{3,11},{12,4},{4,12},... | collective-permute-start | bytes 393224 | tf_op jit(solution)/shard_map/ppermute | solution.py:47
  12.5 8.2 %collective-permute-start.6 = (bf16[64,1024]{1,0:T(8,128)(2,1)S(1)}, bf16[64,1024]{1,0:T(8,128)(2,1)S(1)}, u32[]{:S(2)}, u32[]{:S(2)}) collective-permute-start(bf16[64,1024]{1,0:T(8,128)(2,1)S(1)} %collective-permute-done.5.refs_2_.refs_3_), channel_id=1, source_target_pairs={{8,0},{0,8},{9,1},{1,9},{10,2},{2,10},{11,3},{3,11},{12,4},{4,12},... | collective-permute-start | bytes 393224 | tf_op jit(solution)/shard_map/ppermute | solution.py:47
  12.9 1.6 %copy-start = (bf16[1024,1024]{1,0:T(8,128)(2,1)S(1)}, bf16[1024,1024]{1,0:T(8,128)(2,1)}, u32[]{:S(2)}) copy-start(bf16[1024,1024]{1,0:T(8,128)(2,1)} %w_query_ref.5) | copy-start | bytes 6291460
  14.5 1.2 %copy-start.2 = (bf16[1,512,1024]{2,1,0:T(8,128)(2,1)S(1)}, bf16[1,512,1024]{2,1,0:T(8,128)(2,1)}, u32[]{:S(2)}) copy-start(bf16[1,512,1024]{2,1,0:T(8,128)(2,1)} %keys_ref.5) | copy-start | bytes 3145732
  15.8 1.2 %copy-start.10 = (bf16[1,512,1024]{2,1,0:T(8,128)(2,1)S(1)}, bf16[1,512,1024]{2,1,0:T(8,128)(2,1)}, u32[]{:S(2)}) copy-start(bf16[1,512,1024]{2,1,0:T(8,128)(2,1)} %values_ref.1) | copy-start | bytes 3145732
  17.0 0.9 %copy-start.11 = (bf16[64,1024]{1,0:T(8,128)(2,1)S(1)}, bf16[64,1024]{1,0:T(8,128)(2,1)}, u32[]{:S(2)}) copy-start(bf16[64,1024]{1,0:T(8,128)(2,1)} %refs_0_.1) | copy-start | bytes 393220
  17.9 2.8 %copy-start.1 = (bf16[1024,1024]{1,0:T(8,128)(2,1)S(1)}, bf16[1024,1024]{1,0:T(8,128)(2,1)}, u32[]{:S(2)}) copy-start(bf16[1024,1024]{1,0:T(8,128)(2,1)} %w_query_ref.5) | copy-start | bytes 6291460
  17.9 2.8 %copy-start.3 = (bf16[1,512,1024]{2,1,0:T(8,128)(2,1)S(1)}, bf16[1,512,1024]{2,1,0:T(8,128)(2,1)}, u32[]{:S(2)}) copy-start(bf16[1,512,1024]{2,1,0:T(8,128)(2,1)} %keys_ref.5) | copy-start | bytes 3145732
  19.9 3.5 %copy-start.4 = (bf16[512,1024]{1,0:T(8,128)(2,1)}, bf16[512,1024]{1,0:T(8,128)(2,1)S(1)}, u32[]{:S(2)}) copy-start(bf16[512,1024]{1,0:T(8,128)(2,1)S(1)} %get-tuple-element.23.values_ref) | copy-start | bytes 3145732
  19.9 3.5 %copy-start.22 = (bf16[64,1024]{1,0:T(8,128)(2,1)}, bf16[64,1024]{1,0:T(8,128)(2,1)S(1)}, u32[]{:S(2)}) copy-start(bf16[64,1024]{1,0:T(8,128)(2,1)S(1)} %get-tuple-element.22.refs_0_) | copy-start | bytes 393220
  20.0 4.3 %collective-permute-start.1 = (s32[2,64]{1,0:T(2,128)S(1)}, s32[2,64]{1,0:T(2,128)S(1)}, u32[]{:S(2)}, u32[]{:S(2)}) collective-permute-start(s32[2,64]{1,0:T(2,128)S(1)} %pad_add_fusion.2), channel_id=1, source_target_pairs={{0,2},{1,3},{2,0},{3,1},{4,6},{5,7},{6,4},{7,5},{8,10},{9,11},{10,... | collective-permute-start | bytes 1544 | tf_op jit(solution)/shard_map/ppermute | solution.py:34
  20.7 2.8 %copy-start.13 = (bf16[64,1024]{1,0:T(8,128)(2,1)}, bf16[64,1024]{1,0:T(8,128)(2,1)S(1)}, u32[]{:S(2)}) copy-start(bf16[64,1024]{1,0:T(8,128)(2,1)S(1)} %collective-permute-done.4.refs_1_.refs_2_) | copy-start | bytes 393220
  20.7 2.8 %copy-start.15 = (bf16[64,1024]{1,0:T(8,128)(2,1)}, bf16[64,1024]{1,0:T(8,128)(2,1)S(1)}, u32[]{:S(2)}) copy-start(bf16[64,1024]{1,0:T(8,128)(2,1)S(1)} %collective-permute-done.6.refs_3_.refs_4_) | copy-start | bytes 393220
  23.5 0.8 %copy-start.17 = (bf16[256,1024]{1,0:T(8,128)(2,1)}, bf16[256,1024]{1,0:T(8,128)(2,1)S(1)}, u32[]{:S(2)}) copy-start(bf16[256,1024]{1,0:T(8,128)(2,1)S(1)} %attend_next.2.refs_1_) | copy-start | bytes 1572868
  24.3 6.0 %collective-permute-start.10 = (bf16[64,1024]{1,0:T(8,128)(2,1)}, bf16[64,1024]{1,0:T(8,128)(2,1)}, u32[]{:S(2)}, u32[]{:S(2)}) collective-permute-start(bf16[64,1024]{1,0:T(8,128)(2,1)} %collective-permute-done.8), channel_id=1, source_target_pairs={{8,0},{0,8},{9,1},{1,9},{10,2},{2,10},{11,3},{3,11},{12,4},{4,12},... | collective-permute-start | bytes 393224 | tf_op jit(solution)/shard_map/ppermute | solution.py:47
  24.3 5.2 %collective-permute-start.2 = (s32[4,64]{1,0:T(4,128)S(1)}, s32[4,64]{1,0:T(4,128)}, u32[]{:S(2)}, u32[]{:S(2)}) collective-permute-start(s32[4,64]{1,0:T(4,128)S(1)} %pad_add_fusion.1), channel_id=1, source_target_pairs={{0,4},{1,5},{2,6},{3,7},{4,0},{5,1},{6,2},{7,3},{8,12},{9,13},{10,... | collective-permute-start | bytes 3080 | tf_op jit(solution)/shard_map/ppermute | solution.py:34
  30.2 1.3 %collective-permute-start.9 = (bf16[64,1024]{1,0:T(8,128)(2,1)S(1)}, bf16[64,1024]{1,0:T(8,128)(2,1)S(1)}, u32[]{:S(2)}, u32[]{:S(2)}) collective-permute-start(bf16[64,1024]{1,0:T(8,128)(2,1)S(1)} %collective-permute-done.7.refs_0_.refs_5_), channel_id=1, source_target_pairs={{8,0},{0,8},{9,1},{1,9},{10,2},{2,10},{11,3},{3,11},{12,4},{4,12},... | collective-permute-start | bytes 393224 | tf_op jit(solution)/shard_map/ppermute | solution.py:47
  31.6 1.2 %copy-start.5 = (bf16[512,1024]{1,0:T(8,128)(2,1)S(1)}, bf16[512,1024]{1,0:T(8,128)(2,1)}, u32[]{:S(2)}) copy-start(bf16[512,1024]{1,0:T(8,128)(2,1)} %copy-done.4) | copy-start | bytes 3145732
  32.8 2.4 %copy-start.23 = (bf16[64,1024]{1,0:T(8,128)(2,1)S(1)}, bf16[64,1024]{1,0:T(8,128)(2,1)}, u32[]{:S(2)}) copy-start(bf16[64,1024]{1,0:T(8,128)(2,1)} %copy-done.22) | copy-start | bytes 393220
  32.8 5.7 %copy-start.8 = (bf16[1024,1024]{1,0:T(8,128)(2,1)S(1)}, bf16[1024,1024]{1,0:T(8,128)(2,1)}, u32[]{:S(2)}) copy-start(bf16[1024,1024]{1,0:T(8,128)(2,1)} %w_gate_hbm.1) | copy-start | bytes 6291460
  32.8 5.7 %copy-start.9 = (bf16[1024,1024]{1,0:T(8,128)(2,1)S(1)}, bf16[1024,1024]{1,0:T(8,128)(2,1)}, u32[]{:S(2)}) copy-start(bf16[1024,1024]{1,0:T(8,128)(2,1)} %w_out_hbm.1) | copy-start | bytes 6291460
  32.8 5.7 %copy-start.12 = (bf16[64,1024]{1,0:T(8,128)(2,1)S(1)}, bf16[64,1024]{1,0:T(8,128)(2,1)}, u32[]{:S(2)}) copy-start(bf16[64,1024]{1,0:T(8,128)(2,1)} %refs_0_.1) | copy-start | bytes 393220
  32.8 5.7 %copy-start.14 = (bf16[64,1024]{1,0:T(8,128)(2,1)S(1)}, bf16[64,1024]{1,0:T(8,128)(2,1)}, u32[]{:S(2)}) copy-start(bf16[64,1024]{1,0:T(8,128)(2,1)} %copy-done.13) | copy-start | bytes 393220
  32.8 5.7 %copy-start.16 = (bf16[64,1024]{1,0:T(8,128)(2,1)S(1)}, bf16[64,1024]{1,0:T(8,128)(2,1)}, u32[]{:S(2)}) copy-start(bf16[64,1024]{1,0:T(8,128)(2,1)} %copy-done.15) | copy-start | bytes 393220
  35.3 1.0 %copy-start.18 = (bf16[256,1024]{1,0:T(8,128)(2,1)S(1)}, bf16[256,1024]{1,0:T(8,128)(2,1)}, u32[]{:S(2)}) copy-start(bf16[256,1024]{1,0:T(8,128)(2,1)} %copy-done.17) | copy-start | bytes 1572868
  37.2 22.5 %collective-permute-start.16 = (bf16[2,1024,1024]{2,1,0:T(8,128)(2,1)}, bf16[2,1024,1024]{2,1,0:T(8,128)(2,1)}, u32[]{:S(2)}, u32[]{:S(2)}) collective-permute-start(bf16[2,1024,1024]{2,1,0:T(8,128)(2,1)} %bitcast.1), channel_id=1, source_target_pairs={{8,0},{0,8},{9,1},{1,9},{10,2},{2,10},{11,3},{3,11},{12,4},{4,12},... | collective-permute-start | bytes 12582920 | tf_op jit(solution)/shard_map/ppermute | solution.py:47
  37.4 8.6 %collective-permute-start.11 = (bf16[256,512]{1,0:T(8,128)(2,1)S(1)}, bf16[256,512]{1,0:T(8,128)(2,1)S(1)}, u32[]{:S(2)}, u32[]{:S(2)}) collective-permute-start(bf16[256,512]{1,0:T(8,128)(2,1)S(1)} %get-tuple-element.27), channel_id=1, source_target_pairs={{0,1},{1,0},{2,3},{3,2},{4,5},{5,4},{6,7},{7,6},{8,9},{9,8},{10,11... | collective-permute-start | bytes 786440 | tf_op jit(solution)/shard_map/ppermute | solution.py:34
  37.9 8.3 %collective-permute-start.12 = (bf16[256,512]{1,0:T(8,128)(2,1)S(1)}, bf16[256,512]{1,0:T(8,128)(2,1)S(1)}, u32[]{:S(2)}, u32[]{:S(2)}) collective-permute-start(bf16[256,512]{1,0:T(8,128)(2,1)S(1)} %get-tuple-element.28), channel_id=1, source_target_pairs={{0,2},{1,3},{2,0},{3,1},{4,6},{5,7},{6,4},{7,5},{8,10},{9,11},{10,... | collective-permute-start | bytes 786440 | tf_op jit(solution)/shard_map/ppermute | solution.py:34
  41.1 11.1 %copy-start.6 = (bf16[2,1024,1024]{2,1,0:T(8,128)(2,1)}, bf16[2,1024,1024]{2,1,0:T(8,128)(2,1)S(1)}, u32[]{:S(2)}) copy-start(bf16[2,1024,1024]{2,1,0:T(8,128)(2,1)S(1)} %get-tuple-element.37.refs_0_) | copy-start | bytes 12582916
  46.3 5.0 %collective-permute-start.13 = (bf16[128,512]{1,0:T(8,128)(2,1)S(1)}, bf16[128,512]{1,0:T(8,128)(2,1)S(1)}, u32[]{:S(2)}, u32[]{:S(2)}) collective-permute-start(bf16[128,512]{1,0:T(8,128)(2,1)S(1)} %slice.51), channel_id=1, source_target_pairs={{0,2},{1,3},{2,0},{3,1},{4,6},{5,7},{6,4},{7,5},{8,10},{9,11},{10,... | collective-permute-start | bytes 393224 | tf_op jit(solution)/shard_map/ppermute | solution.py:34
  47.0 12.7 %copy-start.20 = (f32[1024]{0:T(1024)S(1)}, f32[1024]{0:T(1024)}, u32[]{:S(2)}) copy-start(f32[1024]{0:T(1024)} %param.22) | copy-start | bytes 12292
  47.0 12.7 %copy-start.21 = (s32[1,64]{1,0:T(1,128)S(1)}, s32[1,64]{1,0:T(1,128)}, u32[]{:S(2)}) copy-start(s32[1,64]{1,0:T(1,128)} %domain_ref.1) | copy-start | bytes 772
  47.1 5.0 %collective-permute-start.14 = (bf16[128,512]{1,0:T(8,128)(2,1)S(1)}, bf16[128,512]{1,0:T(8,128)(2,1)S(1)}, u32[]{:S(2)}, u32[]{:S(2)}) collective-permute-start(bf16[128,512]{1,0:T(8,128)(2,1)S(1)} %slice.50), channel_id=1, source_target_pairs={{0,1},{1,0},{2,3},{3,2},{4,5},{5,4},{6,7},{7,6},{8,9},{9,8},{10,11... | collective-permute-start | bytes 393224 | tf_op jit(solution)/shard_map/ppermute | solution.py:34
  52.2 7.5 %collective-permute-start.15 = (bf16[64,1024]{1,0:T(8,128)(2,1)S(1)}, bf16[64,1024]{1,0:T(8,128)(2,1)S(1)}, u32[]{:S(2)}, u32[]{:S(2)}) collective-permute-start(bf16[64,1024]{1,0:T(8,128)(2,1)S(1)} %pad_maximum_fusion.1), channel_id=1, source_target_pairs={{0,4},{1,5},{2,6},{3,7},{4,0},{5,1},{6,2},{7,3},{8,12},{9,13},{10,... | collective-permute-start | bytes 393224 | tf_op jit(solution)/shard_map/ppermute | solution.py:34
  59.7 2.2 %copy-start.7 = (bf16[2,1024,1024]{2,1,0:T(8,128)(2,1)S(1)}, bf16[2,1024,1024]{2,1,0:T(8,128)(2,1)}, u32[]{:S(2)}) copy-start(bf16[2,1024,1024]{2,1,0:T(8,128)(2,1)} %copy-done.6) | copy-start | bytes 12582916

commit v4 on v3

v4 whole, which is shorter than its diff:
```python
import functools

import jax
import jax.numpy as jnp
from jax import lax
from jax.experimental import pallas as pl
from jax.experimental.pallas import tpu as pltpu
from jax.sharding import PartitionSpec as P

H = 8
LAYERS = 2
ID_ROWS = 16
ID_BASE = 128
VMEM_LIMIT = 24 * 1024 * 1024
LOADS_BESIDE = 8 * 10**9

norm_eps = 1e-05
F32 = jnp.float32
BF16 = jnp.bfloat16
ANY = pl.BlockSpec(memory_space=pl.ANY)
VMEM = pl.BlockSpec(memory_space=pltpu.VMEM)
SMEM = pl.BlockSpec(memory_space=pltpu.SMEM)
TRANSPOSED = (((0,), (0,)), ((), ()))


def rms_scale(matrix):
    return matrix * lax.rsqrt(jnp.mean(matrix * matrix, axis=-1, keepdims=True) + norm_eps)


def silu(value):
    half = 0.5 * value
    return half + half * jnp.tanh(half)


def swapped(value, flip):
    count = lax.axis_size("hist")
    return lax.ppermute(value, "hist", [(i, i ^ flip) for i in range(count)])


def swapped_by_user(value, flips):
    count = lax.axis_size("hist")
    pairs = [
        (u * count + i, u * count + (i ^ flip)) for u, flip in enumerate(flips) for i in range(count)
    ]
    return lax.ppermute(value, ("user", "hist"), pairs)


def from_user(value, steps):
    count = lax.axis_size("user")
    return lax.ppermute(value, "user", [((i + steps) % count, i) for i in range(count)])


def kernel_call(body, name, out_shapes, in_specs, scratch=(), flops=0, moved=0):
    return pl.pallas_call(
        body,
        out_shape=out_shapes,
        in_specs=in_specs,
        out_specs=[VMEM] * len(out_shapes),
        scratch_shapes=scratch,
        compiler_params=pltpu.CompilerParams(vmem_limit_bytes=VMEM_LIMIT),
        cost_estimate=pl.CostEstimate(flops=flops, bytes_accessed=moved, transcendentals=0),
        name=name,
    )


def core_at(steps):
    return lax.rem(lax.axis_index("user") + steps, lax.axis_size("user"))


def of_core(core, arrivals):
    chosen = arrivals[0]
    for steps in range(1, len(arrivals)):
        chosen = jnp.where(core_at(steps) == core, arrivals[steps], chosen)
    return chosen


def blocks_of(piece, arrivals):
    _, steps, core = piece
    return arrivals[steps : steps + 1] if core is None else arrivals


def flip_of(piece):
    flips, steps, core = piece
    if core is not None:
        return flips[core]
    return sum(jnp.where(core_at(steps) == u, flip, 0) for u, flip in enumerate(flips))


def rows_of(pieces, refs):
    blocks, at = [], 0
    for piece in pieces:
        count = 1 if piece[2] is None else lax.axis_size("user")
        shards = [ref[: ref.shape[0] - ID_ROWS, :] for ref in refs[at : at + count]]
        blocks.append(shards[0] if piece[2] is None else of_core(piece[2], shards))
        at += count
    return jnp.concatenate(blocks, axis=0)


def ids_of(flips, refs, slots):
    rows = refs[0].shape[0] - ID_ROWS
    blocks = [ref[rows:, :slots].astype(F32) for ref in refs]
    row = lax.broadcasted_iota(jnp.int32, (ID_ROWS, slots), 0)
    high_row = 2 * core_at(0)
    weight = jnp.where(row == high_row, float(ID_BASE), jnp.where(row == high_row + 1, 1.0, 0.0))
    return {
        flip: jnp.sum(of_core(core, blocks) * weight, axis=0, keepdims=True).astype(jnp.int32)
        for core, flip in enumerate(flips)
    }


def matches(pieces, shard_rows, ids_row):
    hist_index = lax.axis_index("hist")
    blocks = []
    for piece in pieces:
        item = lax.broadcasted_iota(jnp.int32, (shard_rows, ids_row.shape[1]), 0)
        item += (hist_index ^ flip_of(piece)) * shard_rows
        blocks.append((item == ids_row).astype(F32).astype(BF16))
    return jnp.concatenate(blocks, axis=0)


def payload_kernel(rows_ref, own_ref, *refs):
    other_refs, out_ref = refs[:-1], refs[-1]
    rows, width = rows_ref.shape
    slots = own_ref.shape[1]
    out_ref[:rows, :] = rows_ref[...]
    row = lax.broadcasted_iota(jnp.int32, (ID_ROWS, slots), 0)
    digits = jnp.zeros((ID_ROWS, slots), jnp.int32)
    for steps, ref in enumerate((own_ref, *other_refs)):
        high_row = 2 * core_at(steps)
        high = ref[...] // ID_BASE
        digits = jnp.where(row == high_row, high, digits)
        digits = jnp.where(row == high_row + 1, ref[...] - high * ID_BASE, digits)
    out_ref[rows:, :] = jnp.zeros((ID_ROWS, width), BF16)
    out_ref[rows:, :slots] = digits.astype(F32).astype(BF16)


def payload_of(rows, ids, other_ids):
    return kernel_call(
        payload_kernel,
        "payload",
        [jax.ShapeDtypeStruct((rows.shape[0] + ID_ROWS, rows.shape[1]), BF16)],
        [VMEM] * (2 + len(other_ids)),
        flops=LOADS_BESIDE,
    )(rows, ids, *other_ids)[0]


def attend_rows(pieces, refs, w_query_ref, keys_ref, values_ref, sums_ref):
    width = sums_ref.shape[1]
    head_size = width // H
    rows = rows_of(pieces, refs)
    normed = rms_scale(rows.astype(F32)).astype(BF16)
    queries = jnp.dot(normed, w_query_ref[...], preferred_element_type=F32).astype(BF16)
    for head in range(H):
        cut = slice(head * head_size, (head + 1) * head_size)
        scores = lax.dot_general(
            queries[:, cut], keys_ref[0, :, cut], (((1,), (1,)), ((), ())), preferred_element_type=F32
        )
        half = scores * (0.5 * head_size ** (-0.5))
        weights = (half + half * jnp.tanh(half)).astype(BF16)
        sums_ref[:, cut] = jnp.dot(weights, values_ref[:, cut], preferred_element_type=F32).astype(BF16)


def first_kernel(pieces, length_ref, w_query_ref, keys_ref, values_ref, *refs):
    *refs, sums_ref, masked_ref = refs
    history = masked_ref.shape[0]
    place = lax.broadcasted_iota(jnp.int32, masked_ref.shape, 0) + lax.axis_index("hist") * history
    masked_ref[...] = jnp.where(place < length_ref[0], values_ref[0].astype(F32), 0.0).astype(BF16)
    attend_rows(pieces, refs, w_query_ref, keys_ref, masked_ref, sums_ref)


def next_kernel(pieces, w_query_ref, keys_ref, values_ref, *refs):
    *refs, sums_ref = refs
    attend_rows(pieces, refs, w_query_ref, keys_ref, values_ref, sums_ref)


def attend_cost(rows, width, history):
    return 2 * rows * width * (width + 2 * history)


def attend_first(pieces, blocks, shard_rows, lengths, w_query, keys, values):
    rows, width = len(pieces) * shard_rows, w_query.shape[0]
    return kernel_call(
        functools.partial(first_kernel, pieces),
        "attend_first",
        [jax.ShapeDtypeStruct((rows, width), BF16), jax.ShapeDtypeStruct(values.shape[1:], BF16)],
        [SMEM] + [VMEM] * (3 + len(blocks)),
        flops=attend_cost(rows, width, keys.shape[1]),
    )(lengths, w_query, keys, values, *blocks)


def attend_next(pieces, blocks, shard_rows, w_query, keys, values):
    rows, width = len(pieces) * shard_rows, w_query.shape[0]
    return kernel_call(
        functools.partial(next_kernel, pieces),
        "attend_next",
        [jax.ShapeDtypeStruct((rows, width), BF16)],
        [VMEM] * (3 + len(blocks)),
        flops=attend_cost(rows, width, keys.shape[1]),
    )(w_query, keys, values, *blocks)[0]


def place_kernel(pieces, all_flips, orders, parts, shard_rows, ids_ref, *refs):
    *refs, kept_a, sent_a, kept_b, sent_b = refs
    sums_refs, refs = refs[:parts], refs[parts:]
    slots, users = ids_ref.shape[1], lax.axis_size("user")
    ids = {0: ids_ref[...]}
    for at, flips in enumerate(all_flips):
        ids.update(ids_of(flips, refs[at * users : (at + 1) * users], slots))
    ids_row = jnp.concatenate([ids[flip] for flip in orders[0]], axis=1)
    onehot = matches(pieces, shard_rows, ids_row)
    width = sums_refs[0].shape[1] // 2
    for side, order in enumerate(orders):
        columns = slice(side * width, (side + 1) * width)
        sums = jnp.concatenate([ref[:, columns] for ref in sums_refs], axis=0)
        placed = lax.dot_general(onehot, sums, TRANSPOSED, preferred_element_type=F32).astype(BF16)
        half = len(order) // 2
        for at, flip in enumerate(order):
            block = orders[0].index(flip)
            target = ((kept_a, sent_a), (kept_b, sent_b))[side][at // half]
            target[at % half * slots : (at % half + 1) * slots, :] = placed[block * slots : (block + 1) * slots, :]


def place(pieces, groups, orders, shard_rows, ids, sums):
    devices, slots = len(orders[0]), ids.shape[1]
    width = sums[0].shape[1]
    out = jax.ShapeDtypeStruct((devices * slots // 2, width // 2), BF16)
    all_flips = [flips for flips, _ in groups]
    blocks = [block for _, arrivals in groups for block in arrivals]
    return kernel_call(
        functools.partial(place_kernel, pieces, all_flips, orders, len(sums), shard_rows),
        "place",
        [out] * 4,
        [VMEM] * (1 + len(sums) + len(blocks)),
        flops=2 * sum(part.shape[0] for part in sums) * devices * slots * width,
    )(ids, *sums, *blocks)


def fold_kernel(sides, *refs):
    ins, (kept_ref, sent_ref) = refs[: 2 * sides], refs[2 * sides :]
    half, width = ins[0].shape[0] // 2, ins[0].shape[1]
    for side in range(sides):
        total = ins[2 * side][...].astype(F32) + ins[2 * side + 1][...].astype(F32)
        columns = slice(side * width, (side + 1) * width)
        kept_ref[:, columns] = total[:half]
        sent_ref[:, columns] = total[half:].astype(BF16)


def fold(pairs):
    rows, width = pairs[0][0].shape
    shape = (rows // 2, width * len(pairs))
    blocks = [block for pair in pairs for block in pair]
    return kernel_call(
        functools.partial(fold_kernel, len(pairs)),
        "fold",
        [jax.ShapeDtypeStruct(shape, F32), jax.ShapeDtypeStruct(shape, BF16)],
        [VMEM] * len(blocks),
        moved=8 * rows * width * len(pairs),
    )(*blocks)


def prepare_kernel(pieces, after_ref, ids_ref, w_gate_ref, *refs):
    del after_ref
    *refs, embed_ref, gating_ref = refs
    table = rows_of(pieces, refs)
    onehot = matches(pieces, table.shape[0] // len(pieces), ids_ref[...])
    embedded = lax.dot_general(onehot, table, TRANSPOSED, preferred_element_type=F32)
    embed_ref[...] = embedded
    normed = rms_scale(embedded).astype(BF16)
    gating_ref[...] = silu(jnp.dot(normed, w_gate_ref[...], preferred_element_type=F32))


def prepare(pieces, blocks, shard_rows, after, ids, w_gate):
    slots, width = ids.shape[1], w_gate.shape[0]
    return kernel_call(
        functools.partial(prepare_kernel, pieces),
        "prepare",
        [jax.ShapeDtypeStruct((slots, width), F32)] * 2,
        [ANY, VMEM, VMEM] + [VMEM] * len(blocks),
        flops=2 * slots * width * (width + len(pieces) * shard_rows),
    )(after, ids, w_gate, *blocks)


def finish_kernel(kept_ref, come_ref, embed_ref, gating_ref, gain_ref, count_ref, domain_ref, w_out_ref, *refs):
    expert_refs, out_ref = refs[:-1], refs[-1]
    users = len(expert_refs)
    attended = kept_ref[...] + come_ref[...].astype(F32)
    gated = (rms_scale(attended) * gain_ref[...] * gating_ref[...]).astype(BF16)
    mixed = jnp.dot(gated, w_out_ref[...], preferred_element_type=F32)
    state = (embed_ref[...] + mixed).astype(BF16)

    slots = state.shape[0]
    row_at = lax.broadcasted_iota(jnp.int32, (slots, slots), 0)
    lane_at = lax.broadcasted_iota(jnp.int32, (slots, slots), 1)
    steps_away = lax.rem(domain_ref[...] - lax.axis_index("user") + users, users)
    live = lane_at + lax.axis_index("hist") * slots < count_ref[0]
    wanted = jnp.where(live, steps_away, -1)
    owner = jnp.sum(jnp.where(row_at == lane_at, wanted, 0).astype(F32), axis=1, keepdims=True)

    result = jnp.zeros(state.shape, F32)
    for steps, layers in enumerate(expert_refs):
        current = state
        for layer in range(LAYERS):
            lifted = jnp.dot(current, layers[0, layer], preferred_element_type=F32)
            current = (current.astype(F32) + silu(lifted)).astype(BF16)
        result = jnp.where(owner == steps, current.astype(F32), result)
    out_ref[0] = result.astype(BF16)


def finish(kept, come, embed, gating, gain, counts, domains, w_out, experts):
    slots, width = kept.shape
    return kernel_call(
        finish_kernel,
        "finish",
        [jax.ShapeDtypeStruct((1, slots, width), BF16)],
        [VMEM] * 5 + [SMEM] + [VMEM] * (2 + len(experts)),
        flops=2 * slots * width * width * (1 + LAYERS * len(experts)),
    )(kept, come, embed, gating, gain, counts, domains, w_out, *experts)[0]


def on_device(
    item_table,
    item_ids,
    candidate_counts,
    domain_ids,
    history_lengths,
    history_keys,
    history_values,
    w_query,
    w_gate,
    w_out,
    attn_gain,
    expert_weights,
):
    shard_rows = item_table.shape[0]
    hist_devices = lax.axis_size("hist")
    users = lax.axis_size("user")
    bits = hist_devices.bit_length() - 1
    others = range(1, users)

    payload = payload_of(item_table, item_ids, [from_user(item_ids, steps) for steps in others])
    all_flips = [tuple(range(at, min(at + users, hist_devices))) for at in range(1, hist_devices, users)]
    fetched = [swapped_by_user(payload, flips) for flips in all_flips]

    early = len(all_flips) // 2
    first_pieces = [((0,) * users, 0, None)] + [(flips, 0, None) for flips in all_flips[:early]]
    first_blocks = [payload] + fetched[:early]
    first, masked_values = attend_first(
        first_pieces, first_blocks, shard_rows, history_lengths, w_query, history_keys, history_values
    )
    first, *fetched = lax.optimization_barrier((first, *fetched))
    groups, next_pieces, next_blocks = [], [], []
    for at, (flips, block) in enumerate(zip(all_flips, fetched)):
        arrivals = [block] + [from_user(block, steps) for steps in others]
        groups.append((flips, arrivals))
        found = [(flips, steps, None) for steps in range(users)]
        if at < early:
            found = found[1:]
        elif len(flips) < users:
            found = [(flips, 0, core) for core in range(len(flips))]
        next_pieces += found
        next_blocks += [block for piece in found for block in blocks_of(piece, arrivals)]
    following = attend_next(next_pieces, next_blocks, shard_rows, w_query, history_keys, masked_values)
    pieces, blocks = first_pieces + next_pieces, first_blocks + next_blocks

    turns = [list(range(bits)), list(range(bits))]
    turns[1][:2] = [1, 0]
    orders = [
        [sum(((r >> (bits - 1 - t)) & 1) << bit for t, bit in enumerate(turn)) for r in range(hist_devices)]
        for turn in turns
    ]
    kept_a, sent_a, kept_b, sent_b = place(
        pieces, groups, orders, shard_rows, item_ids, [first, following]
    )
    embed, gating = prepare(pieces, blocks, shard_rows, kept_a, item_ids, w_gate)

    leaving, kept_a = lax.optimization_barrier((expert_weights, kept_a))
    experts = [expert_weights] + [from_user(leaving, steps) for steps in others]

    held = [(kept_a, sent_a), (kept_b, sent_b)]
    for at in range(bits - 1):
        arriving = [swapped(held[side][1], 1 << turn[at]) for side, turn in enumerate(turns)]
        if at == 0:
            *arriving, embed = lax.optimization_barrier((*arriving, embed))
        pairs = [(held[side][0], arriving[side]) for side in range(len(turns))]
        if at < bits - 2:
            held = [fold([pair]) for pair in pairs]
        else:
            kept, sent = fold(pairs)
    come = swapped(sent, 1 << (bits - 1))
    return finish(kept, come, embed, gating, attn_gain[None], candidate_counts, domain_ids, w_out, experts)


def solution(mesh):
    in_specs = (
        P("hist", None),
        P(("groups", "user"), "hist"),
        P(("groups", "user")),
        P(("groups", "user"), "hist"),
        P(("groups", "user")),
        P(("groups", "user"), "hist", None),
        P(("groups", "user"), "hist", None),
        P(),
        P(),
        P(),
        P(),
        P("user", None, None, None),
    )
    out_specs = P(("groups", "user"), "hist", None)
    return jax.shard_map(
        on_device, mesh=mesh, in_specs=in_specs, out_specs=out_specs, check_vma=False
    )
```

time: 67.4 us -> 55 us (0.82)
  waiting for transfers between devices: 14.6 us -> 25 us
  local copies, waits for them, and re-layouts: 10.3 us -> 1.59 us
  starting transfers between devices: 23 us -> 17 us
  Pallas kernels: 15.5 us -> 9.76 us
  other arithmetic: 1.86 us -> 0 us
    unnamed x48 -> x20, local copies, waits for them, and re-layouts: 10.2 us -> 1.59 us
    ppermute x8 -> x5, starting transfers between devices: 12.3 us -> 5.19 us  [swapped(): return lax.ppermute(value, 'hist', [(i, i ^ flip) for i in range(count)])]
    ppermute x4, waiting for transfers between devices: 0.01 us -> 7.05 us  [swapped_by_user(): return lax.ppermute(value, ('user', 'hist'), pairs)]
    pallas_call x6 -> x9, Pallas kernels: 15.5 us -> 9.76 us  [the longest x1 2.83 us: finish(): kernel_call(finish_kernel, 'finish', [jax.ShapeDtypeStruct((1, slots, wid...]
    ppermute x8 -> x5, waiting for transfers between devices: 14.1 us -> 15.9 us  [swapped(): return lax.ppermute(value, 'hist', [(i, i ^ flip) for i in range(count)])]
    ppermute x5 -> x6, waiting for transfers between devices: 0.4 us -> 2.07 us  [from_user(): lax.ppermute(value, 'user', [((i + steps) % count, i) for i in range(coun...]
    ppermute x5 -> x6, starting transfers between devices: 0.78 us -> 1.89 us  [from_user(): lax.ppermute(value, 'user', [((i + steps) % count, i) for i in range(coun...]
    select_n x1 -> x0, other arithmetic: 0.93 us -> none  [traded(): jnp.where((user_index + steps) % users == u, everyone[steps], other)]
  transfers between devices with their start and end apart: 17 -> 15, of which waited for: 7 -> 12; matrix products, arithmetic and copies ran while one was open for 3% -> 0% of each run, Pallas kernels for 11% -> 6%
where the time goes in v4:
time: 55 us; the launch traced here: 54.8 us
  waiting for transfers between devices  25 us (45%)
  starting transfers between devices  17 us (31%)
  Pallas kernels  9.76 us (18%)
  local copies, waits for them, and re-layouts  1.59 us (3%)
  between operations  1.43 us (3%)
    ppermute x5, waiting for transfers between devices, swapped(): return lax.ppermute(value, 'hist', [(i, i ^ flip) for i in range(count)])  15.9 us
    ppermute x4, starting transfers between devices, swapped_by_user(): return lax.ppermute(value, ('user', 'hist'), pairs)  9.92 us
    ppermute x4, waiting for transfers between devices, swapped_by_user(): return lax.ppermute(value, ('user', 'hist'), pairs)  7.05 us
    ppermute x5, starting transfers between devices, swapped(): return lax.ppermute(value, 'hist', [(i, i ^ flip) for i in range(count)])  5.19 us
    pallas_call x1, Pallas kernels, finish(): kernel_call(finish_kernel, 'finish', [jax.ShapeDtypeStruct((1, slots, wid...  2.83 us
    pallas_call x1, Pallas kernels, attend_next(): kernel_call(functools.partial(next_kernel, pieces), 'attend_next', [jax.S...  2.49 us
    pallas_call x1, Pallas kernels, attend_first(): kernel_call(functools.partial(first_kernel, pieces), 'attend_first', [jax...  2.48 us
    ppermute x6, waiting for transfers between devices, from_user(): lax.ppermute(value, 'user', [((i + steps) % count, i) for i in range(coun...  2.07 us
  transfers between devices with their start and end apart: 15, of which 12 were waited for; matrix products, arithmetic and copies ran while one was open for 0% of the time, Pallas kernels for 6%

profile of v4, /device:TPU:0, one launch (start us, length us, event | category | flops | bytes accessed | tf_op | source)
XLA Modules:
  0.0 54.8 jit_solution(16108874898523864693)
XLA Ops:
  0.0 0.5 collective-permute-start
  0.5 1.0 %collective-permute-done.refs_0_ = s32[1,64]{1,0:T(1,128)S(1)} collective-permute-done((s32[1,64]{1,0:T(1,128)}, s32[1,64]{1,0:T(1,128)S(1)}, u32[]{:S(2)}, u32[]{:S(2)}) %collective-permute-start) | collective-permute-done | bytes 288 | tf_op jit(solution)/shard_map/ppermute | solution.py:50
  1.5 0.7 %copy-done.7 = s32[1,64]{1,0:T(1,128)S(1)} copy-done((s32[1,64]{1,0:T(1,128)S(1)}, s32[1,64]{1,0:T(1,128)}, u32[]{:S(2)}) %copy-start.7) | copy-done | bytes 280
  2.1 0.9 %copy-done.9 = bf16[64,1024]{1,0:T(8,128)(2,1)S(1)} copy-done((bf16[64,1024]{1,0:T(8,128)(2,1)S(1)}, bf16[64,1024]{1,0:T(8,128)(2,1)}, u32[]{:S(2)}) %copy-start.9) | copy-done | bytes 131096
  3.1 3.9 %collective-permute-start.2 = (bf16[80,1024]{1,0:T(8,128)(2,1)S(1)}, bf16[80,1024]{1,0:T(8,128)(2,1)S(1)}, u32[]{:S(2)}, u32[]{:S(2)}) collective-permute-start(bf16[80,1024]{1,0:T(8,128)(2,1)S(1)} %payload.1.refs_0_), channel_id=1, source_target_pairs={{0,3},{1,2},{2,1},{3,0},{4,7},{5,6},{6,5},{7,4},{8,12},{9,13},{10,... | collective-permute-start | bytes 491528 | tf_op jit(solution)/shard_map/ppermute | solution.py:45
  7.0 0.5 collective-permute-start.1
  7.5 5.3 %collective-permute-start.4 = (bf16[80,1024]{1,0:T(8,128)(2,1)S(1)}, bf16[80,1024]{1,0:T(8,128)(2,1)S(1)}, u32[]{:S(2)}, u32[]{:S(2)}) collective-permute-start(bf16[80,1024]{1,0:T(8,128)(2,1)S(1)} %payload.1.refs_0_), channel_id=1, source_target_pairs={{0,7},{1,6},{2,5},{3,4},{4,3},{5,2},{6,1},{7,0},{16,23},{17,22},{1... | collective-permute-start | bytes 491528 | tf_op jit(solution)/shard_map/ppermute | solution.py:45
  12.8 0.2 collective-permute-start.3
  13.6 0.0 collective-permute-done.2.refs_2_.refs_4_
  13.7 0.0 collective-permute-done.1.refs_1_.refs_2_
  13.7 0.0 copy-done
  13.7 0.0 copy-done.2
  13.7 0.0 copy-done.5
  13.7 2.5 %attend_first.1 = (bf16[192,1024]{1,0:T(8,128)(2,1)S(1)}, bf16[512,1024]{1,0:T(8,128)(2,1)S(1)}) custom-call(s32[1]{0:T(128)S(6)} %copy.14.length_ref, bf16[1024,1024]{1,0:T(8,128)(2,1)S(1)} %copy-done, bf16[1,512,1024]{2,1,0:T(8,128)(2,1)S(1)} %copy-done.2, bf16[1,512,1024]{2,1,0:T(8,128)(2,1)S(1)} %copy-done.5, bf16[80,1024]{1,0:T(8,128)(2,1)S(1)} %payload.1.refs_0_, ...), custom_call_target="tpu_custom_call" | custom-call | flops 805306368 | tf_op jit(solution)/shard_map/attend_first/pallas_call | solution.py:182
  16.2 2.8 %collective-permute-done.4.refs_4_.refs_8_.refs_7_ = bf16[80,1024]{1,0:T(8,128)(2,1)S(1)} collective-permute-done((bf16[80,1024]{1,0:T(8,128)(2,1)S(1)}, bf16[80,1024]{1,0:T(8,128)(2,1)S(1)}, u32[]{:S(2)}, u32[]{:S(2)}) %collective-permute-start.4) | collective-permute-done | bytes 163872 | tf_op jit(solution)/shard_map/ppermute | solution.py:45
  19.0 4.2 %collective-permute-done.3.refs_2_.refs_6_.refs_5_ = bf16[80,1024]{1,0:T(8,128)(2,1)S(1)} collective-permute-done((bf16[80,1024]{1,0:T(8,128)(2,1)S(1)}, bf16[80,1024]{1,0:T(8,128)(2,1)S(1)}, u32[]{:S(2)}, u32[]{:S(2)}) %collective-permute-start.3) | collective-permute-done | bytes 163872 | tf_op jit(solution)/shard_map/ppermute | solution.py:45
  23.2 0.0 collective-permute-start.5
  23.2 0.5 collective-permute-start.6
  23.7 0.0 collective-permute-start.7
  23.7 0.5 collective-permute-start.8
  24.2 0.4 collective-permute-done.5.refs_0_.refs_3_
  24.6 0.2 collective-permute-done.6.refs_1_.refs_5_.refs_4_
  24.9 0.3 collective-permute-done.7.refs_3_.refs_7_.refs_6_
  25.1 0.2 collective-permute-done.8.refs_5_.refs_9_.refs_8_
  25.4 2.5 %attend_next.1.refs_1_ = bf16[320,1024]{1,0:T(8,128)(2,1)S(1)} custom-call(bf16[1024,1024]{1,0:T(8,128)(2,1)S(1)} %copy-done, bf16[1,512,1024]{2,1,0:T(8,128)(2,1)S(1)} %copy-done.2, bf16[512,1024]{1,0:T(8,128)(2,1)S(1)} %get-tuple-element.31.values_ref, bf16[80,1024]{1,0:T(8,128)(2,1)S(1)} %collective-permute-done.5.refs_0_.refs_3_, ...), custom_call_target="tpu_custom_call" | custom-call | flops 1342177280 | tf_op jit(solution)/shard_map/attend_next/pallas_call | solution.py:193
  27.9 0.0 copy-start.3
  27.9 0.9 %place.1 = (bf16[256,512]{1,0:T(8,128)(2,1)S(1)}, bf16[256,512]{1,0:T(8,128)(2,1)S(1)}, bf16[256,512]{1,0:T(8,128)(2,1)S(1)}, bf16[256,512]{1,0:T(8,128)(2,1)S(1)}) custom-call(s32[1,64]{1,0:T(1,128)S(1)} %copy-done.7, bf16[192,1024]{1,0:T(8,128)(2,1)S(1)} %get-tuple-element.30.refs_0_, bf16[320,1024]{1,0:T(8,128)(2,1)S(1)} %attend_next.1.refs_1_, ...), custom_call_target="tpu_custom_call" | custom-call | flops 536870912 | tf_op jit(solution)/shard_map/place/pallas_call | solution.py:229
  28.8 0.0 copy-done.1
  28.8 0.4 collective-permute-start.14
  29.1 0.8 %collective-permute-start.9 = (bf16[256,512]{1,0:T(8,128)(2,1)S(1)}, bf16[256,512]{1,0:T(8,128)(2,1)S(1)}, u32[]{:S(2)}, u32[]{:S(2)}) collective-permute-start(bf16[256,512]{1,0:T(8,128)(2,1)S(1)} %get-tuple-element.38), channel_id=1, source_target_pairs={{0,1},{1,0},{2,3},{3,2},{4,5},{5,4},{6,7},{7,6},{8,9},{9,8},{10,11... | collective-permute-start | bytes 786440 | tf_op jit(solution)/shard_map/ppermute | solution.py:37
  29.9 0.4 collective-permute-start.10
  30.3 0.0 copy-done.3
  30.3 0.9 %prepare.1 = (f32[64,1024]{1,0:T(8,128)S(1)}, f32[64,1024]{1,0:T(8,128)S(1)}) custom-call(bf16[256,512]{1,0:T(8,128)(2,1)S(1)} %get-tuple-element.37.after_ref.refs_0_, s32[1,64]{1,0:T(1,128)S(1)} %copy-done.7, bf16[1024,1024]{1,0:T(8,128)(2,1)S(1)} %copy-done.3, bf16[80,1024]{1,0:T(8,128)(2,1)S(1)} %payload.1.refs_0_, ...), custom_call_target="tpu_custom_call" | custom-call | flops 201326592 | tf_op jit(solution)/shard_map/prepare/pallas_call | solution.py:274
  31.2 6.3 %collective-permute-done.9.refs_1_ = bf16[256,512]{1,0:T(8,128)(2,1)S(1)} collective-permute-done((bf16[256,512]{1,0:T(8,128)(2,1)S(1)}, bf16[256,512]{1,0:T(8,128)(2,1)S(1)}, u32[]{:S(2)}, u32[]{:S(2)}) %collective-permute-start.9) | collective-permute-done | bytes 262176 | tf_op jit(solution)/shard_map/ppermute | solution.py:37
  37.6 0.5 collective-permute-done.10.refs_1_
  38.1 0.1 fold.4
  38.1 1.3 %collective-permute-start.12 = (bf16[128,512]{1,0:T(8,128)(2,1)S(1)}, bf16[128,512]{1,0:T(8,128)(2,1)S(1)}, u32[]{:S(2)}, u32[]{:S(2)}) collective-permute-start(bf16[128,512]{1,0:T(8,128)(2,1)S(1)} %get-tuple-element.47), channel_id=1, source_target_pairs={{0,1},{1,0},{2,3},{3,2},{4,5},{5,4},{6,7},{7,6},{8,9},{9,8},{10,11... | collective-permute-start | bytes 393224 | tf_op jit(solution)/shard_map/ppermute | solution.py:37
  39.4 0.1 fold.3
  39.5 0.3 collective-permute-start.11
  39.8 3.3 %collective-permute-done.12.refs_3_ = bf16[128,512]{1,0:T(8,128)(2,1)S(1)} collective-permute-done((bf16[128,512]{1,0:T(8,128)(2,1)S(1)}, bf16[128,512]{1,0:T(8,128)(2,1)S(1)}, u32[]{:S(2)}, u32[]{:S(2)}) %collective-permute-start.12) | collective-permute-done | bytes 131104 | tf_op jit(solution)/shard_map/ppermute | solution.py:37
  43.2 1.4 %collective-permute-done.11.refs_1_ = bf16[128,512]{1,0:T(8,128)(2,1)S(1)} collective-permute-done((bf16[128,512]{1,0:T(8,128)(2,1)S(1)}, bf16[128,512]{1,0:T(8,128)(2,1)S(1)}, u32[]{:S(2)}, u32[]{:S(2)}) %collective-permute-start.11) | collective-permute-done | bytes 131104 | tf_op jit(solution)/shard_map/ppermute | solution.py:37
  44.6 2.3 %collective-permute-start.13 = (bf16[64,1024]{1,0:T(8,128)(2,1)S(1)}, bf16[64,1024]{1,0:T(8,128)(2,1)S(1)}, u32[]{:S(2)}, u32[]{:S(2)}) collective-permute-start(bf16[64,1024]{1,0:T(8,128)(2,1)S(1)} %get-tuple-element.49), channel_id=1, source_target_pairs={{0,4},{1,5},{2,6},{3,7},{4,0},{5,1},{6,2},{7,3},{8,12},{9,13},{10,... | collective-permute-start | bytes 393224 | tf_op jit(solution)/shard_map/ppermute | solution.py:37
  47.6 4.3 %collective-permute-done.13.come_ref = bf16[64,1024]{1,0:T(8,128)(2,1)S(1)} collective-permute-done((bf16[64,1024]{1,0:T(8,128)(2,1)S(1)}, bf16[64,1024]{1,0:T(8,128)(2,1)S(1)}, u32[]{:S(2)}, u32[]{:S(2)}) %collective-permute-start.13) | collective-permute-done | bytes 131104 | tf_op jit(solution)/shard_map/ppermute | solution.py:37
  51.9 0.0 collective-permute-done.14.refs_1_
  51.9 0.0 copy-done.4
  51.9 0.0 copy-done.6
  51.9 0.0 copy-done.8
  51.9 2.8 %finish.1 = bf16[1,64,1024]{2,1,0:T(8,128)(2,1)} custom-call(f32[64,1024]{1,0:T(8,128)S(1)} %get-tuple-element.48.kept_ref, bf16[64,1024]{1,0:T(8,128)(2,1)S(1)} %collective-permute-done.13.come_ref, f32[64,1024]{1,0:T(8,128)S(1)} %get-tuple-element.50.embed_ref, f32[64,1024]{1,0:T(8,128)S(1)} %get-tuple-element.51.gating_ref, f32[1,1024]{1,0:T(1,128)S(1)} %bitcast.1, ...), custom_call_target="tpu_custom_call" | custom-call | flops 671088640 | tf_op jit(solution)/shard_map/finish/pallas_call | solution.py:311
  (11 shorter events, 0.1 us)
Async XLA Ops:
  0.0 13.7 %copy-start = (bf16[1024,1024]{1,0:T(8,128)(2,1)S(1)}, bf16[1024,1024]{1,0:T(8,128)(2,1)}, u32[]{:S(2)}) copy-start(bf16[1024,1024]{1,0:T(8,128)(2,1)} %w_query_ref.3) | copy-start | bytes 6291460
  0.0 13.7 %copy-start.2 = (bf16[1,512,1024]{2,1,0:T(8,128)(2,1)S(1)}, bf16[1,512,1024]{2,1,0:T(8,128)(2,1)}, u32[]{:S(2)}) copy-start(bf16[1,512,1024]{2,1,0:T(8,128)(2,1)} %keys_ref.3) | copy-start | bytes 3145732
  0.0 13.7 %copy-start.5 = (bf16[1,512,1024]{2,1,0:T(8,128)(2,1)S(1)}, bf16[1,512,1024]{2,1,0:T(8,128)(2,1)}, u32[]{:S(2)}) copy-start(bf16[1,512,1024]{2,1,0:T(8,128)(2,1)} %values_ref.1) | copy-start | bytes 3145732
  0.0 1.5 %collective-permute-start = (s32[1,64]{1,0:T(1,128)}, s32[1,64]{1,0:T(1,128)S(1)}, u32[]{:S(2)}, u32[]{:S(2)}) collective-permute-start(s32[1,64]{1,0:T(1,128)} %ids_ref.3), channel_id=1, source_target_pairs={{8,0},{0,8},{9,1},{1,9},{10,2},{2,10},{11,3},{3,11},{12,4},{4,12},... | collective-permute-start | bytes 776 | tf_op jit(solution)/shard_map/ppermute | solution.py:50
  1.5 0.7 %copy-start.7 = (s32[1,64]{1,0:T(1,128)S(1)}, s32[1,64]{1,0:T(1,128)}, u32[]{:S(2)}) copy-start(s32[1,64]{1,0:T(1,128)} %ids_ref.3) | copy-start | bytes 772
  2.1 0.9 %copy-start.9 = (bf16[64,1024]{1,0:T(8,128)(2,1)S(1)}, bf16[64,1024]{1,0:T(8,128)(2,1)}, u32[]{:S(2)}) copy-start(bf16[64,1024]{1,0:T(8,128)(2,1)} %rows_ref.1) | copy-start | bytes 393220
  3.1 10.6 %collective-permute-start.2 = (bf16[80,1024]{1,0:T(8,128)(2,1)S(1)}, bf16[80,1024]{1,0:T(8,128)(2,1)S(1)}, u32[]{:S(2)}, u32[]{:S(2)}) collective-permute-start(bf16[80,1024]{1,0:T(8,128)(2,1)S(1)} %payload.1.refs_0_), channel_id=1, source_target_pairs={{0,3},{1,2},{2,1},{3,0},{4,7},{5,6},{6,5},{7,4},{8,12},{9,13},{10,... | collective-permute-start | bytes 491528 | tf_op jit(solution)/shard_map/ppermute | solution.py:45
  7.0 6.7 %collective-permute-start.1 = (bf16[80,1024]{1,0:T(8,128)(2,1)S(1)}, bf16[80,1024]{1,0:T(8,128)(2,1)S(1)}, u32[]{:S(2)}, u32[]{:S(2)}) collective-permute-start(bf16[80,1024]{1,0:T(8,128)(2,1)S(1)} %payload.1.refs_0_), channel_id=1, source_target_pairs={{0,1},{1,0},{2,3},{3,2},{4,5},{5,4},{6,7},{7,6},{8,10},{9,11},{10,... | collective-permute-start | bytes 491528 | tf_op jit(solution)/shard_map/ppermute | solution.py:45
  7.5 11.5 %collective-permute-start.4 = (bf16[80,1024]{1,0:T(8,128)(2,1)S(1)}, bf16[80,1024]{1,0:T(8,128)(2,1)S(1)}, u32[]{:S(2)}, u32[]{:S(2)}) collective-permute-start(bf16[80,1024]{1,0:T(8,128)(2,1)S(1)} %payload.1.refs_0_), channel_id=1, source_target_pairs={{0,7},{1,6},{2,5},{3,4},{4,3},{5,2},{6,1},{7,0},{16,23},{17,22},{1... | collective-permute-start | bytes 491528 | tf_op jit(solution)/shard_map/ppermute | solution.py:45
  12.8 10.4 %collective-permute-start.3 = (bf16[80,1024]{1,0:T(8,128)(2,1)S(1)}, bf16[80,1024]{1,0:T(8,128)(2,1)S(1)}, u32[]{:S(2)}, u32[]{:S(2)}) collective-permute-start(bf16[80,1024]{1,0:T(8,128)(2,1)S(1)} %payload.1.refs_0_), channel_id=1, source_target_pairs={{0,5},{1,4},{2,7},{3,6},{4,1},{5,0},{6,3},{7,2},{8,14},{9,15},{10,... | collective-permute-start | bytes 491528 | tf_op jit(solution)/shard_map/ppermute | solution.py:45
  23.2 1.4 %collective-permute-start.5 = (bf16[80,1024]{1,0:T(8,128)(2,1)S(1)}, bf16[80,1024]{1,0:T(8,128)(2,1)S(1)}, u32[]{:S(2)}, u32[]{:S(2)}) collective-permute-start(bf16[80,1024]{1,0:T(8,128)(2,1)S(1)} %collective-permute-done.1.refs_1_.refs_2_), channel_id=1, source_target_pairs={{8,0},{0,8},{9,1},{1,9},{10,2},{2,10},{11,3},{3,11},{12,4},{4,12},... | collective-permute-start | bytes 491528 | tf_op jit(solution)/shard_map/ppermute | solution.py:50
  23.2 1.6 %collective-permute-start.6 = (bf16[80,1024]{1,0:T(8,128)(2,1)S(1)}, bf16[80,1024]{1,0:T(8,128)(2,1)S(1)}, u32[]{:S(2)}, u32[]{:S(2)}) collective-permute-start(bf16[80,1024]{1,0:T(8,128)(2,1)S(1)} %collective-permute-done.2.refs_2_.refs_4_), channel_id=1, source_target_pairs={{8,0},{0,8},{9,1},{1,9},{10,2},{2,10},{11,3},{3,11},{12,4},{4,12},... | collective-permute-start | bytes 491528 | tf_op jit(solution)/shard_map/ppermute | solution.py:50
  23.7 1.4 %collective-permute-start.7 = (bf16[80,1024]{1,0:T(8,128)(2,1)S(1)}, bf16[80,1024]{1,0:T(8,128)(2,1)S(1)}, u32[]{:S(2)}, u32[]{:S(2)}) collective-permute-start(bf16[80,1024]{1,0:T(8,128)(2,1)S(1)} %collective-permute-done.3.refs_2_.refs_6_.refs_5_), channel_id=1, source_target_pairs={{8,0},{0,8},{9,1},{1,9},{10,2},{2,10},{11,3},{3,11},{12,4},{4,12},... | collective-permute-start | bytes 491528 | tf_op jit(solution)/shard_map/ppermute | solution.py:50
  23.7 1.6 %collective-permute-start.8 = (bf16[80,1024]{1,0:T(8,128)(2,1)S(1)}, bf16[80,1024]{1,0:T(8,128)(2,1)S(1)}, u32[]{:S(2)}, u32[]{:S(2)}) collective-permute-start(bf16[80,1024]{1,0:T(8,128)(2,1)S(1)} %collective-permute-done.4.refs_4_.refs_8_.refs_7_), channel_id=1, source_target_pairs={{8,0},{0,8},{9,1},{1,9},{10,2},{2,10},{11,3},{3,11},{12,4},{4,12},... | collective-permute-start | bytes 491528 | tf_op jit(solution)/shard_map/ppermute | solution.py:50
  25.4 3.4 %copy-start.1 = (bf16[1,2,1024,1024]{3,2,1,0:T(8,128)(2,1)S(1)}, bf16[1,2,1024,1024]{3,2,1,0:T(8,128)(2,1)}, u32[]{:S(2)}) copy-start(bf16[1,2,1024,1024]{3,2,1,0:T(8,128)(2,1)} %refs_0_.1) | copy-start | bytes 12582916
  27.9 2.5 %copy-start.3 = (bf16[1024,1024]{1,0:T(8,128)(2,1)S(1)}, bf16[1024,1024]{1,0:T(8,128)(2,1)}, u32[]{:S(2)}) copy-start(bf16[1024,1024]{1,0:T(8,128)(2,1)} %w_gate_ref.1) | copy-start | bytes 6291460
  28.8 23.2 %collective-permute-start.14 = (bf16[1,2,1024,1024]{3,2,1,0:T(8,128)(2,1)S(1)}, bf16[1,2,1024,1024]{3,2,1,0:T(8,128)(2,1)S(1)}, u32[]{:S(2)}, u32[]{:S(2)}) collective-permute-start(bf16[1,2,1024,1024]{3,2,1,0:T(8,128)(2,1)S(1)} %copy-done.1), channel_id=1, source_target_pairs={{8,0},{0,8},{9,1},{1,9},{10,2},{2,10},{11,3},{3,11},{12,4},{4,12},... | collective-permute-start | bytes 12582920 | tf_op jit(solution)/shard_map/ppermute | solution.py:50
  29.1 8.4 %collective-permute-start.9 = (bf16[256,512]{1,0:T(8,128)(2,1)S(1)}, bf16[256,512]{1,0:T(8,128)(2,1)S(1)}, u32[]{:S(2)}, u32[]{:S(2)}) collective-permute-start(bf16[256,512]{1,0:T(8,128)(2,1)S(1)} %get-tuple-element.38), channel_id=1, source_target_pairs={{0,1},{1,0},{2,3},{3,2},{4,5},{5,4},{6,7},{7,6},{8,9},{9,8},{10,11... | collective-permute-start | bytes 786440 | tf_op jit(solution)/shard_map/ppermute | solution.py:37
  29.9 22.0 %copy-start.4 = (bf16[1024,1024]{1,0:T(8,128)(2,1)S(1)}, bf16[1024,1024]{1,0:T(8,128)(2,1)}, u32[]{:S(2)}) copy-start(bf16[1024,1024]{1,0:T(8,128)(2,1)} %w_out_ref.1) | copy-start | bytes 6291460
  29.9 22.0 %copy-start.6 = (f32[1024]{0:T(1024)S(1)}, f32[1024]{0:T(1024)}, u32[]{:S(2)}) copy-start(f32[1024]{0:T(1024)} %param.22) | copy-start | bytes 12292
  29.9 22.0 %copy-start.8 = (s32[1,64]{1,0:T(1,128)S(1)}, s32[1,64]{1,0:T(1,128)}, u32[]{:S(2)}) copy-start(s32[1,64]{1,0:T(1,128)} %domain_ref.1) | copy-start | bytes 772
  29.9 8.2 %collective-permute-start.10 = (bf16[256,512]{1,0:T(8,128)(2,1)S(1)}, bf16[256,512]{1,0:T(8,128)(2,1)S(1)}, u32[]{:S(2)}, u32[]{:S(2)}) collective-permute-start(bf16[256,512]{1,0:T(8,128)(2,1)S(1)} %get-tuple-element.39), channel_id=1, source_target_pairs={{0,2},{1,3},{2,0},{3,1},{4,6},{5,7},{6,4},{7,5},{8,10},{9,11},{10,... | collective-permute-start | bytes 786440 | tf_op jit(solution)/shard_map/ppermute | solution.py:37
  38.1 5.0 %collective-permute-start.12 = (bf16[128,512]{1,0:T(8,128)(2,1)S(1)}, bf16[128,512]{1,0:T(8,128)(2,1)S(1)}, u32[]{:S(2)}, u32[]{:S(2)}) collective-permute-start(bf16[128,512]{1,0:T(8,128)(2,1)S(1)} %get-tuple-element.47), channel_id=1, source_target_pairs={{0,1},{1,0},{2,3},{3,2},{4,5},{5,4},{6,7},{7,6},{8,9},{9,8},{10,11... | collective-permute-start | bytes 393224 | tf_op jit(solution)/shard_map/ppermute | solution.py:37
  39.5 5.0 %collective-permute-start.11 = (bf16[128,512]{1,0:T(8,128)(2,1)S(1)}, bf16[128,512]{1,0:T(8,128)(2,1)S(1)}, u32[]{:S(2)}, u32[]{:S(2)}) collective-permute-start(bf16[128,512]{1,0:T(8,128)(2,1)S(1)} %get-tuple-element.43), channel_id=1, source_target_pairs={{0,2},{1,3},{2,0},{3,1},{4,6},{5,7},{6,4},{7,5},{8,10},{9,11},{10,... | collective-permute-start | bytes 393224 | tf_op jit(solution)/shard_map/ppermute | solution.py:37
  44.6 7.3 %collective-permute-start.13 = (bf16[64,1024]{1,0:T(8,128)(2,1)S(1)}, bf16[64,1024]{1,0:T(8,128)(2,1)S(1)}, u32[]{:S(2)}, u32[]{:S(2)}) collective-permute-start(bf16[64,1024]{1,0:T(8,128)(2,1)S(1)} %get-tuple-element.49), channel_id=1, source_target_pairs={{0,4},{1,5},{2,6},{3,7},{4,0},{5,1},{6,2},{7,3},{8,12},{9,13},{10,... | collective-permute-start | bytes 393224 | tf_op jit(solution)/shard_map/ppermute | solution.py:37

commit v5 on v4

--- a/solution.py
+++ b/solution.py
@@ -9,8 +9,6 @@
 
 H = 8
 LAYERS = 2
-ID_ROWS = 16
-ID_BASE = 128
 VMEM_LIMIT = 24 * 1024 * 1024
 LOADS_BESIDE = 8 * 10**9
 
@@ -90,22 +88,10 @@
     blocks, at = [], 0
     for piece in pieces:
         count = 1 if piece[2] is None else lax.axis_size("user")
-        shards = [ref[: ref.shape[0] - ID_ROWS, :] for ref in refs[at : at + count]]
+        shards = [ref[...] for ref in refs[at : at + count]]
         blocks.append(shards[0] if piece[2] is None else of_core(piece[2], shards))
         at += count
     return jnp.concatenate(blocks, axis=0)
-
-
-def ids_of(flips, refs, slots):
-    rows = refs[0].shape[0] - ID_ROWS
-    blocks = [ref[rows:, :slots].astype(F32) for ref in refs]
-    row = lax.broadcasted_iota(jnp.int32, (ID_ROWS, slots), 0)
-    high_row = 2 * core_at(0)
-    weight = jnp.where(row == high_row, float(ID_BASE), jnp.where(row == high_row + 1, 1.0, 0.0))
-    return {
-        flip: jnp.sum(of_core(core, blocks) * weight, axis=0, keepdims=True).astype(jnp.int32)
-        for core, flip in enumerate(flips)
-    }
 
 
 def matches(pieces, shard_rows, ids_row):
@@ -118,30 +104,19 @@
     return jnp.concatenate(blocks, axis=0)
 
 
-def payload_kernel(rows_ref, own_ref, *refs):
-    other_refs, out_ref = refs[:-1], refs[-1]
-    rows, width = rows_ref.shape
-    slots = own_ref.shape[1]
-    out_ref[:rows, :] = rows_ref[...]
-    row = lax.broadcasted_iota(jnp.int32, (ID_ROWS, slots), 0)
-    digits = jnp.zeros((ID_ROWS, slots), jnp.int32)
-    for steps, ref in enumerate((own_ref, *other_refs)):
-        high_row = 2 * core_at(steps)
-        high = ref[...] // ID_BASE
-        digits = jnp.where(row == high_row, high, digits)
-        digits = jnp.where(row == high_row + 1, ref[...] - high * ID_BASE, digits)
-    out_ref[rows:, :] = jnp.zeros((ID_ROWS, width), BF16)
-    out_ref[rows:, :slots] = digits.astype(F32).astype(BF16)
-
-
-def payload_of(rows, ids, other_ids):
-    return kernel_call(
-        payload_kernel,
-        "payload",
-        [jax.ShapeDtypeStruct((rows.shape[0] + ID_ROWS, rows.shape[1]), BF16)],
-        [VMEM] * (2 + len(other_ids)),
-        flops=LOADS_BESIDE,
-    )(rows, ids, *other_ids)[0]
+def stack_kernel(*refs):
+    *refs, out_ref = refs
+    at = 0
+    for ref in refs:
+        out_ref[at : at + ref.shape[0], :] = ref[...]
+        at += ref.shape[0]
+
+
+def stack(blocks, flops=0):
+    shape = (sum(block.shape[0] for block in blocks), blocks[0].shape[1])
+    return kernel_call(
+        stack_kernel, "stack", [jax.ShapeDtypeStruct(shape, blocks[0].dtype)], [VMEM] * len(blocks), flops=flops
+    )(*blocks)[0]
 
 
 def attend_rows(pieces, refs, w_query_ref, keys_ref, values_ref, sums_ref):
@@ -199,14 +174,12 @@
     )(w_query, keys, values, *blocks)[0]
 
 
-def place_kernel(pieces, all_flips, orders, parts, shard_rows, ids_ref, *refs):
-    *refs, kept_a, sent_a, kept_b, sent_b = refs
-    sums_refs, refs = refs[:parts], refs[parts:]
-    slots, users = ids_ref.shape[1], lax.axis_size("user")
-    ids = {0: ids_ref[...]}
-    for at, flips in enumerate(all_flips):
-        ids.update(ids_of(flips, refs[at * users : (at + 1) * users], slots))
-    ids_row = jnp.concatenate([ids[flip] for flip in orders[0]], axis=1)
+def place_kernel(pieces, id_flips, orders, shard_rows, near_ids_ref, far_ids_ref, *refs):
+    *sums_refs, kept_a, sent_a, kept_b, sent_b = refs
+    half, slots = near_ids_ref.shape
+    rows = [id_flips.index(flip) for flip in orders[0]]
+    refs_rows = [(near_ids_ref, row) if row < half else (far_ids_ref, row - half) for row in rows]
+    ids_row = jnp.concatenate([ref[row : row + 1, :] for ref, row in refs_rows], axis=1)
     onehot = matches(pieces, shard_rows, ids_row)
     width = sums_refs[0].shape[1] // 2
     for side, order in enumerate(orders):
@@ -220,19 +193,17 @@
             target[at % half * slots : (at % half + 1) * slots, :] = placed[block * slots : (block + 1) * slots, :]
 
 
-def place(pieces, groups, orders, shard_rows, ids, sums):
-    devices, slots = len(orders[0]), ids.shape[1]
+def place(pieces, id_flips, orders, shard_rows, near_ids, far_ids, sums):
+    devices, slots = len(orders[0]), near_ids.shape[1]
     width = sums[0].shape[1]
     out = jax.ShapeDtypeStruct((devices * slots // 2, width // 2), BF16)
-    all_flips = [flips for flips, _ in groups]
-    blocks = [block for _, arrivals in groups for block in arrivals]
-    return kernel_call(
-        functools.partial(place_kernel, pieces, all_flips, orders, len(sums), shard_rows),
+    return kernel_call(
+        functools.partial(place_kernel, pieces, id_flips, orders, shard_rows),
         "place",
         [out] * 4,
-        [VMEM] * (1 + len(sums) + len(blocks)),
+        [VMEM] * (2 + len(sums)),
         flops=2 * sum(part.shape[0] for part in sums) * devices * slots * width,
-    )(ids, *sums, *blocks)
+    )(near_ids, far_ids, *sums)
 
 
 def fold_kernel(sides, *refs):
@@ -337,21 +308,29 @@
     bits = hist_devices.bit_length() - 1
     others = range(1, users)
 
-    payload = payload_of(item_table, item_ids, [from_user(item_ids, steps) for steps in others])
     all_flips = [tuple(range(at, min(at + users, hist_devices))) for at in range(1, hist_devices, users)]
-    fetched = [swapped_by_user(payload, flips) for flips in all_flips]
+    fetched = [swapped_by_user(item_table, flips) for flips in all_flips]
+
+    known_ids, id_flips = [stack([item_ids], flops=LOADS_BESIDE)], [0]
+    for bit in reversed(range(bits)):
+        far_ids = swapped(known_ids[-1], 1 << bit)
+        id_flips += [flip + (1 << bit) for flip in id_flips]
+        if bit:
+            known_ids.append(stack([known_ids[-1], far_ids]))
+    near_ids = known_ids[-1]
 
     early = len(all_flips) // 2
     first_pieces = [((0,) * users, 0, None)] + [(flips, 0, None) for flips in all_flips[:early]]
-    first_blocks = [payload] + fetched[:early]
+    first_blocks = [item_table] + fetched[:early]
+    w_query, _ = lax.optimization_barrier((w_query, known_ids[1]))
     first, masked_values = attend_first(
         first_pieces, first_blocks, shard_rows, history_lengths, w_query, history_keys, history_values
     )
-    first, *fetched = lax.optimization_barrier((first, *fetched))
-    groups, next_pieces, next_blocks = [], [], []
+    first, *fetched[:early] = lax.optimization_barrier((first, *fetched[:early]))
+    first, near_ids, *fetched[early:] = lax.optimization_barrier((first, near_ids, *fetched[early:]))
+    next_pieces, next_blocks = [], []
     for at, (flips, block) in enumerate(zip(all_flips, fetched)):
         arrivals = [block] + [from_user(block, steps) for steps in others]
-        groups.append((flips, arrivals))
         found = [(flips, steps, None) for steps in range(users)]
         if at < early:
             found = found[1:]
@@ -369,7 +348,7 @@
         for turn in turns
     ]
     kept_a, sent_a, kept_b, sent_b = place(
-        pieces, groups, orders, shard_rows, item_ids, [first, following]
+        pieces, id_flips, orders, shard_rows, near_ids, far_ids, [first, following]
     )
     embed, gating = prepare(pieces, blocks, shard_rows, kept_a, item_ids, w_gate)
 

time: 55 us -> 54.5 us (level)
  starting transfers between devices: 17 us -> 25.1 us
  waiting for transfers between devices: 25 us -> 17.2 us
  local copies, waits for them, and re-layouts: 1.59 us -> 0.7 us
    ppermute x5 -> x8, starting transfers between devices: 5.19 us -> 14 us  [swapped(): return lax.ppermute(value, 'hist', [(i, i ^ flip) for i in range(count)])]
    ppermute x4, waiting for transfers between devices: 7.05 us -> 0.01 us  [swapped_by_user(): return lax.ppermute(value, ('user', 'hist'), pairs)]
    ppermute x6 -> x5, waiting for transfers between devices: 2.07 us -> 0.01 us  [from_user(): lax.ppermute(value, 'user', [((i + steps) % count, i) for i in range(coun...]
    ppermute x5 -> x8, waiting for transfers between devices: 15.9 us -> 17.2 us  [swapped(): return lax.ppermute(value, 'hist', [(i, i ^ flip) for i in range(count)])]
    unnamed x20 -> x22, local copies, waits for them, and re-layouts: 1.59 us -> 0.7 us
    ppermute x6 -> x5, starting transfers between devices: 1.89 us -> 1.15 us  [from_user(): lax.ppermute(value, 'user', [((i + steps) % count, i) for i in range(coun...]
  transfers between devices with their start and end apart: 15 -> 17, of which waited for: 12 -> 7; matrix products, arithmetic and copies ran while one was open for 0% -> 0% of each run, Pallas kernels for 6% -> 11%
where the time goes in v5:
time: 54.5 us; the launch traced here: 54.3 us
  starting transfers between devices  25.1 us (46%)
  waiting for transfers between devices  17.2 us (32%)
  Pallas kernels  9.76 us (18%)
  between operations  1.5 us (3%)
  local copies, waits for them, and re-layouts  0.7 us (1%)
    ppermute x8, waiting for transfers between devices, swapped(): return lax.ppermute(value, 'hist', [(i, i ^ flip) for i in range(count)])  17.2 us
    ppermute x8, starting transfers between devices, swapped(): return lax.ppermute(value, 'hist', [(i, i ^ flip) for i in range(count)])  14 us
    ppermute x4, starting transfers between devices, swapped_by_user(): return lax.ppermute(value, ('user', 'hist'), pairs)  10 us
    pallas_call x1, Pallas kernels, finish(): kernel_call(finish_kernel, 'finish', [jax.ShapeDtypeStruct((1, slots, wid...  2.83 us
    pallas_call x1, Pallas kernels, attend_next(): kernel_call(functools.partial(next_kernel, pieces), 'attend_next', [jax.S...  2.51 us
    pallas_call x1, Pallas kernels, attend_first(): kernel_call(functools.partial(first_kernel, pieces), 'attend_first', [jax...  2.48 us
    ppermute x5, starting transfers between devices, from_user(): lax.ppermute(value, 'user', [((i + steps) % count, i) for i in range(coun...  1.15 us
  transfers between devices with their start and end apart: 17, of which 7 were waited for; matrix products, arithmetic and copies ran while one was open for 0% of the time, Pallas kernels for 11%

profile of v5, /device:TPU:0, one launch (start us, length us, event | category | flops | bytes accessed | tf_op | source)
XLA Modules:
  0.0 54.3 jit_solution(6116959392190004430)
XLA Ops:
  0.0 5.1 %collective-permute-start.4 = (bf16[64,1024]{1,0:T(8,128)(2,1)}, bf16[64,1024]{1,0:T(8,128)(2,1)S(1)}, u32[]{:S(2)}, u32[]{:S(2)}) collective-permute-start(bf16[64,1024]{1,0:T(8,128)(2,1)} %refs_0_.6), channel_id=1, source_target_pairs={{0,5},{1,4},{2,7},{3,6},{4,1},{5,0},{6,3},{7,2},{8,14},{9,15},{10,... | collective-permute-start | bytes 393224 | tf_op jit(solution)/shard_map/ppermute | solution.py:43
  5.1 1.5 %collective-permute-start.2 = (bf16[64,1024]{1,0:T(8,128)(2,1)}, bf16[64,1024]{1,0:T(8,128)(2,1)S(1)}, u32[]{:S(2)}, u32[]{:S(2)}) collective-permute-start(bf16[64,1024]{1,0:T(8,128)(2,1)} %refs_0_.6), channel_id=1, source_target_pairs={{0,3},{1,2},{2,1},{3,0},{4,7},{5,6},{6,5},{7,4},{8,12},{9,13},{10,... | collective-permute-start | bytes 393224 | tf_op jit(solution)/shard_map/ppermute | solution.py:43
  6.6 1.5 %collective-permute-start.1 = (bf16[64,1024]{1,0:T(8,128)(2,1)}, bf16[64,1024]{1,0:T(8,128)(2,1)S(1)}, u32[]{:S(2)}, u32[]{:S(2)}) collective-permute-start(bf16[64,1024]{1,0:T(8,128)(2,1)} %refs_0_.6), channel_id=1, source_target_pairs={{0,1},{1,0},{2,3},{3,2},{4,5},{5,4},{6,7},{7,6},{8,10},{9,11},{10,... | collective-permute-start | bytes 393224 | tf_op jit(solution)/shard_map/ppermute | solution.py:43
  8.1 1.9 %collective-permute-start.5 = (bf16[64,1024]{1,0:T(8,128)(2,1)}, bf16[64,1024]{1,0:T(8,128)(2,1)S(1)}, u32[]{:S(2)}, u32[]{:S(2)}) collective-permute-start(bf16[64,1024]{1,0:T(8,128)(2,1)} %refs_0_.6), channel_id=1, source_target_pairs={{0,7},{1,6},{2,5},{3,4},{4,3},{5,2},{6,1},{7,0},{16,23},{17,22},{1... | collective-permute-start | bytes 393224 | tf_op jit(solution)/shard_map/ppermute | solution.py:43
  10.0 0.0 copy-start.9
  10.0 0.6 %copy-done.9 = s32[1,64]{1,0:T(1,128)S(1)} copy-done((s32[1,64]{1,0:T(1,128)S(1)}, s32[1,64]{1,0:T(1,128)}, u32[]{:S(2)}) %copy-start.9) | copy-done | bytes 280
  10.7 1.8 %collective-permute-start = (s32[1,64]{1,0:T(1,128)S(1)}, s32[1,64]{1,0:T(1,128)S(1)}, u32[]{:S(2)}, u32[]{:S(2)}) collective-permute-start(s32[1,64]{1,0:T(1,128)S(1)} %stack.3.refs_0_), channel_id=1, source_target_pairs={{0,4},{1,5},{2,6},{3,7},{4,0},{5,1},{6,2},{7,3},{8,12},{9,13},{10,... | collective-permute-start | bytes 776 | tf_op jit(solution)/shard_map/ppermute | solution.py:35
  12.5 2.6 %collective-permute-done.refs_1_ = s32[1,64]{1,0:T(1,128)S(1)} collective-permute-done((s32[1,64]{1,0:T(1,128)S(1)}, s32[1,64]{1,0:T(1,128)S(1)}, u32[]{:S(2)}, u32[]{:S(2)}) %collective-permute-start) | collective-permute-done | bytes 288 | tf_op jit(solution)/shard_map/ppermute | solution.py:35
  15.1 2.3 %collective-permute-start.3 = (s32[2,64]{1,0:T(2,128)S(1)}, s32[2,64]{1,0:T(2,128)S(1)}, u32[]{:S(2)}, u32[]{:S(2)}) collective-permute-start(s32[2,64]{1,0:T(2,128)S(1)} %stack.4.refs_0_), channel_id=1, source_target_pairs={{0,2},{1,3},{2,0},{3,1},{4,6},{5,7},{6,4},{7,5},{8,10},{9,11},{10,... | collective-permute-start | bytes 1544 | tf_op jit(solution)/shard_map/ppermute | solution.py:35
  18.1 0.9 %collective-permute-done.3.refs_1_ = s32[2,64]{1,0:T(2,128)S(1)} collective-permute-done((s32[2,64]{1,0:T(2,128)S(1)}, s32[2,64]{1,0:T(2,128)S(1)}, u32[]{:S(2)}, u32[]{:S(2)}) %collective-permute-start.3) | collective-permute-done | bytes 544 | tf_op jit(solution)/shard_map/ppermute | solution.py:35
  19.0 0.0 collective-permute-done.2.refs_2_
  19.0 0.0 collective-permute-done.1.refs_1_
  19.0 0.0 copy-done.6
  19.0 0.0 copy-done
  19.1 2.5 %attend_first.1 = (bf16[192,1024]{1,0:T(8,128)(2,1)S(1)}, bf16[512,1024]{1,0:T(8,128)(2,1)S(1)}) custom-call(s32[1]{0:T(128)S(6)} %copy.14.length_ref, bf16[1024,1024]{1,0:T(8,128)(2,1)S(1)} %copy-done, bf16[1,512,1024]{2,1,0:T(8,128)(2,1)S(1)} %copy-done.2, bf16[1,512,1024]{2,1,0:T(8,128)(2,1)S(1)} %copy-done.5, bf16[64,1024]{1,0:T(8,128)(2,1)S(1)} %copy-done.6, ...), custom_call_target="tpu_custom_call" | custom-call | flops 805306368 | tf_op jit(solution)/shard_map/attend_first/pallas_call | solution.py:157
  21.5 0.0 collective-permute-done.4.refs_2_.refs_5_
  21.6 0.0 collective-permute-done.5.refs_4_.refs_7_
  21.6 0.1 collective-permute-start.9
  21.6 0.5 collective-permute-start.10
  22.1 0.1 collective-permute-start.7
  22.2 0.4 collective-permute-start.8
  22.7 1.5 %collective-permute-start.6 = (s32[4,64]{1,0:T(4,128)S(1)}, s32[4,64]{1,0:T(4,128)S(1)}, u32[]{:S(2)}, u32[]{:S(2)}) collective-permute-start(s32[4,64]{1,0:T(4,128)S(1)} %stack.5.near_ids_ref), channel_id=1, source_target_pairs={{0,1},{1,0},{2,3},{3,2},{4,5},{5,4},{6,7},{7,6},{8,9},{9,8},{10,11... | collective-permute-start | bytes 3080 | tf_op jit(solution)/shard_map/ppermute | solution.py:35
  24.2 0.0 collective-permute-done.9.refs_3_.refs_6_
  24.2 0.0 collective-permute-done.10.refs_5_.refs_8_
  24.2 0.0 collective-permute-done.7.refs_0_.refs_3_
  24.2 0.0 collective-permute-done.8.refs_1_.refs_4_
  24.2 0.0 copy-start.1
  24.2 0.0 copy-start.3
  24.2 0.0 copy-start.10
  24.2 2.5 %attend_next.1.refs_1_ = bf16[320,1024]{1,0:T(8,128)(2,1)S(1)} custom-call(bf16[1024,1024]{1,0:T(8,128)(2,1)S(1)} %copy-done, bf16[1,512,1024]{2,1,0:T(8,128)(2,1)S(1)} %copy-done.2, bf16[512,1024]{1,0:T(8,128)(2,1)S(1)} %get-tuple-element.37.values_ref, bf16[64,1024]{1,0:T(8,128)(2,1)S(1)} %collective-permute-done.7.refs_0_.refs_3_, ...), custom_call_target="tpu_custom_call" | custom-call | flops 1342177280 | tf_op jit(solution)/shard_map/attend_next/pallas_call | solution.py:168
  26.8 0.0 collective-permute-done.6.far_ids_ref
  26.8 0.9 %place.1 = (bf16[256,512]{1,0:T(8,128)(2,1)S(1)}, bf16[256,512]{1,0:T(8,128)(2,1)S(1)}, bf16[256,512]{1,0:T(8,128)(2,1)S(1)}, bf16[256,512]{1,0:T(8,128)(2,1)S(1)}) custom-call(s32[4,64]{1,0:T(4,128)S(1)} %stack.5.near_ids_ref, s32[4,64]{1,0:T(4,128)S(1)} %collective-permute-done.6.far_ids_ref, bf16[192,1024]{1,0:T(8,128)(2,1)S(1)} %get-tuple-element.36.refs_0_, ...), custom_call_target="tpu_custom_call" | custom-call | flops 536870912 | tf_op jit(solution)/shard_map/place/pallas_call | solution.py:200
  27.6 0.1 collective-permute-start.16
  27.7 1.3 %collective-permute-start.11 = (bf16[256,512]{1,0:T(8,128)(2,1)S(1)}, bf16[256,512]{1,0:T(8,128)(2,1)S(1)}, u32[]{:S(2)}, u32[]{:S(2)}) collective-permute-start(bf16[256,512]{1,0:T(8,128)(2,1)S(1)} %get-tuple-element.44), channel_id=1, source_target_pairs={{0,1},{1,0},{2,3},{3,2},{4,5},{5,4},{6,7},{7,6},{8,9},{9,8},{10,11... | collective-permute-start | bytes 786440 | tf_op jit(solution)/shard_map/ppermute | solution.py:35
  29.0 2.0 %collective-permute-start.12 = (bf16[256,512]{1,0:T(8,128)(2,1)S(1)}, bf16[256,512]{1,0:T(8,128)(2,1)S(1)}, u32[]{:S(2)}, u32[]{:S(2)}) collective-permute-start(bf16[256,512]{1,0:T(8,128)(2,1)S(1)} %get-tuple-element.45), channel_id=1, source_target_pairs={{0,2},{1,3},{2,0},{3,1},{4,6},{5,7},{6,4},{7,5},{8,10},{9,11},{10,... | collective-permute-start | bytes 786440 | tf_op jit(solution)/shard_map/ppermute | solution.py:35
  31.0 0.9 %prepare.1 = (f32[64,1024]{1,0:T(8,128)S(1)}, f32[64,1024]{1,0:T(8,128)S(1)}) custom-call(bf16[256,512]{1,0:T(8,128)(2,1)S(1)} %get-tuple-element.43.after_ref.refs_0_, s32[1,64]{1,0:T(1,128)S(1)} %copy-done.10, bf16[1024,1024]{1,0:T(8,128)(2,1)S(1)} %copy-done.3, bf16[64,1024]{1,0:T(8,128)(2,1)S(1)} %copy-done.6, ...), custom_call_target="tpu_custom_call" | custom-call | flops 201326592 | tf_op jit(solution)/shard_map/prepare/pallas_call | solution.py:245
  31.9 4.5 %collective-permute-done.11.refs_1_ = bf16[256,512]{1,0:T(8,128)(2,1)S(1)} collective-permute-done((bf16[256,512]{1,0:T(8,128)(2,1)S(1)}, bf16[256,512]{1,0:T(8,128)(2,1)S(1)}, u32[]{:S(2)}, u32[]{:S(2)}) %collective-permute-start.11) | collective-permute-done | bytes 262176 | tf_op jit(solution)/shard_map/ppermute | solution.py:35
  36.4 1.0 %collective-permute-done.12.refs_1_ = bf16[256,512]{1,0:T(8,128)(2,1)S(1)} collective-permute-done((bf16[256,512]{1,0:T(8,128)(2,1)S(1)}, bf16[256,512]{1,0:T(8,128)(2,1)S(1)}, u32[]{:S(2)}, u32[]{:S(2)}) %collective-permute-start.12) | collective-permute-done | bytes 262176 | tf_op jit(solution)/shard_map/ppermute | solution.py:35
  37.4 0.1 fold.4
  37.5 1.1 %collective-permute-start.14 = (bf16[128,512]{1,0:T(8,128)(2,1)S(1)}, bf16[128,512]{1,0:T(8,128)(2,1)S(1)}, u32[]{:S(2)}, u32[]{:S(2)}) collective-permute-start(bf16[128,512]{1,0:T(8,128)(2,1)S(1)} %get-tuple-element.53), channel_id=1, source_target_pairs={{0,1},{1,0},{2,3},{3,2},{4,5},{5,4},{6,7},{7,6},{8,9},{9,8},{10,11... | collective-permute-start | bytes 393224 | tf_op jit(solution)/shard_map/ppermute | solution.py:35
  38.6 0.1 fold.3
  38.7 1.8 %collective-permute-start.13 = (bf16[128,512]{1,0:T(8,128)(2,1)S(1)}, bf16[128,512]{1,0:T(8,128)(2,1)S(1)}, u32[]{:S(2)}, u32[]{:S(2)}) collective-permute-start(bf16[128,512]{1,0:T(8,128)(2,1)S(1)} %get-tuple-element.49), channel_id=1, source_target_pairs={{0,2},{1,3},{2,0},{3,1},{4,6},{5,7},{6,4},{7,5},{8,10},{9,11},{10,... | collective-permute-start | bytes 393224 | tf_op jit(solution)/shard_map/ppermute | solution.py:35
  40.5 2.0 %collective-permute-done.14.refs_3_ = bf16[128,512]{1,0:T(8,128)(2,1)S(1)} collective-permute-done((bf16[128,512]{1,0:T(8,128)(2,1)S(1)}, bf16[128,512]{1,0:T(8,128)(2,1)S(1)}, u32[]{:S(2)}, u32[]{:S(2)}) %collective-permute-start.14) | collective-permute-done | bytes 131104 | tf_op jit(solution)/shard_map/ppermute | solution.py:35
  42.5 1.2 %collective-permute-done.13.refs_1_ = bf16[128,512]{1,0:T(8,128)(2,1)S(1)} collective-permute-done((bf16[128,512]{1,0:T(8,128)(2,1)S(1)}, bf16[128,512]{1,0:T(8,128)(2,1)S(1)}, u32[]{:S(2)}, u32[]{:S(2)}) %collective-permute-start.13) | collective-permute-done | bytes 131104 | tf_op jit(solution)/shard_map/ppermute | solution.py:35
  43.8 2.1 %collective-permute-start.15 = (bf16[64,1024]{1,0:T(8,128)(2,1)S(1)}, bf16[64,1024]{1,0:T(8,128)(2,1)S(1)}, u32[]{:S(2)}, u32[]{:S(2)}) collective-permute-start(bf16[64,1024]{1,0:T(8,128)(2,1)S(1)} %get-tuple-element.55), channel_id=1, source_target_pairs={{0,4},{1,5},{2,6},{3,7},{4,0},{5,1},{6,2},{7,3},{8,12},{9,13},{10,... | collective-permute-start | bytes 393224 | tf_op jit(solution)/shard_map/ppermute | solution.py:35
  46.5 5.0 %collective-permute-done.15.come_ref = bf16[64,1024]{1,0:T(8,128)(2,1)S(1)} collective-permute-done((bf16[64,1024]{1,0:T(8,128)(2,1)S(1)}, bf16[64,1024]{1,0:T(8,128)(2,1)S(1)}, u32[]{:S(2)}, u32[]{:S(2)}) %collective-permute-start.15) | collective-permute-done | bytes 131104 | tf_op jit(solution)/shard_map/ppermute | solution.py:35
  51.5 0.0 collective-permute-done.16.refs_1_
  51.5 2.8 %finish.1 = bf16[1,64,1024]{2,1,0:T(8,128)(2,1)} custom-call(f32[64,1024]{1,0:T(8,128)S(1)} %get-tuple-element.54.kept_ref, bf16[64,1024]{1,0:T(8,128)(2,1)S(1)} %collective-permute-done.15.come_ref, f32[64,1024]{1,0:T(8,128)S(1)} %get-tuple-element.56.embed_ref, f32[64,1024]{1,0:T(8,128)S(1)} %get-tuple-element.57.gating_ref, f32[1,1024]{1,0:T(1,128)S(1)} %bitcast.1, ...), custom_call_target="tpu_custom_call" | custom-call | flops 671088640 | tf_op jit(solution)/shard_map/finish/pallas_call | solution.py:282
  (19 shorter events, 0.1 us)
Async XLA Ops:
  0.0 19.0 %copy-start.6 = (bf16[64,1024]{1,0:T(8,128)(2,1)S(1)}, bf16[64,1024]{1,0:T(8,128)(2,1)}, u32[]{:S(2)}) copy-start(bf16[64,1024]{1,0:T(8,128)(2,1)} %refs_0_.6) | copy-start | bytes 393220
  0.0 19.0 %copy-start = (bf16[1024,1024]{1,0:T(8,128)(2,1)S(1)}, bf16[1024,1024]{1,0:T(8,128)(2,1)}, u32[]{:S(2)}) copy-start(bf16[1024,1024]{1,0:T(8,128)(2,1)} %w_query_ref.1) | copy-start | bytes 6291460
  0.0 19.0 %copy-start.2 = (bf16[1,512,1024]{2,1,0:T(8,128)(2,1)S(1)}, bf16[1,512,1024]{2,1,0:T(8,128)(2,1)}, u32[]{:S(2)}) copy-start(bf16[1,512,1024]{2,1,0:T(8,128)(2,1)} %keys_ref.3) | copy-start | bytes 3145732
  0.0 19.0 %copy-start.5 = (bf16[1,512,1024]{2,1,0:T(8,128)(2,1)S(1)}, bf16[1,512,1024]{2,1,0:T(8,128)(2,1)}, u32[]{:S(2)}) copy-start(bf16[1,512,1024]{2,1,0:T(8,128)(2,1)} %values_ref.1) | copy-start | bytes 3145732
  0.0 21.5 %collective-permute-start.4 = (bf16[64,1024]{1,0:T(8,128)(2,1)}, bf16[64,1024]{1,0:T(8,128)(2,1)S(1)}, u32[]{:S(2)}, u32[]{:S(2)}) collective-permute-start(bf16[64,1024]{1,0:T(8,128)(2,1)} %refs_0_.6), channel_id=1, source_target_pairs={{0,5},{1,4},{2,7},{3,6},{4,1},{5,0},{6,3},{7,2},{8,14},{9,15},{10,... | collective-permute-start | bytes 393224 | tf_op jit(solution)/shard_map/ppermute | solution.py:43
  5.1 13.9 %collective-permute-start.2 = (bf16[64,1024]{1,0:T(8,128)(2,1)}, bf16[64,1024]{1,0:T(8,128)(2,1)S(1)}, u32[]{:S(2)}, u32[]{:S(2)}) collective-permute-start(bf16[64,1024]{1,0:T(8,128)(2,1)} %refs_0_.6), channel_id=1, source_target_pairs={{0,3},{1,2},{2,1},{3,0},{4,7},{5,6},{6,5},{7,4},{8,12},{9,13},{10,... | collective-permute-start | bytes 393224 | tf_op jit(solution)/shard_map/ppermute | solution.py:43
  6.6 12.4 %collective-permute-start.1 = (bf16[64,1024]{1,0:T(8,128)(2,1)}, bf16[64,1024]{1,0:T(8,128)(2,1)S(1)}, u32[]{:S(2)}, u32[]{:S(2)}) collective-permute-start(bf16[64,1024]{1,0:T(8,128)(2,1)} %refs_0_.6), channel_id=1, source_target_pairs={{0,1},{1,0},{2,3},{3,2},{4,5},{5,4},{6,7},{7,6},{8,10},{9,11},{10,... | collective-permute-start | bytes 393224 | tf_op jit(solution)/shard_map/ppermute | solution.py:43
  8.1 13.4 %collective-permute-start.5 = (bf16[64,1024]{1,0:T(8,128)(2,1)}, bf16[64,1024]{1,0:T(8,128)(2,1)S(1)}, u32[]{:S(2)}, u32[]{:S(2)}) collective-permute-start(bf16[64,1024]{1,0:T(8,128)(2,1)} %refs_0_.6), channel_id=1, source_target_pairs={{0,7},{1,6},{2,5},{3,4},{4,3},{5,2},{6,1},{7,0},{16,23},{17,22},{1... | collective-permute-start | bytes 393224 | tf_op jit(solution)/shard_map/ppermute | solution.py:43
  10.0 0.7 %copy-start.9 = (s32[1,64]{1,0:T(1,128)S(1)}, s32[1,64]{1,0:T(1,128)}, u32[]{:S(2)}) copy-start(s32[1,64]{1,0:T(1,128)} %ids_ref.1) | copy-start | bytes 772
  10.7 4.4 %collective-permute-start = (s32[1,64]{1,0:T(1,128)S(1)}, s32[1,64]{1,0:T(1,128)S(1)}, u32[]{:S(2)}, u32[]{:S(2)}) collective-permute-start(s32[1,64]{1,0:T(1,128)S(1)} %stack.3.refs_0_), channel_id=1, source_target_pairs={{0,4},{1,5},{2,6},{3,7},{4,0},{5,1},{6,2},{7,3},{8,12},{9,13},{10,... | collective-permute-start | bytes 776 | tf_op jit(solution)/shard_map/ppermute | solution.py:35
  15.1 3.9 %collective-permute-start.3 = (s32[2,64]{1,0:T(2,128)S(1)}, s32[2,64]{1,0:T(2,128)S(1)}, u32[]{:S(2)}, u32[]{:S(2)}) collective-permute-start(s32[2,64]{1,0:T(2,128)S(1)} %stack.4.refs_0_), channel_id=1, source_target_pairs={{0,2},{1,3},{2,0},{3,1},{4,6},{5,7},{6,4},{7,5},{8,10},{9,11},{10,... | collective-permute-start | bytes 1544 | tf_op jit(solution)/shard_map/ppermute | solution.py:35
  21.6 2.6 %collective-permute-start.9 = (bf16[64,1024]{1,0:T(8,128)(2,1)S(1)}, bf16[64,1024]{1,0:T(8,128)(2,1)S(1)}, u32[]{:S(2)}, u32[]{:S(2)}) collective-permute-start(bf16[64,1024]{1,0:T(8,128)(2,1)S(1)} %collective-permute-done.4.refs_2_.refs_5_), channel_id=1, source_target_pairs={{8,0},{0,8},{9,1},{1,9},{10,2},{2,10},{11,3},{3,11},{12,4},{4,12},... | collective-permute-start | bytes 393224 | tf_op jit(solution)/shard_map/ppermute | solution.py:48
  21.6 2.5 %collective-permute-start.10 = (bf16[64,1024]{1,0:T(8,128)(2,1)S(1)}, bf16[64,1024]{1,0:T(8,128)(2,1)S(1)}, u32[]{:S(2)}, u32[]{:S(2)}) collective-permute-start(bf16[64,1024]{1,0:T(8,128)(2,1)S(1)} %collective-permute-done.5.refs_4_.refs_7_), channel_id=1, source_target_pairs={{8,0},{0,8},{9,1},{1,9},{10,2},{2,10},{11,3},{3,11},{12,4},{4,12},... | collective-permute-start | bytes 393224 | tf_op jit(solution)/shard_map/ppermute | solution.py:48
  22.1 2.0 %collective-permute-start.7 = (bf16[64,1024]{1,0:T(8,128)(2,1)S(1)}, bf16[64,1024]{1,0:T(8,128)(2,1)S(1)}, u32[]{:S(2)}, u32[]{:S(2)}) collective-permute-start(bf16[64,1024]{1,0:T(8,128)(2,1)S(1)} %collective-permute-done.1.refs_1_), channel_id=1, source_target_pairs={{8,0},{0,8},{9,1},{1,9},{10,2},{2,10},{11,3},{3,11},{12,4},{4,12},... | collective-permute-start | bytes 393224 | tf_op jit(solution)/shard_map/ppermute | solution.py:48
  22.2 2.0 %collective-permute-start.8 = (bf16[64,1024]{1,0:T(8,128)(2,1)S(1)}, bf16[64,1024]{1,0:T(8,128)(2,1)S(1)}, u32[]{:S(2)}, u32[]{:S(2)}) collective-permute-start(bf16[64,1024]{1,0:T(8,128)(2,1)S(1)} %collective-permute-done.2.refs_2_), channel_id=1, source_target_pairs={{8,0},{0,8},{9,1},{1,9},{10,2},{2,10},{11,3},{3,11},{12,4},{4,12},... | collective-permute-start | bytes 393224 | tf_op jit(solution)/shard_map/ppermute | solution.py:48
  22.7 4.1 %collective-permute-start.6 = (s32[4,64]{1,0:T(4,128)S(1)}, s32[4,64]{1,0:T(4,128)S(1)}, u32[]{:S(2)}, u32[]{:S(2)}) collective-permute-start(s32[4,64]{1,0:T(4,128)S(1)} %stack.5.near_ids_ref), channel_id=1, source_target_pairs={{0,1},{1,0},{2,3},{3,2},{4,5},{5,4},{6,7},{7,6},{8,9},{9,8},{10,11... | collective-permute-start | bytes 3080 | tf_op jit(solution)/shard_map/ppermute | solution.py:35
  24.2 3.4 %copy-start.1 = (bf16[1,2,1024,1024]{3,2,1,0:T(8,128)(2,1)S(1)}, bf16[1,2,1024,1024]{3,2,1,0:T(8,128)(2,1)}, u32[]{:S(2)}) copy-start(bf16[1,2,1024,1024]{3,2,1,0:T(8,128)(2,1)} %refs_0_.7) | copy-start | bytes 12582916
  24.2 6.8 %copy-start.3 = (bf16[1024,1024]{1,0:T(8,128)(2,1)S(1)}, bf16[1024,1024]{1,0:T(8,128)(2,1)}, u32[]{:S(2)}) copy-start(bf16[1024,1024]{1,0:T(8,128)(2,1)} %w_gate_ref.1) | copy-start | bytes 6291460
  24.2 6.8 %copy-start.10 = (s32[1,64]{1,0:T(1,128)S(1)}, s32[1,64]{1,0:T(1,128)}, u32[]{:S(2)}) copy-start(s32[1,64]{1,0:T(1,128)} %ids_ref.1) | copy-start | bytes 772
  27.6 23.8 %collective-permute-start.16 = (bf16[1,2,1024,1024]{3,2,1,0:T(8,128)(2,1)S(1)}, bf16[1,2,1024,1024]{3,2,1,0:T(8,128)(2,1)S(1)}, u32[]{:S(2)}, u32[]{:S(2)}) collective-permute-start(bf16[1,2,1024,1024]{3,2,1,0:T(8,128)(2,1)S(1)} %copy-done.1), channel_id=1, source_target_pairs={{8,0},{0,8},{9,1},{1,9},{10,2},{2,10},{11,3},{3,11},{12,4},{4,12},... | collective-permute-start | bytes 12582920 | tf_op jit(solution)/shard_map/ppermute | solution.py:48
  27.7 8.7 %collective-permute-start.11 = (bf16[256,512]{1,0:T(8,128)(2,1)S(1)}, bf16[256,512]{1,0:T(8,128)(2,1)S(1)}, u32[]{:S(2)}, u32[]{:S(2)}) collective-permute-start(bf16[256,512]{1,0:T(8,128)(2,1)S(1)} %get-tuple-element.44), channel_id=1, source_target_pairs={{0,1},{1,0},{2,3},{3,2},{4,5},{5,4},{6,7},{7,6},{8,9},{9,8},{10,11... | collective-permute-start | bytes 786440 | tf_op jit(solution)/shard_map/ppermute | solution.py:35
  29.0 22.5 %copy-start.4 = (bf16[1024,1024]{1,0:T(8,128)(2,1)S(1)}, bf16[1024,1024]{1,0:T(8,128)(2,1)}, u32[]{:S(2)}) copy-start(bf16[1024,1024]{1,0:T(8,128)(2,1)} %w_out_ref.1) | copy-start | bytes 6291460
  29.0 22.5 %copy-start.7 = (f32[1024]{0:T(1024)S(1)}, f32[1024]{0:T(1024)}, u32[]{:S(2)}) copy-start(f32[1024]{0:T(1024)} %param.22) | copy-start | bytes 12292
  29.0 22.5 %copy-start.8 = (s32[1,64]{1,0:T(1,128)S(1)}, s32[1,64]{1,0:T(1,128)}, u32[]{:S(2)}) copy-start(s32[1,64]{1,0:T(1,128)} %domain_ref.1) | copy-start | bytes 772
  29.0 8.4 %collective-permute-start.12 = (bf16[256,512]{1,0:T(8,128)(2,1)S(1)}, bf16[256,512]{1,0:T(8,128)(2,1)S(1)}, u32[]{:S(2)}, u32[]{:S(2)}) collective-permute-start(bf16[256,512]{1,0:T(8,128)(2,1)S(1)} %get-tuple-element.45), channel_id=1, source_target_pairs={{0,2},{1,3},{2,0},{3,1},{4,6},{5,7},{6,4},{7,5},{8,10},{9,11},{10,... | collective-permute-start | bytes 786440 | tf_op jit(solution)/shard_map/ppermute | solution.py:35
  37.5 5.0 %collective-permute-start.14 = (bf16[128,512]{1,0:T(8,128)(2,1)S(1)}, bf16[128,512]{1,0:T(8,128)(2,1)S(1)}, u32[]{:S(2)}, u32[]{:S(2)}) collective-permute-start(bf16[128,512]{1,0:T(8,128)(2,1)S(1)} %get-tuple-element.53), channel_id=1, source_target_pairs={{0,1},{1,0},{2,3},{3,2},{4,5},{5,4},{6,7},{7,6},{8,9},{9,8},{10,11... | collective-permute-start | bytes 393224 | tf_op jit(solution)/shard_map/ppermute | solution.py:35
  38.7 5.0 %collective-permute-start.13 = (bf16[128,512]{1,0:T(8,128)(2,1)S(1)}, bf16[128,512]{1,0:T(8,128)(2,1)S(1)}, u32[]{:S(2)}, u32[]{:S(2)}) collective-permute-start(bf16[128,512]{1,0:T(8,128)(2,1)S(1)} %get-tuple-element.49), channel_id=1, source_target_pairs={{0,2},{1,3},{2,0},{3,1},{4,6},{5,7},{6,4},{7,5},{8,10},{9,11},{10,... | collective-permute-start | bytes 393224 | tf_op jit(solution)/shard_map/ppermute | solution.py:35
  43.8 7.7 %collective-permute-start.15 = (bf16[64,1024]{1,0:T(8,128)(2,1)S(1)}, bf16[64,1024]{1,0:T(8,128)(2,1)S(1)}, u32[]{:S(2)}, u32[]{:S(2)}) collective-permute-start(bf16[64,1024]{1,0:T(8,128)(2,1)S(1)} %get-tuple-element.55), channel_id=1, source_target_pairs={{0,4},{1,5},{2,6},{3,7},{4,0},{5,1},{6,2},{7,3},{8,12},{9,13},{10,... | collective-permute-start | bytes 393224 | tf_op jit(solution)/shard_map/ppermute | solution.py:35

commit v6 on v5

--- a/solution.py
+++ b/solution.py
@@ -311,21 +311,24 @@
     all_flips = [tuple(range(at, min(at + users, hist_devices))) for at in range(1, hist_devices, users)]
     fetched = [swapped_by_user(item_table, flips) for flips in all_flips]
 
-    known_ids, id_flips = [stack([item_ids], flops=LOADS_BESIDE)], [0]
-    for bit in reversed(range(bits)):
-        far_ids = swapped(known_ids[-1], 1 << bit)
-        id_flips += [flip + (1 << bit) for flip in id_flips]
-        if bit:
-            known_ids.append(stack([known_ids[-1], far_ids]))
-    near_ids = known_ids[-1]
+    near_ids, id_flips = stack([item_ids], flops=LOADS_BESIDE), [0]
+    far_ids = swapped(near_ids, 1 << (bits - 1))
 
     early = len(all_flips) // 2
     first_pieces = [((0,) * users, 0, None)] + [(flips, 0, None) for flips in all_flips[:early]]
     first_blocks = [item_table] + fetched[:early]
-    w_query, _ = lax.optimization_barrier((w_query, known_ids[1]))
+    id_flips += [flip + (1 << (bits - 1)) for flip in id_flips]
+    near_ids = stack([near_ids, far_ids])
+    w_query, near_ids = lax.optimization_barrier((w_query, near_ids))
     first, masked_values = attend_first(
         first_pieces, first_blocks, shard_rows, history_lengths, w_query, history_keys, history_values
     )
+    for bit in reversed(range(bits - 1)):
+        far_ids = swapped(near_ids, 1 << bit)
+        id_flips += [flip + (1 << bit) for flip in id_flips]
+        if bit:
+            first, far_ids = lax.optimization_barrier((first, far_ids))
+            near_ids = stack([near_ids, far_ids])
     first, *fetched[:early] = lax.optimization_barrier((first, *fetched[:early]))
     first, near_ids, *fetched[early:] = lax.optimization_barrier((first, near_ids, *fetched[early:]))
     next_pieces, next_blocks = [], []

time: 54.5 us -> 52.3 us (0.960)
  starting transfers between devices: 25.1 us -> 23.4 us
    ppermute x8, starting transfers between devices: 14 us -> 12.2 us  [swapped(): return lax.ppermute(value, 'hist', [(i, i ^ flip) for i in range(count)])]
  transfers between devices with their start and end apart: 17 -> 17, of which waited for: 7 -> 6; matrix products, arithmetic and copies ran while one was open for 0% -> 0% of each run, Pallas kernels for 11% -> 12%
where the time goes in v6:
time: 52.3 us; the launch traced here: 52.2 us
  starting transfers between devices  23.4 us (45%)
  waiting for transfers between devices  16.8 us (32%)
  Pallas kernels  9.75 us (19%)
  between operations  1.51 us (3%)
  local copies, waits for them, and re-layouts  0.7 us (1%)
    ppermute x8, waiting for transfers between devices, swapped(): return lax.ppermute(value, 'hist', [(i, i ^ flip) for i in range(count)])  16.8 us
    ppermute x8, starting transfers between devices, swapped(): return lax.ppermute(value, 'hist', [(i, i ^ flip) for i in range(count)])  12.2 us
    ppermute x4, starting transfers between devices, swapped_by_user(): return lax.ppermute(value, ('user', 'hist'), pairs)  10 us
    pallas_call x1, Pallas kernels, finish(): kernel_call(finish_kernel, 'finish', [jax.ShapeDtypeStruct((1, slots, wid...  2.83 us
    pallas_call x1, Pallas kernels, attend_next(): kernel_call(functools.partial(next_kernel, pieces), 'attend_next', [jax.S...  2.51 us
    pallas_call x1, Pallas kernels, attend_first(): kernel_call(functools.partial(first_kernel, pieces), 'attend_first', [jax...  2.48 us
    ppermute x5, starting transfers between devices, from_user(): lax.ppermute(value, 'user', [((i + steps) % count, i) for i in range(coun...  1.15 us
  transfers between devices with their start and end apart: 17, of which 6 were waited for; matrix products, arithmetic and copies ran while one was open for 0% of the time, Pallas kernels for 12%

profile of v6, /device:TPU:0, one launch (start us, length us, event | category | flops | bytes accessed | tf_op | source)
XLA Modules:
  0.0 52.2 jit_solution(17588210638436041920)
XLA Ops:
  0.0 5.1 %collective-permute-start.4 = (bf16[64,1024]{1,0:T(8,128)(2,1)}, bf16[64,1024]{1,0:T(8,128)(2,1)S(1)}, u32[]{:S(2)}, u32[]{:S(2)}) collective-permute-start(bf16[64,1024]{1,0:T(8,128)(2,1)} %refs_0_.6), channel_id=1, source_target_pairs={{0,5},{1,4},{2,7},{3,6},{4,1},{5,0},{6,3},{7,2},{8,14},{9,15},{10,... | collective-permute-start | bytes 393224 | tf_op jit(solution)/shard_map/ppermute | solution.py:43
  5.1 1.5 %collective-permute-start.2 = (bf16[64,1024]{1,0:T(8,128)(2,1)}, bf16[64,1024]{1,0:T(8,128)(2,1)S(1)}, u32[]{:S(2)}, u32[]{:S(2)}) collective-permute-start(bf16[64,1024]{1,0:T(8,128)(2,1)} %refs_0_.6), channel_id=1, source_target_pairs={{0,3},{1,2},{2,1},{3,0},{4,7},{5,6},{6,5},{7,4},{8,12},{9,13},{10,... | collective-permute-start | bytes 393224 | tf_op jit(solution)/shard_map/ppermute | solution.py:43
  6.6 1.5 %collective-permute-start.1 = (bf16[64,1024]{1,0:T(8,128)(2,1)}, bf16[64,1024]{1,0:T(8,128)(2,1)S(1)}, u32[]{:S(2)}, u32[]{:S(2)}) collective-permute-start(bf16[64,1024]{1,0:T(8,128)(2,1)} %refs_0_.6), channel_id=1, source_target_pairs={{0,1},{1,0},{2,3},{3,2},{4,5},{5,4},{6,7},{7,6},{8,10},{9,11},{10,... | collective-permute-start | bytes 393224 | tf_op jit(solution)/shard_map/ppermute | solution.py:43
  8.1 1.9 %collective-permute-start.5 = (bf16[64,1024]{1,0:T(8,128)(2,1)}, bf16[64,1024]{1,0:T(8,128)(2,1)S(1)}, u32[]{:S(2)}, u32[]{:S(2)}) collective-permute-start(bf16[64,1024]{1,0:T(8,128)(2,1)} %refs_0_.6), channel_id=1, source_target_pairs={{0,7},{1,6},{2,5},{3,4},{4,3},{5,2},{6,1},{7,0},{16,23},{17,22},{1... | collective-permute-start | bytes 393224 | tf_op jit(solution)/shard_map/ppermute | solution.py:43
  10.0 0.0 copy-start.9
  10.0 0.6 %copy-done.9 = s32[1,64]{1,0:T(1,128)S(1)} copy-done((s32[1,64]{1,0:T(1,128)S(1)}, s32[1,64]{1,0:T(1,128)}, u32[]{:S(2)}) %copy-start.9) | copy-done | bytes 280
  10.7 1.8 %collective-permute-start = (s32[1,64]{1,0:T(1,128)S(1)}, s32[1,64]{1,0:T(1,128)S(1)}, u32[]{:S(2)}, u32[]{:S(2)}) collective-permute-start(s32[1,64]{1,0:T(1,128)S(1)} %stack.3.refs_0_), channel_id=1, source_target_pairs={{0,4},{1,5},{2,6},{3,7},{4,0},{5,1},{6,2},{7,3},{8,12},{9,13},{10,... | collective-permute-start | bytes 776 | tf_op jit(solution)/shard_map/ppermute | solution.py:35
  13.2 1.9 %collective-permute-done.refs_1_ = s32[1,64]{1,0:T(1,128)S(1)} collective-permute-done((s32[1,64]{1,0:T(1,128)S(1)}, s32[1,64]{1,0:T(1,128)S(1)}, u32[]{:S(2)}, u32[]{:S(2)}) %collective-permute-start) | collective-permute-done | bytes 288 | tf_op jit(solution)/shard_map/ppermute | solution.py:35
  15.1 2.3 %collective-permute-start.3 = (s32[2,64]{1,0:T(2,128)S(1)}, s32[2,64]{1,0:T(2,128)S(1)}, u32[]{:S(2)}, u32[]{:S(2)}) collective-permute-start(s32[2,64]{1,0:T(2,128)S(1)} %stack.4.refs_0_), channel_id=1, source_target_pairs={{0,2},{1,3},{2,0},{3,1},{4,6},{5,7},{6,4},{7,5},{8,10},{9,11},{10,... | collective-permute-start | bytes 1544 | tf_op jit(solution)/shard_map/ppermute | solution.py:35
  17.5 0.0 collective-permute-done.2.refs_2_
  17.5 0.0 collective-permute-done.1.refs_1_
  17.5 0.0 copy-done
  17.5 0.0 copy-done.2
  17.5 2.5 %attend_first.1 = (bf16[192,1024]{1,0:T(8,128)(2,1)S(1)}, bf16[512,1024]{1,0:T(8,128)(2,1)S(1)}) custom-call(s32[1]{0:T(128)S(6)} %copy.14.length_ref, bf16[1024,1024]{1,0:T(8,128)(2,1)S(1)} %copy-done, bf16[1,512,1024]{2,1,0:T(8,128)(2,1)S(1)} %copy-done.2, bf16[1,512,1024]{2,1,0:T(8,128)(2,1)S(1)} %copy-done.5, bf16[64,1024]{1,0:T(8,128)(2,1)S(1)} %copy-done.6, ...), custom_call_target="tpu_custom_call" | custom-call | flops 805306368 | tf_op jit(solution)/shard_map/attend_first/pallas_call | solution.py:157
  20.0 0.0 collective-permute-done.3.refs_1_
  20.0 0.0 collective-permute-done.4.refs_2_.refs_5_
  20.0 0.0 collective-permute-done.5.refs_4_.refs_7_
  20.0 0.1 collective-permute-start.9
  20.1 0.5 collective-permute-start.10
  20.6 0.1 collective-permute-start.7
  20.7 0.4 collective-permute-start.8
  21.1 1.5 %collective-permute-start.6 = (s32[4,64]{1,0:T(4,128)S(1)}, s32[4,64]{1,0:T(4,128)S(1)}, u32[]{:S(2)}, u32[]{:S(2)}) collective-permute-start(s32[4,64]{1,0:T(4,128)S(1)} %stack.5.near_ids_ref), channel_id=1, source_target_pairs={{0,1},{1,0},{2,3},{3,2},{4,5},{5,4},{6,7},{7,6},{8,9},{9,8},{10,11... | collective-permute-start | bytes 3080 | tf_op jit(solution)/shard_map/ppermute | solution.py:35
  22.6 0.0 collective-permute-done.9.refs_3_.refs_6_
  22.6 0.0 collective-permute-done.10.refs_5_.refs_8_
  22.6 0.0 collective-permute-done.7.refs_0_.refs_3_
  22.7 0.0 collective-permute-done.8.refs_1_.refs_4_
  22.7 0.0 copy-start.1
  22.7 0.0 copy-start.3
  22.7 0.0 copy-start.10
  22.7 2.5 %attend_next.1.refs_1_ = bf16[320,1024]{1,0:T(8,128)(2,1)S(1)} custom-call(bf16[1024,1024]{1,0:T(8,128)(2,1)S(1)} %copy-done, bf16[1,512,1024]{2,1,0:T(8,128)(2,1)S(1)} %copy-done.2, bf16[512,1024]{1,0:T(8,128)(2,1)S(1)} %get-tuple-element.43.values_ref, bf16[64,1024]{1,0:T(8,128)(2,1)S(1)} %collective-permute-done.7.refs_0_.refs_3_, ...), custom_call_target="tpu_custom_call" | custom-call | flops 1342177280 | tf_op jit(solution)/shard_map/attend_next/pallas_call | solution.py:168
  25.2 0.0 collective-permute-done.6.far_ids_ref
  25.2 0.9 %place.1 = (bf16[256,512]{1,0:T(8,128)(2,1)S(1)}, bf16[256,512]{1,0:T(8,128)(2,1)S(1)}, bf16[256,512]{1,0:T(8,128)(2,1)S(1)}, bf16[256,512]{1,0:T(8,128)(2,1)S(1)}) custom-call(s32[4,64]{1,0:T(4,128)S(1)} %stack.5.near_ids_ref, s32[4,64]{1,0:T(4,128)S(1)} %collective-permute-done.6.far_ids_ref, bf16[192,1024]{1,0:T(8,128)(2,1)S(1)} %get-tuple-element.42.refs_0_, ...), custom_call_target="tpu_custom_call" | custom-call | flops 536870912 | tf_op jit(solution)/shard_map/place/pallas_call | solution.py:200
  26.1 0.1 collective-permute-start.16
  26.2 1.3 %collective-permute-start.11 = (bf16[256,512]{1,0:T(8,128)(2,1)S(1)}, bf16[256,512]{1,0:T(8,128)(2,1)S(1)}, u32[]{:S(2)}, u32[]{:S(2)}) collective-permute-start(bf16[256,512]{1,0:T(8,128)(2,1)S(1)} %get-tuple-element.50), channel_id=1, source_target_pairs={{0,1},{1,0},{2,3},{3,2},{4,5},{5,4},{6,7},{7,6},{8,9},{9,8},{10,11... | collective-permute-start | bytes 786440 | tf_op jit(solution)/shard_map/ppermute | solution.py:35
  27.5 1.0 %collective-permute-start.12 = (bf16[256,512]{1,0:T(8,128)(2,1)S(1)}, bf16[256,512]{1,0:T(8,128)(2,1)S(1)}, u32[]{:S(2)}, u32[]{:S(2)}) collective-permute-start(bf16[256,512]{1,0:T(8,128)(2,1)S(1)} %get-tuple-element.51), channel_id=1, source_target_pairs={{0,2},{1,3},{2,0},{3,1},{4,6},{5,7},{6,4},{7,5},{8,10},{9,11},{10,... | collective-permute-start | bytes 786440 | tf_op jit(solution)/shard_map/ppermute | solution.py:35
  28.5 0.9 %prepare.1 = (f32[64,1024]{1,0:T(8,128)S(1)}, f32[64,1024]{1,0:T(8,128)S(1)}) custom-call(bf16[256,512]{1,0:T(8,128)(2,1)S(1)} %get-tuple-element.49.after_ref.refs_0_, s32[1,64]{1,0:T(1,128)S(1)} %copy-done.10, bf16[1024,1024]{1,0:T(8,128)(2,1)S(1)} %copy-done.3, bf16[64,1024]{1,0:T(8,128)(2,1)S(1)} %copy-done.6, ...), custom_call_target="tpu_custom_call" | custom-call | flops 201326592 | tf_op jit(solution)/shard_map/prepare/pallas_call | solution.py:245
  29.4 5.5 %collective-permute-done.11.refs_1_ = bf16[256,512]{1,0:T(8,128)(2,1)S(1)} collective-permute-done((bf16[256,512]{1,0:T(8,128)(2,1)S(1)}, bf16[256,512]{1,0:T(8,128)(2,1)S(1)}, u32[]{:S(2)}, u32[]{:S(2)}) %collective-permute-start.11) | collective-permute-done | bytes 262176 | tf_op jit(solution)/shard_map/ppermute | solution.py:35
  34.9 0.7 %collective-permute-done.12.refs_1_ = bf16[256,512]{1,0:T(8,128)(2,1)S(1)} collective-permute-done((bf16[256,512]{1,0:T(8,128)(2,1)S(1)}, bf16[256,512]{1,0:T(8,128)(2,1)S(1)}, u32[]{:S(2)}, u32[]{:S(2)}) %collective-permute-start.12) | collective-permute-done | bytes 262176 | tf_op jit(solution)/shard_map/ppermute | solution.py:35
  35.6 0.1 fold.4
  35.7 1.1 %collective-permute-start.14 = (bf16[128,512]{1,0:T(8,128)(2,1)S(1)}, bf16[128,512]{1,0:T(8,128)(2,1)S(1)}, u32[]{:S(2)}, u32[]{:S(2)}) collective-permute-start(bf16[128,512]{1,0:T(8,128)(2,1)S(1)} %get-tuple-element.59), channel_id=1, source_target_pairs={{0,1},{1,0},{2,3},{3,2},{4,5},{5,4},{6,7},{7,6},{8,9},{9,8},{10,11... | collective-permute-start | bytes 393224 | tf_op jit(solution)/shard_map/ppermute | solution.py:35
  36.8 0.1 fold.3
  36.8 1.1 %collective-permute-start.13 = (bf16[128,512]{1,0:T(8,128)(2,1)S(1)}, bf16[128,512]{1,0:T(8,128)(2,1)S(1)}, u32[]{:S(2)}, u32[]{:S(2)}) collective-permute-start(bf16[128,512]{1,0:T(8,128)(2,1)S(1)} %get-tuple-element.55), channel_id=1, source_target_pairs={{0,2},{1,3},{2,0},{3,1},{4,6},{5,7},{6,4},{7,5},{8,10},{9,11},{10,... | collective-permute-start | bytes 393224 | tf_op jit(solution)/shard_map/ppermute | solution.py:35
  37.9 2.8 %collective-permute-done.14.refs_3_ = bf16[128,512]{1,0:T(8,128)(2,1)S(1)} collective-permute-done((bf16[128,512]{1,0:T(8,128)(2,1)S(1)}, bf16[128,512]{1,0:T(8,128)(2,1)S(1)}, u32[]{:S(2)}, u32[]{:S(2)}) %collective-permute-start.14) | collective-permute-done | bytes 131104 | tf_op jit(solution)/shard_map/ppermute | solution.py:35
  40.7 1.2 %collective-permute-done.13.refs_1_ = bf16[128,512]{1,0:T(8,128)(2,1)S(1)} collective-permute-done((bf16[128,512]{1,0:T(8,128)(2,1)S(1)}, bf16[128,512]{1,0:T(8,128)(2,1)S(1)}, u32[]{:S(2)}, u32[]{:S(2)}) %collective-permute-start.13) | collective-permute-done | bytes 131104 | tf_op jit(solution)/shard_map/ppermute | solution.py:35
  41.9 2.1 %collective-permute-start.15 = (bf16[64,1024]{1,0:T(8,128)(2,1)S(1)}, bf16[64,1024]{1,0:T(8,128)(2,1)S(1)}, u32[]{:S(2)}, u32[]{:S(2)}) collective-permute-start(bf16[64,1024]{1,0:T(8,128)(2,1)S(1)} %get-tuple-element.61), channel_id=1, source_target_pairs={{0,4},{1,5},{2,6},{3,7},{4,0},{5,1},{6,2},{7,3},{8,12},{9,13},{10,... | collective-permute-start | bytes 393224 | tf_op jit(solution)/shard_map/ppermute | solution.py:35
  44.7 4.6 %collective-permute-done.15.come_ref = bf16[64,1024]{1,0:T(8,128)(2,1)S(1)} collective-permute-done((bf16[64,1024]{1,0:T(8,128)(2,1)S(1)}, bf16[64,1024]{1,0:T(8,128)(2,1)S(1)}, u32[]{:S(2)}, u32[]{:S(2)}) %collective-permute-start.15) | collective-permute-done | bytes 131104 | tf_op jit(solution)/shard_map/ppermute | solution.py:35
  49.3 0.0 collective-permute-done.16.refs_1_
  49.3 2.8 %finish.1 = bf16[1,64,1024]{2,1,0:T(8,128)(2,1)} custom-call(f32[64,1024]{1,0:T(8,128)S(1)} %get-tuple-element.60.kept_ref, bf16[64,1024]{1,0:T(8,128)(2,1)S(1)} %collective-permute-done.15.come_ref, f32[64,1024]{1,0:T(8,128)S(1)} %get-tuple-element.62.embed_ref, f32[64,1024]{1,0:T(8,128)S(1)} %get-tuple-element.63.gating_ref, f32[1,1024]{1,0:T(1,128)S(1)} %bitcast.1, ...), custom_call_target="tpu_custom_call" | custom-call | flops 671088640 | tf_op jit(solution)/shard_map/finish/pallas_call | solution.py:282
  (19 shorter events, 0.1 us)
Async XLA Ops:
  0.0 17.5 %copy-start.6 = (bf16[64,1024]{1,0:T(8,128)(2,1)S(1)}, bf16[64,1024]{1,0:T(8,128)(2,1)}, u32[]{:S(2)}) copy-start(bf16[64,1024]{1,0:T(8,128)(2,1)} %refs_0_.6) | copy-start | bytes 393220
  0.0 17.5 %copy-start = (bf16[1024,1024]{1,0:T(8,128)(2,1)S(1)}, bf16[1024,1024]{1,0:T(8,128)(2,1)}, u32[]{:S(2)}) copy-start(bf16[1024,1024]{1,0:T(8,128)(2,1)} %w_query_ref.1) | copy-start | bytes 6291460
  0.0 17.5 %copy-start.2 = (bf16[1,512,1024]{2,1,0:T(8,128)(2,1)S(1)}, bf16[1,512,1024]{2,1,0:T(8,128)(2,1)}, u32[]{:S(2)}) copy-start(bf16[1,512,1024]{2,1,0:T(8,128)(2,1)} %keys_ref.3) | copy-start | bytes 3145732
  0.0 17.5 %copy-start.5 = (bf16[1,512,1024]{2,1,0:T(8,128)(2,1)S(1)}, bf16[1,512,1024]{2,1,0:T(8,128)(2,1)}, u32[]{:S(2)}) copy-start(bf16[1,512,1024]{2,1,0:T(8,128)(2,1)} %values_ref.1) | copy-start | bytes 3145732
  0.0 20.0 %collective-permute-start.4 = (bf16[64,1024]{1,0:T(8,128)(2,1)}, bf16[64,1024]{1,0:T(8,128)(2,1)S(1)}, u32[]{:S(2)}, u32[]{:S(2)}) collective-permute-start(bf16[64,1024]{1,0:T(8,128)(2,1)} %refs_0_.6), channel_id=1, source_target_pairs={{0,5},{1,4},{2,7},{3,6},{4,1},{5,0},{6,3},{7,2},{8,14},{9,15},{10,... | collective-permute-start | bytes 393224 | tf_op jit(solution)/shard_map/ppermute | solution.py:43
  5.1 12.4 %collective-permute-start.2 = (bf16[64,1024]{1,0:T(8,128)(2,1)}, bf16[64,1024]{1,0:T(8,128)(2,1)S(1)}, u32[]{:S(2)}, u32[]{:S(2)}) collective-permute-start(bf16[64,1024]{1,0:T(8,128)(2,1)} %refs_0_.6), channel_id=1, source_target_pairs={{0,3},{1,2},{2,1},{3,0},{4,7},{5,6},{6,5},{7,4},{8,12},{9,13},{10,... | collective-permute-start | bytes 393224 | tf_op jit(solution)/shard_map/ppermute | solution.py:43
  6.6 10.9 %collective-permute-start.1 = (bf16[64,1024]{1,0:T(8,128)(2,1)}, bf16[64,1024]{1,0:T(8,128)(2,1)S(1)}, u32[]{:S(2)}, u32[]{:S(2)}) collective-permute-start(bf16[64,1024]{1,0:T(8,128)(2,1)} %refs_0_.6), channel_id=1, source_target_pairs={{0,1},{1,0},{2,3},{3,2},{4,5},{5,4},{6,7},{7,6},{8,10},{9,11},{10,... | collective-permute-start | bytes 393224 | tf_op jit(solution)/shard_map/ppermute | solution.py:43
  8.1 11.9 %collective-permute-start.5 = (bf16[64,1024]{1,0:T(8,128)(2,1)}, bf16[64,1024]{1,0:T(8,128)(2,1)S(1)}, u32[]{:S(2)}, u32[]{:S(2)}) collective-permute-start(bf16[64,1024]{1,0:T(8,128)(2,1)} %refs_0_.6), channel_id=1, source_target_pairs={{0,7},{1,6},{2,5},{3,4},{4,3},{5,2},{6,1},{7,0},{16,23},{17,22},{1... | collective-permute-start | bytes 393224 | tf_op jit(solution)/shard_map/ppermute | solution.py:43
  10.0 0.7 %copy-start.9 = (s32[1,64]{1,0:T(1,128)S(1)}, s32[1,64]{1,0:T(1,128)}, u32[]{:S(2)}) copy-start(s32[1,64]{1,0:T(1,128)} %ids_ref.1) | copy-start | bytes 772
  10.7 4.4 %collective-permute-start = (s32[1,64]{1,0:T(1,128)S(1)}, s32[1,64]{1,0:T(1,128)S(1)}, u32[]{:S(2)}, u32[]{:S(2)}) collective-permute-start(s32[1,64]{1,0:T(1,128)S(1)} %stack.3.refs_0_), channel_id=1, source_target_pairs={{0,4},{1,5},{2,6},{3,7},{4,0},{5,1},{6,2},{7,3},{8,12},{9,13},{10,... | collective-permute-start | bytes 776 | tf_op jit(solution)/shard_map/ppermute | solution.py:35
  15.1 4.9 %collective-permute-start.3 = (s32[2,64]{1,0:T(2,128)S(1)}, s32[2,64]{1,0:T(2,128)S(1)}, u32[]{:S(2)}, u32[]{:S(2)}) collective-permute-start(s32[2,64]{1,0:T(2,128)S(1)} %stack.4.refs_0_), channel_id=1, source_target_pairs={{0,2},{1,3},{2,0},{3,1},{4,6},{5,7},{6,4},{7,5},{8,10},{9,11},{10,... | collective-permute-start | bytes 1544 | tf_op jit(solution)/shard_map/ppermute | solution.py:35
  20.0 2.6 %collective-permute-start.9 = (bf16[64,1024]{1,0:T(8,128)(2,1)S(1)}, bf16[64,1024]{1,0:T(8,128)(2,1)S(1)}, u32[]{:S(2)}, u32[]{:S(2)}) collective-permute-start(bf16[64,1024]{1,0:T(8,128)(2,1)S(1)} %collective-permute-done.4.refs_2_.refs_5_), channel_id=1, source_target_pairs={{8,0},{0,8},{9,1},{1,9},{10,2},{2,10},{11,3},{3,11},{12,4},{4,12},... | collective-permute-start | bytes 393224 | tf_op jit(solution)/shard_map/ppermute | solution.py:48
  20.1 2.5 %collective-permute-start.10 = (bf16[64,1024]{1,0:T(8,128)(2,1)S(1)}, bf16[64,1024]{1,0:T(8,128)(2,1)S(1)}, u32[]{:S(2)}, u32[]{:S(2)}) collective-permute-start(bf16[64,1024]{1,0:T(8,128)(2,1)S(1)} %collective-permute-done.5.refs_4_.refs_7_), channel_id=1, source_target_pairs={{8,0},{0,8},{9,1},{1,9},{10,2},{2,10},{11,3},{3,11},{12,4},{4,12},... | collective-permute-start | bytes 393224 | tf_op jit(solution)/shard_map/ppermute | solution.py:48
  20.6 2.0 %collective-permute-start.7 = (bf16[64,1024]{1,0:T(8,128)(2,1)S(1)}, bf16[64,1024]{1,0:T(8,128)(2,1)S(1)}, u32[]{:S(2)}, u32[]{:S(2)}) collective-permute-start(bf16[64,1024]{1,0:T(8,128)(2,1)S(1)} %collective-permute-done.1.refs_1_), channel_id=1, source_target_pairs={{8,0},{0,8},{9,1},{1,9},{10,2},{2,10},{11,3},{3,11},{12,4},{4,12},... | collective-permute-start | bytes 393224 | tf_op jit(solution)/shard_map/ppermute | solution.py:48
  20.7 2.0 %collective-permute-start.8 = (bf16[64,1024]{1,0:T(8,128)(2,1)S(1)}, bf16[64,1024]{1,0:T(8,128)(2,1)S(1)}, u32[]{:S(2)}, u32[]{:S(2)}) collective-permute-start(bf16[64,1024]{1,0:T(8,128)(2,1)S(1)} %collective-permute-done.2.refs_2_), channel_id=1, source_target_pairs={{8,0},{0,8},{9,1},{1,9},{10,2},{2,10},{11,3},{3,11},{12,4},{4,12},... | collective-permute-start | bytes 393224 | tf_op jit(solution)/shard_map/ppermute | solution.py:48
  21.1 4.1 %collective-permute-start.6 = (s32[4,64]{1,0:T(4,128)S(1)}, s32[4,64]{1,0:T(4,128)S(1)}, u32[]{:S(2)}, u32[]{:S(2)}) collective-permute-start(s32[4,64]{1,0:T(4,128)S(1)} %stack.5.near_ids_ref), channel_id=1, source_target_pairs={{0,1},{1,0},{2,3},{3,2},{4,5},{5,4},{6,7},{7,6},{8,9},{9,8},{10,11... | collective-permute-start | bytes 3080 | tf_op jit(solution)/shard_map/ppermute | solution.py:35
  22.7 3.4 %copy-start.1 = (bf16[1,2,1024,1024]{3,2,1,0:T(8,128)(2,1)S(1)}, bf16[1,2,1024,1024]{3,2,1,0:T(8,128)(2,1)}, u32[]{:S(2)}) copy-start(bf16[1,2,1024,1024]{3,2,1,0:T(8,128)(2,1)} %refs_0_.7) | copy-start | bytes 12582916
  22.7 5.8 %copy-start.3 = (bf16[1024,1024]{1,0:T(8,128)(2,1)S(1)}, bf16[1024,1024]{1,0:T(8,128)(2,1)}, u32[]{:S(2)}) copy-start(bf16[1024,1024]{1,0:T(8,128)(2,1)} %w_gate_ref.1) | copy-start | bytes 6291460
  22.7 5.8 %copy-start.10 = (s32[1,64]{1,0:T(1,128)S(1)}, s32[1,64]{1,0:T(1,128)}, u32[]{:S(2)}) copy-start(s32[1,64]{1,0:T(1,128)} %ids_ref.1) | copy-start | bytes 772
  26.1 23.2 %collective-permute-start.16 = (bf16[1,2,1024,1024]{3,2,1,0:T(8,128)(2,1)S(1)}, bf16[1,2,1024,1024]{3,2,1,0:T(8,128)(2,1)S(1)}, u32[]{:S(2)}, u32[]{:S(2)}) collective-permute-start(bf16[1,2,1024,1024]{3,2,1,0:T(8,128)(2,1)S(1)} %copy-done.1), channel_id=1, source_target_pairs={{8,0},{0,8},{9,1},{1,9},{10,2},{2,10},{11,3},{3,11},{12,4},{4,12},... | collective-permute-start | bytes 12582920 | tf_op jit(solution)/shard_map/ppermute | solution.py:48
  26.2 8.7 %collective-permute-start.11 = (bf16[256,512]{1,0:T(8,128)(2,1)S(1)}, bf16[256,512]{1,0:T(8,128)(2,1)S(1)}, u32[]{:S(2)}, u32[]{:S(2)}) collective-permute-start(bf16[256,512]{1,0:T(8,128)(2,1)S(1)} %get-tuple-element.50), channel_id=1, source_target_pairs={{0,1},{1,0},{2,3},{3,2},{4,5},{5,4},{6,7},{7,6},{8,9},{9,8},{10,11... | collective-permute-start | bytes 786440 | tf_op jit(solution)/shard_map/ppermute | solution.py:35
  27.4 21.9 %copy-start.4 = (bf16[1024,1024]{1,0:T(8,128)(2,1)S(1)}, bf16[1024,1024]{1,0:T(8,128)(2,1)}, u32[]{:S(2)}) copy-start(bf16[1024,1024]{1,0:T(8,128)(2,1)} %w_out_ref.1) | copy-start | bytes 6291460
  27.5 21.9 %copy-start.7 = (f32[1024]{0:T(1024)S(1)}, f32[1024]{0:T(1024)}, u32[]{:S(2)}) copy-start(f32[1024]{0:T(1024)} %param.22) | copy-start | bytes 12292
  27.5 21.9 %copy-start.8 = (s32[1,64]{1,0:T(1,128)S(1)}, s32[1,64]{1,0:T(1,128)}, u32[]{:S(2)}) copy-start(s32[1,64]{1,0:T(1,128)} %domain_ref.1) | copy-start | bytes 772
  27.5 8.2 %collective-permute-start.12 = (bf16[256,512]{1,0:T(8,128)(2,1)S(1)}, bf16[256,512]{1,0:T(8,128)(2,1)S(1)}, u32[]{:S(2)}, u32[]{:S(2)}) collective-permute-start(bf16[256,512]{1,0:T(8,128)(2,1)S(1)} %get-tuple-element.51), channel_id=1, source_target_pairs={{0,2},{1,3},{2,0},{3,1},{4,6},{5,7},{6,4},{7,5},{8,10},{9,11},{10,... | collective-permute-start | bytes 786440 | tf_op jit(solution)/shard_map/ppermute | solution.py:35
  35.7 5.0 %collective-permute-start.14 = (bf16[128,512]{1,0:T(8,128)(2,1)S(1)}, bf16[128,512]{1,0:T(8,128)(2,1)S(1)}, u32[]{:S(2)}, u32[]{:S(2)}) collective-permute-start(bf16[128,512]{1,0:T(8,128)(2,1)S(1)} %get-tuple-element.59), channel_id=1, source_target_pairs={{0,1},{1,0},{2,3},{3,2},{4,5},{5,4},{6,7},{7,6},{8,9},{9,8},{10,11... | collective-permute-start | bytes 393224 | tf_op jit(solution)/shard_map/ppermute | solution.py:35
  36.8 5.0 %collective-permute-start.13 = (bf16[128,512]{1,0:T(8,128)(2,1)S(1)}, bf16[128,512]{1,0:T(8,128)(2,1)S(1)}, u32[]{:S(2)}, u32[]{:S(2)}) collective-permute-start(bf16[128,512]{1,0:T(8,128)(2,1)S(1)} %get-tuple-element.55), channel_id=1, source_target_pairs={{0,2},{1,3},{2,0},{3,1},{4,6},{5,7},{6,4},{7,5},{8,10},{9,11},{10,... | collective-permute-start | bytes 393224 | tf_op jit(solution)/shard_map/ppermute | solution.py:35
  41.9 7.4 %collective-permute-start.15 = (bf16[64,1024]{1,0:T(8,128)(2,1)S(1)}, bf16[64,1024]{1,0:T(8,128)(2,1)S(1)}, u32[]{:S(2)}, u32[]{:S(2)}) collective-permute-start(bf16[64,1024]{1,0:T(8,128)(2,1)S(1)} %get-tuple-element.61), channel_id=1, source_target_pairs={{0,4},{1,5},{2,6},{3,7},{4,0},{5,1},{6,2},{7,3},{8,12},{9,13},{10,... | collective-permute-start | bytes 393224 | tf_op jit(solution)/shard_map/ppermute | solution.py:35

commit v7 on v6

--- a/solution.py
+++ b/solution.py
@@ -308,15 +308,20 @@
     bits = hist_devices.bit_length() - 1
     others = range(1, users)
 
-    all_flips = [tuple(range(at, min(at + users, hist_devices))) for at in range(1, hist_devices, users)]
-    fetched = [swapped_by_user(item_table, flips) for flips in all_flips]
+    shared = hist_devices // 4
+    far = list(range(hist_devices - 1, hist_devices // 2 - 1, -1))
+    near = [flip for flip in range(1, hist_devices // 2) if flip != shared]
+    far_flips = [tuple(far[at : at + users][:: (-1) ** (at // users)]) for at in range(0, len(far), users)]
+    near_flips = [tuple(near[at : at + users]) for at in range(0, len(near), users)]
+    far_shards = [swapped_by_user(item_table, flips) for flips in far_flips]
+    near_shards = [swapped_by_user(item_table, flips) for flips in near_flips]
+    shared_shard = swapped(item_table, shared)
 
     near_ids, id_flips = stack([item_ids], flops=LOADS_BESIDE), [0]
     far_ids = swapped(near_ids, 1 << (bits - 1))
 
-    early = len(all_flips) // 2
-    first_pieces = [((0,) * users, 0, None)] + [(flips, 0, None) for flips in all_flips[:early]]
-    first_blocks = [item_table] + fetched[:early]
+    first_pieces = [((flip,) * users, 0, None) for flip in (0, shared)] + [(flips, 0, None) for flips in near_flips]
+    first_blocks = [item_table, shared_shard] + near_shards
     id_flips += [flip + (1 << (bits - 1)) for flip in id_flips]
     near_ids = stack([near_ids, far_ids])
     w_query, near_ids = lax.optimization_barrier((w_query, near_ids))
@@ -329,13 +334,13 @@
         if bit:
             first, far_ids = lax.optimization_barrier((first, far_ids))
             near_ids = stack([near_ids, far_ids])
-    first, *fetched[:early] = lax.optimization_barrier((first, *fetched[:early]))
-    first, near_ids, *fetched[early:] = lax.optimization_barrier((first, near_ids, *fetched[early:]))
+    first, *near_shards = lax.optimization_barrier((first, *near_shards))
+    first, near_ids, *far_shards = lax.optimization_barrier((first, near_ids, *far_shards))
     next_pieces, next_blocks = [], []
-    for at, (flips, block) in enumerate(zip(all_flips, fetched)):
+    for flips, block in zip(near_flips + far_flips, near_shards + far_shards):
         arrivals = [block] + [from_user(block, steps) for steps in others]
         found = [(flips, steps, None) for steps in range(users)]
-        if at < early:
+        if flips in near_flips:
             found = found[1:]
         elif len(flips) < users:
             found = [(flips, 0, core) for core in range(len(flips))]

time: 52.3 us -> 51.9 us (level)
  starting transfers between devices: 23.4 us -> 17.8 us
  waiting for transfers between devices: 16.8 us -> 22 us
    ppermute x8 -> x9, waiting for transfers between devices: 16.8 us -> 22 us  [swapped(): return lax.ppermute(value, 'hist', [(i, i ^ flip) for i in range(count)])]
    ppermute x4 -> x3, starting transfers between devices: 10 us -> 7.28 us  [swapped_by_user(): return lax.ppermute(value, ('user', 'hist'), pairs)]
    ppermute x8 -> x9, starting transfers between devices: 12.2 us -> 9.67 us  [swapped(): return lax.ppermute(value, 'hist', [(i, i ^ flip) for i in range(count)])]
    ppermute x5 -> x4, starting transfers between devices: 1.15 us -> 0.87 us  [from_user(): lax.ppermute(value, 'user', [((i + steps) % count, i) for i in range(coun...]
  transfers between devices with their start and end apart: 17 -> 16, of which waited for: 6 -> 7; matrix products, arithmetic and copies ran while one was open for 0% -> 0% of each run, Pallas kernels for 12% -> 12%
where the time goes in v7:
time: 51.9 us; the launch traced here: 51.7 us
  waiting for transfers between devices  22 us (42%)
  starting transfers between devices  17.8 us (34%)
  Pallas kernels  9.73 us (19%)
  between operations  1.47 us (3%)
  local copies, waits for them, and re-layouts  0.7 us (1%)
    ppermute x9, waiting for transfers between devices, swapped(): return lax.ppermute(value, 'hist', [(i, i ^ flip) for i in range(count)])  22 us
    ppermute x9, starting transfers between devices, swapped(): return lax.ppermute(value, 'hist', [(i, i ^ flip) for i in range(count)])  9.67 us
    ppermute x3, starting transfers between devices, swapped_by_user(): return lax.ppermute(value, ('user', 'hist'), pairs)  7.28 us
    pallas_call x1, Pallas kernels, finish(): kernel_call(finish_kernel, 'finish', [jax.ShapeDtypeStruct((1, slots, wid...  2.83 us
    pallas_call x1, Pallas kernels, attend_next(): kernel_call(functools.partial(next_kernel, pieces), 'attend_next', [jax.S...  2.5 us
    pallas_call x1, Pallas kernels, attend_first(): kernel_call(functools.partial(first_kernel, pieces), 'attend_first', [jax...  2.48 us
  transfers between devices with their start and end apart: 16, of which 7 were waited for; matrix products, arithmetic and copies ran while one was open for 0% of the time, Pallas kernels for 12%

profile of v7, /device:TPU:0, one launch (start us, length us, event | category | flops | bytes accessed | tf_op | source)
XLA Modules:
  0.0 51.7 jit_solution(17381964000960466343)
XLA Ops:
  0.0 6.1 %collective-permute-start.4 = (bf16[64,1024]{1,0:T(8,128)(2,1)}, bf16[64,1024]{1,0:T(8,128)(2,1)S(1)}, u32[]{:S(2)}, u32[]{:S(2)}) collective-permute-start(bf16[64,1024]{1,0:T(8,128)(2,1)} %refs_0_.6), channel_id=1, source_target_pairs={{0,7},{1,6},{2,5},{3,4},{4,3},{5,2},{6,1},{7,0},{8,14},{9,15},{10,... | collective-permute-start | bytes 393224 | tf_op jit(solution)/shard_map/ppermute | solution.py:43
  6.1 0.5 collective-permute-start.2
  6.6 0.0 collective-permute-start.1
  6.6 0.7 %collective-permute-start.5 = (bf16[64,1024]{1,0:T(8,128)(2,1)}, bf16[64,1024]{1,0:T(8,128)(2,1)S(1)}, u32[]{:S(2)}, u32[]{:S(2)}) collective-permute-start(bf16[64,1024]{1,0:T(8,128)(2,1)} %refs_0_.6), channel_id=1, source_target_pairs={{0,4},{1,5},{2,6},{3,7},{4,0},{5,1},{6,2},{7,3},{8,13},{9,12},{10,... | collective-permute-start | bytes 393224 | tf_op jit(solution)/shard_map/ppermute | solution.py:43
  7.3 0.7 %copy-done.8 = s32[1,64]{1,0:T(1,128)S(1)} copy-done((s32[1,64]{1,0:T(1,128)S(1)}, s32[1,64]{1,0:T(1,128)}, u32[]{:S(2)}) %copy-start.8) | copy-done | bytes 280
  8.0 2.2 %collective-permute-start = (s32[1,64]{1,0:T(1,128)S(1)}, s32[1,64]{1,0:T(1,128)S(1)}, u32[]{:S(2)}, u32[]{:S(2)}) collective-permute-start(s32[1,64]{1,0:T(1,128)S(1)} %stack.3.refs_0_), channel_id=1, source_target_pairs={{0,4},{1,5},{2,6},{3,7},{4,0},{5,1},{6,2},{7,3},{8,12},{9,13},{10,... | collective-permute-start | bytes 776 | tf_op jit(solution)/shard_map/ppermute | solution.py:35
  10.8 5.8 %collective-permute-done.refs_1_ = s32[1,64]{1,0:T(1,128)S(1)} collective-permute-done((s32[1,64]{1,0:T(1,128)S(1)}, s32[1,64]{1,0:T(1,128)S(1)}, u32[]{:S(2)}, u32[]{:S(2)}) %collective-permute-start) | collective-permute-done | bytes 288 | tf_op jit(solution)/shard_map/ppermute | solution.py:35
  16.7 0.0 collective-permute-start.3
  16.7 0.0 collective-permute-done.2.refs_2_
  16.7 0.0 collective-permute-done.1.refs_1_
  16.7 0.0 copy-done.6
  16.7 0.0 copy-done
  16.7 0.0 copy-done.2
  16.7 0.0 copy-done.5
  16.7 2.5 %attend_first.1 = (bf16[192,1024]{1,0:T(8,128)(2,1)S(1)}, bf16[512,1024]{1,0:T(8,128)(2,1)S(1)}) custom-call(s32[1]{0:T(128)S(6)} %copy.14.length_ref, bf16[1024,1024]{1,0:T(8,128)(2,1)S(1)} %copy-done, bf16[1,512,1024]{2,1,0:T(8,128)(2,1)S(1)} %copy-done.2, bf16[1,512,1024]{2,1,0:T(8,128)(2,1)S(1)} %copy-done.5, bf16[64,1024]{1,0:T(8,128)(2,1)S(1)} %copy-done.6, ...), custom_call_target="tpu_custom_call" | custom-call | flops 805306368 | tf_op jit(solution)/shard_map/attend_first/pallas_call | solution.py:157
  19.2 1.0 %collective-permute-done.3.refs_1_ = s32[2,64]{1,0:T(2,128)S(1)} collective-permute-done((s32[2,64]{1,0:T(2,128)S(1)}, s32[2,64]{1,0:T(2,128)S(1)}, u32[]{:S(2)}, u32[]{:S(2)}) %collective-permute-start.3) | collective-permute-done | bytes 544 | tf_op jit(solution)/shard_map/ppermute | solution.py:35
  20.2 0.0 collective-permute-done.4.refs_1_.refs_4_
  20.2 0.0 collective-permute-done.5.refs_3_.refs_6_
  20.2 0.1 collective-permute-start.8
  20.3 0.5 collective-permute-start.9
  20.8 0.1 collective-permute-start.7
  20.9 1.4 %collective-permute-start.6 = (s32[4,64]{1,0:T(4,128)S(1)}, s32[4,64]{1,0:T(4,128)S(1)}, u32[]{:S(2)}, u32[]{:S(2)}) collective-permute-start(s32[4,64]{1,0:T(4,128)S(1)} %stack.5.near_ids_ref), channel_id=1, source_target_pairs={{0,1},{1,0},{2,3},{3,2},{4,5},{5,4},{6,7},{7,6},{8,9},{9,8},{10,11... | collective-permute-start | bytes 3080 | tf_op jit(solution)/shard_map/ppermute | solution.py:35
  22.3 0.0 collective-permute-done.8.refs_2_.refs_5_
  22.3 0.0 collective-permute-done.9.refs_4_.refs_7_
  22.3 0.0 collective-permute-done.7.refs_0_.refs_3_
  22.3 0.0 copy-start.1
  22.3 0.0 copy-start.3
  22.3 0.0 copy-start.9
  22.3 2.5 %attend_next.1.refs_1_ = bf16[320,1024]{1,0:T(8,128)(2,1)S(1)} custom-call(bf16[1024,1024]{1,0:T(8,128)(2,1)S(1)} %copy-done, bf16[1,512,1024]{2,1,0:T(8,128)(2,1)S(1)} %copy-done.2, bf16[512,1024]{1,0:T(8,128)(2,1)S(1)} %get-tuple-element.42.values_ref, bf16[64,1024]{1,0:T(8,128)(2,1)S(1)} %collective-permute-done.7.refs_0_.refs_3_, ...), custom_call_target="tpu_custom_call" | custom-call | flops 1342177280 | tf_op jit(solution)/shard_map/attend_next/pallas_call | solution.py:168
  24.9 0.0 collective-permute-done.6.far_ids_ref
  24.9 0.9 %place.1 = (bf16[256,512]{1,0:T(8,128)(2,1)S(1)}, bf16[256,512]{1,0:T(8,128)(2,1)S(1)}, bf16[256,512]{1,0:T(8,128)(2,1)S(1)}, bf16[256,512]{1,0:T(8,128)(2,1)S(1)}) custom-call(s32[4,64]{1,0:T(4,128)S(1)} %stack.5.near_ids_ref, s32[4,64]{1,0:T(4,128)S(1)} %collective-permute-done.6.far_ids_ref, bf16[192,1024]{1,0:T(8,128)(2,1)S(1)} %get-tuple-element.41.refs_0_, ...), custom_call_target="tpu_custom_call" | custom-call | flops 536870912 | tf_op jit(solution)/shard_map/place/pallas_call | solution.py:200
  25.7 0.0 copy-done.1
  25.7 0.2 collective-permute-start.15
  26.0 1.3 %collective-permute-start.10 = (bf16[256,512]{1,0:T(8,128)(2,1)S(1)}, bf16[256,512]{1,0:T(8,128)(2,1)S(1)}, u32[]{:S(2)}, u32[]{:S(2)}) collective-permute-start(bf16[256,512]{1,0:T(8,128)(2,1)S(1)} %get-tuple-element.48), channel_id=1, source_target_pairs={{0,1},{1,0},{2,3},{3,2},{4,5},{5,4},{6,7},{7,6},{8,9},{9,8},{10,11... | collective-permute-start | bytes 786440 | tf_op jit(solution)/shard_map/ppermute | solution.py:35
  27.2 1.0 %collective-permute-start.11 = (bf16[256,512]{1,0:T(8,128)(2,1)S(1)}, bf16[256,512]{1,0:T(8,128)(2,1)S(1)}, u32[]{:S(2)}, u32[]{:S(2)}) collective-permute-start(bf16[256,512]{1,0:T(8,128)(2,1)S(1)} %get-tuple-element.49), channel_id=1, source_target_pairs={{0,2},{1,3},{2,0},{3,1},{4,6},{5,7},{6,4},{7,5},{8,10},{9,11},{10,... | collective-permute-start | bytes 786440 | tf_op jit(solution)/shard_map/ppermute | solution.py:35
  28.2 0.9 %prepare.1 = (f32[64,1024]{1,0:T(8,128)S(1)}, f32[64,1024]{1,0:T(8,128)S(1)}) custom-call(bf16[256,512]{1,0:T(8,128)(2,1)S(1)} %get-tuple-element.47.after_ref.refs_0_, s32[1,64]{1,0:T(1,128)S(1)} %copy-done.9, bf16[1024,1024]{1,0:T(8,128)(2,1)S(1)} %copy-done.3, bf16[64,1024]{1,0:T(8,128)(2,1)S(1)} %copy-done.6, ...), custom_call_target="tpu_custom_call" | custom-call | flops 201326592 | tf_op jit(solution)/shard_map/prepare/pallas_call | solution.py:245
  29.1 5.4 %collective-permute-done.10.refs_1_ = bf16[256,512]{1,0:T(8,128)(2,1)S(1)} collective-permute-done((bf16[256,512]{1,0:T(8,128)(2,1)S(1)}, bf16[256,512]{1,0:T(8,128)(2,1)S(1)}, u32[]{:S(2)}, u32[]{:S(2)}) %collective-permute-start.10) | collective-permute-done | bytes 262176 | tf_op jit(solution)/shard_map/ppermute | solution.py:35
  34.5 0.9 %collective-permute-done.11.refs_1_ = bf16[256,512]{1,0:T(8,128)(2,1)S(1)} collective-permute-done((bf16[256,512]{1,0:T(8,128)(2,1)S(1)}, bf16[256,512]{1,0:T(8,128)(2,1)S(1)}, u32[]{:S(2)}, u32[]{:S(2)}) %collective-permute-start.11) | collective-permute-done | bytes 262176 | tf_op jit(solution)/shard_map/ppermute | solution.py:35
  35.5 0.1 fold.4
  35.5 0.9 %collective-permute-start.13 = (bf16[128,512]{1,0:T(8,128)(2,1)S(1)}, bf16[128,512]{1,0:T(8,128)(2,1)S(1)}, u32[]{:S(2)}, u32[]{:S(2)}) collective-permute-start(bf16[128,512]{1,0:T(8,128)(2,1)S(1)} %get-tuple-element.57), channel_id=1, source_target_pairs={{0,1},{1,0},{2,3},{3,2},{4,5},{5,4},{6,7},{7,6},{8,9},{9,8},{10,11... | collective-permute-start | bytes 393224 | tf_op jit(solution)/shard_map/ppermute | solution.py:35
  36.4 0.1 fold.3
  36.5 1.1 %collective-permute-start.12 = (bf16[128,512]{1,0:T(8,128)(2,1)S(1)}, bf16[128,512]{1,0:T(8,128)(2,1)S(1)}, u32[]{:S(2)}, u32[]{:S(2)}) collective-permute-start(bf16[128,512]{1,0:T(8,128)(2,1)S(1)} %get-tuple-element.53), channel_id=1, source_target_pairs={{0,2},{1,3},{2,0},{3,1},{4,6},{5,7},{6,4},{7,5},{8,10},{9,11},{10,... | collective-permute-start | bytes 393224 | tf_op jit(solution)/shard_map/ppermute | solution.py:35
  37.5 3.0 %collective-permute-done.13.refs_3_ = bf16[128,512]{1,0:T(8,128)(2,1)S(1)} collective-permute-done((bf16[128,512]{1,0:T(8,128)(2,1)S(1)}, bf16[128,512]{1,0:T(8,128)(2,1)S(1)}, u32[]{:S(2)}, u32[]{:S(2)}) %collective-permute-start.13) | collective-permute-done | bytes 131104 | tf_op jit(solution)/shard_map/ppermute | solution.py:35
  40.6 0.9 %collective-permute-done.12.refs_1_ = bf16[128,512]{1,0:T(8,128)(2,1)S(1)} collective-permute-done((bf16[128,512]{1,0:T(8,128)(2,1)S(1)}, bf16[128,512]{1,0:T(8,128)(2,1)S(1)}, u32[]{:S(2)}, u32[]{:S(2)}) %collective-permute-start.12) | collective-permute-done | bytes 131104 | tf_op jit(solution)/shard_map/ppermute | solution.py:35
  41.5 1.8 %collective-permute-start.14 = (bf16[64,1024]{1,0:T(8,128)(2,1)S(1)}, bf16[64,1024]{1,0:T(8,128)(2,1)S(1)}, u32[]{:S(2)}, u32[]{:S(2)}) collective-permute-start(bf16[64,1024]{1,0:T(8,128)(2,1)S(1)} %get-tuple-element.59), channel_id=1, source_target_pairs={{0,4},{1,5},{2,6},{3,7},{4,0},{5,1},{6,2},{7,3},{8,12},{9,13},{10,... | collective-permute-start | bytes 393224 | tf_op jit(solution)/shard_map/ppermute | solution.py:35
  44.0 4.9 %collective-permute-done.14.come_ref = bf16[64,1024]{1,0:T(8,128)(2,1)S(1)} collective-permute-done((bf16[64,1024]{1,0:T(8,128)(2,1)S(1)}, bf16[64,1024]{1,0:T(8,128)(2,1)S(1)}, u32[]{:S(2)}, u32[]{:S(2)}) %collective-permute-start.14) | collective-permute-done | bytes 131104 | tf_op jit(solution)/shard_map/ppermute | solution.py:35
  48.9 0.0 collective-permute-done.15.refs_1_
  48.9 2.8 %finish.1 = bf16[1,64,1024]{2,1,0:T(8,128)(2,1)} custom-call(f32[64,1024]{1,0:T(8,128)S(1)} %get-tuple-element.58.kept_ref, bf16[64,1024]{1,0:T(8,128)(2,1)S(1)} %collective-permute-done.14.come_ref, f32[64,1024]{1,0:T(8,128)S(1)} %get-tuple-element.60.embed_ref, f32[64,1024]{1,0:T(8,128)S(1)} %get-tuple-element.61.gating_ref, f32[1,1024]{1,0:T(1,128)S(1)} %bitcast.1, ...), custom_call_target="tpu_custom_call" | custom-call | flops 671088640 | tf_op jit(solution)/shard_map/finish/pallas_call | solution.py:282
  (17 shorter events, 0.1 us)
Async XLA Ops:
  0.0 16.7 %copy-start.6 = (bf16[64,1024]{1,0:T(8,128)(2,1)S(1)}, bf16[64,1024]{1,0:T(8,128)(2,1)}, u32[]{:S(2)}) copy-start(bf16[64,1024]{1,0:T(8,128)(2,1)} %refs_0_.6) | copy-start | bytes 393220
  0.0 16.7 %copy-start = (bf16[1024,1024]{1,0:T(8,128)(2,1)S(1)}, bf16[1024,1024]{1,0:T(8,128)(2,1)}, u32[]{:S(2)}) copy-start(bf16[1024,1024]{1,0:T(8,128)(2,1)} %w_query_ref.1) | copy-start | bytes 6291460
  0.0 16.7 %copy-start.2 = (bf16[1,512,1024]{2,1,0:T(8,128)(2,1)S(1)}, bf16[1,512,1024]{2,1,0:T(8,128)(2,1)}, u32[]{:S(2)}) copy-start(bf16[1,512,1024]{2,1,0:T(8,128)(2,1)} %keys_ref.3) | copy-start | bytes 3145732
  0.0 16.7 %copy-start.5 = (bf16[1,512,1024]{2,1,0:T(8,128)(2,1)S(1)}, bf16[1,512,1024]{2,1,0:T(8,128)(2,1)}, u32[]{:S(2)}) copy-start(bf16[1,512,1024]{2,1,0:T(8,128)(2,1)} %values_ref.1) | copy-start | bytes 3145732
  0.0 20.2 %collective-permute-start.4 = (bf16[64,1024]{1,0:T(8,128)(2,1)}, bf16[64,1024]{1,0:T(8,128)(2,1)S(1)}, u32[]{:S(2)}, u32[]{:S(2)}) collective-permute-start(bf16[64,1024]{1,0:T(8,128)(2,1)} %refs_0_.6), channel_id=1, source_target_pairs={{0,7},{1,6},{2,5},{3,4},{4,3},{5,2},{6,1},{7,0},{8,14},{9,15},{10,... | collective-permute-start | bytes 393224 | tf_op jit(solution)/shard_map/ppermute | solution.py:43
  6.1 10.6 %collective-permute-start.2 = (bf16[64,1024]{1,0:T(8,128)(2,1)}, bf16[64,1024]{1,0:T(8,128)(2,1)S(1)}, u32[]{:S(2)}, u32[]{:S(2)}) collective-permute-start(bf16[64,1024]{1,0:T(8,128)(2,1)} %refs_0_.6), channel_id=1, source_target_pairs={{0,1},{1,0},{2,3},{3,2},{4,5},{5,4},{6,7},{7,6},{8,11},{9,10},{10,... | collective-permute-start | bytes 393224 | tf_op jit(solution)/shard_map/ppermute | solution.py:43
  6.6 10.1 %collective-permute-start.1 = (bf16[64,1024]{1,0:T(8,128)(2,1)}, bf16[64,1024]{1,0:T(8,128)(2,1)S(1)}, u32[]{:S(2)}, u32[]{:S(2)}) collective-permute-start(bf16[64,1024]{1,0:T(8,128)(2,1)} %refs_0_.6), channel_id=1, source_target_pairs={{0,2},{1,3},{2,0},{3,1},{4,6},{5,7},{6,4},{7,5},{8,10},{9,11},{10,... | collective-permute-start | bytes 393224 | tf_op jit(solution)/shard_map/ppermute | solution.py:35
  6.6 13.6 %collective-permute-start.5 = (bf16[64,1024]{1,0:T(8,128)(2,1)}, bf16[64,1024]{1,0:T(8,128)(2,1)S(1)}, u32[]{:S(2)}, u32[]{:S(2)}) collective-permute-start(bf16[64,1024]{1,0:T(8,128)(2,1)} %refs_0_.6), channel_id=1, source_target_pairs={{0,4},{1,5},{2,6},{3,7},{4,0},{5,1},{6,2},{7,3},{8,13},{9,12},{10,... | collective-permute-start | bytes 393224 | tf_op jit(solution)/shard_map/ppermute | solution.py:43
  7.3 0.7 %copy-start.8 = (s32[1,64]{1,0:T(1,128)S(1)}, s32[1,64]{1,0:T(1,128)}, u32[]{:S(2)}) copy-start(s32[1,64]{1,0:T(1,128)} %ids_ref.1) | copy-start | bytes 772
  8.0 8.7 %collective-permute-start = (s32[1,64]{1,0:T(1,128)S(1)}, s32[1,64]{1,0:T(1,128)S(1)}, u32[]{:S(2)}, u32[]{:S(2)}) collective-permute-start(s32[1,64]{1,0:T(1,128)S(1)} %stack.3.refs_0_), channel_id=1, source_target_pairs={{0,4},{1,5},{2,6},{3,7},{4,0},{5,1},{6,2},{7,3},{8,12},{9,13},{10,... | collective-permute-start | bytes 776 | tf_op jit(solution)/shard_map/ppermute | solution.py:35
  16.7 3.6 %collective-permute-start.3 = (s32[2,64]{1,0:T(2,128)S(1)}, s32[2,64]{1,0:T(2,128)S(1)}, u32[]{:S(2)}, u32[]{:S(2)}) collective-permute-start(s32[2,64]{1,0:T(2,128)S(1)} %stack.4.refs_0_), channel_id=1, source_target_pairs={{0,2},{1,3},{2,0},{3,1},{4,6},{5,7},{6,4},{7,5},{8,10},{9,11},{10,... | collective-permute-start | bytes 1544 | tf_op jit(solution)/shard_map/ppermute | solution.py:35
  20.2 2.1 %collective-permute-start.8 = (bf16[64,1024]{1,0:T(8,128)(2,1)S(1)}, bf16[64,1024]{1,0:T(8,128)(2,1)S(1)}, u32[]{:S(2)}, u32[]{:S(2)}) collective-permute-start(bf16[64,1024]{1,0:T(8,128)(2,1)S(1)} %collective-permute-done.4.refs_1_.refs_4_), channel_id=1, source_target_pairs={{8,0},{0,8},{9,1},{1,9},{10,2},{2,10},{11,3},{3,11},{12,4},{4,12},... | collective-permute-start | bytes 393224 | tf_op jit(solution)/shard_map/ppermute | solution.py:48
  20.3 2.0 %collective-permute-start.9 = (bf16[64,1024]{1,0:T(8,128)(2,1)S(1)}, bf16[64,1024]{1,0:T(8,128)(2,1)S(1)}, u32[]{:S(2)}, u32[]{:S(2)}) collective-permute-start(bf16[64,1024]{1,0:T(8,128)(2,1)S(1)} %collective-permute-done.5.refs_3_.refs_6_), channel_id=1, source_target_pairs={{8,0},{0,8},{9,1},{1,9},{10,2},{2,10},{11,3},{3,11},{12,4},{4,12},... | collective-permute-start | bytes 393224 | tf_op jit(solution)/shard_map/ppermute | solution.py:48
  20.8 1.5 %collective-permute-start.7 = (bf16[64,1024]{1,0:T(8,128)(2,1)S(1)}, bf16[64,1024]{1,0:T(8,128)(2,1)S(1)}, u32[]{:S(2)}, u32[]{:S(2)}) collective-permute-start(bf16[64,1024]{1,0:T(8,128)(2,1)S(1)} %collective-permute-done.2.refs_2_), channel_id=1, source_target_pairs={{8,0},{0,8},{9,1},{1,9},{10,2},{2,10},{11,3},{3,11},{12,4},{4,12},... | collective-permute-start | bytes 393224 | tf_op jit(solution)/shard_map/ppermute | solution.py:48
  20.9 4.0 %collective-permute-start.6 = (s32[4,64]{1,0:T(4,128)S(1)}, s32[4,64]{1,0:T(4,128)S(1)}, u32[]{:S(2)}, u32[]{:S(2)}) collective-permute-start(s32[4,64]{1,0:T(4,128)S(1)} %stack.5.near_ids_ref), channel_id=1, source_target_pairs={{0,1},{1,0},{2,3},{3,2},{4,5},{5,4},{6,7},{7,6},{8,9},{9,8},{10,11... | collective-permute-start | bytes 3080 | tf_op jit(solution)/shard_map/ppermute | solution.py:35
  22.3 3.4 %copy-start.1 = (bf16[1,2,1024,1024]{3,2,1,0:T(8,128)(2,1)S(1)}, bf16[1,2,1024,1024]{3,2,1,0:T(8,128)(2,1)}, u32[]{:S(2)}) copy-start(bf16[1,2,1024,1024]{3,2,1,0:T(8,128)(2,1)} %refs_0_.7) | copy-start | bytes 12582916
  22.3 5.9 %copy-start.3 = (bf16[1024,1024]{1,0:T(8,128)(2,1)S(1)}, bf16[1024,1024]{1,0:T(8,128)(2,1)}, u32[]{:S(2)}) copy-start(bf16[1024,1024]{1,0:T(8,128)(2,1)} %w_gate_ref.1) | copy-start | bytes 6291460
  22.3 5.9 %copy-start.9 = (s32[1,64]{1,0:T(1,128)S(1)}, s32[1,64]{1,0:T(1,128)}, u32[]{:S(2)}) copy-start(s32[1,64]{1,0:T(1,128)} %ids_ref.1) | copy-start | bytes 772
  25.7 23.1 %collective-permute-start.15 = (bf16[1,2,1024,1024]{3,2,1,0:T(8,128)(2,1)S(1)}, bf16[1,2,1024,1024]{3,2,1,0:T(8,128)(2,1)S(1)}, u32[]{:S(2)}, u32[]{:S(2)}) collective-permute-start(bf16[1,2,1024,1024]{3,2,1,0:T(8,128)(2,1)S(1)} %copy-done.1), channel_id=1, source_target_pairs={{8,0},{0,8},{9,1},{1,9},{10,2},{2,10},{11,3},{3,11},{12,4},{4,12},... | collective-permute-start | bytes 12582920 | tf_op jit(solution)/shard_map/ppermute | solution.py:48
  26.0 8.6 %collective-permute-start.10 = (bf16[256,512]{1,0:T(8,128)(2,1)S(1)}, bf16[256,512]{1,0:T(8,128)(2,1)S(1)}, u32[]{:S(2)}, u32[]{:S(2)}) collective-permute-start(bf16[256,512]{1,0:T(8,128)(2,1)S(1)} %get-tuple-element.48), channel_id=1, source_target_pairs={{0,1},{1,0},{2,3},{3,2},{4,5},{5,4},{6,7},{7,6},{8,9},{9,8},{10,11... | collective-permute-start | bytes 786440 | tf_op jit(solution)/shard_map/ppermute | solution.py:35
  27.2 21.7 %copy-start.4 = (bf16[1024,1024]{1,0:T(8,128)(2,1)S(1)}, bf16[1024,1024]{1,0:T(8,128)(2,1)}, u32[]{:S(2)}) copy-start(bf16[1024,1024]{1,0:T(8,128)(2,1)} %w_out_ref.1) | copy-start | bytes 6291460
  27.2 21.7 %copy-start.7 = (f32[1024]{0:T(1024)S(1)}, f32[1024]{0:T(1024)}, u32[]{:S(2)}) copy-start(f32[1024]{0:T(1024)} %param.22) | copy-start | bytes 12292
  27.2 21.7 %copy-start.10 = (s32[1,64]{1,0:T(1,128)S(1)}, s32[1,64]{1,0:T(1,128)}, u32[]{:S(2)}) copy-start(s32[1,64]{1,0:T(1,128)} %domain_ref.1) | copy-start | bytes 772
  27.2 8.2 %collective-permute-start.11 = (bf16[256,512]{1,0:T(8,128)(2,1)S(1)}, bf16[256,512]{1,0:T(8,128)(2,1)S(1)}, u32[]{:S(2)}, u32[]{:S(2)}) collective-permute-start(bf16[256,512]{1,0:T(8,128)(2,1)S(1)} %get-tuple-element.49), channel_id=1, source_target_pairs={{0,2},{1,3},{2,0},{3,1},{4,6},{5,7},{6,4},{7,5},{8,10},{9,11},{10,... | collective-permute-start | bytes 786440 | tf_op jit(solution)/shard_map/ppermute | solution.py:35
  35.5 5.0 %collective-permute-start.13 = (bf16[128,512]{1,0:T(8,128)(2,1)S(1)}, bf16[128,512]{1,0:T(8,128)(2,1)S(1)}, u32[]{:S(2)}, u32[]{:S(2)}) collective-permute-start(bf16[128,512]{1,0:T(8,128)(2,1)S(1)} %get-tuple-element.57), channel_id=1, source_target_pairs={{0,1},{1,0},{2,3},{3,2},{4,5},{5,4},{6,7},{7,6},{8,9},{9,8},{10,11... | collective-permute-start | bytes 393224 | tf_op jit(solution)/shard_map/ppermute | solution.py:35
  36.5 5.0 %collective-permute-start.12 = (bf16[128,512]{1,0:T(8,128)(2,1)S(1)}, bf16[128,512]{1,0:T(8,128)(2,1)S(1)}, u32[]{:S(2)}, u32[]{:S(2)}) collective-permute-start(bf16[128,512]{1,0:T(8,128)(2,1)S(1)} %get-tuple-element.53), channel_id=1, source_target_pairs={{0,2},{1,3},{2,0},{3,1},{4,6},{5,7},{6,4},{7,5},{8,10},{9,11},{10,... | collective-permute-start | bytes 393224 | tf_op jit(solution)/shard_map/ppermute | solution.py:35
  41.5 7.3 %collective-permute-start.14 = (bf16[64,1024]{1,0:T(8,128)(2,1)S(1)}, bf16[64,1024]{1,0:T(8,128)(2,1)S(1)}, u32[]{:S(2)}, u32[]{:S(2)}) collective-permute-start(bf16[64,1024]{1,0:T(8,128)(2,1)S(1)} %get-tuple-element.59), channel_id=1, source_target_pairs={{0,4},{1,5},{2,6},{3,7},{4,0},{5,1},{6,2},{7,3},{8,12},{9,13},{10,... | collective-permute-start | bytes 393224 | tf_op jit(solution)/shard_map/ppermute | solution.py:35

commit v8 on v7

--- a/solution.py
+++ b/solution.py
@@ -251,10 +251,11 @@
     )(after, ids, w_gate, *blocks)
 
 
-def finish_kernel(kept_ref, come_ref, embed_ref, gating_ref, gain_ref, count_ref, domain_ref, w_out_ref, *refs):
-    expert_refs, out_ref = refs[:-1], refs[-1]
+def finish_kernel(sides, embed_ref, gating_ref, gain_ref, count_ref, domain_ref, w_out_ref, *refs):
+    *expert_refs, out_ref = refs[2 * sides :]
     users = len(expert_refs)
-    attended = kept_ref[...] + come_ref[...].astype(F32)
+    halves = [refs[2 * side][...] + refs[2 * side + 1][...].astype(F32) for side in range(sides)]
+    attended = jnp.concatenate(halves, axis=1)
     gated = (rms_scale(attended) * gain_ref[...] * gating_ref[...]).astype(BF16)
     mixed = jnp.dot(gated, w_out_ref[...], preferred_element_type=F32)
     state = (embed_ref[...] + mixed).astype(BF16)
@@ -277,15 +278,16 @@
     out_ref[0] = result.astype(BF16)
 
 
-def finish(kept, come, embed, gating, gain, counts, domains, w_out, experts):
-    slots, width = kept.shape
-    return kernel_call(
-        finish_kernel,
+def finish(pairs, embed, gating, gain, counts, domains, w_out, experts):
+    slots, width = embed.shape
+    blocks = [block for pair in pairs for block in pair]
+    return kernel_call(
+        functools.partial(finish_kernel, len(pairs)),
         "finish",
         [jax.ShapeDtypeStruct((1, slots, width), BF16)],
-        [VMEM] * 5 + [SMEM] + [VMEM] * (2 + len(experts)),
+        [VMEM] * 3 + [SMEM] + [VMEM] * (2 + len(blocks) + len(experts)),
         flops=2 * slots * width * width * (1 + LAYERS * len(experts)),
-    )(kept, come, embed, gating, gain, counts, domains, w_out, *experts)[0]
+    )(embed, gating, gain, counts, domains, w_out, *blocks, *experts)[0]
 
 
 def on_device(
@@ -317,21 +319,20 @@
     near_shards = [swapped_by_user(item_table, flips) for flips in near_flips]
     shared_shard = swapped(item_table, shared)
 
-    near_ids, id_flips = stack([item_ids], flops=LOADS_BESIDE), [0]
-    far_ids = swapped(near_ids, 1 << (bits - 1))
+    turns = [bits - 1, 0] + list(range(1, bits - 1))
+    far_ids, id_flips = swapped(item_ids, 1 << turns[0]), [0, 1 << turns[0]]
 
     first_pieces = [((flip,) * users, 0, None) for flip in (0, shared)] + [(flips, 0, None) for flips in near_flips]
     first_blocks = [item_table, shared_shard] + near_shards
-    id_flips += [flip + (1 << (bits - 1)) for flip in id_flips]
-    near_ids = stack([near_ids, far_ids])
+    near_ids = stack([item_ids, far_ids], flops=LOADS_BESIDE)
     w_query, near_ids = lax.optimization_barrier((w_query, near_ids))
     first, masked_values = attend_first(
         first_pieces, first_blocks, shard_rows, history_lengths, w_query, history_keys, history_values
     )
-    for bit in reversed(range(bits - 1)):
+    for bit in turns[1:]:
         far_ids = swapped(near_ids, 1 << bit)
         id_flips += [flip + (1 << bit) for flip in id_flips]
-        if bit:
+        if bit != turns[-1]:
             first, far_ids = lax.optimization_barrier((first, far_ids))
             near_ids = stack([near_ids, far_ids])
     first, *near_shards = lax.optimization_barrier((first, *near_shards))
@@ -349,11 +350,11 @@
     following = attend_next(next_pieces, next_blocks, shard_rows, w_query, history_keys, masked_values)
     pieces, blocks = first_pieces + next_pieces, first_blocks + next_blocks
 
-    turns = [list(range(bits)), list(range(bits))]
-    turns[1][:2] = [1, 0]
+    side_turns = [list(range(bits)), list(range(bits))]
+    side_turns[1][:2] = [1, 0]
     orders = [
         [sum(((r >> (bits - 1 - t)) & 1) << bit for t, bit in enumerate(turn)) for r in range(hist_devices)]
-        for turn in turns
+        for turn in side_turns
     ]
     kept_a, sent_a, kept_b, sent_b = place(
         pieces, id_flips, orders, shard_rows, near_ids, far_ids, [first, following]
@@ -364,17 +365,14 @@
     experts = [expert_weights] + [from_user(leaving, steps) for steps in others]
 
     held = [(kept_a, sent_a), (kept_b, sent_b)]
-    for at in range(bits - 1):
-        arriving = [swapped(held[side][1], 1 << turn[at]) for side, turn in enumerate(turns)]
+    for at in range(bits):
+        arriving = [swapped(sent, 1 << turn[at]) for (_, sent), turn in zip(held, side_turns)]
         if at == 0:
             *arriving, embed = lax.optimization_barrier((*arriving, embed))
-        pairs = [(held[side][0], arriving[side]) for side in range(len(turns))]
-        if at < bits - 2:
+        pairs = [(kept, come) for (kept, _), come in zip(held, arriving)]
+        if at < bits - 1:
             held = [fold([pair]) for pair in pairs]
-        else:
-            kept, sent = fold(pairs)
-    come = swapped(sent, 1 << (bits - 1))
-    return finish(kept, come, embed, gating, attn_gain[None], candidate_counts, domain_ids, w_out, experts)
+    return finish(pairs, embed, gating, attn_gain[None], candidate_counts, domain_ids, w_out, experts)
 
 
 def solution(mesh):

time: 51.9 us -> 50.6 us (0.975)
  waiting for transfers between devices: 22 us -> 18.7 us
  starting transfers between devices: 17.8 us -> 19.8 us
    ppermute x9 -> x10, waiting for transfers between devices: 22 us -> 16.7 us  [swapped(): return lax.ppermute(value, 'hist', [(i, i ^ flip) for i in range(count)])]
    ppermute x9 -> x10, starting transfers between devices: 9.67 us -> 12.7 us  [swapped(): return lax.ppermute(value, 'hist', [(i, i ^ flip) for i in range(count)])]
    ppermute x3, starting transfers between devices: 7.28 us -> 5.56 us  [swapped_by_user(): return lax.ppermute(value, ('user', 'hist'), pairs)]
    ppermute x4, waiting for transfers between devices: 0.01 us -> 1.02 us  [from_user(): lax.ppermute(value, 'user', [((i + steps) % count, i) for i in range(coun...]
    ppermute x3, waiting for transfers between devices: 0.01 us -> 0.92 us  [swapped_by_user(): return lax.ppermute(value, ('user', 'hist'), pairs)]
    ppermute x4, starting transfers between devices: 0.87 us -> 1.47 us  [from_user(): lax.ppermute(value, 'user', [((i + steps) % count, i) for i in range(coun...]
  transfers between devices with their start and end apart: 16 -> 17, of which waited for: 7 -> 11; matrix products, arithmetic and copies ran while one was open for 0% -> 0% of each run, Pallas kernels for 12% -> 12%
where the time goes in v8:
time: 50.6 us; the launch traced here: 50.5 us
  starting transfers between devices  19.8 us (39%)
  waiting for transfers between devices  18.7 us (37%)
  Pallas kernels  9.74 us (19%)
  between operations  1.47 us (3%)
  local copies, waits for them, and re-layouts  0.84 us (2%)
    ppermute x10, waiting for transfers between devices, swapped(): return lax.ppermute(value, 'hist', [(i, i ^ flip) for i in range(count)])  16.7 us
    ppermute x10, starting transfers between devices, swapped(): return lax.ppermute(value, 'hist', [(i, i ^ flip) for i in range(count)])  12.7 us
    ppermute x3, starting transfers between devices, swapped_by_user(): return lax.ppermute(value, ('user', 'hist'), pairs)  5.56 us
    pallas_call x1, Pallas kernels, finish(): kernel_call(functools.partial(finish_kernel, len(pairs)), 'finish', [jax....  2.83 us
    pallas_call x1, Pallas kernels, attend_next(): kernel_call(functools.partial(next_kernel, pieces), 'attend_next', [jax.S...  2.49 us
    pallas_call x1, Pallas kernels, attend_first(): kernel_call(functools.partial(first_kernel, pieces), 'attend_first', [jax...  2.48 us
    ppermute x4, starting transfers between devices, from_user(): lax.ppermute(value, 'user', [((i + steps) % count, i) for i in range(coun...  1.47 us
    ppermute x4, waiting for transfers between devices, from_user(): lax.ppermute(value, 'user', [((i + steps) % count, i) for i in range(coun...  1.02 us
  transfers between devices with their start and end apart: 17, of which 11 were waited for; matrix products, arithmetic and copies ran while one was open for 0% of the time, Pallas kernels for 12%

profile of v8, /device:TPU:0, one launch (start us, length us, event | category | flops | bytes accessed | tf_op | source)
XLA Modules:
  0.0 50.5 jit_solution(4959420042942138085)
XLA Ops:
  0.0 4.0 %collective-permute-start = (s32[1,64]{1,0:T(1,128)}, s32[1,64]{1,0:T(1,128)S(1)}, u32[]{:S(2)}, u32[]{:S(2)}) collective-permute-start(s32[1,64]{1,0:T(1,128)} %ids_ref.1), channel_id=1, source_target_pairs={{0,4},{1,5},{2,6},{3,7},{4,0},{5,1},{6,2},{7,3},{8,12},{9,13},{10,... | collective-permute-start | bytes 776 | tf_op jit(solution)/shard_map/ppermute | solution.py:35
  4.0 2.3 %collective-permute-start.4 = (bf16[64,1024]{1,0:T(8,128)(2,1)}, bf16[64,1024]{1,0:T(8,128)(2,1)S(1)}, u32[]{:S(2)}, u32[]{:S(2)}) collective-permute-start(bf16[64,1024]{1,0:T(8,128)(2,1)} %refs_0_.5), channel_id=1, source_target_pairs={{0,7},{1,6},{2,5},{3,4},{4,3},{5,2},{6,1},{7,0},{8,14},{9,15},{10,... | collective-permute-start | bytes 393224 | tf_op jit(solution)/shard_map/ppermute | solution.py:43
  6.3 0.5 %collective-permute-start.2 = (bf16[64,1024]{1,0:T(8,128)(2,1)}, bf16[64,1024]{1,0:T(8,128)(2,1)S(1)}, u32[]{:S(2)}, u32[]{:S(2)}) collective-permute-start(bf16[64,1024]{1,0:T(8,128)(2,1)} %refs_0_.5), channel_id=1, source_target_pairs={{0,1},{1,0},{2,3},{3,2},{4,5},{5,4},{6,7},{7,6},{8,11},{9,10},{10,... | collective-permute-start | bytes 393224 | tf_op jit(solution)/shard_map/ppermute | solution.py:43
  6.8 0.3 collective-permute-start.1
  7.1 2.8 %collective-permute-start.5 = (bf16[64,1024]{1,0:T(8,128)(2,1)}, bf16[64,1024]{1,0:T(8,128)(2,1)S(1)}, u32[]{:S(2)}, u32[]{:S(2)}) collective-permute-start(bf16[64,1024]{1,0:T(8,128)(2,1)} %refs_0_.5), channel_id=1, source_target_pairs={{0,4},{1,5},{2,6},{3,7},{4,0},{5,1},{6,2},{7,3},{8,13},{9,12},{10,... | collective-permute-start | bytes 393224 | tf_op jit(solution)/shard_map/ppermute | solution.py:43
  10.5 0.0 copy-start
  10.6 0.0 copy-start.2
  10.6 0.0 copy-start.5
  10.6 0.0 copy-start.6
  10.6 0.0 collective-permute-done.refs_1_
  10.6 0.0 copy-start.8
  10.6 0.8 %copy-done.8 = s32[1,64]{1,0:T(1,128)S(1)} copy-done((s32[1,64]{1,0:T(1,128)S(1)}, s32[1,64]{1,0:T(1,128)}, u32[]{:S(2)}) %copy-start.8) | copy-done | bytes 280
  11.4 1.5 %collective-permute-start.3 = (s32[2,64]{1,0:T(2,128)S(1)}, s32[2,64]{1,0:T(2,128)S(1)}, u32[]{:S(2)}, u32[]{:S(2)}) collective-permute-start(s32[2,64]{1,0:T(2,128)S(1)} %stack.2.refs_0_), channel_id=1, source_target_pairs={{0,1},{1,0},{2,3},{3,2},{4,5},{5,4},{6,7},{7,6},{8,9},{9,8},{10,11... | collective-permute-start | bytes 1544 | tf_op jit(solution)/shard_map/ppermute | solution.py:35
  12.9 0.9 %collective-permute-done.2.refs_2_ = bf16[64,1024]{1,0:T(8,128)(2,1)S(1)} collective-permute-done((bf16[64,1024]{1,0:T(8,128)(2,1)}, bf16[64,1024]{1,0:T(8,128)(2,1)S(1)}, u32[]{:S(2)}, u32[]{:S(2)}) %collective-permute-start.2) | collective-permute-done | bytes 131104 | tf_op jit(solution)/shard_map/ppermute | solution.py:43
  13.8 3.4 %collective-permute-done.1.refs_1_ = bf16[64,1024]{1,0:T(8,128)(2,1)S(1)} collective-permute-done((bf16[64,1024]{1,0:T(8,128)(2,1)}, bf16[64,1024]{1,0:T(8,128)(2,1)S(1)}, u32[]{:S(2)}, u32[]{:S(2)}) %collective-permute-start.1) | collective-permute-done | bytes 131104 | tf_op jit(solution)/shard_map/ppermute | solution.py:35
  17.3 0.0 copy-done
  17.3 2.5 %attend_first.1 = (bf16[192,1024]{1,0:T(8,128)(2,1)S(1)}, bf16[512,1024]{1,0:T(8,128)(2,1)S(1)}) custom-call(s32[1]{0:T(128)S(6)} %copy.14.length_ref, bf16[1024,1024]{1,0:T(8,128)(2,1)S(1)} %copy-done, bf16[1,512,1024]{2,1,0:T(8,128)(2,1)S(1)} %copy-done.2, bf16[1,512,1024]{2,1,0:T(8,128)(2,1)S(1)} %copy-done.5, bf16[64,1024]{1,0:T(8,128)(2,1)S(1)} %copy-done.6, ...), custom_call_target="tpu_custom_call" | custom-call | flops 805306368 | tf_op jit(solution)/shard_map/attend_first/pallas_call | solution.py:157
  19.8 0.0 collective-permute-done.3.refs_1_
  19.8 0.0 collective-permute-done.4.refs_1_.refs_4_
  19.8 0.0 collective-permute-done.5.refs_3_.refs_6_
  19.8 0.6 %collective-permute-start.8 = (bf16[64,1024]{1,0:T(8,128)(2,1)S(1)}, bf16[64,1024]{1,0:T(8,128)(2,1)S(1)}, u32[]{:S(2)}, u32[]{:S(2)}) collective-permute-start(bf16[64,1024]{1,0:T(8,128)(2,1)S(1)} %collective-permute-done.4.refs_1_.refs_4_), channel_id=1, source_target_pairs={{8,0},{0,8},{9,1},{1,9},{10,2},{2,10},{11,3},{3,11},{12,4},{4,12},... | collective-permute-start | bytes 393224 | tf_op jit(solution)/shard_map/ppermute | solution.py:48
  20.4 0.1 collective-permute-start.9
  20.5 0.4 collective-permute-start.7
  20.9 0.0 collective-permute-start.6
  20.9 0.5 collective-permute-done.8.refs_2_.refs_5_
  21.4 0.4 collective-permute-done.9.refs_4_.refs_7_
  21.8 0.2 collective-permute-done.7.refs_0_.refs_3_
  22.0 2.5 %attend_next.1.refs_1_ = bf16[320,1024]{1,0:T(8,128)(2,1)S(1)} custom-call(bf16[1024,1024]{1,0:T(8,128)(2,1)S(1)} %copy-done, bf16[1,512,1024]{2,1,0:T(8,128)(2,1)S(1)} %copy-done.2, bf16[512,1024]{1,0:T(8,128)(2,1)S(1)} %get-tuple-element.44.values_ref, bf16[64,1024]{1,0:T(8,128)(2,1)S(1)} %collective-permute-done.7.refs_0_.refs_3_, ...), custom_call_target="tpu_custom_call" | custom-call | flops 1342177280 | tf_op jit(solution)/shard_map/attend_next/pallas_call | solution.py:168
  24.5 0.1 collective-permute-done.6.far_ids_ref
  24.5 0.8 %place.1 = (bf16[256,512]{1,0:T(8,128)(2,1)S(1)}, bf16[256,512]{1,0:T(8,128)(2,1)S(1)}, bf16[256,512]{1,0:T(8,128)(2,1)S(1)}, bf16[256,512]{1,0:T(8,128)(2,1)S(1)}) custom-call(s32[4,64]{1,0:T(4,128)S(1)} %stack.3.near_ids_ref, s32[4,64]{1,0:T(4,128)S(1)} %collective-permute-done.6.far_ids_ref, bf16[192,1024]{1,0:T(8,128)(2,1)S(1)} %get-tuple-element.43.refs_0_, ...), custom_call_target="tpu_custom_call" | custom-call | flops 536870912 | tf_op jit(solution)/shard_map/place/pallas_call | solution.py:200
  25.4 0.4 collective-permute-start.16
  25.7 0.7 %collective-permute-start.10 = (bf16[256,512]{1,0:T(8,128)(2,1)S(1)}, bf16[256,512]{1,0:T(8,128)(2,1)S(1)}, u32[]{:S(2)}, u32[]{:S(2)}) collective-permute-start(bf16[256,512]{1,0:T(8,128)(2,1)S(1)} %get-tuple-element.48), channel_id=1, source_target_pairs={{0,1},{1,0},{2,3},{3,2},{4,5},{5,4},{6,7},{7,6},{8,9},{9,8},{10,11... | collective-permute-start | bytes 786440 | tf_op jit(solution)/shard_map/ppermute | solution.py:35
  26.4 0.8 %collective-permute-start.11 = (bf16[256,512]{1,0:T(8,128)(2,1)S(1)}, bf16[256,512]{1,0:T(8,128)(2,1)S(1)}, u32[]{:S(2)}, u32[]{:S(2)}) collective-permute-start(bf16[256,512]{1,0:T(8,128)(2,1)S(1)} %get-tuple-element.49), channel_id=1, source_target_pairs={{0,2},{1,3},{2,0},{3,1},{4,6},{5,7},{6,4},{7,5},{8,10},{9,11},{10,... | collective-permute-start | bytes 786440 | tf_op jit(solution)/shard_map/ppermute | solution.py:35
  27.2 0.9 %prepare.1 = (f32[64,1024]{1,0:T(8,128)S(1)}, f32[64,1024]{1,0:T(8,128)S(1)}) custom-call(bf16[256,512]{1,0:T(8,128)(2,1)S(1)} %get-tuple-element.54.after_ref.refs_0_, s32[1,64]{1,0:T(1,128)S(1)} %copy-done.9, bf16[1024,1024]{1,0:T(8,128)(2,1)S(1)} %copy-done.3, bf16[64,1024]{1,0:T(8,128)(2,1)S(1)} %copy-done.6, ...), custom_call_target="tpu_custom_call" | custom-call | flops 201326592 | tf_op jit(solution)/shard_map/prepare/pallas_call | solution.py:245
  28.1 6.1 %collective-permute-done.10.refs_1_ = bf16[256,512]{1,0:T(8,128)(2,1)S(1)} collective-permute-done((bf16[256,512]{1,0:T(8,128)(2,1)S(1)}, bf16[256,512]{1,0:T(8,128)(2,1)S(1)}, u32[]{:S(2)}, u32[]{:S(2)}) %collective-permute-start.10) | collective-permute-done | bytes 262176 | tf_op jit(solution)/shard_map/ppermute | solution.py:35
  34.2 0.5 %collective-permute-done.11.refs_1_ = bf16[256,512]{1,0:T(8,128)(2,1)S(1)} collective-permute-done((bf16[256,512]{1,0:T(8,128)(2,1)S(1)}, bf16[256,512]{1,0:T(8,128)(2,1)S(1)}, u32[]{:S(2)}, u32[]{:S(2)}) %collective-permute-start.11) | collective-permute-done | bytes 262176 | tf_op jit(solution)/shard_map/ppermute | solution.py:35
  34.7 0.1 fold.6
  34.7 1.3 %collective-permute-start.14 = (bf16[128,512]{1,0:T(8,128)(2,1)S(1)}, bf16[128,512]{1,0:T(8,128)(2,1)S(1)}, u32[]{:S(2)}, u32[]{:S(2)}) collective-permute-start(bf16[128,512]{1,0:T(8,128)(2,1)S(1)} %get-tuple-element.63), channel_id=1, source_target_pairs={{0,1},{1,0},{2,3},{3,2},{4,5},{5,4},{6,7},{7,6},{8,9},{9,8},{10,11... | collective-permute-start | bytes 393224 | tf_op jit(solution)/shard_map/ppermute | solution.py:35
  36.0 0.1 fold.4
  36.1 1.1 %collective-permute-start.12 = (bf16[128,512]{1,0:T(8,128)(2,1)S(1)}, bf16[128,512]{1,0:T(8,128)(2,1)S(1)}, u32[]{:S(2)}, u32[]{:S(2)}) collective-permute-start(bf16[128,512]{1,0:T(8,128)(2,1)S(1)} %get-tuple-element.57), channel_id=1, source_target_pairs={{0,2},{1,3},{2,0},{3,1},{4,6},{5,7},{6,4},{7,5},{8,10},{9,11},{10,... | collective-permute-start | bytes 393224 | tf_op jit(solution)/shard_map/ppermute | solution.py:35
  37.2 2.6 %collective-permute-done.14.refs_1_ = bf16[128,512]{1,0:T(8,128)(2,1)S(1)} collective-permute-done((bf16[128,512]{1,0:T(8,128)(2,1)S(1)}, bf16[128,512]{1,0:T(8,128)(2,1)S(1)}, u32[]{:S(2)}, u32[]{:S(2)}) %collective-permute-start.14) | collective-permute-done | bytes 131104 | tf_op jit(solution)/shard_map/ppermute | solution.py:35
  39.8 1.9 %collective-permute-start.15 = (bf16[64,512]{1,0:T(8,128)(2,1)S(1)}, bf16[64,512]{1,0:T(8,128)(2,1)S(1)}, u32[]{:S(2)}, u32[]{:S(2)}) collective-permute-start(bf16[64,512]{1,0:T(8,128)(2,1)S(1)} %get-tuple-element.65), channel_id=1, source_target_pairs={{0,4},{1,5},{2,6},{3,7},{4,0},{5,1},{6,2},{7,3},{8,12},{9,13},{10,... | collective-permute-start | bytes 196616 | tf_op jit(solution)/shard_map/ppermute | solution.py:35
  41.7 0.0 collective-permute-done.12.refs_1_
  41.7 1.2 %collective-permute-start.13 = (bf16[64,512]{1,0:T(8,128)(2,1)S(1)}, bf16[64,512]{1,0:T(8,128)(2,1)S(1)}, u32[]{:S(2)}, u32[]{:S(2)}) collective-permute-start(bf16[64,512]{1,0:T(8,128)(2,1)S(1)} %get-tuple-element.59), channel_id=1, source_target_pairs={{0,4},{1,5},{2,6},{3,7},{4,0},{5,1},{6,2},{7,3},{8,12},{9,13},{10,... | collective-permute-start | bytes 196616 | tf_op jit(solution)/shard_map/ppermute | solution.py:35
  43.6 2.4 %collective-permute-done.15.refs_3_ = bf16[64,512]{1,0:T(8,128)(2,1)S(1)} collective-permute-done((bf16[64,512]{1,0:T(8,128)(2,1)S(1)}, bf16[64,512]{1,0:T(8,128)(2,1)S(1)}, u32[]{:S(2)}, u32[]{:S(2)}) %collective-permute-start.15) | collective-permute-done | bytes 65568 | tf_op jit(solution)/shard_map/ppermute | solution.py:35
  46.0 1.7 %collective-permute-done.13.refs_1_ = bf16[64,512]{1,0:T(8,128)(2,1)S(1)} collective-permute-done((bf16[64,512]{1,0:T(8,128)(2,1)S(1)}, bf16[64,512]{1,0:T(8,128)(2,1)S(1)}, u32[]{:S(2)}, u32[]{:S(2)}) %collective-permute-start.13) | collective-permute-done | bytes 65568 | tf_op jit(solution)/shard_map/ppermute | solution.py:35
  47.6 0.0 collective-permute-done.16.refs_5_
  47.7 2.8 %finish.1 = bf16[1,64,1024]{2,1,0:T(8,128)(2,1)} custom-call(f32[64,1024]{1,0:T(8,128)S(1)} %get-tuple-element.52.embed_ref, f32[64,1024]{1,0:T(8,128)S(1)} %get-tuple-element.53.gating_ref, f32[1,1024]{1,0:T(1,128)S(1)} %bitcast.1, s32[1]{0:T(128)S(6)} %copy.13.count_ref, s32[1,64]{1,0:T(1,128)S(1)} %copy-done.10, bf16[1024,1024]{1,0:T(8,128)(2,1)S(1)} %copy-done.4, ...), custom_call_target="tpu_custom_call" | custom-call | flops 671088640 | tf_op jit(solution)/shard_map/finish/pallas_call | solution.py:284
  (19 shorter events, 0.1 us)
Async XLA Ops:
  0.0 10.6 %collective-permute-start = (s32[1,64]{1,0:T(1,128)}, s32[1,64]{1,0:T(1,128)S(1)}, u32[]{:S(2)}, u32[]{:S(2)}) collective-permute-start(s32[1,64]{1,0:T(1,128)} %ids_ref.1), channel_id=1, source_target_pairs={{0,4},{1,5},{2,6},{3,7},{4,0},{5,1},{6,2},{7,3},{8,12},{9,13},{10,... | collective-permute-start | bytes 776 | tf_op jit(solution)/shard_map/ppermute | solution.py:35
  4.0 15.8 %collective-permute-start.4 = (bf16[64,1024]{1,0:T(8,128)(2,1)}, bf16[64,1024]{1,0:T(8,128)(2,1)S(1)}, u32[]{:S(2)}, u32[]{:S(2)}) collective-permute-start(bf16[64,1024]{1,0:T(8,128)(2,1)} %refs_0_.5), channel_id=1, source_target_pairs={{0,7},{1,6},{2,5},{3,4},{4,3},{5,2},{6,1},{7,0},{8,14},{9,15},{10,... | collective-permute-start | bytes 393224 | tf_op jit(solution)/shard_map/ppermute | solution.py:43
  6.3 7.5 %collective-permute-start.2 = (bf16[64,1024]{1,0:T(8,128)(2,1)}, bf16[64,1024]{1,0:T(8,128)(2,1)S(1)}, u32[]{:S(2)}, u32[]{:S(2)}) collective-permute-start(bf16[64,1024]{1,0:T(8,128)(2,1)} %refs_0_.5), channel_id=1, source_target_pairs={{0,1},{1,0},{2,3},{3,2},{4,5},{5,4},{6,7},{7,6},{8,11},{9,10},{10,... | collective-permute-start | bytes 393224 | tf_op jit(solution)/shard_map/ppermute | solution.py:43
  6.8 10.4 %collective-permute-start.1 = (bf16[64,1024]{1,0:T(8,128)(2,1)}, bf16[64,1024]{1,0:T(8,128)(2,1)S(1)}, u32[]{:S(2)}, u32[]{:S(2)}) collective-permute-start(bf16[64,1024]{1,0:T(8,128)(2,1)} %refs_0_.5), channel_id=1, source_target_pairs={{0,2},{1,3},{2,0},{3,1},{4,6},{5,7},{6,4},{7,5},{8,10},{9,11},{10,... | collective-permute-start | bytes 393224 | tf_op jit(solution)/shard_map/ppermute | solution.py:35
  7.1 12.7 %collective-permute-start.5 = (bf16[64,1024]{1,0:T(8,128)(2,1)}, bf16[64,1024]{1,0:T(8,128)(2,1)S(1)}, u32[]{:S(2)}, u32[]{:S(2)}) collective-permute-start(bf16[64,1024]{1,0:T(8,128)(2,1)} %refs_0_.5), channel_id=1, source_target_pairs={{0,4},{1,5},{2,6},{3,7},{4,0},{5,1},{6,2},{7,3},{8,13},{9,12},{10,... | collective-permute-start | bytes 393224 | tf_op jit(solution)/shard_map/ppermute | solution.py:43
  10.5 6.7 %copy-start = (bf16[1024,1024]{1,0:T(8,128)(2,1)S(1)}, bf16[1024,1024]{1,0:T(8,128)(2,1)}, u32[]{:S(2)}) copy-start(bf16[1024,1024]{1,0:T(8,128)(2,1)} %w_query_ref.1) | copy-start | bytes 6291460
  10.6 6.7 %copy-start.2 = (bf16[1,512,1024]{2,1,0:T(8,128)(2,1)S(1)}, bf16[1,512,1024]{2,1,0:T(8,128)(2,1)}, u32[]{:S(2)}) copy-start(bf16[1,512,1024]{2,1,0:T(8,128)(2,1)} %keys_ref.3) | copy-start | bytes 3145732
  10.6 6.7 %copy-start.5 = (bf16[1,512,1024]{2,1,0:T(8,128)(2,1)S(1)}, bf16[1,512,1024]{2,1,0:T(8,128)(2,1)}, u32[]{:S(2)}) copy-start(bf16[1,512,1024]{2,1,0:T(8,128)(2,1)} %values_ref.1) | copy-start | bytes 3145732
  10.6 6.7 %copy-start.6 = (bf16[64,1024]{1,0:T(8,128)(2,1)S(1)}, bf16[64,1024]{1,0:T(8,128)(2,1)}, u32[]{:S(2)}) copy-start(bf16[64,1024]{1,0:T(8,128)(2,1)} %refs_0_.5) | copy-start | bytes 393220
  10.6 0.8 %copy-start.8 = (s32[1,64]{1,0:T(1,128)S(1)}, s32[1,64]{1,0:T(1,128)}, u32[]{:S(2)}) copy-start(s32[1,64]{1,0:T(1,128)} %ids_ref.1) | copy-start | bytes 772
  11.4 8.4 %collective-permute-start.3 = (s32[2,64]{1,0:T(2,128)S(1)}, s32[2,64]{1,0:T(2,128)S(1)}, u32[]{:S(2)}, u32[]{:S(2)}) collective-permute-start(s32[2,64]{1,0:T(2,128)S(1)} %stack.2.refs_0_), channel_id=1, source_target_pairs={{0,1},{1,0},{2,3},{3,2},{4,5},{5,4},{6,7},{7,6},{8,9},{9,8},{10,11... | collective-permute-start | bytes 1544 | tf_op jit(solution)/shard_map/ppermute | solution.py:35
  19.8 1.6 %collective-permute-start.8 = (bf16[64,1024]{1,0:T(8,128)(2,1)S(1)}, bf16[64,1024]{1,0:T(8,128)(2,1)S(1)}, u32[]{:S(2)}, u32[]{:S(2)}) collective-permute-start(bf16[64,1024]{1,0:T(8,128)(2,1)S(1)} %collective-permute-done.4.refs_1_.refs_4_), channel_id=1, source_target_pairs={{8,0},{0,8},{9,1},{1,9},{10,2},{2,10},{11,3},{3,11},{12,4},{4,12},... | collective-permute-start | bytes 393224 | tf_op jit(solution)/shard_map/ppermute | solution.py:48
  20.4 1.3 %collective-permute-start.9 = (bf16[64,1024]{1,0:T(8,128)(2,1)S(1)}, bf16[64,1024]{1,0:T(8,128)(2,1)S(1)}, u32[]{:S(2)}, u32[]{:S(2)}) collective-permute-start(bf16[64,1024]{1,0:T(8,128)(2,1)S(1)} %collective-permute-done.5.refs_3_.refs_6_), channel_id=1, source_target_pairs={{8,0},{0,8},{9,1},{1,9},{10,2},{2,10},{11,3},{3,11},{12,4},{4,12},... | collective-permute-start | bytes 393224 | tf_op jit(solution)/shard_map/ppermute | solution.py:48
  20.5 1.5 %collective-permute-start.7 = (bf16[64,1024]{1,0:T(8,128)(2,1)S(1)}, bf16[64,1024]{1,0:T(8,128)(2,1)S(1)}, u32[]{:S(2)}, u32[]{:S(2)}) collective-permute-start(bf16[64,1024]{1,0:T(8,128)(2,1)S(1)} %collective-permute-done.2.refs_2_), channel_id=1, source_target_pairs={{8,0},{0,8},{9,1},{1,9},{10,2},{2,10},{11,3},{3,11},{12,4},{4,12},... | collective-permute-start | bytes 393224 | tf_op jit(solution)/shard_map/ppermute | solution.py:48
  20.9 3.6 %collective-permute-start.6 = (s32[4,64]{1,0:T(4,128)S(1)}, s32[4,64]{1,0:T(4,128)S(1)}, u32[]{:S(2)}, u32[]{:S(2)}) collective-permute-start(s32[4,64]{1,0:T(4,128)S(1)} %stack.3.near_ids_ref), channel_id=1, source_target_pairs={{0,2},{1,3},{2,0},{3,1},{4,6},{5,7},{6,4},{7,5},{8,10},{9,11},{10,... | collective-permute-start | bytes 3080 | tf_op jit(solution)/shard_map/ppermute | solution.py:35
  22.0 3.4 %copy-start.1 = (bf16[1,2,1024,1024]{3,2,1,0:T(8,128)(2,1)S(1)}, bf16[1,2,1024,1024]{3,2,1,0:T(8,128)(2,1)}, u32[]{:S(2)}) copy-start(bf16[1,2,1024,1024]{3,2,1,0:T(8,128)(2,1)} %refs_4_.1) | copy-start | bytes 12582916
  22.0 5.2 %copy-start.3 = (bf16[1024,1024]{1,0:T(8,128)(2,1)S(1)}, bf16[1024,1024]{1,0:T(8,128)(2,1)}, u32[]{:S(2)}) copy-start(bf16[1024,1024]{1,0:T(8,128)(2,1)} %w_gate_ref.1) | copy-start | bytes 6291460
  22.0 5.2 %copy-start.9 = (s32[1,64]{1,0:T(1,128)S(1)}, s32[1,64]{1,0:T(1,128)}, u32[]{:S(2)}) copy-start(s32[1,64]{1,0:T(1,128)} %ids_ref.1) | copy-start | bytes 772
  25.4 22.3 %collective-permute-start.16 = (bf16[1,2,1024,1024]{3,2,1,0:T(8,128)(2,1)S(1)}, bf16[1,2,1024,1024]{3,2,1,0:T(8,128)(2,1)S(1)}, u32[]{:S(2)}, u32[]{:S(2)}) collective-permute-start(bf16[1,2,1024,1024]{3,2,1,0:T(8,128)(2,1)S(1)} %copy-done.1), channel_id=1, source_target_pairs={{8,0},{0,8},{9,1},{1,9},{10,2},{2,10},{11,3},{3,11},{12,4},{4,12},... | collective-permute-start | bytes 12582920 | tf_op jit(solution)/shard_map/ppermute | solution.py:48
  25.7 8.4 %collective-permute-start.10 = (bf16[256,512]{1,0:T(8,128)(2,1)S(1)}, bf16[256,512]{1,0:T(8,128)(2,1)S(1)}, u32[]{:S(2)}, u32[]{:S(2)}) collective-permute-start(bf16[256,512]{1,0:T(8,128)(2,1)S(1)} %get-tuple-element.48), channel_id=1, source_target_pairs={{0,1},{1,0},{2,3},{3,2},{4,5},{5,4},{6,7},{7,6},{8,9},{9,8},{10,11... | collective-permute-start | bytes 786440 | tf_op jit(solution)/shard_map/ppermute | solution.py:35
  26.4 21.2 %copy-start.4 = (bf16[1024,1024]{1,0:T(8,128)(2,1)S(1)}, bf16[1024,1024]{1,0:T(8,128)(2,1)}, u32[]{:S(2)}) copy-start(bf16[1024,1024]{1,0:T(8,128)(2,1)} %w_out_ref.1) | copy-start | bytes 6291460
  26.4 21.2 %copy-start.7 = (f32[1024]{0:T(1024)S(1)}, f32[1024]{0:T(1024)}, u32[]{:S(2)}) copy-start(f32[1024]{0:T(1024)} %param.22) | copy-start | bytes 12292
  26.4 21.2 %copy-start.10 = (s32[1,64]{1,0:T(1,128)S(1)}, s32[1,64]{1,0:T(1,128)}, u32[]{:S(2)}) copy-start(s32[1,64]{1,0:T(1,128)} %domain_ref.1) | copy-start | bytes 772
  26.4 8.3 %collective-permute-start.11 = (bf16[256,512]{1,0:T(8,128)(2,1)S(1)}, bf16[256,512]{1,0:T(8,128)(2,1)S(1)}, u32[]{:S(2)}, u32[]{:S(2)}) collective-permute-start(bf16[256,512]{1,0:T(8,128)(2,1)S(1)} %get-tuple-element.49), channel_id=1, source_target_pairs={{0,2},{1,3},{2,0},{3,1},{4,6},{5,7},{6,4},{7,5},{8,10},{9,11},{10,... | collective-permute-start | bytes 786440 | tf_op jit(solution)/shard_map/ppermute | solution.py:35
  34.7 5.0 %collective-permute-start.14 = (bf16[128,512]{1,0:T(8,128)(2,1)S(1)}, bf16[128,512]{1,0:T(8,128)(2,1)S(1)}, u32[]{:S(2)}, u32[]{:S(2)}) collective-permute-start(bf16[128,512]{1,0:T(8,128)(2,1)S(1)} %get-tuple-element.63), channel_id=1, source_target_pairs={{0,1},{1,0},{2,3},{3,2},{4,5},{5,4},{6,7},{7,6},{8,9},{9,8},{10,11... | collective-permute-start | bytes 393224 | tf_op jit(solution)/shard_map/ppermute | solution.py:35
  36.1 5.6 %collective-permute-start.12 = (bf16[128,512]{1,0:T(8,128)(2,1)S(1)}, bf16[128,512]{1,0:T(8,128)(2,1)S(1)}, u32[]{:S(2)}, u32[]{:S(2)}) collective-permute-start(bf16[128,512]{1,0:T(8,128)(2,1)S(1)} %get-tuple-element.57), channel_id=1, source_target_pairs={{0,2},{1,3},{2,0},{3,1},{4,6},{5,7},{6,4},{7,5},{8,10},{9,11},{10,... | collective-permute-start | bytes 393224 | tf_op jit(solution)/shard_map/ppermute | solution.py:35
  39.8 6.2 %collective-permute-start.15 = (bf16[64,512]{1,0:T(8,128)(2,1)S(1)}, bf16[64,512]{1,0:T(8,128)(2,1)S(1)}, u32[]{:S(2)}, u32[]{:S(2)}) collective-permute-start(bf16[64,512]{1,0:T(8,128)(2,1)S(1)} %get-tuple-element.65), channel_id=1, source_target_pairs={{0,4},{1,5},{2,6},{3,7},{4,0},{5,1},{6,2},{7,3},{8,12},{9,13},{10,... | collective-permute-start | bytes 196616 | tf_op jit(solution)/shard_map/ppermute | solution.py:35
  41.7 5.9 %collective-permute-start.13 = (bf16[64,512]{1,0:T(8,128)(2,1)S(1)}, bf16[64,512]{1,0:T(8,128)(2,1)S(1)}, u32[]{:S(2)}, u32[]{:S(2)}) collective-permute-start(bf16[64,512]{1,0:T(8,128)(2,1)S(1)} %get-tuple-element.59), channel_id=1, source_target_pairs={{0,4},{1,5},{2,6},{3,7},{4,0},{5,1},{6,2},{7,3},{8,12},{9,13},{10,... | collective-permute-start | bytes 196616 | tf_op jit(solution)/shard_map/ppermute | solution.py:35

commit v9 on v8

--- a/solution.py
+++ b/solution.py
@@ -310,7 +310,7 @@
     bits = hist_devices.bit_length() - 1
     others = range(1, users)
 
-    shared = hist_devices // 4
+    shared = 1
     far = list(range(hist_devices - 1, hist_devices // 2 - 1, -1))
     near = [flip for flip in range(1, hist_devices // 2) if flip != shared]
     far_flips = [tuple(far[at : at + users][:: (-1) ** (at // users)]) for at in range(0, len(far), users)]
@@ -319,7 +319,7 @@
     near_shards = [swapped_by_user(item_table, flips) for flips in near_flips]
     shared_shard = swapped(item_table, shared)
 
-    turns = [bits - 1, 0] + list(range(1, bits - 1))
+    turns = [1] + list(range(2, bits)) + [0]
     far_ids, id_flips = swapped(item_ids, 1 << turns[0]), [0, 1 << turns[0]]
 
     first_pieces = [((flip,) * users, 0, None) for flip in (0, shared)] + [(flips, 0, None) for flips in near_flips]

time: 50.6 us -> 48 us (0.949)
  waiting for transfers between devices: 18.7 us -> 14.8 us
  starting transfers between devices: 19.8 us -> 21 us
    ppermute x10, waiting for transfers between devices: 16.7 us -> 12.6 us  [swapped(): return lax.ppermute(value, 'hist', [(i, i ^ flip) for i in range(count)])]
    ppermute x10, starting transfers between devices: 12.7 us -> 14.7 us  [swapped(): return lax.ppermute(value, 'hist', [(i, i ^ flip) for i in range(count)])]
    ppermute x3, waiting for transfers between devices: 0.92 us -> 1.91 us  [swapped_by_user(): return lax.ppermute(value, ('user', 'hist'), pairs)]
    ppermute x4, waiting for transfers between devices: 1.02 us -> 0.29 us  [from_user(): lax.ppermute(value, 'user', [((i + steps) % count, i) for i in range(coun...]
    ppermute x4, starting transfers between devices: 1.47 us -> 0.89 us  [from_user(): lax.ppermute(value, 'user', [((i + steps) % count, i) for i in range(coun...]
  transfers between devices with their start and end apart: 17 -> 17, of which waited for: 11 -> 8; matrix products, arithmetic and copies ran while one was open for 0% -> 0% of each run, Pallas kernels for 12% -> 13%
where the time goes in v9:
time: 48 us; the launch traced here: 47.9 us
  starting transfers between devices  21 us (44%)
  waiting for transfers between devices  14.8 us (31%)
  Pallas kernels  9.76 us (20%)
  between operations  1.49 us (3%)
  local copies, waits for them, and re-layouts  0.84 us (2%)
    ppermute x10, starting transfers between devices, swapped(): return lax.ppermute(value, 'hist', [(i, i ^ flip) for i in range(count)])  14.7 us
    ppermute x10, waiting for transfers between devices, swapped(): return lax.ppermute(value, 'hist', [(i, i ^ flip) for i in range(count)])  12.6 us
    ppermute x3, starting transfers between devices, swapped_by_user(): return lax.ppermute(value, ('user', 'hist'), pairs)  5.34 us
    pallas_call x1, Pallas kernels, finish(): kernel_call(functools.partial(finish_kernel, len(pairs)), 'finish', [jax....  2.84 us
    pallas_call x1, Pallas kernels, attend_next(): kernel_call(functools.partial(next_kernel, pieces), 'attend_next', [jax.S...  2.49 us
    pallas_call x1, Pallas kernels, attend_first(): kernel_call(functools.partial(first_kernel, pieces), 'attend_first', [jax...  2.49 us
    ppermute x3, waiting for transfers between devices, swapped_by_user(): return lax.ppermute(value, ('user', 'hist'), pairs)  1.91 us
  transfers between devices with their start and end apart: 17, of which 8 were waited for; matrix products, arithmetic and copies ran while one was open for 0% of the time, Pallas kernels for 13%

profile of v9, /device:TPU:0, one launch (start us, length us, event | category | flops | bytes accessed | tf_op | source)
XLA Modules:
  0.0 47.9 jit_solution(13792024399929880121)
XLA Ops:
  0.0 3.0 %collective-permute-start = (s32[1,64]{1,0:T(1,128)}, s32[1,64]{1,0:T(1,128)S(1)}, u32[]{:S(2)}, u32[]{:S(2)}) collective-permute-start(s32[1,64]{1,0:T(1,128)} %ids_ref.1), channel_id=1, source_target_pairs={{0,2},{1,3},{2,0},{3,1},{4,6},{5,7},{6,4},{7,5},{8,10},{9,11},{10,... | collective-permute-start | bytes 776 | tf_op jit(solution)/shard_map/ppermute | solution.py:35
  3.0 3.4 %collective-permute-start.4 = (bf16[64,1024]{1,0:T(8,128)(2,1)}, bf16[64,1024]{1,0:T(8,128)(2,1)S(1)}, u32[]{:S(2)}, u32[]{:S(2)}) collective-permute-start(bf16[64,1024]{1,0:T(8,128)(2,1)} %refs_0_.5), channel_id=1, source_target_pairs={{0,7},{1,6},{2,5},{3,4},{4,3},{5,2},{6,1},{7,0},{8,14},{9,15},{10,... | collective-permute-start | bytes 393224 | tf_op jit(solution)/shard_map/ppermute | solution.py:43
  6.5 0.7 %collective-permute-start.2 = (bf16[64,1024]{1,0:T(8,128)(2,1)}, bf16[64,1024]{1,0:T(8,128)(2,1)S(1)}, u32[]{:S(2)}, u32[]{:S(2)}) collective-permute-start(bf16[64,1024]{1,0:T(8,128)(2,1)} %refs_0_.5), channel_id=1, source_target_pairs={{0,2},{1,3},{2,0},{3,1},{4,6},{5,7},{6,4},{7,5},{8,11},{9,10},{10,... | collective-permute-start | bytes 393224 | tf_op jit(solution)/shard_map/ppermute | solution.py:43
  7.1 0.5 %collective-permute-start.1 = (bf16[64,1024]{1,0:T(8,128)(2,1)}, bf16[64,1024]{1,0:T(8,128)(2,1)S(1)}, u32[]{:S(2)}, u32[]{:S(2)}) collective-permute-start(bf16[64,1024]{1,0:T(8,128)(2,1)} %refs_0_.5), channel_id=1, source_target_pairs={{0,1},{1,0},{2,3},{3,2},{4,5},{5,4},{6,7},{7,6},{8,9},{9,8},{10,11... | collective-permute-start | bytes 393224 | tf_op jit(solution)/shard_map/ppermute | solution.py:35
  7.6 1.2 %collective-permute-start.5 = (bf16[64,1024]{1,0:T(8,128)(2,1)}, bf16[64,1024]{1,0:T(8,128)(2,1)S(1)}, u32[]{:S(2)}, u32[]{:S(2)}) collective-permute-start(bf16[64,1024]{1,0:T(8,128)(2,1)} %refs_0_.5), channel_id=1, source_target_pairs={{0,4},{1,5},{2,6},{3,7},{4,0},{5,1},{6,2},{7,3},{8,13},{9,12},{10,... | collective-permute-start | bytes 393224 | tf_op jit(solution)/shard_map/ppermute | solution.py:43
  9.5 0.0 copy-start
  9.5 0.0 copy-start.2
  9.5 0.0 copy-start.5
  9.6 0.0 copy-start.6
  9.6 0.0 collective-permute-done.refs_1_
  9.6 0.0 copy-start.8
  9.6 0.8 %copy-done.8 = s32[1,64]{1,0:T(1,128)S(1)} copy-done((s32[1,64]{1,0:T(1,128)S(1)}, s32[1,64]{1,0:T(1,128)}, u32[]{:S(2)}) %copy-start.8) | copy-done | bytes 280
  10.4 1.7 %collective-permute-start.3 = (s32[2,64]{1,0:T(2,128)S(1)}, s32[2,64]{1,0:T(2,128)S(1)}, u32[]{:S(2)}, u32[]{:S(2)}) collective-permute-start(s32[2,64]{1,0:T(2,128)S(1)} %stack.2.refs_0_), channel_id=1, source_target_pairs={{0,4},{1,5},{2,6},{3,7},{4,0},{5,1},{6,2},{7,3},{8,12},{9,13},{10,... | collective-permute-start | bytes 1544 | tf_op jit(solution)/shard_map/ppermute | solution.py:35
  12.1 1.9 %collective-permute-done.2.refs_2_ = bf16[64,1024]{1,0:T(8,128)(2,1)S(1)} collective-permute-done((bf16[64,1024]{1,0:T(8,128)(2,1)}, bf16[64,1024]{1,0:T(8,128)(2,1)S(1)}, u32[]{:S(2)}, u32[]{:S(2)}) %collective-permute-start.2) | collective-permute-done | bytes 131104 | tf_op jit(solution)/shard_map/ppermute | solution.py:43
  14.0 1.5 %collective-permute-done.1.refs_1_ = bf16[64,1024]{1,0:T(8,128)(2,1)S(1)} collective-permute-done((bf16[64,1024]{1,0:T(8,128)(2,1)}, bf16[64,1024]{1,0:T(8,128)(2,1)S(1)}, u32[]{:S(2)}, u32[]{:S(2)}) %collective-permute-start.1) | collective-permute-done | bytes 131104 | tf_op jit(solution)/shard_map/ppermute | solution.py:35
  15.5 0.0 copy-done
  15.6 2.5 %attend_first.1 = (bf16[192,1024]{1,0:T(8,128)(2,1)S(1)}, bf16[512,1024]{1,0:T(8,128)(2,1)S(1)}) custom-call(s32[1]{0:T(128)S(6)} %copy.14.length_ref, bf16[1024,1024]{1,0:T(8,128)(2,1)S(1)} %copy-done, bf16[1,512,1024]{2,1,0:T(8,128)(2,1)S(1)} %copy-done.2, bf16[1,512,1024]{2,1,0:T(8,128)(2,1)S(1)} %copy-done.5, bf16[64,1024]{1,0:T(8,128)(2,1)S(1)} %copy-done.6, ...), custom_call_target="tpu_custom_call" | custom-call | flops 805306368 | tf_op jit(solution)/shard_map/attend_first/pallas_call | solution.py:157
  18.1 0.0 collective-permute-done.3.refs_1_
  18.1 0.0 collective-permute-done.4.refs_1_.refs_4_
  18.1 0.0 collective-permute-done.5.refs_3_.refs_6_
  18.1 0.1 collective-permute-start.8
  18.2 0.5 %collective-permute-start.9 = (bf16[64,1024]{1,0:T(8,128)(2,1)S(1)}, bf16[64,1024]{1,0:T(8,128)(2,1)S(1)}, u32[]{:S(2)}, u32[]{:S(2)}) collective-permute-start(bf16[64,1024]{1,0:T(8,128)(2,1)S(1)} %collective-permute-done.5.refs_3_.refs_6_), channel_id=1, source_target_pairs={{8,0},{0,8},{9,1},{1,9},{10,2},{2,10},{11,3},{3,11},{12,4},{4,12},... | collective-permute-start | bytes 393224 | tf_op jit(solution)/shard_map/ppermute | solution.py:48
  18.7 0.1 collective-permute-start.7
  18.8 1.0 %collective-permute-start.6 = (s32[4,64]{1,0:T(4,128)S(1)}, s32[4,64]{1,0:T(4,128)S(1)}, u32[]{:S(2)}, u32[]{:S(2)}) collective-permute-start(s32[4,64]{1,0:T(4,128)S(1)} %stack.3.near_ids_ref), channel_id=1, source_target_pairs={{0,1},{1,0},{2,3},{3,2},{4,5},{5,4},{6,7},{7,6},{8,9},{9,8},{10,11... | collective-permute-start | bytes 3080 | tf_op jit(solution)/shard_map/ppermute | solution.py:35
  19.7 0.0 collective-permute-done.8.refs_2_.refs_5_
  19.7 0.0 collective-permute-done.9.refs_4_.refs_7_
  19.7 0.3 collective-permute-done.7.refs_0_.refs_3_
  20.0 2.5 %attend_next.1.refs_1_ = bf16[320,1024]{1,0:T(8,128)(2,1)S(1)} custom-call(bf16[1024,1024]{1,0:T(8,128)(2,1)S(1)} %copy-done, bf16[1,512,1024]{2,1,0:T(8,128)(2,1)S(1)} %copy-done.2, bf16[512,1024]{1,0:T(8,128)(2,1)S(1)} %get-tuple-element.44.values_ref, bf16[64,1024]{1,0:T(8,128)(2,1)S(1)} %collective-permute-done.7.refs_0_.refs_3_, ...), custom_call_target="tpu_custom_call" | custom-call | flops 1342177280 | tf_op jit(solution)/shard_map/attend_next/pallas_call | solution.py:168
  22.5 0.0 collective-permute-done.6.far_ids_ref
  22.5 0.9 %place.1 = (bf16[256,512]{1,0:T(8,128)(2,1)S(1)}, bf16[256,512]{1,0:T(8,128)(2,1)S(1)}, bf16[256,512]{1,0:T(8,128)(2,1)S(1)}, bf16[256,512]{1,0:T(8,128)(2,1)S(1)}) custom-call(s32[4,64]{1,0:T(4,128)S(1)} %stack.3.near_ids_ref, s32[4,64]{1,0:T(4,128)S(1)} %collective-permute-done.6.far_ids_ref, bf16[192,1024]{1,0:T(8,128)(2,1)S(1)} %get-tuple-element.43.refs_0_, ...), custom_call_target="tpu_custom_call" | custom-call | flops 536870912 | tf_op jit(solution)/shard_map/place/pallas_call | solution.py:200
  23.4 0.2 collective-permute-start.16
  23.7 1.0 %collective-permute-start.10 = (bf16[256,512]{1,0:T(8,128)(2,1)S(1)}, bf16[256,512]{1,0:T(8,128)(2,1)S(1)}, u32[]{:S(2)}, u32[]{:S(2)}) collective-permute-start(bf16[256,512]{1,0:T(8,128)(2,1)S(1)} %get-tuple-element.48), channel_id=1, source_target_pairs={{0,1},{1,0},{2,3},{3,2},{4,5},{5,4},{6,7},{7,6},{8,9},{9,8},{10,11... | collective-permute-start | bytes 786440 | tf_op jit(solution)/shard_map/ppermute | solution.py:35
  24.7 1.6 %collective-permute-start.11 = (bf16[256,512]{1,0:T(8,128)(2,1)S(1)}, bf16[256,512]{1,0:T(8,128)(2,1)S(1)}, u32[]{:S(2)}, u32[]{:S(2)}) collective-permute-start(bf16[256,512]{1,0:T(8,128)(2,1)S(1)} %get-tuple-element.49), channel_id=1, source_target_pairs={{0,2},{1,3},{2,0},{3,1},{4,6},{5,7},{6,4},{7,5},{8,10},{9,11},{10,... | collective-permute-start | bytes 786440 | tf_op jit(solution)/shard_map/ppermute | solution.py:35
  26.2 0.9 %prepare.1 = (f32[64,1024]{1,0:T(8,128)S(1)}, f32[64,1024]{1,0:T(8,128)S(1)}) custom-call(bf16[256,512]{1,0:T(8,128)(2,1)S(1)} %get-tuple-element.54.after_ref.refs_0_, s32[1,64]{1,0:T(1,128)S(1)} %copy-done.9, bf16[1024,1024]{1,0:T(8,128)(2,1)S(1)} %copy-done.3, bf16[64,1024]{1,0:T(8,128)(2,1)S(1)} %copy-done.6, ...), custom_call_target="tpu_custom_call" | custom-call | flops 201326592 | tf_op jit(solution)/shard_map/prepare/pallas_call | solution.py:245
  27.1 5.1 %collective-permute-done.10.refs_1_ = bf16[256,512]{1,0:T(8,128)(2,1)S(1)} collective-permute-done((bf16[256,512]{1,0:T(8,128)(2,1)S(1)}, bf16[256,512]{1,0:T(8,128)(2,1)S(1)}, u32[]{:S(2)}, u32[]{:S(2)}) %collective-permute-start.10) | collective-permute-done | bytes 262176 | tf_op jit(solution)/shard_map/ppermute | solution.py:35
  32.2 0.7 %collective-permute-done.11.refs_1_ = bf16[256,512]{1,0:T(8,128)(2,1)S(1)} collective-permute-done((bf16[256,512]{1,0:T(8,128)(2,1)S(1)}, bf16[256,512]{1,0:T(8,128)(2,1)S(1)}, u32[]{:S(2)}, u32[]{:S(2)}) %collective-permute-start.11) | collective-permute-done | bytes 262176 | tf_op jit(solution)/shard_map/ppermute | solution.py:35
  32.9 0.1 fold.6
  33.0 1.1 %collective-permute-start.14 = (bf16[128,512]{1,0:T(8,128)(2,1)S(1)}, bf16[128,512]{1,0:T(8,128)(2,1)S(1)}, u32[]{:S(2)}, u32[]{:S(2)}) collective-permute-start(bf16[128,512]{1,0:T(8,128)(2,1)S(1)} %get-tuple-element.63), channel_id=1, source_target_pairs={{0,1},{1,0},{2,3},{3,2},{4,5},{5,4},{6,7},{7,6},{8,9},{9,8},{10,11... | collective-permute-start | bytes 393224 | tf_op jit(solution)/shard_map/ppermute | solution.py:35
  34.1 0.1 fold.4
  34.2 1.8 %collective-permute-start.12 = (bf16[128,512]{1,0:T(8,128)(2,1)S(1)}, bf16[128,512]{1,0:T(8,128)(2,1)S(1)}, u32[]{:S(2)}, u32[]{:S(2)}) collective-permute-start(bf16[128,512]{1,0:T(8,128)(2,1)S(1)} %get-tuple-element.57), channel_id=1, source_target_pairs={{0,2},{1,3},{2,0},{3,1},{4,6},{5,7},{6,4},{7,5},{8,10},{9,11},{10,... | collective-permute-start | bytes 393224 | tf_op jit(solution)/shard_map/ppermute | solution.py:35
  36.0 2.0 %collective-permute-done.14.refs_1_ = bf16[128,512]{1,0:T(8,128)(2,1)S(1)} collective-permute-done((bf16[128,512]{1,0:T(8,128)(2,1)S(1)}, bf16[128,512]{1,0:T(8,128)(2,1)S(1)}, u32[]{:S(2)}, u32[]{:S(2)}) %collective-permute-start.14) | collective-permute-done | bytes 131104 | tf_op jit(solution)/shard_map/ppermute | solution.py:35
  38.0 1.5 %collective-permute-start.15 = (bf16[64,512]{1,0:T(8,128)(2,1)S(1)}, bf16[64,512]{1,0:T(8,128)(2,1)S(1)}, u32[]{:S(2)}, u32[]{:S(2)}) collective-permute-start(bf16[64,512]{1,0:T(8,128)(2,1)S(1)} %get-tuple-element.65), channel_id=1, source_target_pairs={{0,4},{1,5},{2,6},{3,7},{4,0},{5,1},{6,2},{7,3},{8,12},{9,13},{10,... | collective-permute-start | bytes 196616 | tf_op jit(solution)/shard_map/ppermute | solution.py:35
  39.6 0.0 collective-permute-done.12.refs_1_
  39.6 1.5 %collective-permute-start.13 = (bf16[64,512]{1,0:T(8,128)(2,1)S(1)}, bf16[64,512]{1,0:T(8,128)(2,1)S(1)}, u32[]{:S(2)}, u32[]{:S(2)}) collective-permute-start(bf16[64,512]{1,0:T(8,128)(2,1)S(1)} %get-tuple-element.59), channel_id=1, source_target_pairs={{0,4},{1,5},{2,6},{3,7},{4,0},{5,1},{6,2},{7,3},{8,12},{9,13},{10,... | collective-permute-start | bytes 196616 | tf_op jit(solution)/shard_map/ppermute | solution.py:35
  41.8 1.7 %collective-permute-done.15.refs_3_ = bf16[64,512]{1,0:T(8,128)(2,1)S(1)} collective-permute-done((bf16[64,512]{1,0:T(8,128)(2,1)S(1)}, bf16[64,512]{1,0:T(8,128)(2,1)S(1)}, u32[]{:S(2)}, u32[]{:S(2)}) %collective-permute-start.15) | collective-permute-done | bytes 65568 | tf_op jit(solution)/shard_map/ppermute | solution.py:35
  43.5 1.5 %collective-permute-done.13.refs_1_ = bf16[64,512]{1,0:T(8,128)(2,1)S(1)} collective-permute-done((bf16[64,512]{1,0:T(8,128)(2,1)S(1)}, bf16[64,512]{1,0:T(8,128)(2,1)S(1)}, u32[]{:S(2)}, u32[]{:S(2)}) %collective-permute-start.13) | collective-permute-done | bytes 65568 | tf_op jit(solution)/shard_map/ppermute | solution.py:35
  45.0 0.0 collective-permute-done.16.refs_5_
  45.0 2.8 %finish.1 = bf16[1,64,1024]{2,1,0:T(8,128)(2,1)} custom-call(f32[64,1024]{1,0:T(8,128)S(1)} %get-tuple-element.52.embed_ref, f32[64,1024]{1,0:T(8,128)S(1)} %get-tuple-element.53.gating_ref, f32[1,1024]{1,0:T(1,128)S(1)} %bitcast.1, s32[1]{0:T(128)S(6)} %copy.13.count_ref, s32[1,64]{1,0:T(1,128)S(1)} %copy-done.10, bf16[1024,1024]{1,0:T(8,128)(2,1)S(1)} %copy-done.4, ...), custom_call_target="tpu_custom_call" | custom-call | flops 671088640 | tf_op jit(solution)/shard_map/finish/pallas_call | solution.py:284
  (19 shorter events, 0.1 us)
Async XLA Ops:
  0.0 9.6 %collective-permute-start = (s32[1,64]{1,0:T(1,128)}, s32[1,64]{1,0:T(1,128)S(1)}, u32[]{:S(2)}, u32[]{:S(2)}) collective-permute-start(s32[1,64]{1,0:T(1,128)} %ids_ref.1), channel_id=1, source_target_pairs={{0,2},{1,3},{2,0},{3,1},{4,6},{5,7},{6,4},{7,5},{8,10},{9,11},{10,... | collective-permute-start | bytes 776 | tf_op jit(solution)/shard_map/ppermute | solution.py:35
  3.0 15.1 %collective-permute-start.4 = (bf16[64,1024]{1,0:T(8,128)(2,1)}, bf16[64,1024]{1,0:T(8,128)(2,1)S(1)}, u32[]{:S(2)}, u32[]{:S(2)}) collective-permute-start(bf16[64,1024]{1,0:T(8,128)(2,1)} %refs_0_.5), channel_id=1, source_target_pairs={{0,7},{1,6},{2,5},{3,4},{4,3},{5,2},{6,1},{7,0},{8,14},{9,15},{10,... | collective-permute-start | bytes 393224 | tf_op jit(solution)/shard_map/ppermute | solution.py:43
  6.5 7.5 %collective-permute-start.2 = (bf16[64,1024]{1,0:T(8,128)(2,1)}, bf16[64,1024]{1,0:T(8,128)(2,1)S(1)}, u32[]{:S(2)}, u32[]{:S(2)}) collective-permute-start(bf16[64,1024]{1,0:T(8,128)(2,1)} %refs_0_.5), channel_id=1, source_target_pairs={{0,2},{1,3},{2,0},{3,1},{4,6},{5,7},{6,4},{7,5},{8,11},{9,10},{10,... | collective-permute-start | bytes 393224 | tf_op jit(solution)/shard_map/ppermute | solution.py:43
  7.1 8.4 %collective-permute-start.1 = (bf16[64,1024]{1,0:T(8,128)(2,1)}, bf16[64,1024]{1,0:T(8,128)(2,1)S(1)}, u32[]{:S(2)}, u32[]{:S(2)}) collective-permute-start(bf16[64,1024]{1,0:T(8,128)(2,1)} %refs_0_.5), channel_id=1, source_target_pairs={{0,1},{1,0},{2,3},{3,2},{4,5},{5,4},{6,7},{7,6},{8,9},{9,8},{10,11... | collective-permute-start | bytes 393224 | tf_op jit(solution)/shard_map/ppermute | solution.py:35
  7.6 10.4 %collective-permute-start.5 = (bf16[64,1024]{1,0:T(8,128)(2,1)}, bf16[64,1024]{1,0:T(8,128)(2,1)S(1)}, u32[]{:S(2)}, u32[]{:S(2)}) collective-permute-start(bf16[64,1024]{1,0:T(8,128)(2,1)} %refs_0_.5), channel_id=1, source_target_pairs={{0,4},{1,5},{2,6},{3,7},{4,0},{5,1},{6,2},{7,3},{8,13},{9,12},{10,... | collective-permute-start | bytes 393224 | tf_op jit(solution)/shard_map/ppermute | solution.py:43
  9.5 6.0 %copy-start = (bf16[1024,1024]{1,0:T(8,128)(2,1)S(1)}, bf16[1024,1024]{1,0:T(8,128)(2,1)}, u32[]{:S(2)}) copy-start(bf16[1024,1024]{1,0:T(8,128)(2,1)} %w_query_ref.1) | copy-start | bytes 6291460
  9.5 6.0 %copy-start.2 = (bf16[1,512,1024]{2,1,0:T(8,128)(2,1)S(1)}, bf16[1,512,1024]{2,1,0:T(8,128)(2,1)}, u32[]{:S(2)}) copy-start(bf16[1,512,1024]{2,1,0:T(8,128)(2,1)} %keys_ref.3) | copy-start | bytes 3145732
  9.5 6.0 %copy-start.5 = (bf16[1,512,1024]{2,1,0:T(8,128)(2,1)S(1)}, bf16[1,512,1024]{2,1,0:T(8,128)(2,1)}, u32[]{:S(2)}) copy-start(bf16[1,512,1024]{2,1,0:T(8,128)(2,1)} %values_ref.1) | copy-start | bytes 3145732
  9.6 6.0 %copy-start.6 = (bf16[64,1024]{1,0:T(8,128)(2,1)S(1)}, bf16[64,1024]{1,0:T(8,128)(2,1)}, u32[]{:S(2)}) copy-start(bf16[64,1024]{1,0:T(8,128)(2,1)} %refs_0_.5) | copy-start | bytes 393220
  9.6 0.8 %copy-start.8 = (s32[1,64]{1,0:T(1,128)S(1)}, s32[1,64]{1,0:T(1,128)}, u32[]{:S(2)}) copy-start(s32[1,64]{1,0:T(1,128)} %ids_ref.1) | copy-start | bytes 772
  10.4 7.7 %collective-permute-start.3 = (s32[2,64]{1,0:T(2,128)S(1)}, s32[2,64]{1,0:T(2,128)S(1)}, u32[]{:S(2)}, u32[]{:S(2)}) collective-permute-start(s32[2,64]{1,0:T(2,128)S(1)} %stack.2.refs_0_), channel_id=1, source_target_pairs={{0,4},{1,5},{2,6},{3,7},{4,0},{5,1},{6,2},{7,3},{8,12},{9,13},{10,... | collective-permute-start | bytes 1544 | tf_op jit(solution)/shard_map/ppermute | solution.py:35
  18.1 1.6 %collective-permute-start.8 = (bf16[64,1024]{1,0:T(8,128)(2,1)S(1)}, bf16[64,1024]{1,0:T(8,128)(2,1)S(1)}, u32[]{:S(2)}, u32[]{:S(2)}) collective-permute-start(bf16[64,1024]{1,0:T(8,128)(2,1)S(1)} %collective-permute-done.4.refs_1_.refs_4_), channel_id=1, source_target_pairs={{8,0},{0,8},{9,1},{1,9},{10,2},{2,10},{11,3},{3,11},{12,4},{4,12},... | collective-permute-start | bytes 393224 | tf_op jit(solution)/shard_map/ppermute | solution.py:48
  18.2 1.6 %collective-permute-start.9 = (bf16[64,1024]{1,0:T(8,128)(2,1)S(1)}, bf16[64,1024]{1,0:T(8,128)(2,1)S(1)}, u32[]{:S(2)}, u32[]{:S(2)}) collective-permute-start(bf16[64,1024]{1,0:T(8,128)(2,1)S(1)} %collective-permute-done.5.refs_3_.refs_6_), channel_id=1, source_target_pairs={{8,0},{0,8},{9,1},{1,9},{10,2},{2,10},{11,3},{3,11},{12,4},{4,12},... | collective-permute-start | bytes 393224 | tf_op jit(solution)/shard_map/ppermute | solution.py:48
  18.7 1.3 %collective-permute-start.7 = (bf16[64,1024]{1,0:T(8,128)(2,1)S(1)}, bf16[64,1024]{1,0:T(8,128)(2,1)S(1)}, u32[]{:S(2)}, u32[]{:S(2)}) collective-permute-start(bf16[64,1024]{1,0:T(8,128)(2,1)S(1)} %collective-permute-done.2.refs_2_), channel_id=1, source_target_pairs={{8,0},{0,8},{9,1},{1,9},{10,2},{2,10},{11,3},{3,11},{12,4},{4,12},... | collective-permute-start | bytes 393224 | tf_op jit(solution)/shard_map/ppermute | solution.py:48
  18.8 3.8 %collective-permute-start.6 = (s32[4,64]{1,0:T(4,128)S(1)}, s32[4,64]{1,0:T(4,128)S(1)}, u32[]{:S(2)}, u32[]{:S(2)}) collective-permute-start(s32[4,64]{1,0:T(4,128)S(1)} %stack.3.near_ids_ref), channel_id=1, source_target_pairs={{0,1},{1,0},{2,3},{3,2},{4,5},{5,4},{6,7},{7,6},{8,9},{9,8},{10,11... | collective-permute-start | bytes 3080 | tf_op jit(solution)/shard_map/ppermute | solution.py:35
  20.0 3.4 %copy-start.1 = (bf16[1,2,1024,1024]{3,2,1,0:T(8,128)(2,1)S(1)}, bf16[1,2,1024,1024]{3,2,1,0:T(8,128)(2,1)}, u32[]{:S(2)}) copy-start(bf16[1,2,1024,1024]{3,2,1,0:T(8,128)(2,1)} %refs_4_.1) | copy-start | bytes 12582916
  20.0 6.2 %copy-start.3 = (bf16[1024,1024]{1,0:T(8,128)(2,1)S(1)}, bf16[1024,1024]{1,0:T(8,128)(2,1)}, u32[]{:S(2)}) copy-start(bf16[1024,1024]{1,0:T(8,128)(2,1)} %w_gate_ref.1) | copy-start | bytes 6291460
  20.0 6.2 %copy-start.9 = (s32[1,64]{1,0:T(1,128)S(1)}, s32[1,64]{1,0:T(1,128)}, u32[]{:S(2)}) copy-start(s32[1,64]{1,0:T(1,128)} %ids_ref.1) | copy-start | bytes 772
  23.4 21.6 %collective-permute-start.16 = (bf16[1,2,1024,1024]{3,2,1,0:T(8,128)(2,1)S(1)}, bf16[1,2,1024,1024]{3,2,1,0:T(8,128)(2,1)S(1)}, u32[]{:S(2)}, u32[]{:S(2)}) collective-permute-start(bf16[1,2,1024,1024]{3,2,1,0:T(8,128)(2,1)S(1)} %copy-done.1), channel_id=1, source_target_pairs={{8,0},{0,8},{9,1},{1,9},{10,2},{2,10},{11,3},{3,11},{12,4},{4,12},... | collective-permute-start | bytes 12582920 | tf_op jit(solution)/shard_map/ppermute | solution.py:48
  23.7 8.5 %collective-permute-start.10 = (bf16[256,512]{1,0:T(8,128)(2,1)S(1)}, bf16[256,512]{1,0:T(8,128)(2,1)S(1)}, u32[]{:S(2)}, u32[]{:S(2)}) collective-permute-start(bf16[256,512]{1,0:T(8,128)(2,1)S(1)} %get-tuple-element.48), channel_id=1, source_target_pairs={{0,1},{1,0},{2,3},{3,2},{4,5},{5,4},{6,7},{7,6},{8,9},{9,8},{10,11... | collective-permute-start | bytes 786440 | tf_op jit(solution)/shard_map/ppermute | solution.py:35
  24.6 20.4 %copy-start.4 = (bf16[1024,1024]{1,0:T(8,128)(2,1)S(1)}, bf16[1024,1024]{1,0:T(8,128)(2,1)}, u32[]{:S(2)}) copy-start(bf16[1024,1024]{1,0:T(8,128)(2,1)} %w_out_ref.1) | copy-start | bytes 6291460
  24.6 20.4 %copy-start.7 = (f32[1024]{0:T(1024)S(1)}, f32[1024]{0:T(1024)}, u32[]{:S(2)}) copy-start(f32[1024]{0:T(1024)} %param.22) | copy-start | bytes 12292
  24.7 20.4 %copy-start.10 = (s32[1,64]{1,0:T(1,128)S(1)}, s32[1,64]{1,0:T(1,128)}, u32[]{:S(2)}) copy-start(s32[1,64]{1,0:T(1,128)} %domain_ref.1) | copy-start | bytes 772
  24.7 8.3 %collective-permute-start.11 = (bf16[256,512]{1,0:T(8,128)(2,1)S(1)}, bf16[256,512]{1,0:T(8,128)(2,1)S(1)}, u32[]{:S(2)}, u32[]{:S(2)}) collective-permute-start(bf16[256,512]{1,0:T(8,128)(2,1)S(1)} %get-tuple-element.49), channel_id=1, source_target_pairs={{0,2},{1,3},{2,0},{3,1},{4,6},{5,7},{6,4},{7,5},{8,10},{9,11},{10,... | collective-permute-start | bytes 786440 | tf_op jit(solution)/shard_map/ppermute | solution.py:35
  33.0 5.0 %collective-permute-start.14 = (bf16[128,512]{1,0:T(8,128)(2,1)S(1)}, bf16[128,512]{1,0:T(8,128)(2,1)S(1)}, u32[]{:S(2)}, u32[]{:S(2)}) collective-permute-start(bf16[128,512]{1,0:T(8,128)(2,1)S(1)} %get-tuple-element.63), channel_id=1, source_target_pairs={{0,1},{1,0},{2,3},{3,2},{4,5},{5,4},{6,7},{7,6},{8,9},{9,8},{10,11... | collective-permute-start | bytes 393224 | tf_op jit(solution)/shard_map/ppermute | solution.py:35
  34.2 5.4 %collective-permute-start.12 = (bf16[128,512]{1,0:T(8,128)(2,1)S(1)}, bf16[128,512]{1,0:T(8,128)(2,1)S(1)}, u32[]{:S(2)}, u32[]{:S(2)}) collective-permute-start(bf16[128,512]{1,0:T(8,128)(2,1)S(1)} %get-tuple-element.57), channel_id=1, source_target_pairs={{0,2},{1,3},{2,0},{3,1},{4,6},{5,7},{6,4},{7,5},{8,10},{9,11},{10,... | collective-permute-start | bytes 393224 | tf_op jit(solution)/shard_map/ppermute | solution.py:35
  38.0 5.5 %collective-permute-start.15 = (bf16[64,512]{1,0:T(8,128)(2,1)S(1)}, bf16[64,512]{1,0:T(8,128)(2,1)S(1)}, u32[]{:S(2)}, u32[]{:S(2)}) collective-permute-start(bf16[64,512]{1,0:T(8,128)(2,1)S(1)} %get-tuple-element.65), channel_id=1, source_target_pairs={{0,4},{1,5},{2,6},{3,7},{4,0},{5,1},{6,2},{7,3},{8,12},{9,13},{10,... | collective-permute-start | bytes 196616 | tf_op jit(solution)/shard_map/ppermute | solution.py:35
  39.6 5.4 %collective-permute-start.13 = (bf16[64,512]{1,0:T(8,128)(2,1)S(1)}, bf16[64,512]{1,0:T(8,128)(2,1)S(1)}, u32[]{:S(2)}, u32[]{:S(2)}) collective-permute-start(bf16[64,512]{1,0:T(8,128)(2,1)S(1)} %get-tuple-element.59), channel_id=1, source_target_pairs={{0,4},{1,5},{2,6},{3,7},{4,0},{5,1},{6,2},{7,3},{8,12},{9,13},{10,... | collective-permute-start | bytes 196616 | tf_op jit(solution)/shard_map/ppermute | solution.py:35

commit v10 on v9

--- a/solution.py
+++ b/solution.py
@@ -311,7 +311,8 @@
     others = range(1, users)
 
     shared = 1
-    far = list(range(hist_devices - 1, hist_devices // 2 - 1, -1))
+    far = list(range(hist_devices // 2, hist_devices))
+    far = [flip for pair in zip(far[::-1], far) for flip in pair][: len(far)]
     near = [flip for flip in range(1, hist_devices // 2) if flip != shared]
     far_flips = [tuple(far[at : at + users][:: (-1) ** (at // users)]) for at in range(0, len(far), users)]
     near_flips = [tuple(near[at : at + users]) for at in range(0, len(near), users)]

time: 48 us -> 47.8 us (level)
  starting transfers between devices: 21 us -> 20.5 us
    ppermute x10, starting transfers between devices: 14.7 us -> 13.4 us  [swapped(): return lax.ppermute(value, 'hist', [(i, i ^ flip) for i in range(count)])]
    ppermute x3, starting transfers between devices: 5.34 us -> 6.3 us  [swapped_by_user(): return lax.ppermute(value, ('user', 'hist'), pairs)]
    ppermute x3, waiting for transfers between devices: 1.91 us -> 2.8 us  [swapped_by_user(): return lax.ppermute(value, ('user', 'hist'), pairs)]
    ppermute x10, waiting for transfers between devices: 12.6 us -> 11.7 us  [swapped(): return lax.ppermute(value, 'hist', [(i, i ^ flip) for i in range(count)])]
  transfers between devices with their start and end apart: 17 -> 17, of which waited for: 8 -> 10; matrix products, arithmetic and copies ran while one was open for 0% -> 0% of each run, Pallas kernels for 13% -> 13%
where the time goes in v10:
time: 47.8 us; the launch traced here: 47.7 us
  starting transfers between devices  20.5 us (43%)
  waiting for transfers between devices  15.1 us (32%)
  Pallas kernels  9.75 us (20%)
  between operations  1.48 us (3%)
  local copies, waits for them, and re-layouts  0.84 us (2%)
    ppermute x10, starting transfers between devices, swapped(): return lax.ppermute(value, 'hist', [(i, i ^ flip) for i in range(count)])  13.4 us
    ppermute x10, waiting for transfers between devices, swapped(): return lax.ppermute(value, 'hist', [(i, i ^ flip) for i in range(count)])  11.7 us
    ppermute x3, starting transfers between devices, swapped_by_user(): return lax.ppermute(value, ('user', 'hist'), pairs)  6.3 us
    pallas_call x1, Pallas kernels, finish(): kernel_call(functools.partial(finish_kernel, len(pairs)), 'finish', [jax....  2.84 us
    ppermute x3, waiting for transfers between devices, swapped_by_user(): return lax.ppermute(value, ('user', 'hist'), pairs)  2.8 us
    pallas_call x1, Pallas kernels, attend_next(): kernel_call(functools.partial(next_kernel, pieces), 'attend_next', [jax.S...  2.49 us
    pallas_call x1, Pallas kernels, attend_first(): kernel_call(functools.partial(first_kernel, pieces), 'attend_first', [jax...  2.49 us
  transfers between devices with their start and end apart: 17, of which 10 were waited for; matrix products, arithmetic and copies ran while one was open for 0% of the time, Pallas kernels for 13%

profile of v10, /device:TPU:0, one launch (start us, length us, event | category | flops | bytes accessed | tf_op | source)
XLA Modules:
  0.0 47.7 jit_solution(5002621348384772899)
XLA Ops:
  0.0 3.0 %collective-permute-start = (s32[1,64]{1,0:T(1,128)}, s32[1,64]{1,0:T(1,128)S(1)}, u32[]{:S(2)}, u32[]{:S(2)}) collective-permute-start(s32[1,64]{1,0:T(1,128)} %ids_ref.1), channel_id=1, source_target_pairs={{0,2},{1,3},{2,0},{3,1},{4,6},{5,7},{6,4},{7,5},{8,10},{9,11},{10,... | collective-permute-start | bytes 776 | tf_op jit(solution)/shard_map/ppermute | solution.py:35
  3.0 3.4 %collective-permute-start.4 = (bf16[64,1024]{1,0:T(8,128)(2,1)}, bf16[64,1024]{1,0:T(8,128)(2,1)S(1)}, u32[]{:S(2)}, u32[]{:S(2)}) collective-permute-start(bf16[64,1024]{1,0:T(8,128)(2,1)} %refs_0_.5), channel_id=1, source_target_pairs={{0,7},{1,6},{2,5},{3,4},{4,3},{5,2},{6,1},{7,0},{8,12},{9,13},{10,... | collective-permute-start | bytes 393224 | tf_op jit(solution)/shard_map/ppermute | solution.py:43
  6.5 0.7 %collective-permute-start.2 = (bf16[64,1024]{1,0:T(8,128)(2,1)}, bf16[64,1024]{1,0:T(8,128)(2,1)S(1)}, u32[]{:S(2)}, u32[]{:S(2)}) collective-permute-start(bf16[64,1024]{1,0:T(8,128)(2,1)} %refs_0_.5), channel_id=1, source_target_pairs={{0,2},{1,3},{2,0},{3,1},{4,6},{5,7},{6,4},{7,5},{8,11},{9,10},{10,... | collective-permute-start | bytes 393224 | tf_op jit(solution)/shard_map/ppermute | solution.py:43
  7.1 0.5 %collective-permute-start.1 = (bf16[64,1024]{1,0:T(8,128)(2,1)}, bf16[64,1024]{1,0:T(8,128)(2,1)S(1)}, u32[]{:S(2)}, u32[]{:S(2)}) collective-permute-start(bf16[64,1024]{1,0:T(8,128)(2,1)} %refs_0_.5), channel_id=1, source_target_pairs={{0,1},{1,0},{2,3},{3,2},{4,5},{5,4},{6,7},{7,6},{8,9},{9,8},{10,11... | collective-permute-start | bytes 393224 | tf_op jit(solution)/shard_map/ppermute | solution.py:35
  7.6 2.2 %collective-permute-start.5 = (bf16[64,1024]{1,0:T(8,128)(2,1)}, bf16[64,1024]{1,0:T(8,128)(2,1)S(1)}, u32[]{:S(2)}, u32[]{:S(2)}) collective-permute-start(bf16[64,1024]{1,0:T(8,128)(2,1)} %refs_0_.5), channel_id=1, source_target_pairs={{0,5},{1,4},{2,7},{3,6},{4,1},{5,0},{6,3},{7,2},{8,14},{9,15},{10,... | collective-permute-start | bytes 393224 | tf_op jit(solution)/shard_map/ppermute | solution.py:43
  10.5 0.0 copy-start
  10.5 0.0 copy-start.2
  10.5 0.0 copy-start.5
  10.5 0.0 collective-permute-done.refs_1_
  10.5 0.0 copy-start.8
  10.5 0.8 %copy-done.8 = s32[1,64]{1,0:T(1,128)S(1)} copy-done((s32[1,64]{1,0:T(1,128)S(1)}, s32[1,64]{1,0:T(1,128)}, u32[]{:S(2)}) %copy-start.8) | copy-done | bytes 280
  11.3 1.7 %collective-permute-start.3 = (s32[2,64]{1,0:T(2,128)S(1)}, s32[2,64]{1,0:T(2,128)S(1)}, u32[]{:S(2)}, u32[]{:S(2)}) collective-permute-start(s32[2,64]{1,0:T(2,128)S(1)} %stack.2.refs_0_), channel_id=1, source_target_pairs={{0,4},{1,5},{2,6},{3,7},{4,0},{5,1},{6,2},{7,3},{8,12},{9,13},{10,... | collective-permute-start | bytes 1544 | tf_op jit(solution)/shard_map/ppermute | solution.py:35
  13.0 2.3 %collective-permute-done.2.refs_2_ = bf16[64,1024]{1,0:T(8,128)(2,1)S(1)} collective-permute-done((bf16[64,1024]{1,0:T(8,128)(2,1)}, bf16[64,1024]{1,0:T(8,128)(2,1)S(1)}, u32[]{:S(2)}, u32[]{:S(2)}) %collective-permute-start.2) | collective-permute-done | bytes 131104 | tf_op jit(solution)/shard_map/ppermute | solution.py:43
  15.3 0.0 collective-permute-done.1.refs_1_
  15.3 0.0 copy-done.2
  15.4 2.5 %attend_first.1 = (bf16[192,1024]{1,0:T(8,128)(2,1)S(1)}, bf16[512,1024]{1,0:T(8,128)(2,1)S(1)}) custom-call(s32[1]{0:T(128)S(6)} %copy.14.length_ref, bf16[1024,1024]{1,0:T(8,128)(2,1)S(1)} %copy-done, bf16[1,512,1024]{2,1,0:T(8,128)(2,1)S(1)} %copy-done.2, bf16[1,512,1024]{2,1,0:T(8,128)(2,1)S(1)} %copy-done.5, bf16[64,1024]{1,0:T(8,128)(2,1)S(1)} %copy-done.6, ...), custom_call_target="tpu_custom_call" | custom-call | flops 805306368 | tf_op jit(solution)/shard_map/attend_first/pallas_call | solution.py:157
  17.8 0.0 collective-permute-done.3.refs_1_
  17.9 0.0 collective-permute-done.4.refs_1_.refs_4_
  17.9 0.5 %collective-permute-done.5.refs_3_.refs_6_ = bf16[64,1024]{1,0:T(8,128)(2,1)S(1)} collective-permute-done((bf16[64,1024]{1,0:T(8,128)(2,1)}, bf16[64,1024]{1,0:T(8,128)(2,1)S(1)}, u32[]{:S(2)}, u32[]{:S(2)}) %collective-permute-start.5) | collective-permute-done | bytes 131104 | tf_op jit(solution)/shard_map/ppermute | solution.py:43
  18.4 0.0 collective-permute-start.8
  18.4 0.5 %collective-permute-start.9 = (bf16[64,1024]{1,0:T(8,128)(2,1)S(1)}, bf16[64,1024]{1,0:T(8,128)(2,1)S(1)}, u32[]{:S(2)}, u32[]{:S(2)}) collective-permute-start(bf16[64,1024]{1,0:T(8,128)(2,1)S(1)} %collective-permute-done.5.refs_3_.refs_6_), channel_id=1, source_target_pairs={{8,0},{0,8},{9,1},{1,9},{10,2},{2,10},{11,3},{3,11},{12,4},{4,12},... | collective-permute-start | bytes 393224 | tf_op jit(solution)/shard_map/ppermute | solution.py:48
  18.9 0.0 collective-permute-start.7
  18.9 0.7 %collective-permute-start.6 = (s32[4,64]{1,0:T(4,128)S(1)}, s32[4,64]{1,0:T(4,128)S(1)}, u32[]{:S(2)}, u32[]{:S(2)}) collective-permute-start(s32[4,64]{1,0:T(4,128)S(1)} %stack.3.near_ids_ref), channel_id=1, source_target_pairs={{0,1},{1,0},{2,3},{3,2},{4,5},{5,4},{6,7},{7,6},{8,9},{9,8},{10,11... | collective-permute-start | bytes 3080 | tf_op jit(solution)/shard_map/ppermute | solution.py:35
  19.6 0.1 collective-permute-done.8.refs_2_.refs_5_
  19.7 0.2 collective-permute-done.9.refs_4_.refs_7_
  19.9 0.3 collective-permute-done.7.refs_0_.refs_3_
  20.3 2.5 %attend_next.1.refs_1_ = bf16[320,1024]{1,0:T(8,128)(2,1)S(1)} custom-call(bf16[1024,1024]{1,0:T(8,128)(2,1)S(1)} %copy-done, bf16[1,512,1024]{2,1,0:T(8,128)(2,1)S(1)} %copy-done.2, bf16[512,1024]{1,0:T(8,128)(2,1)S(1)} %get-tuple-element.44.values_ref, bf16[64,1024]{1,0:T(8,128)(2,1)S(1)} %collective-permute-done.7.refs_0_.refs_3_, ...), custom_call_target="tpu_custom_call" | custom-call | flops 1342177280 | tf_op jit(solution)/shard_map/attend_next/pallas_call | solution.py:168
  22.8 0.0 collective-permute-done.6.far_ids_ref
  22.8 0.9 %place.1 = (bf16[256,512]{1,0:T(8,128)(2,1)S(1)}, bf16[256,512]{1,0:T(8,128)(2,1)S(1)}, bf16[256,512]{1,0:T(8,128)(2,1)S(1)}, bf16[256,512]{1,0:T(8,128)(2,1)S(1)}) custom-call(s32[4,64]{1,0:T(4,128)S(1)} %stack.3.near_ids_ref, s32[4,64]{1,0:T(4,128)S(1)} %collective-permute-done.6.far_ids_ref, bf16[192,1024]{1,0:T(8,128)(2,1)S(1)} %get-tuple-element.43.refs_0_, ...), custom_call_target="tpu_custom_call" | custom-call | flops 536870912 | tf_op jit(solution)/shard_map/place/pallas_call | solution.py:200
  23.6 0.3 collective-permute-start.16
  23.9 0.8 %collective-permute-start.10 = (bf16[256,512]{1,0:T(8,128)(2,1)S(1)}, bf16[256,512]{1,0:T(8,128)(2,1)S(1)}, u32[]{:S(2)}, u32[]{:S(2)}) collective-permute-start(bf16[256,512]{1,0:T(8,128)(2,1)S(1)} %get-tuple-element.48), channel_id=1, source_target_pairs={{0,1},{1,0},{2,3},{3,2},{4,5},{5,4},{6,7},{7,6},{8,9},{9,8},{10,11... | collective-permute-start | bytes 786440 | tf_op jit(solution)/shard_map/ppermute | solution.py:35
  24.7 1.1 %collective-permute-start.11 = (bf16[256,512]{1,0:T(8,128)(2,1)S(1)}, bf16[256,512]{1,0:T(8,128)(2,1)S(1)}, u32[]{:S(2)}, u32[]{:S(2)}) collective-permute-start(bf16[256,512]{1,0:T(8,128)(2,1)S(1)} %get-tuple-element.49), channel_id=1, source_target_pairs={{0,2},{1,3},{2,0},{3,1},{4,6},{5,7},{6,4},{7,5},{8,10},{9,11},{10,... | collective-permute-start | bytes 786440 | tf_op jit(solution)/shard_map/ppermute | solution.py:35
  25.8 0.9 %prepare.1 = (f32[64,1024]{1,0:T(8,128)S(1)}, f32[64,1024]{1,0:T(8,128)S(1)}) custom-call(bf16[256,512]{1,0:T(8,128)(2,1)S(1)} %get-tuple-element.54.after_ref.refs_0_, s32[1,64]{1,0:T(1,128)S(1)} %copy-done.9, bf16[1024,1024]{1,0:T(8,128)(2,1)S(1)} %copy-done.3, bf16[64,1024]{1,0:T(8,128)(2,1)S(1)} %copy-done.6, ...), custom_call_target="tpu_custom_call" | custom-call | flops 201326592 | tf_op jit(solution)/shard_map/prepare/pallas_call | solution.py:245
  26.7 5.7 %collective-permute-done.10.refs_1_ = bf16[256,512]{1,0:T(8,128)(2,1)S(1)} collective-permute-done((bf16[256,512]{1,0:T(8,128)(2,1)S(1)}, bf16[256,512]{1,0:T(8,128)(2,1)S(1)}, u32[]{:S(2)}, u32[]{:S(2)}) %collective-permute-start.10) | collective-permute-done | bytes 262176 | tf_op jit(solution)/shard_map/ppermute | solution.py:35
  32.4 0.5 collective-permute-done.11.refs_1_
  32.9 0.1 fold.6
  33.0 1.4 %collective-permute-start.14 = (bf16[128,512]{1,0:T(8,128)(2,1)S(1)}, bf16[128,512]{1,0:T(8,128)(2,1)S(1)}, u32[]{:S(2)}, u32[]{:S(2)}) collective-permute-start(bf16[128,512]{1,0:T(8,128)(2,1)S(1)} %get-tuple-element.63), channel_id=1, source_target_pairs={{0,1},{1,0},{2,3},{3,2},{4,5},{5,4},{6,7},{7,6},{8,9},{9,8},{10,11... | collective-permute-start | bytes 393224 | tf_op jit(solution)/shard_map/ppermute | solution.py:35
  34.3 0.1 fold.4
  34.4 1.2 %collective-permute-start.12 = (bf16[128,512]{1,0:T(8,128)(2,1)S(1)}, bf16[128,512]{1,0:T(8,128)(2,1)S(1)}, u32[]{:S(2)}, u32[]{:S(2)}) collective-permute-start(bf16[128,512]{1,0:T(8,128)(2,1)S(1)} %get-tuple-element.57), channel_id=1, source_target_pairs={{0,2},{1,3},{2,0},{3,1},{4,6},{5,7},{6,4},{7,5},{8,10},{9,11},{10,... | collective-permute-start | bytes 393224 | tf_op jit(solution)/shard_map/ppermute | solution.py:35
  35.5 2.4 %collective-permute-done.14.refs_1_ = bf16[128,512]{1,0:T(8,128)(2,1)S(1)} collective-permute-done((bf16[128,512]{1,0:T(8,128)(2,1)S(1)}, bf16[128,512]{1,0:T(8,128)(2,1)S(1)}, u32[]{:S(2)}, u32[]{:S(2)}) %collective-permute-start.14) | collective-permute-done | bytes 131104 | tf_op jit(solution)/shard_map/ppermute | solution.py:35
  38.0 1.5 %collective-permute-start.15 = (bf16[64,512]{1,0:T(8,128)(2,1)S(1)}, bf16[64,512]{1,0:T(8,128)(2,1)S(1)}, u32[]{:S(2)}, u32[]{:S(2)}) collective-permute-start(bf16[64,512]{1,0:T(8,128)(2,1)S(1)} %get-tuple-element.65), channel_id=1, source_target_pairs={{0,4},{1,5},{2,6},{3,7},{4,0},{5,1},{6,2},{7,3},{8,12},{9,13},{10,... | collective-permute-start | bytes 196616 | tf_op jit(solution)/shard_map/ppermute | solution.py:35
  39.5 0.0 collective-permute-done.12.refs_1_
  39.6 1.5 %collective-permute-start.13 = (bf16[64,512]{1,0:T(8,128)(2,1)S(1)}, bf16[64,512]{1,0:T(8,128)(2,1)S(1)}, u32[]{:S(2)}, u32[]{:S(2)}) collective-permute-start(bf16[64,512]{1,0:T(8,128)(2,1)S(1)} %get-tuple-element.59), channel_id=1, source_target_pairs={{0,4},{1,5},{2,6},{3,7},{4,0},{5,1},{6,2},{7,3},{8,12},{9,13},{10,... | collective-permute-start | bytes 196616 | tf_op jit(solution)/shard_map/ppermute | solution.py:35
  41.8 2.4 %collective-permute-done.15.refs_3_ = bf16[64,512]{1,0:T(8,128)(2,1)S(1)} collective-permute-done((bf16[64,512]{1,0:T(8,128)(2,1)S(1)}, bf16[64,512]{1,0:T(8,128)(2,1)S(1)}, u32[]{:S(2)}, u32[]{:S(2)}) %collective-permute-start.15) | collective-permute-done | bytes 65568 | tf_op jit(solution)/shard_map/ppermute | solution.py:35
  44.1 0.7 %collective-permute-done.13.refs_1_ = bf16[64,512]{1,0:T(8,128)(2,1)S(1)} collective-permute-done((bf16[64,512]{1,0:T(8,128)(2,1)S(1)}, bf16[64,512]{1,0:T(8,128)(2,1)S(1)}, u32[]{:S(2)}, u32[]{:S(2)}) %collective-permute-start.13) | collective-permute-done | bytes 65568 | tf_op jit(solution)/shard_map/ppermute | solution.py:35
  44.8 0.0 collective-permute-done.16.refs_5_
  44.8 0.0 copy-done.4
  44.9 2.8 %finish.1 = bf16[1,64,1024]{2,1,0:T(8,128)(2,1)} custom-call(f32[64,1024]{1,0:T(8,128)S(1)} %get-tuple-element.52.embed_ref, f32[64,1024]{1,0:T(8,128)S(1)} %get-tuple-element.53.gating_ref, f32[1,1024]{1,0:T(1,128)S(1)} %bitcast.1, s32[1]{0:T(128)S(6)} %copy.13.count_ref, s32[1,64]{1,0:T(1,128)S(1)} %copy-done.10, bf16[1024,1024]{1,0:T(8,128)(2,1)S(1)} %copy-done.4, ...), custom_call_target="tpu_custom_call" | custom-call | flops 671088640 | tf_op jit(solution)/shard_map/finish/pallas_call | solution.py:284
  (19 shorter events, 0.1 us)
Async XLA Ops:
  0.0 10.5 %collective-permute-start = (s32[1,64]{1,0:T(1,128)}, s32[1,64]{1,0:T(1,128)S(1)}, u32[]{:S(2)}, u32[]{:S(2)}) collective-permute-start(s32[1,64]{1,0:T(1,128)} %ids_ref.1), channel_id=1, source_target_pairs={{0,2},{1,3},{2,0},{3,1},{4,6},{5,7},{6,4},{7,5},{8,10},{9,11},{10,... | collective-permute-start | bytes 776 | tf_op jit(solution)/shard_map/ppermute | solution.py:35
  3.0 14.8 %collective-permute-start.4 = (bf16[64,1024]{1,0:T(8,128)(2,1)}, bf16[64,1024]{1,0:T(8,128)(2,1)S(1)}, u32[]{:S(2)}, u32[]{:S(2)}) collective-permute-start(bf16[64,1024]{1,0:T(8,128)(2,1)} %refs_0_.5), channel_id=1, source_target_pairs={{0,7},{1,6},{2,5},{3,4},{4,3},{5,2},{6,1},{7,0},{8,12},{9,13},{10,... | collective-permute-start | bytes 393224 | tf_op jit(solution)/shard_map/ppermute | solution.py:43
  6.5 8.9 %collective-permute-start.2 = (bf16[64,1024]{1,0:T(8,128)(2,1)}, bf16[64,1024]{1,0:T(8,128)(2,1)S(1)}, u32[]{:S(2)}, u32[]{:S(2)}) collective-permute-start(bf16[64,1024]{1,0:T(8,128)(2,1)} %refs_0_.5), channel_id=1, source_target_pairs={{0,2},{1,3},{2,0},{3,1},{4,6},{5,7},{6,4},{7,5},{8,11},{9,10},{10,... | collective-permute-start | bytes 393224 | tf_op jit(solution)/shard_map/ppermute | solution.py:43
  7.1 8.2 %collective-permute-start.1 = (bf16[64,1024]{1,0:T(8,128)(2,1)}, bf16[64,1024]{1,0:T(8,128)(2,1)S(1)}, u32[]{:S(2)}, u32[]{:S(2)}) collective-permute-start(bf16[64,1024]{1,0:T(8,128)(2,1)} %refs_0_.5), channel_id=1, source_target_pairs={{0,1},{1,0},{2,3},{3,2},{4,5},{5,4},{6,7},{7,6},{8,9},{9,8},{10,11... | collective-permute-start | bytes 393224 | tf_op jit(solution)/shard_map/ppermute | solution.py:35
  7.6 10.8 %collective-permute-start.5 = (bf16[64,1024]{1,0:T(8,128)(2,1)}, bf16[64,1024]{1,0:T(8,128)(2,1)S(1)}, u32[]{:S(2)}, u32[]{:S(2)}) collective-permute-start(bf16[64,1024]{1,0:T(8,128)(2,1)} %refs_0_.5), channel_id=1, source_target_pairs={{0,5},{1,4},{2,7},{3,6},{4,1},{5,0},{6,3},{7,2},{8,14},{9,15},{10,... | collective-permute-start | bytes 393224 | tf_op jit(solution)/shard_map/ppermute | solution.py:43
  10.5 4.8 %copy-start = (bf16[1024,1024]{1,0:T(8,128)(2,1)S(1)}, bf16[1024,1024]{1,0:T(8,128)(2,1)}, u32[]{:S(2)}) copy-start(bf16[1024,1024]{1,0:T(8,128)(2,1)} %w_query_ref.1) | copy-start | bytes 6291460
  10.5 4.8 %copy-start.2 = (bf16[1,512,1024]{2,1,0:T(8,128)(2,1)S(1)}, bf16[1,512,1024]{2,1,0:T(8,128)(2,1)}, u32[]{:S(2)}) copy-start(bf16[1,512,1024]{2,1,0:T(8,128)(2,1)} %keys_ref.3) | copy-start | bytes 3145732
  10.5 4.8 %copy-start.5 = (bf16[1,512,1024]{2,1,0:T(8,128)(2,1)S(1)}, bf16[1,512,1024]{2,1,0:T(8,128)(2,1)}, u32[]{:S(2)}) copy-start(bf16[1,512,1024]{2,1,0:T(8,128)(2,1)} %values_ref.1) | copy-start | bytes 3145732
  10.5 4.8 %copy-start.6 = (bf16[64,1024]{1,0:T(8,128)(2,1)S(1)}, bf16[64,1024]{1,0:T(8,128)(2,1)}, u32[]{:S(2)}) copy-start(bf16[64,1024]{1,0:T(8,128)(2,1)} %refs_0_.5) | copy-start | bytes 393220
  10.5 0.8 %copy-start.8 = (s32[1,64]{1,0:T(1,128)S(1)}, s32[1,64]{1,0:T(1,128)}, u32[]{:S(2)}) copy-start(s32[1,64]{1,0:T(1,128)} %ids_ref.1) | copy-start | bytes 772
  11.3 6.5 %collective-permute-start.3 = (s32[2,64]{1,0:T(2,128)S(1)}, s32[2,64]{1,0:T(2,128)S(1)}, u32[]{:S(2)}, u32[]{:S(2)}) collective-permute-start(s32[2,64]{1,0:T(2,128)S(1)} %stack.2.refs_0_), channel_id=1, source_target_pairs={{0,4},{1,5},{2,6},{3,7},{4,0},{5,1},{6,2},{7,3},{8,12},{9,13},{10,... | collective-permute-start | bytes 1544 | tf_op jit(solution)/shard_map/ppermute | solution.py:35
  18.4 1.3 %collective-permute-start.8 = (bf16[64,1024]{1,0:T(8,128)(2,1)S(1)}, bf16[64,1024]{1,0:T(8,128)(2,1)S(1)}, u32[]{:S(2)}, u32[]{:S(2)}) collective-permute-start(bf16[64,1024]{1,0:T(8,128)(2,1)S(1)} %collective-permute-done.4.refs_1_.refs_4_), channel_id=1, source_target_pairs={{8,0},{0,8},{9,1},{1,9},{10,2},{2,10},{11,3},{3,11},{12,4},{4,12},... | collective-permute-start | bytes 393224 | tf_op jit(solution)/shard_map/ppermute | solution.py:48
  18.4 1.5 %collective-permute-start.9 = (bf16[64,1024]{1,0:T(8,128)(2,1)S(1)}, bf16[64,1024]{1,0:T(8,128)(2,1)S(1)}, u32[]{:S(2)}, u32[]{:S(2)}) collective-permute-start(bf16[64,1024]{1,0:T(8,128)(2,1)S(1)} %collective-permute-done.5.refs_3_.refs_6_), channel_id=1, source_target_pairs={{8,0},{0,8},{9,1},{1,9},{10,2},{2,10},{11,3},{3,11},{12,4},{4,12},... | collective-permute-start | bytes 393224 | tf_op jit(solution)/shard_map/ppermute | solution.py:48
  18.9 1.3 %collective-permute-start.7 = (bf16[64,1024]{1,0:T(8,128)(2,1)S(1)}, bf16[64,1024]{1,0:T(8,128)(2,1)S(1)}, u32[]{:S(2)}, u32[]{:S(2)}) collective-permute-start(bf16[64,1024]{1,0:T(8,128)(2,1)S(1)} %collective-permute-done.2.refs_2_), channel_id=1, source_target_pairs={{8,0},{0,8},{9,1},{1,9},{10,2},{2,10},{11,3},{3,11},{12,4},{4,12},... | collective-permute-start | bytes 393224 | tf_op jit(solution)/shard_map/ppermute | solution.py:48
  18.9 3.8 %collective-permute-start.6 = (s32[4,64]{1,0:T(4,128)S(1)}, s32[4,64]{1,0:T(4,128)S(1)}, u32[]{:S(2)}, u32[]{:S(2)}) collective-permute-start(s32[4,64]{1,0:T(4,128)S(1)} %stack.3.near_ids_ref), channel_id=1, source_target_pairs={{0,1},{1,0},{2,3},{3,2},{4,5},{5,4},{6,7},{7,6},{8,9},{9,8},{10,11... | collective-permute-start | bytes 3080 | tf_op jit(solution)/shard_map/ppermute | solution.py:35
  20.3 3.4 %copy-start.1 = (bf16[1,2,1024,1024]{3,2,1,0:T(8,128)(2,1)S(1)}, bf16[1,2,1024,1024]{3,2,1,0:T(8,128)(2,1)}, u32[]{:S(2)}) copy-start(bf16[1,2,1024,1024]{3,2,1,0:T(8,128)(2,1)} %refs_4_.1) | copy-start | bytes 12582916
  20.3 5.5 %copy-start.3 = (bf16[1024,1024]{1,0:T(8,128)(2,1)S(1)}, bf16[1024,1024]{1,0:T(8,128)(2,1)}, u32[]{:S(2)}) copy-start(bf16[1024,1024]{1,0:T(8,128)(2,1)} %w_gate_ref.1) | copy-start | bytes 6291460
  20.3 5.5 %copy-start.9 = (s32[1,64]{1,0:T(1,128)S(1)}, s32[1,64]{1,0:T(1,128)}, u32[]{:S(2)}) copy-start(s32[1,64]{1,0:T(1,128)} %ids_ref.1) | copy-start | bytes 772
  23.6 21.2 %collective-permute-start.16 = (bf16[1,2,1024,1024]{3,2,1,0:T(8,128)(2,1)S(1)}, bf16[1,2,1024,1024]{3,2,1,0:T(8,128)(2,1)S(1)}, u32[]{:S(2)}, u32[]{:S(2)}) collective-permute-start(bf16[1,2,1024,1024]{3,2,1,0:T(8,128)(2,1)S(1)} %copy-done.1), channel_id=1, source_target_pairs={{8,0},{0,8},{9,1},{1,9},{10,2},{2,10},{11,3},{3,11},{12,4},{4,12},... | collective-permute-start | bytes 12582920 | tf_op jit(solution)/shard_map/ppermute | solution.py:48
  23.9 8.5 %collective-permute-start.10 = (bf16[256,512]{1,0:T(8,128)(2,1)S(1)}, bf16[256,512]{1,0:T(8,128)(2,1)S(1)}, u32[]{:S(2)}, u32[]{:S(2)}) collective-permute-start(bf16[256,512]{1,0:T(8,128)(2,1)S(1)} %get-tuple-element.48), channel_id=1, source_target_pairs={{0,1},{1,0},{2,3},{3,2},{4,5},{5,4},{6,7},{7,6},{8,9},{9,8},{10,11... | collective-permute-start | bytes 786440 | tf_op jit(solution)/shard_map/ppermute | solution.py:35
  24.7 20.2 %copy-start.4 = (bf16[1024,1024]{1,0:T(8,128)(2,1)S(1)}, bf16[1024,1024]{1,0:T(8,128)(2,1)}, u32[]{:S(2)}) copy-start(bf16[1024,1024]{1,0:T(8,128)(2,1)} %w_out_ref.1) | copy-start | bytes 6291460
  24.7 20.2 %copy-start.7 = (f32[1024]{0:T(1024)S(1)}, f32[1024]{0:T(1024)}, u32[]{:S(2)}) copy-start(f32[1024]{0:T(1024)} %param.22) | copy-start | bytes 12292
  24.7 20.2 %copy-start.10 = (s32[1,64]{1,0:T(1,128)S(1)}, s32[1,64]{1,0:T(1,128)}, u32[]{:S(2)}) copy-start(s32[1,64]{1,0:T(1,128)} %domain_ref.1) | copy-start | bytes 772
  24.7 8.2 %collective-permute-start.11 = (bf16[256,512]{1,0:T(8,128)(2,1)S(1)}, bf16[256,512]{1,0:T(8,128)(2,1)S(1)}, u32[]{:S(2)}, u32[]{:S(2)}) collective-permute-start(bf16[256,512]{1,0:T(8,128)(2,1)S(1)} %get-tuple-element.49), channel_id=1, source_target_pairs={{0,2},{1,3},{2,0},{3,1},{4,6},{5,7},{6,4},{7,5},{8,10},{9,11},{10,... | collective-permute-start | bytes 786440 | tf_op jit(solution)/shard_map/ppermute | solution.py:35
  33.0 5.0 %collective-permute-start.14 = (bf16[128,512]{1,0:T(8,128)(2,1)S(1)}, bf16[128,512]{1,0:T(8,128)(2,1)S(1)}, u32[]{:S(2)}, u32[]{:S(2)}) collective-permute-start(bf16[128,512]{1,0:T(8,128)(2,1)S(1)} %get-tuple-element.63), channel_id=1, source_target_pairs={{0,1},{1,0},{2,3},{3,2},{4,5},{5,4},{6,7},{7,6},{8,9},{9,8},{10,11... | collective-permute-start | bytes 393224 | tf_op jit(solution)/shard_map/ppermute | solution.py:35
  34.4 5.2 %collective-permute-start.12 = (bf16[128,512]{1,0:T(8,128)(2,1)S(1)}, bf16[128,512]{1,0:T(8,128)(2,1)S(1)}, u32[]{:S(2)}, u32[]{:S(2)}) collective-permute-start(bf16[128,512]{1,0:T(8,128)(2,1)S(1)} %get-tuple-element.57), channel_id=1, source_target_pairs={{0,2},{1,3},{2,0},{3,1},{4,6},{5,7},{6,4},{7,5},{8,10},{9,11},{10,... | collective-permute-start | bytes 393224 | tf_op jit(solution)/shard_map/ppermute | solution.py:35
  38.0 6.1 %collective-permute-start.15 = (bf16[64,512]{1,0:T(8,128)(2,1)S(1)}, bf16[64,512]{1,0:T(8,128)(2,1)S(1)}, u32[]{:S(2)}, u32[]{:S(2)}) collective-permute-start(bf16[64,512]{1,0:T(8,128)(2,1)S(1)} %get-tuple-element.65), channel_id=1, source_target_pairs={{0,4},{1,5},{2,6},{3,7},{4,0},{5,1},{6,2},{7,3},{8,12},{9,13},{10,... | collective-permute-start | bytes 196616 | tf_op jit(solution)/shard_map/ppermute | solution.py:35
  39.6 5.3 %collective-permute-start.13 = (bf16[64,512]{1,0:T(8,128)(2,1)S(1)}, bf16[64,512]{1,0:T(8,128)(2,1)S(1)}, u32[]{:S(2)}, u32[]{:S(2)}) collective-permute-start(bf16[64,512]{1,0:T(8,128)(2,1)S(1)} %get-tuple-element.59), channel_id=1, source_target_pairs={{0,4},{1,5},{2,6},{3,7},{4,0},{5,1},{6,2},{7,3},{8,12},{9,13},{10,... | collective-permute-start | bytes 196616 | tf_op jit(solution)/shard_map/ppermute | solution.py:35

commit v11 on v10

--- a/solution.py
+++ b/solution.py
@@ -251,14 +251,38 @@
     )(after, ids, w_gate, *blocks)
 
 
-def finish_kernel(sides, embed_ref, gating_ref, gain_ref, count_ref, domain_ref, w_out_ref, *refs):
-    *expert_refs, out_ref = refs[2 * sides :]
+def mixed_part(start, kept_ref, come_ref, gating_ref, gain_ref, w_out_ref):
+    attended = kept_ref[...] + come_ref[...].astype(F32)
+    columns = slice(start, start + attended.shape[1])
+    gated = (attended * gain_ref[:, columns] * gating_ref[:, columns]).astype(BF16)
+    squares = jnp.sum(attended * attended, axis=1, keepdims=True)
+    return squares, jnp.dot(gated, w_out_ref[columns, :], preferred_element_type=F32)
+
+
+def mix_kernel(kept_ref, come_ref, gating_ref, gain_ref, w_out_ref, squares_ref, mixed_ref):
+    squares, mixed = mixed_part(0, kept_ref, come_ref, gating_ref, gain_ref, w_out_ref)
+    squares_ref[...] = jnp.broadcast_to(squares, squares_ref.shape)
+    mixed_ref[...] = mixed
+
+
+def mix(pair, gating, gain, w_out):
+    slots, width = gating.shape
+    return kernel_call(
+        mix_kernel,
+        "mix",
+        [jax.ShapeDtypeStruct((slots, 128), F32), jax.ShapeDtypeStruct((slots, width), F32)],
+        [VMEM] * 5,
+        flops=2 * slots * width * pair[0].shape[1],
+    )(*pair, gating, gain, w_out)
+
+
+def finish_kernel(kept_ref, come_ref, squares_ref, mixed_ref, embed_ref, gating_ref, gain_ref, *refs):
+    count_ref, domain_ref, w_out_ref, *expert_refs, out_ref = refs
     users = len(expert_refs)
-    halves = [refs[2 * side][...] + refs[2 * side + 1][...].astype(F32) for side in range(sides)]
-    attended = jnp.concatenate(halves, axis=1)
-    gated = (rms_scale(attended) * gain_ref[...] * gating_ref[...]).astype(BF16)
-    mixed = jnp.dot(gated, w_out_ref[...], preferred_element_type=F32)
-    state = (embed_ref[...] + mixed).astype(BF16)
+    width = embed_ref.shape[1]
+    squares, mixed = mixed_part(width - kept_ref.shape[1], kept_ref, come_ref, gating_ref, gain_ref, w_out_ref)
+    scale = lax.rsqrt((squares_ref[:, :1] + squares) / width + norm_eps)
+    state = (embed_ref[...] + (mixed_ref[...] + mixed) * scale).astype(BF16)
 
     slots = state.shape[0]
     row_at = lax.broadcasted_iota(jnp.int32, (slots, slots), 0)
@@ -280,14 +304,15 @@
 
 def finish(pairs, embed, gating, gain, counts, domains, w_out, experts):
     slots, width = embed.shape
-    blocks = [block for pair in pairs for block in pair]
-    return kernel_call(
-        functools.partial(finish_kernel, len(pairs)),
+    first, last = pairs
+    squares, mixed = mix(first, gating, gain, w_out)
+    return kernel_call(
+        finish_kernel,
         "finish",
         [jax.ShapeDtypeStruct((1, slots, width), BF16)],
-        [VMEM] * 3 + [SMEM] + [VMEM] * (2 + len(blocks) + len(experts)),
+        [VMEM] * 7 + [SMEM] + [VMEM] * (2 + len(experts)),
         flops=2 * slots * width * width * (1 + LAYERS * len(experts)),
-    )(embed, gating, gain, counts, domains, w_out, *blocks, *experts)[0]
+    )(*last, squares, mixed, embed, gating, gain, counts, domains, w_out, *experts)[0]
 
 
 def on_device(

time: 47.8 us -> 47.6 us (level)
  waiting for transfers between devices: 15.1 us -> 14.5 us
    ppermute x10, waiting for transfers between devices: 11.7 us -> 11.1 us  [swapped(): return lax.ppermute(value, 'hist', [(i, i ^ flip) for i in range(count)])]
    pallas_call x1 -> x2, Pallas kernels: 2.84 us -> 2.91 us  [the longest x1 2.61 us: finish(): kernel_call(finish_kernel, 'finish', [jax.ShapeDtypeStruct((1, slots, wid...]
where the time goes in v11:
time: 47.6 us; the launch traced here: 47.5 us
  starting transfers between devices  20.8 us (44%)
  waiting for transfers between devices  14.5 us (30%)
  Pallas kernels  9.84 us (21%)
  between operations  1.48 us (3%)
  local copies, waits for them, and re-layouts  0.84 us (2%)
    ppermute x10, starting transfers between devices, swapped(): return lax.ppermute(value, 'hist', [(i, i ^ flip) for i in range(count)])  13.7 us
    ppermute x10, waiting for transfers between devices, swapped(): return lax.ppermute(value, 'hist', [(i, i ^ flip) for i in range(count)])  11.1 us
    ppermute x3, starting transfers between devices, swapped_by_user(): return lax.ppermute(value, ('user', 'hist'), pairs)  6.3 us
    ppermute x3, waiting for transfers between devices, swapped_by_user(): return lax.ppermute(value, ('user', 'hist'), pairs)  2.79 us
    pallas_call x1, Pallas kernels, finish(): kernel_call(finish_kernel, 'finish', [jax.ShapeDtypeStruct((1, slots, wid...  2.61 us
    pallas_call x1, Pallas kernels, attend_next(): kernel_call(functools.partial(next_kernel, pieces), 'attend_next', [jax.S...  2.5 us
    pallas_call x1, Pallas kernels, attend_first(): kernel_call(functools.partial(first_kernel, pieces), 'attend_first', [jax...  2.5 us
  transfers between devices with their start and end apart: 17, of which 10 were waited for; matrix products, arithmetic and copies ran while one was open for 0% of the time, Pallas kernels for 13%

profile of v11, /device:TPU:0, one launch (start us, length us, event | category | flops | bytes accessed | tf_op | source)
XLA Modules:
  0.0 47.5 jit_solution(4874984148800750192)
XLA Ops:
  0.0 3.0 %collective-permute-start = (s32[1,64]{1,0:T(1,128)}, s32[1,64]{1,0:T(1,128)S(1)}, u32[]{:S(2)}, u32[]{:S(2)}) collective-permute-start(s32[1,64]{1,0:T(1,128)} %ids_ref.1), channel_id=1, source_target_pairs={{0,2},{1,3},{2,0},{3,1},{4,6},{5,7},{6,4},{7,5},{8,10},{9,11},{10,... | collective-permute-start | bytes 776 | tf_op jit(solution)/shard_map/ppermute | solution.py:35
  3.0 3.4 %collective-permute-start.4 = (bf16[64,1024]{1,0:T(8,128)(2,1)}, bf16[64,1024]{1,0:T(8,128)(2,1)S(1)}, u32[]{:S(2)}, u32[]{:S(2)}) collective-permute-start(bf16[64,1024]{1,0:T(8,128)(2,1)} %refs_0_.6), channel_id=1, source_target_pairs={{0,7},{1,6},{2,5},{3,4},{4,3},{5,2},{6,1},{7,0},{8,12},{9,13},{10,... | collective-permute-start | bytes 393224 | tf_op jit(solution)/shard_map/ppermute | solution.py:43
  6.5 0.7 %collective-permute-start.2 = (bf16[64,1024]{1,0:T(8,128)(2,1)}, bf16[64,1024]{1,0:T(8,128)(2,1)S(1)}, u32[]{:S(2)}, u32[]{:S(2)}) collective-permute-start(bf16[64,1024]{1,0:T(8,128)(2,1)} %refs_0_.6), channel_id=1, source_target_pairs={{0,2},{1,3},{2,0},{3,1},{4,6},{5,7},{6,4},{7,5},{8,11},{9,10},{10,... | collective-permute-start | bytes 393224 | tf_op jit(solution)/shard_map/ppermute | solution.py:43
  7.1 0.5 %collective-permute-start.1 = (bf16[64,1024]{1,0:T(8,128)(2,1)}, bf16[64,1024]{1,0:T(8,128)(2,1)S(1)}, u32[]{:S(2)}, u32[]{:S(2)}) collective-permute-start(bf16[64,1024]{1,0:T(8,128)(2,1)} %refs_0_.6), channel_id=1, source_target_pairs={{0,1},{1,0},{2,3},{3,2},{4,5},{5,4},{6,7},{7,6},{8,9},{9,8},{10,11... | collective-permute-start | bytes 393224 | tf_op jit(solution)/shard_map/ppermute | solution.py:35
  7.6 2.2 %collective-permute-start.5 = (bf16[64,1024]{1,0:T(8,128)(2,1)}, bf16[64,1024]{1,0:T(8,128)(2,1)S(1)}, u32[]{:S(2)}, u32[]{:S(2)}) collective-permute-start(bf16[64,1024]{1,0:T(8,128)(2,1)} %refs_0_.6), channel_id=1, source_target_pairs={{0,5},{1,4},{2,7},{3,6},{4,1},{5,0},{6,3},{7,2},{8,14},{9,15},{10,... | collective-permute-start | bytes 393224 | tf_op jit(solution)/shard_map/ppermute | solution.py:43
  10.5 0.0 copy-start
  10.5 0.0 copy-start.3
  10.5 0.0 collective-permute-done.refs_1_
  10.5 0.0 copy-start.8
  10.5 0.8 %copy-done.8 = s32[1,64]{1,0:T(1,128)S(1)} copy-done((s32[1,64]{1,0:T(1,128)S(1)}, s32[1,64]{1,0:T(1,128)}, u32[]{:S(2)}) %copy-start.8) | copy-done | bytes 280
  11.3 1.7 %collective-permute-start.3 = (s32[2,64]{1,0:T(2,128)S(1)}, s32[2,64]{1,0:T(2,128)S(1)}, u32[]{:S(2)}, u32[]{:S(2)}) collective-permute-start(s32[2,64]{1,0:T(2,128)S(1)} %stack.2.refs_0_), channel_id=1, source_target_pairs={{0,4},{1,5},{2,6},{3,7},{4,0},{5,1},{6,2},{7,3},{8,12},{9,13},{10,... | collective-permute-start | bytes 1544 | tf_op jit(solution)/shard_map/ppermute | solution.py:35
  13.0 2.3 %collective-permute-done.2.refs_2_ = bf16[64,1024]{1,0:T(8,128)(2,1)S(1)} collective-permute-done((bf16[64,1024]{1,0:T(8,128)(2,1)}, bf16[64,1024]{1,0:T(8,128)(2,1)S(1)}, u32[]{:S(2)}, u32[]{:S(2)}) %collective-permute-start.2) | collective-permute-done | bytes 131104 | tf_op jit(solution)/shard_map/ppermute | solution.py:43
  15.3 0.0 collective-permute-done.1.refs_1_
  15.3 0.0 copy-done.3
  15.4 2.5 %attend_first.1 = (bf16[192,1024]{1,0:T(8,128)(2,1)S(1)}, bf16[512,1024]{1,0:T(8,128)(2,1)S(1)}) custom-call(s32[1]{0:T(128)S(6)} %copy.14.length_ref, bf16[1024,1024]{1,0:T(8,128)(2,1)S(1)} %copy-done, bf16[1,512,1024]{2,1,0:T(8,128)(2,1)S(1)} %copy-done.3, bf16[1,512,1024]{2,1,0:T(8,128)(2,1)S(1)} %copy-done.5, bf16[64,1024]{1,0:T(8,128)(2,1)S(1)} %copy-done.6, ...), custom_call_target="tpu_custom_call" | custom-call | flops 805306368 | tf_op jit(solution)/shard_map/attend_first/pallas_call | solution.py:157
  17.9 0.0 collective-permute-done.3.refs_1_
  17.9 0.0 collective-permute-done.4.refs_1_.refs_4_
  17.9 0.5 %collective-permute-done.5.refs_3_.refs_6_ = bf16[64,1024]{1,0:T(8,128)(2,1)S(1)} collective-permute-done((bf16[64,1024]{1,0:T(8,128)(2,1)}, bf16[64,1024]{1,0:T(8,128)(2,1)S(1)}, u32[]{:S(2)}, u32[]{:S(2)}) %collective-permute-start.5) | collective-permute-done | bytes 131104 | tf_op jit(solution)/shard_map/ppermute | solution.py:43
  18.4 0.0 collective-permute-start.8
  18.4 0.5 %collective-permute-start.9 = (bf16[64,1024]{1,0:T(8,128)(2,1)S(1)}, bf16[64,1024]{1,0:T(8,128)(2,1)S(1)}, u32[]{:S(2)}, u32[]{:S(2)}) collective-permute-start(bf16[64,1024]{1,0:T(8,128)(2,1)S(1)} %collective-permute-done.5.refs_3_.refs_6_), channel_id=1, source_target_pairs={{8,0},{0,8},{9,1},{1,9},{10,2},{2,10},{11,3},{3,11},{12,4},{4,12},... | collective-permute-start | bytes 393224 | tf_op jit(solution)/shard_map/ppermute | solution.py:48
  18.9 0.0 collective-permute-start.7
  18.9 0.7 %collective-permute-start.6 = (s32[4,64]{1,0:T(4,128)S(1)}, s32[4,64]{1,0:T(4,128)S(1)}, u32[]{:S(2)}, u32[]{:S(2)}) collective-permute-start(s32[4,64]{1,0:T(4,128)S(1)} %stack.3.near_ids_ref), channel_id=1, source_target_pairs={{0,1},{1,0},{2,3},{3,2},{4,5},{5,4},{6,7},{7,6},{8,9},{9,8},{10,11... | collective-permute-start | bytes 3080 | tf_op jit(solution)/shard_map/ppermute | solution.py:35
  19.6 0.1 collective-permute-done.8.refs_2_.refs_5_
  19.7 0.2 collective-permute-done.9.refs_4_.refs_7_
  19.9 0.3 collective-permute-done.7.refs_0_.refs_3_
  20.3 2.5 %attend_next.1.refs_1_ = bf16[320,1024]{1,0:T(8,128)(2,1)S(1)} custom-call(bf16[1024,1024]{1,0:T(8,128)(2,1)S(1)} %copy-done, bf16[1,512,1024]{2,1,0:T(8,128)(2,1)S(1)} %copy-done.3, bf16[512,1024]{1,0:T(8,128)(2,1)S(1)} %get-tuple-element.46.values_ref, bf16[64,1024]{1,0:T(8,128)(2,1)S(1)} %collective-permute-done.7.refs_0_.refs_3_, ...), custom_call_target="tpu_custom_call" | custom-call | flops 1342177280 | tf_op jit(solution)/shard_map/attend_next/pallas_call | solution.py:168
  22.8 0.0 collective-permute-done.6.far_ids_ref
  22.8 0.9 %place.1 = (bf16[256,512]{1,0:T(8,128)(2,1)S(1)}, bf16[256,512]{1,0:T(8,128)(2,1)S(1)}, bf16[256,512]{1,0:T(8,128)(2,1)S(1)}, bf16[256,512]{1,0:T(8,128)(2,1)S(1)}) custom-call(s32[4,64]{1,0:T(4,128)S(1)} %stack.3.near_ids_ref, s32[4,64]{1,0:T(4,128)S(1)} %collective-permute-done.6.far_ids_ref, bf16[192,1024]{1,0:T(8,128)(2,1)S(1)} %get-tuple-element.45.refs_0_, ...), custom_call_target="tpu_custom_call" | custom-call | flops 536870912 | tf_op jit(solution)/shard_map/place/pallas_call | solution.py:200
  23.6 0.3 collective-permute-start.16
  23.9 0.8 %collective-permute-start.10 = (bf16[256,512]{1,0:T(8,128)(2,1)S(1)}, bf16[256,512]{1,0:T(8,128)(2,1)S(1)}, u32[]{:S(2)}, u32[]{:S(2)}) collective-permute-start(bf16[256,512]{1,0:T(8,128)(2,1)S(1)} %get-tuple-element.51), channel_id=1, source_target_pairs={{0,1},{1,0},{2,3},{3,2},{4,5},{5,4},{6,7},{7,6},{8,9},{9,8},{10,11... | collective-permute-start | bytes 786440 | tf_op jit(solution)/shard_map/ppermute | solution.py:35
  24.7 1.1 %collective-permute-start.11 = (bf16[256,512]{1,0:T(8,128)(2,1)S(1)}, bf16[256,512]{1,0:T(8,128)(2,1)S(1)}, u32[]{:S(2)}, u32[]{:S(2)}) collective-permute-start(bf16[256,512]{1,0:T(8,128)(2,1)S(1)} %get-tuple-element.52), channel_id=1, source_target_pairs={{0,2},{1,3},{2,0},{3,1},{4,6},{5,7},{6,4},{7,5},{8,10},{9,11},{10,... | collective-permute-start | bytes 786440 | tf_op jit(solution)/shard_map/ppermute | solution.py:35
  25.8 0.9 %prepare.1 = (f32[64,1024]{1,0:T(8,128)S(1)}, f32[64,1024]{1,0:T(8,128)S(1)}) custom-call(bf16[256,512]{1,0:T(8,128)(2,1)S(1)} %get-tuple-element.60.after_ref.refs_0_, s32[1,64]{1,0:T(1,128)S(1)} %copy-done.9, bf16[1024,1024]{1,0:T(8,128)(2,1)S(1)} %copy-done.4, bf16[64,1024]{1,0:T(8,128)(2,1)S(1)} %copy-done.6, ...), custom_call_target="tpu_custom_call" | custom-call | flops 201326592 | tf_op jit(solution)/shard_map/prepare/pallas_call | solution.py:245
  26.7 5.7 %collective-permute-done.10.refs_1_ = bf16[256,512]{1,0:T(8,128)(2,1)S(1)} collective-permute-done((bf16[256,512]{1,0:T(8,128)(2,1)S(1)}, bf16[256,512]{1,0:T(8,128)(2,1)S(1)}, u32[]{:S(2)}, u32[]{:S(2)}) %collective-permute-start.10) | collective-permute-done | bytes 262176 | tf_op jit(solution)/shard_map/ppermute | solution.py:35
  32.4 0.5 collective-permute-done.11.refs_1_
  32.9 0.1 fold.6
  32.9 1.3 %collective-permute-start.14 = (bf16[128,512]{1,0:T(8,128)(2,1)S(1)}, bf16[128,512]{1,0:T(8,128)(2,1)S(1)}, u32[]{:S(2)}, u32[]{:S(2)}) collective-permute-start(bf16[128,512]{1,0:T(8,128)(2,1)S(1)} %get-tuple-element.63), channel_id=1, source_target_pairs={{0,2},{1,3},{2,0},{3,1},{4,6},{5,7},{6,4},{7,5},{8,10},{9,11},{10,... | collective-permute-start | bytes 393224 | tf_op jit(solution)/shard_map/ppermute | solution.py:35
  34.2 0.1 fold.4
  34.3 1.3 %collective-permute-start.12 = (bf16[128,512]{1,0:T(8,128)(2,1)S(1)}, bf16[128,512]{1,0:T(8,128)(2,1)S(1)}, u32[]{:S(2)}, u32[]{:S(2)}) collective-permute-start(bf16[128,512]{1,0:T(8,128)(2,1)S(1)} %get-tuple-element.57), channel_id=1, source_target_pairs={{0,1},{1,0},{2,3},{3,2},{4,5},{5,4},{6,7},{7,6},{8,9},{9,8},{10,11... | collective-permute-start | bytes 393224 | tf_op jit(solution)/shard_map/ppermute | solution.py:35
  35.6 2.4 %collective-permute-done.14.refs_1_ = bf16[128,512]{1,0:T(8,128)(2,1)S(1)} collective-permute-done((bf16[128,512]{1,0:T(8,128)(2,1)S(1)}, bf16[128,512]{1,0:T(8,128)(2,1)S(1)}, u32[]{:S(2)}, u32[]{:S(2)}) %collective-permute-start.14) | collective-permute-done | bytes 131104 | tf_op jit(solution)/shard_map/ppermute | solution.py:35
  38.0 1.5 %collective-permute-start.15 = (bf16[64,512]{1,0:T(8,128)(2,1)S(1)}, bf16[64,512]{1,0:T(8,128)(2,1)S(1)}, u32[]{:S(2)}, u32[]{:S(2)}) collective-permute-start(bf16[64,512]{1,0:T(8,128)(2,1)S(1)} %get-tuple-element.65), channel_id=1, source_target_pairs={{0,4},{1,5},{2,6},{3,7},{4,0},{5,1},{6,2},{7,3},{8,12},{9,13},{10,... | collective-permute-start | bytes 196616 | tf_op jit(solution)/shard_map/ppermute | solution.py:35
  39.5 0.0 collective-permute-done.12.refs_1_
  39.6 1.8 %collective-permute-start.13 = (bf16[64,512]{1,0:T(8,128)(2,1)S(1)}, bf16[64,512]{1,0:T(8,128)(2,1)S(1)}, u32[]{:S(2)}, u32[]{:S(2)}) collective-permute-start(bf16[64,512]{1,0:T(8,128)(2,1)S(1)} %get-tuple-element.59), channel_id=1, source_target_pairs={{0,4},{1,5},{2,6},{3,7},{4,0},{5,1},{6,2},{7,3},{8,12},{9,13},{10,... | collective-permute-start | bytes 196616 | tf_op jit(solution)/shard_map/ppermute | solution.py:35
  42.0 2.1 %collective-permute-done.15.come_ref = bf16[64,512]{1,0:T(8,128)(2,1)S(1)} collective-permute-done((bf16[64,512]{1,0:T(8,128)(2,1)S(1)}, bf16[64,512]{1,0:T(8,128)(2,1)S(1)}, u32[]{:S(2)}, u32[]{:S(2)}) %collective-permute-start.15) | collective-permute-done | bytes 65568 | tf_op jit(solution)/shard_map/ppermute | solution.py:35
  44.1 0.0 copy-done.1
  44.1 0.3 mix.1
  44.4 0.4 collective-permute-done.13.come_ref
  44.8 0.0 collective-permute-done.16.refs_4_
  44.8 2.6 %finish.1 = bf16[1,64,1024]{2,1,0:T(8,128)(2,1)} custom-call(f32[64,512]{1,0:T(8,128)S(1)} %get-tuple-element.58.kept_ref, bf16[64,512]{1,0:T(8,128)(2,1)S(1)} %collective-permute-done.13.come_ref, f32[64,128]{1,0:T(8,128)S(1)} %get-tuple-element.67.squares_ref, f32[64,1024]{1,0:T(8,128)S(1)} %get-tuple-element.68.mixed_ref, ...), custom_call_target="tpu_custom_call" | custom-call | flops 671088640 | tf_op jit(solution)/shard_map/finish/pallas_call | solution.py:309
  (20 shorter events, 0.1 us)
Async XLA Ops:
  0.0 10.5 %collective-permute-start = (s32[1,64]{1,0:T(1,128)}, s32[1,64]{1,0:T(1,128)S(1)}, u32[]{:S(2)}, u32[]{:S(2)}) collective-permute-start(s32[1,64]{1,0:T(1,128)} %ids_ref.1), channel_id=1, source_target_pairs={{0,2},{1,3},{2,0},{3,1},{4,6},{5,7},{6,4},{7,5},{8,10},{9,11},{10,... | collective-permute-start | bytes 776 | tf_op jit(solution)/shard_map/ppermute | solution.py:35
  3.0 14.9 %collective-permute-start.4 = (bf16[64,1024]{1,0:T(8,128)(2,1)}, bf16[64,1024]{1,0:T(8,128)(2,1)S(1)}, u32[]{:S(2)}, u32[]{:S(2)}) collective-permute-start(bf16[64,1024]{1,0:T(8,128)(2,1)} %refs_0_.6), channel_id=1, source_target_pairs={{0,7},{1,6},{2,5},{3,4},{4,3},{5,2},{6,1},{7,0},{8,12},{9,13},{10,... | collective-permute-start | bytes 393224 | tf_op jit(solution)/shard_map/ppermute | solution.py:43
  6.5 8.9 %collective-permute-start.2 = (bf16[64,1024]{1,0:T(8,128)(2,1)}, bf16[64,1024]{1,0:T(8,128)(2,1)S(1)}, u32[]{:S(2)}, u32[]{:S(2)}) collective-permute-start(bf16[64,1024]{1,0:T(8,128)(2,1)} %refs_0_.6), channel_id=1, source_target_pairs={{0,2},{1,3},{2,0},{3,1},{4,6},{5,7},{6,4},{7,5},{8,11},{9,10},{10,... | collective-permute-start | bytes 393224 | tf_op jit(solution)/shard_map/ppermute | solution.py:43
  7.1 8.2 %collective-permute-start.1 = (bf16[64,1024]{1,0:T(8,128)(2,1)}, bf16[64,1024]{1,0:T(8,128)(2,1)S(1)}, u32[]{:S(2)}, u32[]{:S(2)}) collective-permute-start(bf16[64,1024]{1,0:T(8,128)(2,1)} %refs_0_.6), channel_id=1, source_target_pairs={{0,1},{1,0},{2,3},{3,2},{4,5},{5,4},{6,7},{7,6},{8,9},{9,8},{10,11... | collective-permute-start | bytes 393224 | tf_op jit(solution)/shard_map/ppermute | solution.py:35
  7.6 10.8 %collective-permute-start.5 = (bf16[64,1024]{1,0:T(8,128)(2,1)}, bf16[64,1024]{1,0:T(8,128)(2,1)S(1)}, u32[]{:S(2)}, u32[]{:S(2)}) collective-permute-start(bf16[64,1024]{1,0:T(8,128)(2,1)} %refs_0_.6), channel_id=1, source_target_pairs={{0,5},{1,4},{2,7},{3,6},{4,1},{5,0},{6,3},{7,2},{8,14},{9,15},{10,... | collective-permute-start | bytes 393224 | tf_op jit(solution)/shard_map/ppermute | solution.py:43
  10.5 4.8 %copy-start = (bf16[1024,1024]{1,0:T(8,128)(2,1)S(1)}, bf16[1024,1024]{1,0:T(8,128)(2,1)}, u32[]{:S(2)}) copy-start(bf16[1024,1024]{1,0:T(8,128)(2,1)} %w_query_ref.1) | copy-start | bytes 6291460
  10.5 4.8 %copy-start.3 = (bf16[1,512,1024]{2,1,0:T(8,128)(2,1)S(1)}, bf16[1,512,1024]{2,1,0:T(8,128)(2,1)}, u32[]{:S(2)}) copy-start(bf16[1,512,1024]{2,1,0:T(8,128)(2,1)} %keys_ref.3) | copy-start | bytes 3145732
  10.5 4.8 %copy-start.5 = (bf16[1,512,1024]{2,1,0:T(8,128)(2,1)S(1)}, bf16[1,512,1024]{2,1,0:T(8,128)(2,1)}, u32[]{:S(2)}) copy-start(bf16[1,512,1024]{2,1,0:T(8,128)(2,1)} %values_ref.1) | copy-start | bytes 3145732
  10.5 4.8 %copy-start.6 = (bf16[64,1024]{1,0:T(8,128)(2,1)S(1)}, bf16[64,1024]{1,0:T(8,128)(2,1)}, u32[]{:S(2)}) copy-start(bf16[64,1024]{1,0:T(8,128)(2,1)} %refs_0_.6) | copy-start | bytes 393220
  10.5 0.8 %copy-start.8 = (s32[1,64]{1,0:T(1,128)S(1)}, s32[1,64]{1,0:T(1,128)}, u32[]{:S(2)}) copy-start(s32[1,64]{1,0:T(1,128)} %ids_ref.1) | copy-start | bytes 772
  11.3 6.5 %collective-permute-start.3 = (s32[2,64]{1,0:T(2,128)S(1)}, s32[2,64]{1,0:T(2,128)S(1)}, u32[]{:S(2)}, u32[]{:S(2)}) collective-permute-start(s32[2,64]{1,0:T(2,128)S(1)} %stack.2.refs_0_), channel_id=1, source_target_pairs={{0,4},{1,5},{2,6},{3,7},{4,0},{5,1},{6,2},{7,3},{8,12},{9,13},{10,... | collective-permute-start | bytes 1544 | tf_op jit(solution)/shard_map/ppermute | solution.py:35
  18.4 1.3 %collective-permute-start.8 = (bf16[64,1024]{1,0:T(8,128)(2,1)S(1)}, bf16[64,1024]{1,0:T(8,128)(2,1)S(1)}, u32[]{:S(2)}, u32[]{:S(2)}) collective-permute-start(bf16[64,1024]{1,0:T(8,128)(2,1)S(1)} %collective-permute-done.4.refs_1_.refs_4_), channel_id=1, source_target_pairs={{8,0},{0,8},{9,1},{1,9},{10,2},{2,10},{11,3},{3,11},{12,4},{4,12},... | collective-permute-start | bytes 393224 | tf_op jit(solution)/shard_map/ppermute | solution.py:48
  18.4 1.5 %collective-permute-start.9 = (bf16[64,1024]{1,0:T(8,128)(2,1)S(1)}, bf16[64,1024]{1,0:T(8,128)(2,1)S(1)}, u32[]{:S(2)}, u32[]{:S(2)}) collective-permute-start(bf16[64,1024]{1,0:T(8,128)(2,1)S(1)} %collective-permute-done.5.refs_3_.refs_6_), channel_id=1, source_target_pairs={{8,0},{0,8},{9,1},{1,9},{10,2},{2,10},{11,3},{3,11},{12,4},{4,12},... | collective-permute-start | bytes 393224 | tf_op jit(solution)/shard_map/ppermute | solution.py:48
  18.9 1.3 %collective-permute-start.7 = (bf16[64,1024]{1,0:T(8,128)(2,1)S(1)}, bf16[64,1024]{1,0:T(8,128)(2,1)S(1)}, u32[]{:S(2)}, u32[]{:S(2)}) collective-permute-start(bf16[64,1024]{1,0:T(8,128)(2,1)S(1)} %collective-permute-done.2.refs_2_), channel_id=1, source_target_pairs={{8,0},{0,8},{9,1},{1,9},{10,2},{2,10},{11,3},{3,11},{12,4},{4,12},... | collective-permute-start | bytes 393224 | tf_op jit(solution)/shard_map/ppermute | solution.py:48
  18.9 3.9 %collective-permute-start.6 = (s32[4,64]{1,0:T(4,128)S(1)}, s32[4,64]{1,0:T(4,128)S(1)}, u32[]{:S(2)}, u32[]{:S(2)}) collective-permute-start(s32[4,64]{1,0:T(4,128)S(1)} %stack.3.near_ids_ref), channel_id=1, source_target_pairs={{0,1},{1,0},{2,3},{3,2},{4,5},{5,4},{6,7},{7,6},{8,9},{9,8},{10,11... | collective-permute-start | bytes 3080 | tf_op jit(solution)/shard_map/ppermute | solution.py:35
  20.3 3.4 %copy-start.2 = (bf16[1,2,1024,1024]{3,2,1,0:T(8,128)(2,1)S(1)}, bf16[1,2,1024,1024]{3,2,1,0:T(8,128)(2,1)}, u32[]{:S(2)}) copy-start(bf16[1,2,1024,1024]{3,2,1,0:T(8,128)(2,1)} %refs_3_.1) | copy-start | bytes 12582916
  20.3 5.5 %copy-start.4 = (bf16[1024,1024]{1,0:T(8,128)(2,1)S(1)}, bf16[1024,1024]{1,0:T(8,128)(2,1)}, u32[]{:S(2)}) copy-start(bf16[1024,1024]{1,0:T(8,128)(2,1)} %w_gate_ref.1) | copy-start | bytes 6291460
  20.3 5.5 %copy-start.9 = (s32[1,64]{1,0:T(1,128)S(1)}, s32[1,64]{1,0:T(1,128)}, u32[]{:S(2)}) copy-start(s32[1,64]{1,0:T(1,128)} %ids_ref.1) | copy-start | bytes 772
  23.6 21.2 %collective-permute-start.16 = (bf16[1,2,1024,1024]{3,2,1,0:T(8,128)(2,1)S(1)}, bf16[1,2,1024,1024]{3,2,1,0:T(8,128)(2,1)S(1)}, u32[]{:S(2)}, u32[]{:S(2)}) collective-permute-start(bf16[1,2,1024,1024]{3,2,1,0:T(8,128)(2,1)S(1)} %copy-done.2), channel_id=1, source_target_pairs={{8,0},{0,8},{9,1},{1,9},{10,2},{2,10},{11,3},{3,11},{12,4},{4,12},... | collective-permute-start | bytes 12582920 | tf_op jit(solution)/shard_map/ppermute | solution.py:48
  23.9 8.5 %collective-permute-start.10 = (bf16[256,512]{1,0:T(8,128)(2,1)S(1)}, bf16[256,512]{1,0:T(8,128)(2,1)S(1)}, u32[]{:S(2)}, u32[]{:S(2)}) collective-permute-start(bf16[256,512]{1,0:T(8,128)(2,1)S(1)} %get-tuple-element.51), channel_id=1, source_target_pairs={{0,1},{1,0},{2,3},{3,2},{4,5},{5,4},{6,7},{7,6},{8,9},{9,8},{10,11... | collective-permute-start | bytes 786440 | tf_op jit(solution)/shard_map/ppermute | solution.py:35
  24.7 19.5 %copy-start.1 = (bf16[1024,1024]{1,0:T(8,128)(2,1)S(1)}, bf16[1024,1024]{1,0:T(8,128)(2,1)}, u32[]{:S(2)}) copy-start(bf16[1024,1024]{1,0:T(8,128)(2,1)} %refs_2_.1) | copy-start | bytes 6291460
  24.7 19.5 %copy-start.7 = (f32[1024]{0:T(1024)S(1)}, f32[1024]{0:T(1024)}, u32[]{:S(2)}) copy-start(f32[1024]{0:T(1024)} %param.22) | copy-start | bytes 12292
  24.7 8.2 %collective-permute-start.11 = (bf16[256,512]{1,0:T(8,128)(2,1)S(1)}, bf16[256,512]{1,0:T(8,128)(2,1)S(1)}, u32[]{:S(2)}, u32[]{:S(2)}) collective-permute-start(bf16[256,512]{1,0:T(8,128)(2,1)S(1)} %get-tuple-element.52), channel_id=1, source_target_pairs={{0,2},{1,3},{2,0},{3,1},{4,6},{5,7},{6,4},{7,5},{8,10},{9,11},{10,... | collective-permute-start | bytes 786440 | tf_op jit(solution)/shard_map/ppermute | solution.py:35
  32.9 12.0 %copy-start.10 = (s32[1,64]{1,0:T(1,128)S(1)}, s32[1,64]{1,0:T(1,128)}, u32[]{:S(2)}) copy-start(s32[1,64]{1,0:T(1,128)} %refs_1_.1) | copy-start | bytes 772
  32.9 5.0 %collective-permute-start.14 = (bf16[128,512]{1,0:T(8,128)(2,1)S(1)}, bf16[128,512]{1,0:T(8,128)(2,1)S(1)}, u32[]{:S(2)}, u32[]{:S(2)}) collective-permute-start(bf16[128,512]{1,0:T(8,128)(2,1)S(1)} %get-tuple-element.63), channel_id=1, source_target_pairs={{0,2},{1,3},{2,0},{3,1},{4,6},{5,7},{6,4},{7,5},{8,10},{9,11},{10,... | collective-permute-start | bytes 393224 | tf_op jit(solution)/shard_map/ppermute | solution.py:35
  34.3 5.3 %collective-permute-start.12 = (bf16[128,512]{1,0:T(8,128)(2,1)S(1)}, bf16[128,512]{1,0:T(8,128)(2,1)S(1)}, u32[]{:S(2)}, u32[]{:S(2)}) collective-permute-start(bf16[128,512]{1,0:T(8,128)(2,1)S(1)} %get-tuple-element.57), channel_id=1, source_target_pairs={{0,1},{1,0},{2,3},{3,2},{4,5},{5,4},{6,7},{7,6},{8,9},{9,8},{10,11... | collective-permute-start | bytes 393224 | tf_op jit(solution)/shard_map/ppermute | solution.py:35
  38.0 6.1 %collective-permute-start.15 = (bf16[64,512]{1,0:T(8,128)(2,1)S(1)}, bf16[64,512]{1,0:T(8,128)(2,1)S(1)}, u32[]{:S(2)}, u32[]{:S(2)}) collective-permute-start(bf16[64,512]{1,0:T(8,128)(2,1)S(1)} %get-tuple-element.65), channel_id=1, source_target_pairs={{0,4},{1,5},{2,6},{3,7},{4,0},{5,1},{6,2},{7,3},{8,12},{9,13},{10,... | collective-permute-start | bytes 196616 | tf_op jit(solution)/shard_map/ppermute | solution.py:35
  39.6 5.3 %collective-permute-start.13 = (bf16[64,512]{1,0:T(8,128)(2,1)S(1)}, bf16[64,512]{1,0:T(8,128)(2,1)S(1)}, u32[]{:S(2)}, u32[]{:S(2)}) collective-permute-start(bf16[64,512]{1,0:T(8,128)(2,1)S(1)} %get-tuple-element.59), channel_id=1, source_target_pairs={{0,4},{1,5},{2,6},{3,7},{4,0},{5,1},{6,2},{7,3},{8,12},{9,13},{10,... | collective-permute-start | bytes 196616 | tf_op jit(solution)/shard_map/ppermute | solution.py:35

commit v12 on v11

--- a/solution.py
+++ b/solution.py
@@ -102,6 +102,25 @@
         item += (hist_index ^ flip_of(piece)) * shard_rows
         blocks.append((item == ids_row).astype(F32).astype(BF16))
     return jnp.concatenate(blocks, axis=0)
+
+
+def first_ids_kernel(own_hbm, far_ref, out_ref, own_ref, sem):
+    copy = pltpu.make_async_copy(own_hbm, own_ref, sem)
+    copy.start()
+    copy.wait()
+    out_ref[:1, :] = own_ref[...]
+    out_ref[1:, :] = far_ref[...]
+
+
+def first_ids(own, far):
+    return kernel_call(
+        first_ids_kernel,
+        "first_ids",
+        [jax.ShapeDtypeStruct((2, own.shape[1]), own.dtype)],
+        [ANY, VMEM],
+        scratch=[pltpu.VMEM(own.shape, own.dtype), pltpu.SemaphoreType.DMA],
+        flops=LOADS_BESIDE,
+    )(own, far)[0]
 
 
 def stack_kernel(*refs):
@@ -350,7 +369,7 @@
 
     first_pieces = [((flip,) * users, 0, None) for flip in (0, shared)] + [(flips, 0, None) for flips in near_flips]
     first_blocks = [item_table, shared_shard] + near_shards
-    near_ids = stack([item_ids, far_ids], flops=LOADS_BESIDE)
+    near_ids = first_ids(item_ids, far_ids)
     w_query, near_ids = lax.optimization_barrier((w_query, near_ids))
     first, masked_values = attend_first(
         first_pieces, first_blocks, shard_rows, history_lengths, w_query, history_keys, history_values
@@ -394,7 +413,7 @@
     for at in range(bits):
         arriving = [swapped(sent, 1 << turn[at]) for (_, sent), turn in zip(held, side_turns)]
         if at == 0:
-            *arriving, embed = lax.optimization_barrier((*arriving, embed))
+            arriving[0], embed = lax.optimization_barrier((arriving[0], embed))
         pairs = [(kept, come) for (kept, _), come in zip(held, arriving)]
         if at < bits - 1:
             held = [fold([pair]) for pair in pairs]

time: 47.6 us -> 47.6 us (level)
  transfers between devices with their start and end apart: 17 -> 17, of which waited for: 10 -> 9; matrix products, arithmetic and copies ran while one was open for 0% -> 0% of each run, Pallas kernels for 13% -> 13%
where the time goes in v12:
time: 47.6 us; the launch traced here: 47.4 us
  starting transfers between devices  20.4 us (43%)
  waiting for transfers between devices  14.8 us (31%)
  Pallas kernels  9.86 us (21%)
  between operations  1.49 us (3%)
  local copies, waits for them, and re-layouts  0.84 us (2%)
    ppermute x10, starting transfers between devices, swapped(): return lax.ppermute(value, 'hist', [(i, i ^ flip) for i in range(count)])  13.3 us
    ppermute x10, waiting for transfers between devices, swapped(): return lax.ppermute(value, 'hist', [(i, i ^ flip) for i in range(count)])  11.5 us
    ppermute x3, starting transfers between devices, swapped_by_user(): return lax.ppermute(value, ('user', 'hist'), pairs)  6.3 us
    ppermute x3, waiting for transfers between devices, swapped_by_user(): return lax.ppermute(value, ('user', 'hist'), pairs)  2.71 us
    pallas_call x1, Pallas kernels, finish(): kernel_call(finish_kernel, 'finish', [jax.ShapeDtypeStruct((1, slots, wid...  2.61 us
    pallas_call x1, Pallas kernels, attend_next(): kernel_call(functools.partial(next_kernel, pieces), 'attend_next', [jax.S...  2.5 us
    pallas_call x1, Pallas kernels, attend_first(): kernel_call(functools.partial(first_kernel, pieces), 'attend_first', [jax...  2.5 us
  transfers between devices with their start and end apart: 17, of which 9 were waited for; matrix products, arithmetic and copies ran while one was open for 0% of the time, Pallas kernels for 13%

profile of v12, /device:TPU:0, one launch (start us, length us, event | category | flops | bytes accessed | tf_op | source)
XLA Modules:
  0.0 47.4 jit_solution(12106358107767773427)
XLA Ops:
  0.0 3.0 %collective-permute-start = (s32[1,64]{1,0:T(1,128)}, s32[1,64]{1,0:T(1,128)S(1)}, u32[]{:S(2)}, u32[]{:S(2)}) collective-permute-start(s32[1,64]{1,0:T(1,128)} %ids_ref.1), channel_id=1, source_target_pairs={{0,2},{1,3},{2,0},{3,1},{4,6},{5,7},{6,4},{7,5},{8,10},{9,11},{10,... | collective-permute-start | bytes 776 | tf_op jit(solution)/shard_map/ppermute | solution.py:35
  3.0 3.4 %collective-permute-start.4 = (bf16[64,1024]{1,0:T(8,128)(2,1)}, bf16[64,1024]{1,0:T(8,128)(2,1)S(1)}, u32[]{:S(2)}, u32[]{:S(2)}) collective-permute-start(bf16[64,1024]{1,0:T(8,128)(2,1)} %refs_0_.4), channel_id=1, source_target_pairs={{0,7},{1,6},{2,5},{3,4},{4,3},{5,2},{6,1},{7,0},{8,12},{9,13},{10,... | collective-permute-start | bytes 393224 | tf_op jit(solution)/shard_map/ppermute | solution.py:43
  6.5 0.7 %collective-permute-start.2 = (bf16[64,1024]{1,0:T(8,128)(2,1)}, bf16[64,1024]{1,0:T(8,128)(2,1)S(1)}, u32[]{:S(2)}, u32[]{:S(2)}) collective-permute-start(bf16[64,1024]{1,0:T(8,128)(2,1)} %refs_0_.4), channel_id=1, source_target_pairs={{0,2},{1,3},{2,0},{3,1},{4,6},{5,7},{6,4},{7,5},{8,11},{9,10},{10,... | collective-permute-start | bytes 393224 | tf_op jit(solution)/shard_map/ppermute | solution.py:43
  7.1 0.5 %collective-permute-start.1 = (bf16[64,1024]{1,0:T(8,128)(2,1)}, bf16[64,1024]{1,0:T(8,128)(2,1)S(1)}, u32[]{:S(2)}, u32[]{:S(2)}) collective-permute-start(bf16[64,1024]{1,0:T(8,128)(2,1)} %refs_0_.4), channel_id=1, source_target_pairs={{0,1},{1,0},{2,3},{3,2},{4,5},{5,4},{6,7},{7,6},{8,9},{9,8},{10,11... | collective-permute-start | bytes 393224 | tf_op jit(solution)/shard_map/ppermute | solution.py:35
  7.6 2.2 %collective-permute-start.5 = (bf16[64,1024]{1,0:T(8,128)(2,1)}, bf16[64,1024]{1,0:T(8,128)(2,1)S(1)}, u32[]{:S(2)}, u32[]{:S(2)}) collective-permute-start(bf16[64,1024]{1,0:T(8,128)(2,1)} %refs_0_.4), channel_id=1, source_target_pairs={{0,5},{1,4},{2,7},{3,6},{4,1},{5,0},{6,3},{7,2},{8,14},{9,15},{10,... | collective-permute-start | bytes 393224 | tf_op jit(solution)/shard_map/ppermute | solution.py:43
  10.5 0.0 copy-start
  10.5 0.0 copy-start.3
  10.5 0.0 collective-permute-done.far_ref
  10.5 0.0 copy-start.8
  10.5 0.8 %copy-done.8 = s32[1,64]{1,0:T(1,128)S(1)} copy-done((s32[1,64]{1,0:T(1,128)S(1)}, s32[1,64]{1,0:T(1,128)}, u32[]{:S(2)}) %copy-start.8) | copy-done | bytes 280
  11.4 1.8 %collective-permute-start.3 = (s32[2,64]{1,0:T(2,128)S(1)}, s32[2,64]{1,0:T(2,128)S(1)}, u32[]{:S(2)}, u32[]{:S(2)}) collective-permute-start(s32[2,64]{1,0:T(2,128)S(1)} %first_ids.1.refs_0_), channel_id=1, source_target_pairs={{0,4},{1,5},{2,6},{3,7},{4,0},{5,1},{6,2},{7,3},{8,12},{9,13},{10,... | collective-permute-start | bytes 1544 | tf_op jit(solution)/shard_map/ppermute | solution.py:35
  13.1 2.2 %collective-permute-done.2.refs_2_ = bf16[64,1024]{1,0:T(8,128)(2,1)S(1)} collective-permute-done((bf16[64,1024]{1,0:T(8,128)(2,1)}, bf16[64,1024]{1,0:T(8,128)(2,1)S(1)}, u32[]{:S(2)}, u32[]{:S(2)}) %collective-permute-start.2) | collective-permute-done | bytes 131104 | tf_op jit(solution)/shard_map/ppermute | solution.py:43
  15.3 0.0 collective-permute-done.1.refs_1_
  15.3 0.0 copy-done.3
  15.4 2.5 %attend_first.1 = (bf16[192,1024]{1,0:T(8,128)(2,1)S(1)}, bf16[512,1024]{1,0:T(8,128)(2,1)S(1)}) custom-call(s32[1]{0:T(128)S(6)} %copy.14.length_ref, bf16[1024,1024]{1,0:T(8,128)(2,1)S(1)} %copy-done, bf16[1,512,1024]{2,1,0:T(8,128)(2,1)S(1)} %copy-done.3, bf16[1,512,1024]{2,1,0:T(8,128)(2,1)S(1)} %copy-done.5, bf16[64,1024]{1,0:T(8,128)(2,1)S(1)} %copy-done.6, ...), custom_call_target="tpu_custom_call" | custom-call | flops 805306368 | tf_op jit(solution)/shard_map/attend_first/pallas_call | solution.py:176
  17.9 0.0 collective-permute-done.3.refs_1_
  17.9 0.0 collective-permute-done.4.refs_1_.refs_4_
  17.9 0.5 %collective-permute-done.5.refs_3_.refs_6_ = bf16[64,1024]{1,0:T(8,128)(2,1)S(1)} collective-permute-done((bf16[64,1024]{1,0:T(8,128)(2,1)}, bf16[64,1024]{1,0:T(8,128)(2,1)S(1)}, u32[]{:S(2)}, u32[]{:S(2)}) %collective-permute-start.5) | collective-permute-done | bytes 131104 | tf_op jit(solution)/shard_map/ppermute | solution.py:43
  18.4 0.0 collective-permute-start.8
  18.4 0.5 %collective-permute-start.9 = (bf16[64,1024]{1,0:T(8,128)(2,1)S(1)}, bf16[64,1024]{1,0:T(8,128)(2,1)S(1)}, u32[]{:S(2)}, u32[]{:S(2)}) collective-permute-start(bf16[64,1024]{1,0:T(8,128)(2,1)S(1)} %collective-permute-done.5.refs_3_.refs_6_), channel_id=1, source_target_pairs={{8,0},{0,8},{9,1},{1,9},{10,2},{2,10},{11,3},{3,11},{12,4},{4,12},... | collective-permute-start | bytes 393224 | tf_op jit(solution)/shard_map/ppermute | solution.py:48
  18.9 0.0 collective-permute-start.7
  18.9 0.7 %collective-permute-start.6 = (s32[4,64]{1,0:T(4,128)S(1)}, s32[4,64]{1,0:T(4,128)S(1)}, u32[]{:S(2)}, u32[]{:S(2)}) collective-permute-start(s32[4,64]{1,0:T(4,128)S(1)} %stack.1.near_ids_ref), channel_id=1, source_target_pairs={{0,1},{1,0},{2,3},{3,2},{4,5},{5,4},{6,7},{7,6},{8,9},{9,8},{10,11... | collective-permute-start | bytes 3080 | tf_op jit(solution)/shard_map/ppermute | solution.py:35
  19.6 0.1 collective-permute-done.8.refs_2_.refs_5_
  19.7 0.2 collective-permute-done.9.refs_4_.refs_7_
  19.9 0.3 collective-permute-done.7.refs_0_.refs_3_
  20.3 2.5 %attend_next.1.refs_1_ = bf16[320,1024]{1,0:T(8,128)(2,1)S(1)} custom-call(bf16[1024,1024]{1,0:T(8,128)(2,1)S(1)} %copy-done, bf16[1,512,1024]{2,1,0:T(8,128)(2,1)S(1)} %copy-done.3, bf16[512,1024]{1,0:T(8,128)(2,1)S(1)} %get-tuple-element.45.values_ref, bf16[64,1024]{1,0:T(8,128)(2,1)S(1)} %collective-permute-done.7.refs_0_.refs_3_, ...), custom_call_target="tpu_custom_call" | custom-call | flops 1342177280 | tf_op jit(solution)/shard_map/attend_next/pallas_call | solution.py:187
  22.8 0.0 collective-permute-done.6.far_ids_ref
  22.8 0.9 %place.1 = (bf16[256,512]{1,0:T(8,128)(2,1)S(1)}, bf16[256,512]{1,0:T(8,128)(2,1)S(1)}, bf16[256,512]{1,0:T(8,128)(2,1)S(1)}, bf16[256,512]{1,0:T(8,128)(2,1)S(1)}) custom-call(s32[4,64]{1,0:T(4,128)S(1)} %stack.1.near_ids_ref, s32[4,64]{1,0:T(4,128)S(1)} %collective-permute-done.6.far_ids_ref, bf16[192,1024]{1,0:T(8,128)(2,1)S(1)} %get-tuple-element.44.refs_0_, ...), custom_call_target="tpu_custom_call" | custom-call | flops 536870912 | tf_op jit(solution)/shard_map/place/pallas_call | solution.py:219
  23.6 0.3 collective-permute-start.16
  23.9 0.8 %collective-permute-start.13 = (bf16[256,512]{1,0:T(8,128)(2,1)S(1)}, bf16[256,512]{1,0:T(8,128)(2,1)S(1)}, u32[]{:S(2)}, u32[]{:S(2)}) collective-permute-start(bf16[256,512]{1,0:T(8,128)(2,1)S(1)} %get-tuple-element.57), channel_id=1, source_target_pairs={{0,1},{1,0},{2,3},{3,2},{4,5},{5,4},{6,7},{7,6},{8,9},{9,8},{10,11... | collective-permute-start | bytes 786440 | tf_op jit(solution)/shard_map/ppermute | solution.py:35
  24.7 1.1 %collective-permute-start.10 = (bf16[256,512]{1,0:T(8,128)(2,1)S(1)}, bf16[256,512]{1,0:T(8,128)(2,1)S(1)}, u32[]{:S(2)}, u32[]{:S(2)}) collective-permute-start(bf16[256,512]{1,0:T(8,128)(2,1)S(1)} %get-tuple-element.50), channel_id=1, source_target_pairs={{0,2},{1,3},{2,0},{3,1},{4,6},{5,7},{6,4},{7,5},{8,10},{9,11},{10,... | collective-permute-start | bytes 786440 | tf_op jit(solution)/shard_map/ppermute | solution.py:35
  25.8 0.9 %prepare.1 = (f32[64,1024]{1,0:T(8,128)S(1)}, f32[64,1024]{1,0:T(8,128)S(1)}) custom-call(bf16[256,512]{1,0:T(8,128)(2,1)S(1)} %get-tuple-element.56.after_ref.refs_0_, s32[1,64]{1,0:T(1,128)S(1)} %copy-done.9, bf16[1024,1024]{1,0:T(8,128)(2,1)S(1)} %copy-done.4, bf16[64,1024]{1,0:T(8,128)(2,1)S(1)} %copy-done.6, ...), custom_call_target="tpu_custom_call" | custom-call | flops 201326592 | tf_op jit(solution)/shard_map/prepare/pallas_call | solution.py:264
  26.7 5.7 %collective-permute-done.13.refs_1_ = bf16[256,512]{1,0:T(8,128)(2,1)S(1)} collective-permute-done((bf16[256,512]{1,0:T(8,128)(2,1)S(1)}, bf16[256,512]{1,0:T(8,128)(2,1)S(1)}, u32[]{:S(2)}, u32[]{:S(2)}) %collective-permute-start.13) | collective-permute-done | bytes 262176 | tf_op jit(solution)/shard_map/ppermute | solution.py:35
  32.4 0.1 fold.6
  32.5 1.2 %collective-permute-start.14 = (bf16[128,512]{1,0:T(8,128)(2,1)S(1)}, bf16[128,512]{1,0:T(8,128)(2,1)S(1)}, u32[]{:S(2)}, u32[]{:S(2)}) collective-permute-start(bf16[128,512]{1,0:T(8,128)(2,1)S(1)} %get-tuple-element.61), channel_id=1, source_target_pairs={{0,2},{1,3},{2,0},{3,1},{4,6},{5,7},{6,4},{7,5},{8,10},{9,11},{10,... | collective-permute-start | bytes 393224 | tf_op jit(solution)/shard_map/ppermute | solution.py:35
  33.7 0.0 collective-permute-done.10.refs_1_
  33.7 0.1 fold.4
  33.7 0.9 %collective-permute-start.11 = (bf16[128,512]{1,0:T(8,128)(2,1)S(1)}, bf16[128,512]{1,0:T(8,128)(2,1)S(1)}, u32[]{:S(2)}, u32[]{:S(2)}) collective-permute-start(bf16[128,512]{1,0:T(8,128)(2,1)S(1)} %get-tuple-element.52), channel_id=1, source_target_pairs={{0,1},{1,0},{2,3},{3,2},{4,5},{5,4},{6,7},{7,6},{8,9},{9,8},{10,11... | collective-permute-start | bytes 393224 | tf_op jit(solution)/shard_map/ppermute | solution.py:35
  34.6 2.9 %collective-permute-done.14.refs_1_ = bf16[128,512]{1,0:T(8,128)(2,1)S(1)} collective-permute-done((bf16[128,512]{1,0:T(8,128)(2,1)S(1)}, bf16[128,512]{1,0:T(8,128)(2,1)S(1)}, u32[]{:S(2)}, u32[]{:S(2)}) %collective-permute-start.14) | collective-permute-done | bytes 131104 | tf_op jit(solution)/shard_map/ppermute | solution.py:35
  37.6 1.5 %collective-permute-start.15 = (bf16[64,512]{1,0:T(8,128)(2,1)S(1)}, bf16[64,512]{1,0:T(8,128)(2,1)S(1)}, u32[]{:S(2)}, u32[]{:S(2)}) collective-permute-start(bf16[64,512]{1,0:T(8,128)(2,1)S(1)} %get-tuple-element.63), channel_id=1, source_target_pairs={{0,4},{1,5},{2,6},{3,7},{4,0},{5,1},{6,2},{7,3},{8,12},{9,13},{10,... | collective-permute-start | bytes 196616 | tf_op jit(solution)/shard_map/ppermute | solution.py:35
  39.1 0.0 collective-permute-done.11.refs_1_
  39.1 1.9 %collective-permute-start.12 = (bf16[64,512]{1,0:T(8,128)(2,1)S(1)}, bf16[64,512]{1,0:T(8,128)(2,1)S(1)}, u32[]{:S(2)}, u32[]{:S(2)}) collective-permute-start(bf16[64,512]{1,0:T(8,128)(2,1)S(1)} %get-tuple-element.54), channel_id=1, source_target_pairs={{0,4},{1,5},{2,6},{3,7},{4,0},{5,1},{6,2},{7,3},{8,12},{9,13},{10,... | collective-permute-start | bytes 196616 | tf_op jit(solution)/shard_map/ppermute | solution.py:35
  41.6 2.5 %collective-permute-done.15.come_ref = bf16[64,512]{1,0:T(8,128)(2,1)S(1)} collective-permute-done((bf16[64,512]{1,0:T(8,128)(2,1)S(1)}, bf16[64,512]{1,0:T(8,128)(2,1)S(1)}, u32[]{:S(2)}, u32[]{:S(2)}) %collective-permute-start.15) | collective-permute-done | bytes 65568 | tf_op jit(solution)/shard_map/ppermute | solution.py:35
  44.1 0.0 copy-done.1
  44.1 0.3 mix.1
  44.4 0.4 collective-permute-done.12.come_ref
  44.8 0.0 collective-permute-done.16.refs_4_
  44.8 2.6 %finish.1 = bf16[1,64,1024]{2,1,0:T(8,128)(2,1)} custom-call(f32[64,512]{1,0:T(8,128)S(1)} %get-tuple-element.53.kept_ref, bf16[64,512]{1,0:T(8,128)(2,1)S(1)} %collective-permute-done.12.come_ref, f32[64,128]{1,0:T(8,128)S(1)} %get-tuple-element.65.squares_ref, f32[64,1024]{1,0:T(8,128)S(1)} %get-tuple-element.66.mixed_ref, ...), custom_call_target="tpu_custom_call" | custom-call | flops 671088640 | tf_op jit(solution)/shard_map/finish/pallas_call | solution.py:328
  (20 shorter events, 0.1 us)
Async XLA Ops:
  0.0 10.5 %collective-permute-start = (s32[1,64]{1,0:T(1,128)}, s32[1,64]{1,0:T(1,128)S(1)}, u32[]{:S(2)}, u32[]{:S(2)}) collective-permute-start(s32[1,64]{1,0:T(1,128)} %ids_ref.1), channel_id=1, source_target_pairs={{0,2},{1,3},{2,0},{3,1},{4,6},{5,7},{6,4},{7,5},{8,10},{9,11},{10,... | collective-permute-start | bytes 776 | tf_op jit(solution)/shard_map/ppermute | solution.py:35
  3.0 14.9 %collective-permute-start.4 = (bf16[64,1024]{1,0:T(8,128)(2,1)}, bf16[64,1024]{1,0:T(8,128)(2,1)S(1)}, u32[]{:S(2)}, u32[]{:S(2)}) collective-permute-start(bf16[64,1024]{1,0:T(8,128)(2,1)} %refs_0_.4), channel_id=1, source_target_pairs={{0,7},{1,6},{2,5},{3,4},{4,3},{5,2},{6,1},{7,0},{8,12},{9,13},{10,... | collective-permute-start | bytes 393224 | tf_op jit(solution)/shard_map/ppermute | solution.py:43
  6.5 8.9 %collective-permute-start.2 = (bf16[64,1024]{1,0:T(8,128)(2,1)}, bf16[64,1024]{1,0:T(8,128)(2,1)S(1)}, u32[]{:S(2)}, u32[]{:S(2)}) collective-permute-start(bf16[64,1024]{1,0:T(8,128)(2,1)} %refs_0_.4), channel_id=1, source_target_pairs={{0,2},{1,3},{2,0},{3,1},{4,6},{5,7},{6,4},{7,5},{8,11},{9,10},{10,... | collective-permute-start | bytes 393224 | tf_op jit(solution)/shard_map/ppermute | solution.py:43
  7.1 8.2 %collective-permute-start.1 = (bf16[64,1024]{1,0:T(8,128)(2,1)}, bf16[64,1024]{1,0:T(8,128)(2,1)S(1)}, u32[]{:S(2)}, u32[]{:S(2)}) collective-permute-start(bf16[64,1024]{1,0:T(8,128)(2,1)} %refs_0_.4), channel_id=1, source_target_pairs={{0,1},{1,0},{2,3},{3,2},{4,5},{5,4},{6,7},{7,6},{8,9},{9,8},{10,11... | collective-permute-start | bytes 393224 | tf_op jit(solution)/shard_map/ppermute | solution.py:35
  7.6 10.8 %collective-permute-start.5 = (bf16[64,1024]{1,0:T(8,128)(2,1)}, bf16[64,1024]{1,0:T(8,128)(2,1)S(1)}, u32[]{:S(2)}, u32[]{:S(2)}) collective-permute-start(bf16[64,1024]{1,0:T(8,128)(2,1)} %refs_0_.4), channel_id=1, source_target_pairs={{0,5},{1,4},{2,7},{3,6},{4,1},{5,0},{6,3},{7,2},{8,14},{9,15},{10,... | collective-permute-start | bytes 393224 | tf_op jit(solution)/shard_map/ppermute | solution.py:43
  10.5 4.8 %copy-start = (bf16[1024,1024]{1,0:T(8,128)(2,1)S(1)}, bf16[1024,1024]{1,0:T(8,128)(2,1)}, u32[]{:S(2)}) copy-start(bf16[1024,1024]{1,0:T(8,128)(2,1)} %w_query_ref.1) | copy-start | bytes 6291460
  10.5 4.8 %copy-start.3 = (bf16[1,512,1024]{2,1,0:T(8,128)(2,1)S(1)}, bf16[1,512,1024]{2,1,0:T(8,128)(2,1)}, u32[]{:S(2)}) copy-start(bf16[1,512,1024]{2,1,0:T(8,128)(2,1)} %keys_ref.3) | copy-start | bytes 3145732
  10.5 4.8 %copy-start.5 = (bf16[1,512,1024]{2,1,0:T(8,128)(2,1)S(1)}, bf16[1,512,1024]{2,1,0:T(8,128)(2,1)}, u32[]{:S(2)}) copy-start(bf16[1,512,1024]{2,1,0:T(8,128)(2,1)} %values_ref.1) | copy-start | bytes 3145732
  10.5 4.8 %copy-start.6 = (bf16[64,1024]{1,0:T(8,128)(2,1)S(1)}, bf16[64,1024]{1,0:T(8,128)(2,1)}, u32[]{:S(2)}) copy-start(bf16[64,1024]{1,0:T(8,128)(2,1)} %refs_0_.4) | copy-start | bytes 393220
  10.5 0.8 %copy-start.8 = (s32[1,64]{1,0:T(1,128)S(1)}, s32[1,64]{1,0:T(1,128)}, u32[]{:S(2)}) copy-start(s32[1,64]{1,0:T(1,128)} %ids_ref.1) | copy-start | bytes 772
  11.4 6.5 %collective-permute-start.3 = (s32[2,64]{1,0:T(2,128)S(1)}, s32[2,64]{1,0:T(2,128)S(1)}, u32[]{:S(2)}, u32[]{:S(2)}) collective-permute-start(s32[2,64]{1,0:T(2,128)S(1)} %first_ids.1.refs_0_), channel_id=1, source_target_pairs={{0,4},{1,5},{2,6},{3,7},{4,0},{5,1},{6,2},{7,3},{8,12},{9,13},{10,... | collective-permute-start | bytes 1544 | tf_op jit(solution)/shard_map/ppermute | solution.py:35
  18.4 1.3 %collective-permute-start.8 = (bf16[64,1024]{1,0:T(8,128)(2,1)S(1)}, bf16[64,1024]{1,0:T(8,128)(2,1)S(1)}, u32[]{:S(2)}, u32[]{:S(2)}) collective-permute-start(bf16[64,1024]{1,0:T(8,128)(2,1)S(1)} %collective-permute-done.4.refs_1_.refs_4_), channel_id=1, source_target_pairs={{8,0},{0,8},{9,1},{1,9},{10,2},{2,10},{11,3},{3,11},{12,4},{4,12},... | collective-permute-start | bytes 393224 | tf_op jit(solution)/shard_map/ppermute | solution.py:48
  18.4 1.5 %collective-permute-start.9 = (bf16[64,1024]{1,0:T(8,128)(2,1)S(1)}, bf16[64,1024]{1,0:T(8,128)(2,1)S(1)}, u32[]{:S(2)}, u32[]{:S(2)}) collective-permute-start(bf16[64,1024]{1,0:T(8,128)(2,1)S(1)} %collective-permute-done.5.refs_3_.refs_6_), channel_id=1, source_target_pairs={{8,0},{0,8},{9,1},{1,9},{10,2},{2,10},{11,3},{3,11},{12,4},{4,12},... | collective-permute-start | bytes 393224 | tf_op jit(solution)/shard_map/ppermute | solution.py:48
  18.9 1.3 %collective-permute-start.7 = (bf16[64,1024]{1,0:T(8,128)(2,1)S(1)}, bf16[64,1024]{1,0:T(8,128)(2,1)S(1)}, u32[]{:S(2)}, u32[]{:S(2)}) collective-permute-start(bf16[64,1024]{1,0:T(8,128)(2,1)S(1)} %collective-permute-done.2.refs_2_), channel_id=1, source_target_pairs={{8,0},{0,8},{9,1},{1,9},{10,2},{2,10},{11,3},{3,11},{12,4},{4,12},... | collective-permute-start | bytes 393224 | tf_op jit(solution)/shard_map/ppermute | solution.py:48
  18.9 3.9 %collective-permute-start.6 = (s32[4,64]{1,0:T(4,128)S(1)}, s32[4,64]{1,0:T(4,128)S(1)}, u32[]{:S(2)}, u32[]{:S(2)}) collective-permute-start(s32[4,64]{1,0:T(4,128)S(1)} %stack.1.near_ids_ref), channel_id=1, source_target_pairs={{0,1},{1,0},{2,3},{3,2},{4,5},{5,4},{6,7},{7,6},{8,9},{9,8},{10,11... | collective-permute-start | bytes 3080 | tf_op jit(solution)/shard_map/ppermute | solution.py:35
  20.3 3.4 %copy-start.2 = (bf16[1,2,1024,1024]{3,2,1,0:T(8,128)(2,1)S(1)}, bf16[1,2,1024,1024]{3,2,1,0:T(8,128)(2,1)}, u32[]{:S(2)}) copy-start(bf16[1,2,1024,1024]{3,2,1,0:T(8,128)(2,1)} %refs_3_.1) | copy-start | bytes 12582916
  20.3 5.5 %copy-start.4 = (bf16[1024,1024]{1,0:T(8,128)(2,1)S(1)}, bf16[1024,1024]{1,0:T(8,128)(2,1)}, u32[]{:S(2)}) copy-start(bf16[1024,1024]{1,0:T(8,128)(2,1)} %w_gate_ref.1) | copy-start | bytes 6291460
  20.3 5.5 %copy-start.9 = (s32[1,64]{1,0:T(1,128)S(1)}, s32[1,64]{1,0:T(1,128)}, u32[]{:S(2)}) copy-start(s32[1,64]{1,0:T(1,128)} %ids_ref.1) | copy-start | bytes 772
  23.6 21.2 %collective-permute-start.16 = (bf16[1,2,1024,1024]{3,2,1,0:T(8,128)(2,1)S(1)}, bf16[1,2,1024,1024]{3,2,1,0:T(8,128)(2,1)S(1)}, u32[]{:S(2)}, u32[]{:S(2)}) collective-permute-start(bf16[1,2,1024,1024]{3,2,1,0:T(8,128)(2,1)S(1)} %copy-done.2), channel_id=1, source_target_pairs={{8,0},{0,8},{9,1},{1,9},{10,2},{2,10},{11,3},{3,11},{12,4},{4,12},... | collective-permute-start | bytes 12582920 | tf_op jit(solution)/shard_map/ppermute | solution.py:48
  23.9 8.5 %collective-permute-start.13 = (bf16[256,512]{1,0:T(8,128)(2,1)S(1)}, bf16[256,512]{1,0:T(8,128)(2,1)S(1)}, u32[]{:S(2)}, u32[]{:S(2)}) collective-permute-start(bf16[256,512]{1,0:T(8,128)(2,1)S(1)} %get-tuple-element.57), channel_id=1, source_target_pairs={{0,1},{1,0},{2,3},{3,2},{4,5},{5,4},{6,7},{7,6},{8,9},{9,8},{10,11... | collective-permute-start | bytes 786440 | tf_op jit(solution)/shard_map/ppermute | solution.py:35
  24.7 19.4 %copy-start.1 = (bf16[1024,1024]{1,0:T(8,128)(2,1)S(1)}, bf16[1024,1024]{1,0:T(8,128)(2,1)}, u32[]{:S(2)}) copy-start(bf16[1024,1024]{1,0:T(8,128)(2,1)} %refs_2_.1) | copy-start | bytes 6291460
  24.7 19.4 %copy-start.7 = (f32[1024]{0:T(1024)S(1)}, f32[1024]{0:T(1024)}, u32[]{:S(2)}) copy-start(f32[1024]{0:T(1024)} %param.22) | copy-start | bytes 12292
  24.7 9.0 %collective-permute-start.10 = (bf16[256,512]{1,0:T(8,128)(2,1)S(1)}, bf16[256,512]{1,0:T(8,128)(2,1)S(1)}, u32[]{:S(2)}, u32[]{:S(2)}) collective-permute-start(bf16[256,512]{1,0:T(8,128)(2,1)S(1)} %get-tuple-element.50), channel_id=1, source_target_pairs={{0,2},{1,3},{2,0},{3,1},{4,6},{5,7},{6,4},{7,5},{8,10},{9,11},{10,... | collective-permute-start | bytes 786440 | tf_op jit(solution)/shard_map/ppermute | solution.py:35
  32.4 12.4 %copy-start.10 = (s32[1,64]{1,0:T(1,128)S(1)}, s32[1,64]{1,0:T(1,128)}, u32[]{:S(2)}) copy-start(s32[1,64]{1,0:T(1,128)} %refs_1_.1) | copy-start | bytes 772
  32.5 5.0 %collective-permute-start.14 = (bf16[128,512]{1,0:T(8,128)(2,1)S(1)}, bf16[128,512]{1,0:T(8,128)(2,1)S(1)}, u32[]{:S(2)}, u32[]{:S(2)}) collective-permute-start(bf16[128,512]{1,0:T(8,128)(2,1)S(1)} %get-tuple-element.61), channel_id=1, source_target_pairs={{0,2},{1,3},{2,0},{3,1},{4,6},{5,7},{6,4},{7,5},{8,10},{9,11},{10,... | collective-permute-start | bytes 393224 | tf_op jit(solution)/shard_map/ppermute | solution.py:35
  33.7 5.3 %collective-permute-start.11 = (bf16[128,512]{1,0:T(8,128)(2,1)S(1)}, bf16[128,512]{1,0:T(8,128)(2,1)S(1)}, u32[]{:S(2)}, u32[]{:S(2)}) collective-permute-start(bf16[128,512]{1,0:T(8,128)(2,1)S(1)} %get-tuple-element.52), channel_id=1, source_target_pairs={{0,1},{1,0},{2,3},{3,2},{4,5},{5,4},{6,7},{7,6},{8,9},{9,8},{10,11... | collective-permute-start | bytes 393224 | tf_op jit(solution)/shard_map/ppermute | solution.py:35
  37.6 6.5 %collective-permute-start.15 = (bf16[64,512]{1,0:T(8,128)(2,1)S(1)}, bf16[64,512]{1,0:T(8,128)(2,1)S(1)}, u32[]{:S(2)}, u32[]{:S(2)}) collective-permute-start(bf16[64,512]{1,0:T(8,128)(2,1)S(1)} %get-tuple-element.63), channel_id=1, source_target_pairs={{0,4},{1,5},{2,6},{3,7},{4,0},{5,1},{6,2},{7,3},{8,12},{9,13},{10,... | collective-permute-start | bytes 196616 | tf_op jit(solution)/shard_map/ppermute | solution.py:35
  39.1 5.7 %collective-permute-start.12 = (bf16[64,512]{1,0:T(8,128)(2,1)S(1)}, bf16[64,512]{1,0:T(8,128)(2,1)S(1)}, u32[]{:S(2)}, u32[]{:S(2)}) collective-permute-start(bf16[64,512]{1,0:T(8,128)(2,1)S(1)} %get-tuple-element.54), channel_id=1, source_target_pairs={{0,4},{1,5},{2,6},{3,7},{4,0},{5,1},{6,2},{7,3},{8,12},{9,13},{10,... | collective-permute-start | bytes 196616 | tf_op jit(solution)/shard_map/ppermute | solution.py:35
